TPU v7x, 32 devices: a whole 2x2x4 slice. The times are simulated.
32 devices in a mesh: groups: 2 (over x), expert: 8 (over z, y), dp: 2 (over core).
Axes of the slice: x: 2, y: 2, z: 4, core: 2. Of those that a mesh axis runs over, the one named last changes fastest.
Arguments:
- tokens: bfloat16 [1024, 3584], P(('groups', 'expert', 'dp')), parts along dimension 0, may hold values from -6 to 6
- cotangent: bfloat16 [1024, 3584], P(('groups', 'expert', 'dp')), parts along dimension 0, may hold values from -60 to 60
- expert_choice_index: int32 [1024, 8], P(('groups', 'expert', 'dp')), parts along dimension 0, may hold values from 0 to 15, all different within a row; in each aligned block of 32 rows (0 to 31, 32 to 63, ...) at most 16 rows name the same one
- capacity: int32 [32], P(('groups', 'expert', 'dp')), parts along dimension 0, may hold values from 128 to 384, as said below
- router_matrix: bfloat16 [3584, 16], replicated, may hold values from -0.09375 to 0.09375
- gate_matrix: bfloat16 [16, 3584, 1024], P(('expert', 'dp')), may hold values from -0.09375 to 0.09375
- up_matrix: bfloat16 [16, 3584, 1024], P(('expert', 'dp')), may hold values from -0.09375 to 0.09375
- down_matrix: bfloat16 [16, 1024, 3584], P(('expert', 'dp')), may hold values from -0.1875 to 0.1875
- up_adapter_first: bfloat16 [16, 3584, 64], P(('expert', 'dp')), may hold values from -0.09375 to 0.09375
- up_adapter_second: bfloat16 [16, 64, 1024], P(('expert', 'dp')), may hold values from -0.75 to 0.75
- down_adapter_first: bfloat16 [16, 1024, 64], P(('expert', 'dp')), may hold values from -0.1875 to 0.1875
- down_adapter_second: bfloat16 [16, 64, 3584], P(('expert', 'dp')), may hold values from -0.75 to 0.75
Outputs:
- mixed: bfloat16 [1024, 3584], P(('groups', 'expert', 'dp')), parts along dimension 0
- input_grad: bfloat16 [1024, 3584], P(('groups', 'expert', 'dp')), parts along dimension 0
- router_grad: float32 [7168, 16], P('groups'), parts along dimension 0
- grad_up_a: bfloat16 [32, 3584, 64], P(('groups', 'expert', 'dp')), parts along dimension 0
- grad_up_b: bfloat16 [32, 64, 1024], P(('groups', 'expert', 'dp')), parts along dimension 0
- grad_down_a: bfloat16 [32, 1024, 64], P(('groups', 'expert', 'dp')), parts along dimension 0
- grad_down_b: bfloat16 [32, 64, 3584], P(('groups', 'expert', 'dp')), parts along dimension 0
There are 2 independent parts, one for each index of `groups`. A program takes and returns all parts, laid end to end along the dimension named above; an argument that names none is the same for every part. Nothing has to cross between parts.
Inputs may be any that keep to these rules, and one draw needn't show every extreme that they name: `expert_choice_index`: each token names 8 different experts. Among the tokens of one device no expert is named more than 16 times, a bound that some block reaches. Some expert has capacity exactly 384.
All inputs are finite; a program needn't handle non-finite values.
Results may differ from a plain program's by a relative error of at most 0.015.
Values may be sent and summed in bfloat16 or wider, within the bound.
No kernel may reach another device: no remote copies, remote signals or barrier semaphores. Data moves between devices by JAX's collectives and lax.ppermute only.
A program may use at most 128 MiB of HBM per device.

v0:
```python
import jax
import jax.numpy as jnp
from jax import lax
from jax.sharding import PartitionSpec as P

MOST = 16


route_scale = 2.5
adapter_scale = 2.0


def contract_product(left_side, right_side, axes_pair):
    return lax.dot_general(
        left_side,
        right_side,
        ((axes_pair[0], axes_pair[1]), ((), ())),
        preferred_element_type=jnp.float32,
    )


def silu_parts(pre_act):
    logistic = jax.nn.sigmoid(pre_act)
    return (pre_act * logistic, logistic * (1.0 + pre_act * (1.0 - logistic)))


def expert_forward(block_of_rows, mask_of_rows, weight_bundle):
    (
        gate_weight_local,
        up_weight_local,
        down_weight_local,
        up_factor_first,
        up_factor_second,
        down_factor_first,
        down_factor_second,
    ) = weight_bundle
    lowrank_upward = contract_product(block_of_rows, up_factor_first, ((1,), (0,))).astype(
        jnp.bfloat16
    )
    pre_gate = contract_product(block_of_rows, gate_weight_local, ((1,), (0,)))
    upward_preactivation = contract_product(
        block_of_rows, up_weight_local, ((1,), (0,))
    ) + adapter_scale * contract_product(lowrank_upward, up_factor_second, ((1,), (0,)))
    active, gate_slope = silu_parts(pre_gate)
    inner_activation = (active * upward_preactivation).astype(jnp.bfloat16)
    lowrank_downward = contract_product(inner_activation, down_factor_first, ((1,), (0,))).astype(
        jnp.bfloat16
    )
    final_output = (
        mask_of_rows[:, None]
        * (
            contract_product(inner_activation, down_weight_local, ((1,), (0,)))
            + adapter_scale * contract_product(lowrank_downward, down_factor_second, ((1,), (0,)))
        )
    ).astype(jnp.bfloat16)
    return (
        final_output,
        (
            block_of_rows,
            lowrank_upward,
            upward_preactivation,
            active,
            gate_slope,
            inner_activation,
            lowrank_downward,
        ),
    )


def expert_reverse_pass(stored_state, output_gradient, weight_bundle):
    (
        block_of_rows,
        lowrank_upward,
        upward_preactivation,
        active,
        gate_slope,
        inner_activation,
        lowrank_downward,
    ) = stored_state
    (
        gate_weight_local,
        up_weight_local,
        down_weight_local,
        up_factor_first,
        up_factor_second,
        down_factor_first,
        down_factor_second,
    ) = weight_bundle
    backward_lowrank = contract_product(output_gradient, down_factor_second, ((1,), (1,))).astype(
        jnp.bfloat16
    )
    inner_gradient = contract_product(
        output_gradient, down_weight_local, ((1,), (1,))
    ) + adapter_scale * contract_product(backward_lowrank, down_factor_first, ((1,), (1,)))
    gate_gradient = (inner_gradient * upward_preactivation * gate_slope).astype(jnp.bfloat16)
    upward_gradient = (inner_gradient * active).astype(jnp.bfloat16)
    backward_upward = contract_product(upward_gradient, up_factor_second, ((1,), (1,))).astype(
        jnp.bfloat16
    )
    backward_row_set = (
        contract_product(gate_gradient, gate_weight_local, ((1,), (1,)))
        + contract_product(upward_gradient, up_weight_local, ((1,), (1,)))
        + adapter_scale * contract_product(backward_upward, up_factor_first, ((1,), (1,)))
    ).astype(jnp.bfloat16)
    adapter_gradient_set = (
        adapter_scale * contract_product(block_of_rows, backward_upward, ((0,), (0,))),
        adapter_scale * contract_product(lowrank_upward, upward_gradient, ((0,), (0,))),
        adapter_scale * contract_product(inner_activation, backward_lowrank, ((0,), (0,))),
        adapter_scale * contract_product(lowrank_downward, output_gradient, ((0,), (0,))),
    )
    return (backward_row_set, adapter_gradient_set)


def arrange(keep_flag):
    return (None, keep_flag.astype(jnp.float32))


def per_device(
    tokens,
    cotangent,
    expert_choice_index,
    capacity,
    router_matrix,
    gate_matrix,
    up_matrix,
    down_matrix,
    up_adapter_first,
    up_adapter_second,
    down_adapter_first,
    down_adapter_second,
):
    tok_count, feat_width = tokens.shape
    top_count = expert_choice_index.shape[1]
    expert_group = router_matrix.shape[1]
    slot_count = expert_group * MOST
    logits = jnp.dot(tokens, router_matrix, preferred_element_type=jnp.float32)
    affinity = jax.nn.sigmoid(logits)
    hit_table = (
        expert_choice_index[:, :, None] == jnp.arange(expert_group, dtype=jnp.int32)[None, None, :]
    ).astype(jnp.int32)
    hit_float = hit_table.astype(jnp.float32)
    chosen = jnp.sum(hit_float * affinity[:, None, :], axis=2)
    chosen_sum = jnp.sum(chosen, axis=1, keepdims=True)
    gate_vals = route_scale * chosen / chosen_sum
    per_token = jnp.sum(hit_table, axis=1)
    earlier = jnp.cumsum(per_token, axis=0, dtype=jnp.int32) - per_token
    position = jnp.sum(hit_table * earlier[:, None, :], axis=2)
    target = (expert_choice_index * MOST + position).reshape(-1)
    slot_table = target[:, None] == jnp.arange(slot_count, dtype=jnp.int32)[None, :]
    select = slot_table.astype(jnp.bfloat16)
    spread = jnp.sum(select.reshape(tok_count, top_count, slot_count), axis=1)
    valid_flag = jnp.sum(slot_table.astype(jnp.int32), axis=0).reshape(expert_group, MOST)
    send_rows = (
        contract_product(spread, tokens, ((0,), (0,)))
        .astype(jnp.bfloat16)
        .reshape(expert_group, MOST, feat_width)
    )
    cot_float = cotangent.astype(jnp.float32)
    scaled = (
        (gate_vals[:, :, None] * cot_float[:, None, :])
        .astype(jnp.bfloat16)
        .reshape(tok_count * top_count, feat_width)
    )
    send_grads = (
        contract_product(select, scaled, ((0,), (0,)))
        .astype(jnp.bfloat16)
        .reshape(expert_group, MOST, feat_width)
    )
    weight_bundle = (
        gate_matrix[0],
        up_matrix[0],
        down_matrix[0],
        up_adapter_first[0],
        up_adapter_second[0],
        down_adapter_first[0],
        down_adapter_second[0],
    )
    cap_here = capacity[0]
    arrived_rows, arrived_valid = (
        lax.all_to_all(send_rows, ("expert", "dp"), split_axis=0, concat_axis=0, tiled=True),
        lax.all_to_all(valid_flag, ("expert", "dp"), split_axis=0, concat_axis=0, tiled=True),
    )
    flat_valid = arrived_valid.reshape(-1)
    slot_rank = jnp.cumsum(flat_valid, dtype=jnp.int32) - flat_valid
    keep_flag, slot_rank = (flat_valid * (slot_rank < cap_here).astype(jnp.int32), slot_rank)
    layout, mask_of_rows = arrange(keep_flag)
    final_output, stored_state = expert_forward(
        arrived_rows.reshape(-1, feat_width), mask_of_rows, weight_bundle
    )
    returned = lax.all_to_all(
        final_output.reshape(expert_group, MOST, feat_width),
        ("expert", "dp"),
        split_axis=0,
        concat_axis=0,
        tiled=True,
    )
    arrived_grads = lax.all_to_all(
        send_grads, ("expert", "dp"), split_axis=0, concat_axis=0, tiled=True
    )
    output_gradient = (
        arrived_grads.reshape(-1, feat_width) * mask_of_rows.astype(jnp.bfloat16)[:, None]
    )
    backward_row_set, adapter_gradient_set = expert_reverse_pass(
        stored_state, output_gradient, weight_bundle
    )
    returned_back = lax.all_to_all(
        backward_row_set.reshape(expert_group, MOST, feat_width),
        ("expert", "dp"),
        split_axis=0,
        concat_axis=0,
        tiled=True,
    )
    outputs = contract_product(
        select, returned.reshape(slot_count, feat_width), ((1,), (0,))
    ).reshape(tok_count, top_count, feat_width)
    mixed = jnp.sum(gate_vals[:, :, None] * outputs, axis=1).astype(jnp.bfloat16)
    grad_gates = jnp.sum(cot_float[:, None, :] * outputs, axis=2)
    grad_chosen = route_scale * (
        grad_gates / chosen_sum
        - jnp.sum(grad_gates * chosen, axis=1, keepdims=True) / (chosen_sum * chosen_sum)
    )
    grad_logits = (
        jnp.sum(hit_float * grad_chosen[:, :, None], axis=1) * affinity * (1.0 - affinity)
    ).astype(jnp.bfloat16)
    back_slots = contract_product(
        select, returned_back.reshape(slot_count, feat_width), ((1,), (0,))
    ).reshape(tok_count, top_count, feat_width)
    input_grad = (
        jnp.sum(back_slots, axis=1) + contract_product(grad_logits, router_matrix, ((1,), (1,)))
    ).astype(jnp.bfloat16)
    router_term = contract_product(tokens, grad_logits, ((0,), (0,)))
    router_grad = lax.psum(router_term.astype(jnp.bfloat16), ("expert", "dp")).astype(jnp.float32)
    return (
        mixed,
        input_grad,
        router_grad,
        adapter_gradient_set[0].astype(jnp.bfloat16)[None],
        adapter_gradient_set[1].astype(jnp.bfloat16)[None],
        adapter_gradient_set[2].astype(jnp.bfloat16)[None],
        adapter_gradient_set[3].astype(jnp.bfloat16)[None],
    )


def solution(mesh):
    placed = (
        P(("groups", "expert", "dp"), None),
        P(("groups", "expert", "dp"), None),
        P(("groups", "expert", "dp"), None),
        P(("groups", "expert", "dp")),
        P(),
        P(("expert", "dp"), None, None),
        P(("expert", "dp"), None, None),
        P(("expert", "dp"), None, None),
        P(("expert", "dp"), None, None),
        P(("expert", "dp"), None, None),
        P(("expert", "dp"), None, None),
        P(("expert", "dp"), None, None),
    )
    return jax.shard_map(
        per_device,
        mesh=mesh,
        in_specs=placed,
        out_specs=(
            P(("groups", "expert", "dp"), None),
            P(("groups", "expert", "dp"), None),
            P("groups", None),
            P(("groups", "expert", "dp"), None, None),
            P(("groups", "expert", "dp"), None, None),
            P(("groups", "expert", "dp"), None, None),
            P(("groups", "expert", "dp"), None, None),
        ),
        check_vma=False,
    )
```

profile of v0, /device:TPU:0, one launch (start us, length us, event | category | flops | bytes accessed | tf_op | source)
XLA Modules:
  0.0 299.4 jit_solution(13841585739299947279)
XLA Ops:
  10.6 7.4 %all-to-all-start = ((s32[16,1,16]{2,1,0:T(1,128)}), s32[16,1,16]{2,1,0:T(1,128)S(1)}, u32[]{:S(2)}, u32[]{:S(2)}) async-start(s32[16,1,16]{2,1,0:T(1,128)} %all_to_all.18), calls=%async_computation | async-start | bytes 16384 | tf_op jit(solution)/shard_map/all_to_all | solution.py:181
  18.2 2.8 convolution_convert_fusion.1
  21.0 3.3 %all-to-all-done = s32[16,1,16]{2,1,0:T(1,128)S(1)} async-done(((s32[16,1,16]{2,1,0:T(1,128)}), s32[16,1,16]{2,1,0:T(1,128)S(1)}, u32[]{:S(2)}, u32[]{:S(2)}) %all-to-all-start) | async-done | bytes 1056 | tf_op jit(solution)/shard_map/all_to_all | solution.py:181
  24.3 3.7 %all-to-all-start.1 = ((bf16[16,16,3584]{2,1,0:T(8,128)(2,1)}), bf16[16,16,3584]{2,1,0:T(8,128)(2,1)S(1)}, u32[]{:S(2)}, u32[]{:S(2)}) async-start(bf16[16,16,3584]{2,1,0:T(8,128)(2,1)} %bitcast.121), calls=%async_computation.1 | async-start | bytes 3670016 | tf_op jit(solution)/shard_map/all_to_all | solution.py:180
  29.9 2.0 convolution_convert_fusion
  32.0 32.6 %all-to-all-done.1 = bf16[16,16,3584]{2,1,0:T(8,128)(2,1)S(1)} async-done(((bf16[16,16,3584]{2,1,0:T(8,128)(2,1)}), bf16[16,16,3584]{2,1,0:T(8,128)(2,1)S(1)}, u32[]{:S(2)}, u32[]{:S(2)}) %all-to-all-start.1) | async-done | bytes 1835040 | tf_op jit(solution)/shard_map/all_to_all | solution.py:180
  64.5 10.2 %all-to-all-start.3 = ((bf16[16,16,3584]{2,1,0:T(8,128)(2,1)}), bf16[16,16,3584]{2,1,0:T(8,128)(2,1)}, u32[]{:S(2)}, u32[]{:S(2)}) async-start(bf16[16,16,3584]{2,1,0:T(8,128)(2,1)} %bitcast.120), calls=%async_computation.3 | async-start | bytes 3670016 | tf_op jit(solution)/shard_map/all_to_all | solution.py:197
  78.9 6.5 %fusion.10 = f32[256,1024]{1,0:T(8,128)} fusion(bf16[256,3584]{1,0:T(8,128)(2,1)S(1)} %bitcast.116, bf16[1,3584,1024]{2,1,0:T(8,128)(2,1)} %param.17), kind=kOutput, calls=%fused_computation.10 | convolution fusion | flops 1879048192 | bytes 10223616 | tf_op jit(solution)/shard_map/dot_general | solution.py:14
  85.4 3.1 %fusion.6 = f32[256,1024]{1,0:T(8,128)} fusion(bf16[256,3584]{1,0:T(8,128)(2,1)S(1)} %bitcast.117, bf16[1,3584,1024]{2,1,0:T(8,128)(2,1)S(1)} %bitcast.130), kind=kOutput, calls=%fused_computation.6 | convolution fusion | flops 1879048192 | bytes 10223616 | tf_op jit(solution)/shard_map/dot_general | solution.py:14
  88.5 22.8 %all-to-all-done.3 = bf16[16,16,3584]{2,1,0:T(8,128)(2,1)} async-done(((bf16[16,16,3584]{2,1,0:T(8,128)(2,1)}), bf16[16,16,3584]{2,1,0:T(8,128)(2,1)}, u32[]{:S(2)}, u32[]{:S(2)}) %all-to-all-start.3) | async-done | bytes 1835040 | tf_op jit(solution)/shard_map/all_to_all | solution.py:197
  113.8 5.7 %fusion = f32[256,1024]{1,0:T(8,128)S(1)} fusion(bf16[256,3584]{1,0:T(8,128)(2,1)S(1)} %bitcast.124, bf16[1,1024,3584]{2,1,0:T(8,128)(2,1)} %param.19), kind=kOutput, calls=%fused_computation | convolution fusion | flops 1879048192 | bytes 10223616 | tf_op jit(solution)/shard_map/dot_general | solution.py:14
  119.9 1.7 multiply_convert_fusion
  121.9 2.1 fusion.2
  124.0 2.0 fusion.18
  125.9 10.2 %all-to-all-start.2 = ((bf16[16,16,3584]{2,1,0:T(8,128)(2,1)}), bf16[16,16,3584]{2,1,0:T(8,128)(2,1)}, u32[]{:S(2)}, u32[]{:S(2)}) async-start(bf16[16,16,3584]{2,1,0:T(8,128)(2,1)} %bitcast.122), calls=%async_computation.2 | async-start | bytes 3670016 | tf_op jit(solution)/shard_map/all_to_all | solution.py:190
  137.5 5.5 %fusion.4 = f32[256,3584]{1,0:T(8,128)S(1)} fusion(bf16[256,1024]{1,0:T(8,128)(2,1)} %get-tuple-element.13, bf16[1,3584,1024]{2,1,0:T(8,128)(2,1)} %param.18), kind=kOutput, calls=%fused_computation.4 | convolution fusion | flops 1879048192 | bytes 11534336 | tf_op jit(solution)/shard_map/dot_general | solution.py:14
  143.0 5.5 %fusion.15 = f32[256,3584]{1,0:T(8,128)S(1)} fusion(f32[256,3584]{1,0:T(8,128)S(1)} %fusion.4, bf16[1,3584,1024]{2,1,0:T(8,128)(2,1)} %param.17, f32[256,1024]{1,0:T(8,128)S(1)} %copy-done.11, f32[256,1024]{1,0:T(8,128)S(1)} %copy-done.12, f32[256,1024]{1,0:T(8,128)S(1)} %fusion.31), kind=kOutput, calls=%fused_computation.17 | convolution fusion | flops 1882587136 | bytes 17825792 | tf_op jit(solution)/shard_map/dot_general | solution.py:14
  148.6 1.9 fusion.19
  150.5 22.2 %all-to-all-done.2 = bf16[16,16,3584]{2,1,0:T(8,128)(2,1)} async-done(((bf16[16,16,3584]{2,1,0:T(8,128)(2,1)}), bf16[16,16,3584]{2,1,0:T(8,128)(2,1)}, u32[]{:S(2)}, u32[]{:S(2)}) %all-to-all-start.2) | async-done | bytes 1835040 | tf_op jit(solution)/shard_map/all_to_all | solution.py:190
  172.8 10.3 %all-to-all-start.4 = ((bf16[16,16,3584]{2,1,0:T(8,128)(2,1)}), bf16[16,16,3584]{2,1,0:T(8,128)(2,1)}, u32[]{:S(2)}, u32[]{:S(2)}) async-start(bf16[16,16,3584]{2,1,0:T(8,128)(2,1)} %bitcast.119), calls=%async_computation.4 | async-start | bytes 3670016 | tf_op jit(solution)/shard_map/all_to_all | solution.py:206
  189.1 3.9 %multiply_reduce_fusion = (f32[32,8]{1,0:T(8,128)S(1)}, bf16[32,3584]{1,0:T(8,128)(2,1)}) fusion(f32[32,3584]{1,0:T(8,128)S(1)} %copy-done.9, f32[32,8]{1,0:T(8,128)S(1)} %copy-done.28, bf16[256,3584,1]{1,0,2:T(8,128)(2,1)} %bitcast.14, s32[32,8]{1,0:T(8,128)S(1)} %copy.45), kind=kOutput, calls=%fused_computation.34 | convolution fusion | flops 473382656 | bytes 2526208 | tf_op jit(solution)/shard_map/dot_general | solution.py:14
  194.0 26.3 %all-to-all-done.4 = bf16[16,16,3584]{2,1,0:T(8,128)(2,1)} async-done(((bf16[16,16,3584]{2,1,0:T(8,128)(2,1)}), bf16[16,16,3584]{2,1,0:T(8,128)(2,1)}, u32[]{:S(2)}, u32[]{:S(2)}) %all-to-all-start.4) | async-done | bytes 1835040 | tf_op jit(solution)/shard_map/all_to_all | solution.py:206
  220.4 2.7 convolution_reduce_fusion
  224.0 67.0 %all-reduce.2.cloned.1.call-done = bf16[3584,16]{0,1:T(8,128)(2,1)} async-done(((bf16[3584,16]{0,1:T(8,128)(2,1)}), bf16[3584,16]{0,1:T(8,128)(2,1)}) %all-reduce.2.cloned.1.call-update) | async-done | bytes 114704 | tf_op jit(solution)/shard_map/psum | solution.py:232
  (133 shorter events, 22.6 us)
Async XLA Ops:
  7.2 105.9 %copy-start = (bf16[1,64,3584]{2,1,0:T(8,128)(2,1)S(1)}, bf16[1,64,3584]{2,1,0:T(8,128)(2,1)}, u32[]{:S(2)}) copy-start(bf16[1,64,3584]{2,1,0:T(8,128)(2,1)} %param.23) | copy-start | bytes 1376260
  7.2 21.1 %copy-start.23 = (s32[32,8]{0,1:T(8,128)S(1)}, s32[32,8]{0,1:T(8,128)}, u32[]{:S(2)}) copy-start(s32[32,8]{0,1:T(8,128)} %param.14) | copy-start | bytes 3076
  7.2 20.9 %copy-start.4 = (bf16[32,3584]{1,0:T(8,128)(2,1)S(1)}, bf16[32,3584]{1,0:T(8,128)(2,1)}, u32[]{:S(2)}) copy-start(bf16[32,3584]{1,0:T(8,128)(2,1)} %param.12) | copy-start | bytes 688132
  7.2 20.9 %copy-start.15 = (bf16[3584,16]{0,1:T(8,128)(2,1)S(1)}, bf16[3584,16]{0,1:T(8,128)(2,1)}, u32[]{:S(2)}) copy-start(bf16[3584,16]{0,1:T(8,128)(2,1)} %param.16) | copy-start | bytes 344068
  7.2 21.9 %copy-start.19 = (bf16[32,3584]{1,0:T(8,128)(2,1)S(1)}, bf16[32,3584]{1,0:T(8,128)(2,1)}, u32[]{:S(2)}) copy-start(bf16[32,3584]{1,0:T(8,128)(2,1)} %param.13) | copy-start | bytes 688132
  10.6 13.7 %all-to-all-start = ((s32[16,1,16]{2,1,0:T(1,128)}), s32[16,1,16]{2,1,0:T(1,128)S(1)}, u32[]{:S(2)}, u32[]{:S(2)}) async-start(s32[16,1,16]{2,1,0:T(1,128)} %all_to_all.18), calls=%async_computation | async-start | bytes 16384 | tf_op jit(solution)/shard_map/all_to_all | solution.py:181
  24.3 40.2 %all-to-all-start.1 = ((bf16[16,16,3584]{2,1,0:T(8,128)(2,1)}), bf16[16,16,3584]{2,1,0:T(8,128)(2,1)S(1)}, u32[]{:S(2)}, u32[]{:S(2)}) async-start(bf16[16,16,3584]{2,1,0:T(8,128)(2,1)} %bitcast.121), calls=%async_computation.1 | async-start | bytes 3670016 | tf_op jit(solution)/shard_map/all_to_all | solution.py:180
  28.1 50.1 %copy-start.6 = (bf16[1,3584,64]{1,2,0:T(8,128)(2,1)S(1)}, bf16[1,3584,64]{1,2,0:T(8,128)(2,1)}, u32[]{:S(2)}) copy-start(bf16[1,3584,64]{1,2,0:T(8,128)(2,1)} %param.20) | copy-start | bytes 1376260
  28.3 50.6 %copy-start.25 = (f32[32,16]{0,1:T(8,128)}, f32[32,16]{0,1:T(8,128)S(1)}, u32[]{:S(2)}) copy-start(f32[32,16]{0,1:T(8,128)S(1)} %fusion.38) | copy-start | bytes 6148
  28.3 47.0 %copy-start.31 = (f32[32]{0:T(128)}, f32[32]{0:T(128)S(1)}, u32[]{:S(2)}) copy-start(f32[32]{0:T(128)S(1)} %get-tuple-element.9) | copy-start | bytes 388
  29.0 49.9 %copy-start.27 = (f32[32,8]{1,0:T(8,128)}, f32[32,8]{1,0:T(8,128)S(1)}, u32[]{:S(2)}) copy-start(f32[32,8]{1,0:T(8,128)S(1)} %copy.41) | copy-start | bytes 3076
  64.5 46.8 %all-to-all-start.3 = ((bf16[16,16,3584]{2,1,0:T(8,128)(2,1)}), bf16[16,16,3584]{2,1,0:T(8,128)(2,1)}, u32[]{:S(2)}, u32[]{:S(2)}) async-start(bf16[16,16,3584]{2,1,0:T(8,128)(2,1)} %bitcast.120), calls=%async_computation.3 | async-start | bytes 3670016 | tf_op jit(solution)/shard_map/all_to_all | solution.py:197
  113.0 8.8 %slice-start = ((s8[7340032]{0:T(1024)(128)(4,1)}), s8[4194304]{0:T(1024)(128)(4,1)S(1)}, s32[]{:S(2)}) async-start(s8[7340032]{0:T(1024)(128)(4,1)} %bitcast.127), calls=%async_computation.6 | async-start | bytes 8388608
  113.8 8.1 %slice-start.1 = ((s8[7340032]{0:T(1024)(128)(4,1)}), s8[3145728]{0:T(1024)(128)(4,1)S(1)}, s32[]{:S(2)}) async-start(s8[7340032]{0:T(1024)(128)(4,1)} %bitcast.127), calls=%async_computation.7 | async-start | bytes 6291456
  125.9 46.8 %all-to-all-start.2 = ((bf16[16,16,3584]{2,1,0:T(8,128)(2,1)}), bf16[16,16,3584]{2,1,0:T(8,128)(2,1)}, u32[]{:S(2)}, u32[]{:S(2)}) async-start(bf16[16,16,3584]{2,1,0:T(8,128)(2,1)} %bitcast.122), calls=%async_computation.2 | async-start | bytes 3670016 | tf_op jit(solution)/shard_map/all_to_all | solution.py:190
  137.5 11.1 %copy-start.17 = (bf16[256,64]{0,1:T(8,128)(2,1)}, bf16[256,64]{0,1:T(8,128)(2,1)S(1)}, u32[]{:S(2)}) copy-start(bf16[256,64]{0,1:T(8,128)(2,1)S(1)} %convolution_convert_fusion.3) | copy-start | bytes 98308
  148.6 34.5 %copy-start.3 = (bf16[256,1024]{1,0:T(8,128)(2,1)S(1)}, bf16[256,1024]{1,0:T(8,128)(2,1)}, u32[]{:S(2)}) copy-start(bf16[256,1024]{1,0:T(8,128)(2,1)} %get-tuple-element.13) | copy-start | bytes 1572868
  150.5 33.5 %copy-start.2 = (bf16[256,1024]{1,0:T(8,128)(2,1)S(1)}, bf16[256,1024]{1,0:T(8,128)(2,1)}, u32[]{:S(2)}) copy-start(bf16[256,1024]{1,0:T(8,128)(2,1)} %copy-done.1) | copy-start | bytes 1572868
  150.5 33.5 %copy-start.21 = (bf16[256,64]{0,1:T(8,128)(2,1)S(1)}, bf16[256,64]{0,1:T(8,128)(2,1)}, u32[]{:S(2)}) copy-start(bf16[256,64]{0,1:T(8,128)(2,1)} %copy-done.20) | copy-start | bytes 98308
  150.5 34.4 %copy-start.18 = (bf16[256,64]{0,1:T(8,128)(2,1)S(1)}, bf16[256,64]{0,1:T(8,128)(2,1)}, u32[]{:S(2)}) copy-start(bf16[256,64]{0,1:T(8,128)(2,1)} %copy-done.17) | copy-start | bytes 98308
  172.8 13.4 %copy-start.34 = (bf16[256]{0:T(256)(128)(2,1)S(1)}, bf16[256]{0:T(256)(128)(2,1)}, u32[]{:S(2)}) copy-start(bf16[256]{0:T(256)(128)(2,1)} %get-tuple-element.11) | copy-start | bytes 1540
  172.8 47.6 %all-to-all-start.4 = ((bf16[16,16,3584]{2,1,0:T(8,128)(2,1)}), bf16[16,16,3584]{2,1,0:T(8,128)(2,1)}, u32[]{:S(2)}, u32[]{:S(2)}) async-start(bf16[16,16,3584]{2,1,0:T(8,128)(2,1)} %bitcast.119), calls=%async_computation.4 | async-start | bytes 3670016 | tf_op jit(solution)/shard_map/all_to_all | solution.py:206
  183.1 107.9 %all-reduce.2.cloned.1.call-start = ((), (), s32[]{:S(2)}) async-start(), calls=%async_computation.5 | async-start | bytes 229376 | tf_op jit(solution)/shard_map/psum | solution.py:232
  189.1 34.0 %copy-start.16 = (bf16[3584,16]{0,1:T(8,128)(2,1)S(1)}, bf16[3584,16]{0,1:T(8,128)(2,1)}, u32[]{:S(2)}) copy-start(bf16[3584,16]{0,1:T(8,128)(2,1)} %param.16) | copy-start | bytes 344068
  (21 other events, 100.7 us)
Sparse Core Ops, SparseCore 0:
  194.1 96.7 all-reduce.1
where the time goes:
time: 302 us; the launch traced here: 299 us
  waiting for transfers between devices  174 us (58%)
  matrix products  54.7 us (18%)
  starting transfers between devices  41.9 us (14%)
  between operations  15.3 us (5%)
  other arithmetic  9.37 us (3%)
  local copies, waits for them, and re-layouts  3.87 us (1%)
    psum x1, waiting for transfers between devices, per_device(): lax.psum(router_term.astype(jnp.bfloat16), ('expert', 'dp'))  67 us
    dot_general x24, matrix products, contract_product(): lax.dot_general(left_side, right_side, ((axes_pair[0], axes_pair[1]), (()...  54.5 us
    all_to_all x1, waiting for transfers between devices, per_device(): lax.all_to_all(send_rows, ('expert', 'dp'), split_axis=0, concat_axis=0,...  32.6 us
    all_to_all x1, waiting for transfers between devices, per_device(): lax.all_to_all(backward_row_set.reshape(expert_group, MOST, feat_width),...  26.3 us
    all_to_all x1, waiting for transfers between devices, per_device(): lax.all_to_all(send_grads, ('expert', 'dp'), split_axis=0, concat_axis=0,...  22.8 us
    all_to_all x1, waiting for transfers between devices, per_device(): lax.all_to_all(final_output.reshape(expert_group, MOST, feat_width), ('ex...  22.2 us
    all_to_all x1, starting transfers between devices, per_device(): lax.all_to_all(backward_row_set.reshape(expert_group, MOST, feat_width),...  10.3 us
    all_to_all x1, starting transfers between devices, per_device(): lax.all_to_all(final_output.reshape(expert_group, MOST, feat_width), ('ex...  10.2 us
  transfers between devices with their start and end apart: 6, of which 6 were waited for; matrix products, arithmetic and copies ran while one was open for 16% of the time, Pallas kernels for 0%

commit v1 on v0

v1 whole, which is shorter than its diff:
```python
import jax
import jax.numpy as jnp
from jax import lax
from jax.sharding import PartitionSpec as P

MOST = 16
LANES = 128

route_scale = 2.5
adapter_scale = 2.0


def mm(left, right, axes):
    return lax.dot_general(
        left, right, ((axes[0], axes[1]), ((), ())), preferred_element_type=jnp.float32
    )


def silu_parts(pre_act):
    logistic = jax.nn.sigmoid(pre_act)
    return (pre_act * logistic, logistic * (1.0 + pre_act * (1.0 - logistic)))


def high_low(value):
    high = lax.reduce_precision(value, 8, 7)
    return high.astype(jnp.bfloat16), (value - high).astype(jnp.bfloat16)


def ring_of(count):
    if count == 8:
        order = [0, 2, 4, 6, 7, 5, 3, 1]
    else:
        order = list(range(count))
    ahead = [(order[i], order[(i + 1) % count]) for i in range(count)]
    back = [(b, a) for a, b in ahead]
    return order, ahead, back


def offsets_of(count):
    half = count // 2
    return [0] + [-k for k in range(1, half)] + list(range(1, half)) + [half]


def ring_gather(block, count):
    _, ahead, back = ring_of(count)
    half, rows = count // 2, block.shape[0] // 2
    from_behind, from_front = [block], [block]
    for _ in range(1, half):
        from_behind.append(lax.ppermute(from_behind[-1], "expert", ahead))
        from_front.append(lax.ppermute(from_front[-1], "expert", back))
    top = lax.ppermute(from_behind[-1][:rows], "expert", ahead)
    low = lax.ppermute(from_front[-1][rows:], "expert", back)
    return from_behind + from_front[1:] + [jnp.concatenate([top, low], axis=0)]


def ring_scatter(part_of, count, rows):
    _, ahead, back = ring_of(count)
    half = count // 2
    narrow = lambda v: v.astype(jnp.bfloat16)
    wide = lambda v: v.astype(jnp.float32)
    opposite = narrow(part_of(count - 1))
    forth = lax.ppermute(opposite[:rows], "expert", ahead)
    hither = lax.ppermute(opposite[rows:], "expert", back)
    for k in range(half - 1, 0, -1):
        front, rear = part_of(half - 1 + k), part_of(k)
        if k == half - 1:
            front = jnp.concatenate([front[:rows] + wide(forth), front[rows:]], axis=0)
            rear = jnp.concatenate([rear[:rows], rear[rows:] + wide(hither)], axis=0)
        else:
            front, rear = front + wide(forth), rear + wide(hither)
        forth = lax.ppermute(narrow(front), "expert", ahead)
        hither = lax.ppermute(narrow(rear), "expert", back)
    return part_of(0) + wide(forth) + wide(hither)


def swap_cores(value):
    return lax.ppermute(value, "dp", [(0, 1), (1, 0)])


def make_per_device(count):
    order, _, _ = ring_of(count)
    offsets = offsets_of(count)
    place = [order.index(chip) for chip in range(count)]

    def per_device(
        tokens,
        cotangent,
        expert_choice_index,
        capacity,
        router_matrix,
        gate_matrix,
        up_matrix,
        down_matrix,
        up_adapter_first,
        up_adapter_second,
        down_adapter_first,
        down_adapter_second,
    ):
        tok_count, width = tokens.shape
        experts = router_matrix.shape[1]
        bf16, f32 = jnp.bfloat16, jnp.float32
        chip, core = lax.axis_index("expert"), lax.axis_index("dp")
        position = jnp.asarray(place, jnp.int32)[chip]
        chips = jnp.asarray(order, jnp.int32)[
            (position + jnp.asarray(offsets, jnp.int32) + count) % count
        ]
        mine, other = 2 * chip + core, 2 * chip + 1 - core
        names = jnp.arange(experts, dtype=jnp.int32)
        own_name = (names == mine).astype(f32)
        sibling_name = (names == other).astype(f32)

        hits = jnp.sum(
            (expert_choice_index[:, :, None] == names[None, None, :]).astype(f32), axis=1
        )
        tail = (-(2 * experts)) % LANES
        token_tail = jnp.pad(hits.astype(bf16), ((0, 0), (0, experts + tail)))
        token_load = jnp.concatenate([tokens, token_tail], axis=1)
        logits = jnp.dot(tokens, router_matrix, preferred_element_type=f32)
        affinity = jax.nn.sigmoid(logits)
        chosen = hits * affinity
        chosen_sum = jnp.sum(chosen, axis=1, keepdims=True)
        gates = route_scale * chosen / chosen_sum
        gate_high, gate_low = high_low(gates)
        cot_load = jnp.concatenate(
            [cotangent, gate_high, gate_low, jnp.zeros((tok_count, tail), bf16)], axis=1
        )

        token_blocks = jnp.stack(ring_gather(token_load, count))
        cot_blocks = jnp.stack(ring_gather(cot_load, count))

        block_hits = token_blocks[:, :, width : width + experts].astype(f32)
        member = jnp.stack(
            [
                jnp.sum(block_hits * own_name, axis=2),
                jnp.sum(block_hits * sibling_name, axis=2),
            ],
            axis=1,
        )
        earlier = (
            jnp.arange(tok_count)[:, None] < jnp.arange(tok_count)[None, :]
        ).astype(bf16)
        before = lax.dot_general(
            member.astype(bf16), earlier, (((2,), (0,)), ((), ())), preferred_element_type=f32
        )
        spots = jnp.arange(MOST, dtype=jnp.int32).astype(f32)
        select = (
            jnp.where(before[:, :, None, :] == spots[None, None, :, None], 1.0, 0.0)
            * member[:, :, None, :]
        ).astype(bf16)
        select = select.reshape(count, 2 * MOST, tok_count)

        def to_slots(blocks):
            rows = lax.dot_general(
                select, blocks, (((2,), (1,)), ((0,), (0,))), preferred_element_type=f32
            ).astype(bf16)
            kept = rows[:, :MOST].reshape(count * MOST, -1)
            sent = rows[:, MOST:].reshape(count * MOST, -1)
            return jnp.concatenate([kept, swap_cores(sent)], axis=0)

        token_rows = to_slots(token_blocks)
        cot_rows = to_slots(cot_blocks)

        valid = jnp.sum(
            token_rows[:, width : width + experts].astype(f32) * own_name, axis=1
        ).reshape(2 * count, MOST)
        sources = jnp.concatenate([2 * chips + core, 2 * chips + 1 - core])
        loads = jnp.sum(valid, axis=1)
        ahead_of = jnp.sum(
            jnp.where(sources[None, :] < sources[:, None], loads[None, :], 0.0), axis=1
        )
        rank = ahead_of[:, None] + spots[None, :]
        keep = jnp.where(rank < capacity[0].astype(f32), valid, 0.0).reshape(-1)
        gate_cols = cot_rows[:, width : width + 2 * experts].astype(f32)
        slot_gate = jnp.sum(
            gate_cols * jnp.concatenate([own_name, own_name]), axis=1
        )

        block = token_rows[:, :width]
        cot_block = cot_rows[:, :width].astype(f32)
        gate_w, up_w, down_w = gate_matrix[0], up_matrix[0], down_matrix[0]
        up_a, up_b = up_adapter_first[0], up_adapter_second[0]
        down_a, down_b = down_adapter_first[0], down_adapter_second[0]

        low_up = mm(block, up_a, ((1,), (0,))).astype(bf16)
        pre_gate = mm(block, gate_w, ((1,), (0,)))
        pre_up = mm(block, up_w, ((1,), (0,))) + adapter_scale * mm(low_up, up_b, ((1,), (0,)))
        active, gate_slope = silu_parts(pre_gate)
        inner = (active * pre_up).astype(bf16)
        low_down = mm(inner, down_a, ((1,), (0,))).astype(bf16)
        routed = (
            keep[:, None]
            * (
                mm(inner, down_w, ((1,), (0,)))
                + adapter_scale * mm(low_down, down_b, ((1,), (0,)))
            )
        ).astype(bf16)
        routed_f32 = routed.astype(f32)
        slot_dots = jnp.sum(cot_block * routed_f32, axis=1)
        dot_high, dot_low = high_low(slot_dots)
        weighted = jnp.concatenate(
            [
                (slot_gate[:, None] * routed_f32).astype(bf16),
                dot_high[:, None] * own_name.astype(bf16)[None, :],
                dot_low[:, None] * own_name.astype(bf16)[None, :],
                jnp.zeros((2 * count * MOST, tail), bf16),
            ],
            axis=1,
        )

        def to_tokens(rows):
            kept = rows[: count * MOST].reshape(count, MOST, -1)
            came = swap_cores(rows[count * MOST :]).reshape(count, MOST, -1)
            both = jnp.concatenate([kept, came], axis=1)

            def part_of(i):
                return mm(select[i], both[i], ((0,), (0,)))

            return ring_scatter(part_of, count, tok_count // 2)

        mixed_all = to_tokens(weighted)
        mixed = mixed_all[:, :width].astype(bf16)

        grad_routed = (keep[:, None] * (slot_gate[:, None] * cot_block)).astype(bf16)
        back_low = mm(grad_routed, down_b, ((1,), (1,))).astype(bf16)
        grad_inner = mm(grad_routed, down_w, ((1,), (1,))) + adapter_scale * mm(
            back_low, down_a, ((1,), (1,))
        )
        grad_gate = (grad_inner * pre_up * gate_slope).astype(bf16)
        grad_up = (grad_inner * active).astype(bf16)
        back_up = mm(grad_up, up_b, ((1,), (1,))).astype(bf16)
        back_routed = (
            mm(grad_gate, gate_w, ((1,), (1,)))
            + mm(grad_up, up_w, ((1,), (1,)))
            + adapter_scale * mm(back_up, up_a, ((1,), (1,)))
        ).astype(bf16)
        back_all = to_tokens(back_routed)
        grad_up_a = adapter_scale * mm(block, back_up, ((0,), (0,)))
        grad_up_b = adapter_scale * mm(low_up, grad_up, ((0,), (0,)))
        grad_down_a = adapter_scale * mm(inner, back_low, ((0,), (0,)))
        grad_down_b = adapter_scale * mm(low_down, grad_routed, ((0,), (0,)))

        grad_gates = (
            mixed_all[:, width : width + experts]
            + mixed_all[:, width + experts : width + 2 * experts]
        )
        grad_chosen = route_scale * (
            grad_gates / chosen_sum
            - jnp.sum(grad_gates * chosen, axis=1, keepdims=True) / (chosen_sum * chosen_sum)
        )
        grad_logits = (hits * grad_chosen * affinity * (1.0 - affinity)).astype(bf16)
        input_grad = (back_all + mm(grad_logits, router_matrix, ((1,), (1,)))).astype(bf16)
        gathered, step = grad_logits[None], 1
        while step < count:
            came = lax.ppermute(gathered, "expert", [(i, i ^ step) for i in range(count)])
            gathered = jnp.concatenate([gathered, came], axis=0)
            step *= 2
        pick = ((chips ^ chip)[:, None] == jnp.arange(count, dtype=jnp.int32)[None, :]).astype(bf16)
        ordered = mm(pick, gathered.reshape(count, -1), ((1,), (0,))).astype(bf16)
        router_half = mm(
            ordered.reshape(count * tok_count, experts),
            token_blocks[:, :, :width].reshape(count * tok_count, width),
            ((0,), (0,)),
        )
        router_grad = (router_half + swap_cores(router_half)).T
        return (
            mixed,
            input_grad,
            router_grad,
            grad_up_a.astype(bf16)[None],
            grad_up_b.astype(bf16)[None],
            grad_down_a.astype(bf16)[None],
            grad_down_b.astype(bf16)[None],
        )

    return per_device


def solution(mesh):
    rows = P(("groups", "expert", "dp"), None)
    whole = P(("groups", "expert", "dp"), None, None)
    weight = P(("expert", "dp"), None, None)
    return jax.shard_map(
        make_per_device(mesh.shape["expert"]),
        mesh=mesh,
        in_specs=(rows, rows, rows, P(("groups", "expert", "dp")), P()) + (weight,) * 7,
        out_specs=(rows, rows, P("groups", None), whole, whole, whole, whole),
        check_vma=False,
    )
```

time: 302 us -> 161 us (0.53)
  waiting for transfers between devices: 174 us -> 39.5 us
  local copies, waits for them, and re-layouts: 3.87 us -> 20.6 us
  between operations: 15.3 us -> 2.3 us
  matrix products: 54.7 us -> 46.2 us
  other arithmetic: 9.37 us -> 12.5 us
    all_to_all x5 -> x0, waiting for transfers between devices: 107 us -> none  [the longest x1 32.6 us: per_device(): lax.all_to_all(send_rows, ('expert', 'dp'), split_axis=0, concat_axis=0,...]
    psum x1 -> x0, waiting for transfers between devices: 67 us -> none  [per_device(): lax.psum(router_term.astype(jnp.bfloat16), ('expert', 'dp'))]
    all_to_all x5 -> x0, starting transfers between devices: 41.8 us -> none  [the longest x1 10.3 us: per_device(): lax.all_to_all(backward_row_set.reshape(expert_group, MOST, feat_width),...]
    ppermute x0 -> x40, waiting for transfers between devices: none -> 39.5 us  [the longest x6 13.6 us: ring_scatter(): forth = lax.ppermute(narrow(front), 'expert', ahead)]
    ppermute x0 -> x40, starting transfers between devices: none -> 39.1 us  [the longest x6 13.1 us: ring_gather(): from_behind.append(lax.ppermute(from_behind[-1], 'expert', ahead))]
    dot_general x25 -> x41, matrix products: 54.7 us -> 46.2 us  [the longest x37 42.9 us: mm(): lax.dot_general(left, right, ((axes[0], axes[1]), ((), ())), preferred_el...]
    slice x1 -> x17, local copies, waits for them, and re-layouts: 0.07 us -> 6.89 us  [the longest x2 2.8 us: to_tokens(): kept = rows[:count * MOST].reshape(count, MOST, -1)]
    concatenate x0 -> x6, local copies, waits for them, and re-layouts: none -> 5.22 us  [the longest x1 3.82 us: per_device(): jnp.concatenate([(slot_gate[:, None] * routed_f32).astype(bf16), dot_high...]
  transfers between devices with their start and end apart: 6 -> 40, of which waited for: 6 -> 18; matrix products, arithmetic and copies ran while one was open for 16% -> 35% of each run, Pallas kernels for 0% -> 0%
where the time goes in v1:
time: 161 us; the launch traced here: 160 us
  matrix products  46.2 us (29%)
  waiting for transfers between devices  39.5 us (25%)
  starting transfers between devices  39.1 us (24%)
  local copies, waits for them, and re-layouts  20.6 us (13%)
  other arithmetic  12.5 us (8%)
  between operations  2.3 us (1%)
    dot_general x37, matrix products, mm(): lax.dot_general(left, right, ((axes[0], axes[1]), ((), ())), preferred_el...  42.9 us
    ppermute x6, waiting for transfers between devices, ring_scatter(): forth = lax.ppermute(narrow(front), 'expert', ahead)  13.6 us
    ppermute x6, starting transfers between devices, ring_gather(): from_behind.append(lax.ppermute(from_behind[-1], 'expert', ahead))  13.1 us
    ppermute x6, waiting for transfers between devices, ring_gather(): from_behind.append(lax.ppermute(from_behind[-1], 'expert', ahead))  11.7 us
    ppermute x6, starting transfers between devices, ring_scatter(): forth = lax.ppermute(narrow(front), 'expert', ahead)  9.1 us
    ppermute x6, waiting for transfers between devices, ring_scatter(): hither = lax.ppermute(narrow(rear), 'expert', back)  5.53 us
    ppermute x3, starting transfers between devices, per_device(): lax.ppermute(gathered, 'expert', [(i, i ^ step) for i in range(count)])  5.14 us
    ppermute x2, starting transfers between devices, ring_gather(): top = lax.ppermute(from_behind[-1][:rows], 'expert', ahead)  4.13 us
  transfers between devices with their start and end apart: 40, of which 18 were waited for; matrix products, arithmetic and copies ran while one was open for 35% of the time, Pallas kernels for 0%

profile of v1, /device:TPU:0, one launch (start us, length us, event | category | flops | bytes accessed | tf_op | source)
XLA Modules:
  0.0 160.2 jit_solution(17017788468068885743)
XLA Ops:
  3.2 3.0 %collective-permute-start = (bf16[32,3712]{1,0:T(8,128)(2,1)}, bf16[32,3712]{1,0:T(8,128)(2,1)S(1)}, u32[]{:S(2)}, u32[]{:S(2)}) collective-permute-start(bf16[32,3712]{1,0:T(8,128)(2,1)} %fusion.55), channel_id=1, source_target_pairs={{0,4},{4,8},{8,12},{12,14},{14,10},{10,6},{6,2},{2,0},{1,5},{5,9},... | collective-permute-start | bytes 712712 | tf_op jit(solution)/shard_map/ppermute | solution.py:49
  9.9 2.1 %collective-permute-start.8 = (bf16[32,3712]{1,0:T(8,128)(2,1)S(1)}, bf16[32,3712]{1,0:T(8,128)(2,1)S(1)}, u32[]{:S(2)}, u32[]{:S(2)}) collective-permute-start(bf16[32,3712]{1,0:T(8,128)(2,1)S(1)} %concatenate.71), channel_id=1, source_target_pairs={{0,4},{4,8},{8,12},{12,14},{14,10},{10,6},{6,2},{2,0},{1,5},{5,9},... | collective-permute-start | bytes 712712 | tf_op jit(solution)/shard_map/ppermute | solution.py:49
  29.4 3.8 %collective-permute-done.1 = bf16[32,3712]{1,0:T(8,128)(2,1)S(1)} collective-permute-done((bf16[32,3712]{1,0:T(8,128)(2,1)S(1)}, bf16[32,3712]{1,0:T(8,128)(2,1)S(1)}, u32[]{:S(2)}, u32[]{:S(2)}) %collective-permute-start.1) | collective-permute-done | bytes 237600 | tf_op jit(solution)/shard_map/ppermute | solution.py:49
  35.4 3.0 %collective-permute-done.9 = bf16[32,3712]{1,0:T(8,128)(2,1)S(1)} collective-permute-done((bf16[32,3712]{1,0:T(8,128)(2,1)S(1)}, bf16[32,3712]{1,0:T(8,128)(2,1)S(1)}, u32[]{:S(2)}, u32[]{:S(2)}) %collective-permute-start.9) | collective-permute-done | bytes 237600 | tf_op jit(solution)/shard_map/ppermute | solution.py:49
  41.1 2.3 %collective-permute-done.2 = bf16[32,3712]{1,0:T(8,128)(2,1)S(1)} collective-permute-done((bf16[32,3712]{1,0:T(8,128)(2,1)S(1)}, bf16[32,3712]{1,0:T(8,128)(2,1)S(1)}, u32[]{:S(2)}, u32[]{:S(2)}) %collective-permute-start.2) | collective-permute-done | bytes 237600 | tf_op jit(solution)/shard_map/ppermute | solution.py:49
  43.4 2.1 %collective-permute-start.6 = (bf16[16,3712]{1,0:T(8,128)(2,1)S(1)}, bf16[16,3712]{1,0:T(8,128)(2,1)S(1)}, u32[]{:S(2)}, u32[]{:S(2)}) collective-permute-start(bf16[16,3712]{1,0:T(8,128)(2,1)S(1)} %slice.251), channel_id=1, source_target_pairs={{0,4},{4,8},{8,12},{12,14},{14,10},{10,6},{6,2},{2,0},{1,5},{5,9},... | collective-permute-start | bytes 356360 | tf_op jit(solution)/shard_map/ppermute | solution.py:51
  45.6 2.6 %collective-permute-done.10 = bf16[32,3712]{1,0:T(8,128)(2,1)S(1)} collective-permute-done((bf16[32,3712]{1,0:T(8,128)(2,1)S(1)}, bf16[32,3712]{1,0:T(8,128)(2,1)S(1)}, u32[]{:S(2)}, u32[]{:S(2)}) %collective-permute-start.10) | collective-permute-done | bytes 237600 | tf_op jit(solution)/shard_map/ppermute | solution.py:49
  48.2 2.1 %collective-permute-start.14 = (bf16[16,3712]{1,0:T(8,128)(2,1)S(1)}, bf16[16,3712]{1,0:T(8,128)(2,1)S(1)}, u32[]{:S(2)}, u32[]{:S(2)}) collective-permute-start(bf16[16,3712]{1,0:T(8,128)(2,1)S(1)} %slice.255), channel_id=1, source_target_pairs={{0,4},{4,8},{8,12},{12,14},{14,10},{10,6},{6,2},{2,0},{1,5},{5,9},... | collective-permute-start | bytes 356360 | tf_op jit(solution)/shard_map/ppermute | solution.py:51
  60.5 5.3 %fusion.10 = f32[256,1024]{1,0:T(8,128)S(1)} fusion(bf16[1,3584,1024]{2,1,0:T(8,128)(2,1)} %param.20, bf16[128,3712]{1,0:T(8,128)(2,1)S(1)} %collective-permute-done.17, bf16[128,3712]{1,0:T(8,128)(2,1)S(1)} %bitcast.270), kind=kOutput, calls=%fused_computation.11 | convolution fusion | flops 1882718208 | bytes 10289152 | tf_op jit(solution)/shard_map/dot_general | solution.py:14
  65.9 3.6 %multiply_convert_fusion.3 = (bf16[256,1024]{1,0:T(8,128)(2,1)S(1)}, f32[256,1024]{1,0:T(8,128)S(1)}) fusion(f32[256,1024]{1,0:T(8,128)S(1)} %fusion.10, f32[256,1024]{1,0:T(8,128)S(1)} %convolution_multiply_fusion.5, bf16[1,3584,1024]{2,1,0:T(8,128)(2,1)S(1)} %bitcast.302, bf16[128,3712]{1,0:T(8,128)(2,1)} %copy-done.10, bf16[128,3712]{1,0:T(8,128)(2,1)S(1)} %bitcast.271), kind=kOutput, calls=%fused_computation.89 | convolution fusion | flops 1884553216 | bytes 12910592 | tf_op jit(solution)/shard_map/dot_general | solution.py:14
  69.8 2.1 %fusion.2 = f32[256,3584]{1,0:T(8,128)S(1)} fusion(bf16[256,1024]{1,0:T(8,128)(2,1)S(1)} %get-tuple-element.71, bf16[1,1024,3584]{2,1,0:T(8,128)(2,1)S(1)} %bitcast.300), kind=kOutput, calls=%fused_computation.3 | convolution fusion | flops 1879048192 | bytes 11534336 | tf_op jit(solution)/shard_map/dot_general | solution.py:14
  72.8 5.3 %fusion.25 = (f32[256]{0:T(256)S(1)}, bf16[256,3584]{1,0:T(8,128)(2,1)}, bf16[256,3584]{1,0:T(8,128)(2,1)S(1)}) fusion(bf16[128,3712]{1,0:T(8,128)(2,1)} %collective-permute-done.16, bf16[128,3712]{1,0:T(8,128)(2,1)S(1)} %bitcast.274, f32[256]{0:T(256)S(1)} %multiply_reduce_fusion.1, f32[256]{0:T(256)S(1)} %broadcast_select_fusion, ...), kind=kOutput, calls=%fused_computation.34 | convolution fusion | flops 132120320 | bytes 9735168 | tf_op jit(solution)/shard_map/dot_general | solution.py:14
  79.1 2.2 %multiply_convert_fusion.1 = (bf16[256,1024]{1,0:T(8,128)(2,1)S(1)}, f32[256,1024]{1,0:T(8,128)S(1)}) fusion(f32[256,1024]{1,0:T(8,128)S(1)} %fusion.10, f32[256,1024]{1,0:T(8,128)S(1)} %convolution_multiply_fusion.4, bf16[256,3584]{1,0:T(8,128)(2,1)S(1)} %get-tuple-element.41, bf16[1,1024,3584]{2,1,0:T(8,128)(2,1)S(1)} %bitcast.300), kind=kOutput, calls=%fused_computation.87 | convolution fusion | flops 1880883200 | bytes 12845056 | tf_op jit(solution)/shard_map/dot_general | solution.py:14
  81.6 5.2 %fusion.4 = f32[256,3584]{1,0:T(8,128)S(1)} fusion(bf16[256,1024]{1,0:T(8,128)(2,1)S(1)} %get-tuple-element.74, bf16[1,3584,1024]{2,1,0:T(8,128)(2,1)} %param.21), kind=kOutput, calls=%fused_computation.5 | convolution fusion | flops 1879048192 | bytes 11534336 | tf_op jit(solution)/shard_map/dot_general | solution.py:14
  86.9 2.3 %fusion.15 = f32[256,3584]{1,0:T(8,128)S(1)} fusion(f32[256,3584]{1,0:T(8,128)S(1)} %fusion.4, bf16[1,3584,1024]{2,1,0:T(8,128)(2,1)S(1)} %bitcast.267, f32[256,1024]{1,0:T(8,128)S(1)} %fusion.10, f32[256,1024]{1,0:T(8,128)S(1)} %get-tuple-element.75, f32[256,1024]{1,0:T(8,128)S(1)} %get-tuple-element.72), kind=kOutput, calls=%fused_computation.18 | convolution fusion | flops 1882587136 | bytes 17825792 | tf_op jit(solution)/shard_map/dot_general | solution.py:14
  91.6 3.8 %concatenate.77 = bf16[256,3712]{1,0:T(8,128)(2,1)} concatenate(bf16[256,3584]{1,0:T(8,128)(2,1)} %get-tuple-element.40, bf16[256,16]{1,0:T(8,128)(2,1)S(1)} %get-tuple-element.70, bf16[256,16]{1,0:T(8,128)(2,1)S(1)} %get-tuple-element.69, bf16[256,96]{1,0:T(8,128)(2,1)S(1)} %broadcast_in_dim.87), dimensions={1} | concatenate | bytes 3801088 | tf_op jit(solution)/shard_map/concatenate | solution.py:200
  107.9 2.9 %collective-permute-done.19 = bf16[16,3712]{1,0:T(8,128)(2,1)S(1)} collective-permute-done((bf16[16,3712]{1,0:T(8,128)(2,1)S(1)}, bf16[16,3712]{1,0:T(8,128)(2,1)S(1)}, u32[]{:S(2)}, u32[]{:S(2)}) %collective-permute-start.19) | collective-permute-done | bytes 118816 | tf_op jit(solution)/shard_map/ppermute | solution.py:62
  114.7 4.9 %collective-permute-done.20 = bf16[32,3712]{1,0:T(8,128)(2,1)S(1)} collective-permute-done((bf16[32,3712]{1,0:T(8,128)(2,1)S(1)}, bf16[32,3712]{1,0:T(8,128)(2,1)S(1)}, u32[]{:S(2)}, u32[]{:S(2)}) %collective-permute-start.20) | collective-permute-done | bytes 237600 | tf_op jit(solution)/shard_map/ppermute | solution.py:71
  122.6 5.1 %collective-permute-done.21 = bf16[32,3712]{1,0:T(8,128)(2,1)S(1)} collective-permute-done((bf16[32,3712]{1,0:T(8,128)(2,1)S(1)}, bf16[32,3712]{1,0:T(8,128)(2,1)S(1)}, u32[]{:S(2)}, u32[]{:S(2)}) %collective-permute-start.21) | collective-permute-done | bytes 237600 | tf_op jit(solution)/shard_map/ppermute | solution.py:71
  130.7 2.1 %collective-permute-start.30 = (bf16[32,3584]{1,0:T(8,128)(2,1)S(1)}, bf16[32,3584]{1,0:T(8,128)(2,1)S(1)}, u32[]{:S(2)}, u32[]{:S(2)}) collective-permute-start(bf16[32,3584]{1,0:T(8,128)(2,1)S(1)} %add_convert_fusion.8), channel_id=1, source_target_pairs={{0,4},{4,8},{8,12},{12,14},{14,10},{10,6},{6,2},{2,0},{1,5},{5,9},... | collective-permute-start | bytes 688136 | tf_op jit(solution)/shard_map/ppermute | solution.py:71
  132.8 3.6 %collective-permute-done.22 = bf16[32,3712]{1,0:T(8,128)(2,1)S(1)} collective-permute-done((bf16[32,3712]{1,0:T(8,128)(2,1)S(1)}, bf16[32,3712]{1,0:T(8,128)(2,1)S(1)}, u32[]{:S(2)}, u32[]{:S(2)}) %collective-permute-start.22) | collective-permute-done | bytes 237600 | tf_op jit(solution)/shard_map/ppermute | solution.py:71
  144.4 2.5 %collective-permute-done.37 = bf16[2,32,16]{2,1,0:T(8,128)(2,1)S(1)} collective-permute-done((bf16[2,32,16]{2,1,0:T(8,128)(2,1)S(1)}, bf16[2,32,16]{2,1,0:T(8,128)(2,1)S(1)}, u32[]{:S(2)}, u32[]{:S(2)}) %collective-permute-start.37) | collective-permute-done | bytes 2080 | tf_op jit(solution)/shard_map/ppermute | solution.py:254
  147.6 2.9 %collective-permute-start.38 = (bf16[4,32,16]{2,1,0:T(8,128)(2,1)}, bf16[4,32,16]{2,1,0:T(8,128)(2,1)S(1)}, u32[]{:S(2)}, u32[]{:S(2)}) collective-permute-start(bf16[4,32,16]{2,1,0:T(8,128)(2,1)} %pad_maximum_fusion.8), channel_id=1, source_target_pairs={{0,8},{2,10},{4,12},{6,14},{8,0},{10,2},{12,4},{14,6},{1,9},{3,11}... | collective-permute-start | bytes 12296 | tf_op jit(solution)/shard_map/ppermute | solution.py:254
  155.2 2.4 %collective-permute-done.35 = bf16[32,3584]{1,0:T(8,128)(2,1)S(1)} collective-permute-done((bf16[32,3584]{1,0:T(8,128)(2,1)}, bf16[32,3584]{1,0:T(8,128)(2,1)S(1)}, u32[]{:S(2)}, u32[]{:S(2)}) %collective-permute-start.35) | collective-permute-done | bytes 229408 | tf_op jit(solution)/shard_map/ppermute | solution.py:72
  (275 shorter events, 80.7 us)
Async XLA Ops:
  3.2 21.3 %collective-permute-start = (bf16[32,3712]{1,0:T(8,128)(2,1)}, bf16[32,3712]{1,0:T(8,128)(2,1)S(1)}, u32[]{:S(2)}, u32[]{:S(2)}) collective-permute-start(bf16[32,3712]{1,0:T(8,128)(2,1)} %fusion.55), channel_id=1, source_target_pairs={{0,4},{4,8},{8,12},{12,14},{14,10},{10,6},{6,2},{2,0},{1,5},{5,9},... | collective-permute-start | bytes 712712 | tf_op jit(solution)/shard_map/ppermute | solution.py:49
  6.2 20.4 %collective-permute-start.3 = (bf16[32,3712]{1,0:T(8,128)(2,1)}, bf16[32,3712]{1,0:T(8,128)(2,1)S(1)}, u32[]{:S(2)}, u32[]{:S(2)}) collective-permute-start(bf16[32,3712]{1,0:T(8,128)(2,1)} %fusion.55), channel_id=1, source_target_pairs={{4,0},{8,4},{12,8},{14,12},{10,14},{6,10},{2,6},{0,2},{5,1},{9,5},... | collective-permute-start | bytes 712712 | tf_op jit(solution)/shard_map/ppermute | solution.py:50
  9.9 16.8 %collective-permute-start.8 = (bf16[32,3712]{1,0:T(8,128)(2,1)S(1)}, bf16[32,3712]{1,0:T(8,128)(2,1)S(1)}, u32[]{:S(2)}, u32[]{:S(2)}) collective-permute-start(bf16[32,3712]{1,0:T(8,128)(2,1)S(1)} %concatenate.71), channel_id=1, source_target_pairs={{0,4},{4,8},{8,12},{12,14},{14,10},{10,6},{6,2},{2,0},{1,5},{5,9},... | collective-permute-start | bytes 712712 | tf_op jit(solution)/shard_map/ppermute | solution.py:49
  12.0 17.4 %collective-permute-start.11 = (bf16[32,3712]{1,0:T(8,128)(2,1)S(1)}, bf16[32,3712]{1,0:T(8,128)(2,1)S(1)}, u32[]{:S(2)}, u32[]{:S(2)}) collective-permute-start(bf16[32,3712]{1,0:T(8,128)(2,1)S(1)} %concatenate.71), channel_id=1, source_target_pairs={{4,0},{8,4},{12,8},{14,12},{10,14},{6,10},{2,6},{0,2},{5,1},{9,5},... | collective-permute-start | bytes 712712 | tf_op jit(solution)/shard_map/ppermute | solution.py:50
  24.5 8.7 %collective-permute-start.1 = (bf16[32,3712]{1,0:T(8,128)(2,1)S(1)}, bf16[32,3712]{1,0:T(8,128)(2,1)S(1)}, u32[]{:S(2)}, u32[]{:S(2)}) collective-permute-start(bf16[32,3712]{1,0:T(8,128)(2,1)S(1)} %collective-permute-done), channel_id=1, source_target_pairs={{0,4},{4,8},{8,12},{12,14},{14,10},{10,6},{6,2},{2,0},{1,5},{5,9},... | collective-permute-start | bytes 712712 | tf_op jit(solution)/shard_map/ppermute | solution.py:49
  26.6 8.8 %collective-permute-start.4 = (bf16[32,3712]{1,0:T(8,128)(2,1)S(1)}, bf16[32,3712]{1,0:T(8,128)(2,1)S(1)}, u32[]{:S(2)}, u32[]{:S(2)}) collective-permute-start(bf16[32,3712]{1,0:T(8,128)(2,1)S(1)} %collective-permute-done.3), channel_id=1, source_target_pairs={{4,0},{8,4},{12,8},{14,12},{10,14},{6,10},{2,6},{0,2},{5,1},{9,5},... | collective-permute-start | bytes 712712 | tf_op jit(solution)/shard_map/ppermute | solution.py:50
  26.6 11.7 %collective-permute-start.9 = (bf16[32,3712]{1,0:T(8,128)(2,1)S(1)}, bf16[32,3712]{1,0:T(8,128)(2,1)S(1)}, u32[]{:S(2)}, u32[]{:S(2)}) collective-permute-start(bf16[32,3712]{1,0:T(8,128)(2,1)S(1)} %collective-permute-done.8), channel_id=1, source_target_pairs={{0,4},{4,8},{8,12},{12,14},{14,10},{10,6},{6,2},{2,0},{1,5},{5,9},... | collective-permute-start | bytes 712712 | tf_op jit(solution)/shard_map/ppermute | solution.py:49
  29.4 11.1 %collective-permute-start.12 = (bf16[32,3712]{1,0:T(8,128)(2,1)S(1)}, bf16[32,3712]{1,0:T(8,128)(2,1)S(1)}, u32[]{:S(2)}, u32[]{:S(2)}) collective-permute-start(bf16[32,3712]{1,0:T(8,128)(2,1)S(1)} %collective-permute-done.11), channel_id=1, source_target_pairs={{4,0},{8,4},{12,8},{14,12},{10,14},{6,10},{2,6},{0,2},{5,1},{9,5},... | collective-permute-start | bytes 712712 | tf_op jit(solution)/shard_map/ppermute | solution.py:50
  33.2 10.2 %collective-permute-start.2 = (bf16[32,3712]{1,0:T(8,128)(2,1)S(1)}, bf16[32,3712]{1,0:T(8,128)(2,1)S(1)}, u32[]{:S(2)}, u32[]{:S(2)}) collective-permute-start(bf16[32,3712]{1,0:T(8,128)(2,1)S(1)} %collective-permute-done.1), channel_id=1, source_target_pairs={{0,4},{4,8},{8,12},{12,14},{14,10},{10,6},{6,2},{2,0},{1,5},{5,9},... | collective-permute-start | bytes 712712 | tf_op jit(solution)/shard_map/ppermute | solution.py:49
  35.3 10.2 %collective-permute-start.5 = (bf16[32,3712]{1,0:T(8,128)(2,1)S(1)}, bf16[32,3712]{1,0:T(8,128)(2,1)S(1)}, u32[]{:S(2)}, u32[]{:S(2)}) collective-permute-start(bf16[32,3712]{1,0:T(8,128)(2,1)S(1)} %collective-permute-done.4), channel_id=1, source_target_pairs={{4,0},{8,4},{12,8},{14,12},{10,14},{6,10},{2,6},{0,2},{5,1},{9,5},... | collective-permute-start | bytes 712712 | tf_op jit(solution)/shard_map/ppermute | solution.py:50
  38.3 9.9 %collective-permute-start.10 = (bf16[32,3712]{1,0:T(8,128)(2,1)S(1)}, bf16[32,3712]{1,0:T(8,128)(2,1)S(1)}, u32[]{:S(2)}, u32[]{:S(2)}) collective-permute-start(bf16[32,3712]{1,0:T(8,128)(2,1)S(1)} %collective-permute-done.9), channel_id=1, source_target_pairs={{0,4},{4,8},{8,12},{12,14},{14,10},{10,6},{6,2},{2,0},{1,5},{5,9},... | collective-permute-start | bytes 712712 | tf_op jit(solution)/shard_map/ppermute | solution.py:49
  40.4 9.9 %collective-permute-start.13 = (bf16[32,3712]{1,0:T(8,128)(2,1)S(1)}, bf16[32,3712]{1,0:T(8,128)(2,1)S(1)}, u32[]{:S(2)}, u32[]{:S(2)}) collective-permute-start(bf16[32,3712]{1,0:T(8,128)(2,1)S(1)} %collective-permute-done.12), channel_id=1, source_target_pairs={{4,0},{8,4},{12,8},{14,12},{10,14},{6,10},{2,6},{0,2},{5,1},{9,5},... | collective-permute-start | bytes 712712 | tf_op jit(solution)/shard_map/ppermute | solution.py:50
  57.0 14.9 %collective-permute-start.16 = (bf16[128,3712]{1,0:T(8,128)(2,1)}, bf16[128,3712]{1,0:T(8,128)(2,1)}, u32[]{:S(2)}, u32[]{:S(2)}) collective-permute-start(bf16[128,3712]{1,0:T(8,128)(2,1)} %bitcast.23), channel_id=1, source_target_pairs={{0,1},{1,0},{2,3},{3,2},{4,5},{5,4},{6,7},{7,6},{8,9},{9,8},{10,11... | collective-permute-start | bytes 2850824 | tf_op jit(solution)/shard_map/ppermute | solution.py:77
  91.0 10.5 %collective-permute-start.27 = (bf16[128,3584]{1,0:T(8,128)(2,1)}, bf16[128,3584]{1,0:T(8,128)(2,1)S(1)}, u32[]{:S(2)}, u32[]{:S(2)}) collective-permute-start(bf16[128,3584]{1,0:T(8,128)(2,1)} %get-tuple-element.49), channel_id=1, source_target_pairs={{0,1},{1,0},{2,3},{3,2},{4,5},{5,4},{6,7},{7,6},{8,9},{9,8},{10,11... | collective-permute-start | bytes 2752520 | tf_op jit(solution)/shard_map/ppermute | solution.py:77
  103.7 18.9 %collective-permute-start.32 = (bf16[16,3584]{1,0:T(8,128)(2,1)S(1)}, bf16[16,3584]{1,0:T(8,128)(2,1)S(1)}, u32[]{:S(2)}, u32[]{:S(2)}) collective-permute-start(bf16[16,3584]{1,0:T(8,128)(2,1)S(1)} %get-tuple-element.53), channel_id=1, source_target_pairs={{4,0},{8,4},{12,8},{14,12},{10,14},{6,10},{2,6},{0,2},{5,1},{9,5},... | collective-permute-start | bytes 344072 | tf_op jit(solution)/shard_map/ppermute | solution.py:63
  110.9 8.8 %collective-permute-start.20 = (bf16[32,3712]{1,0:T(8,128)(2,1)S(1)}, bf16[32,3712]{1,0:T(8,128)(2,1)S(1)}, u32[]{:S(2)}, u32[]{:S(2)}) collective-permute-start(bf16[32,3712]{1,0:T(8,128)(2,1)S(1)} %pad_maximum_fusion.3), channel_id=1, source_target_pairs={{0,4},{4,8},{8,12},{12,14},{14,10},{10,6},{6,2},{2,0},{1,5},{5,9},... | collective-permute-start | bytes 712712 | tf_op jit(solution)/shard_map/ppermute | solution.py:71
  112.6 9.0 %collective-permute-start.24 = (bf16[32,3712]{1,0:T(8,128)(2,1)S(1)}, bf16[32,3712]{1,0:T(8,128)(2,1)S(1)}, u32[]{:S(2)}, u32[]{:S(2)}) collective-permute-start(bf16[32,3712]{1,0:T(8,128)(2,1)S(1)} %pad_maximum_fusion.4), channel_id=1, source_target_pairs={{4,0},{8,4},{12,8},{14,12},{10,14},{6,10},{2,6},{0,2},{5,1},{9,5},... | collective-permute-start | bytes 712712 | tf_op jit(solution)/shard_map/ppermute | solution.py:72
  113.1 17.4 %collective-permute-start.29 = (bf16[32,3584]{1,0:T(8,128)(2,1)S(1)}, bf16[32,3584]{1,0:T(8,128)(2,1)S(1)}, u32[]{:S(2)}, u32[]{:S(2)}) collective-permute-start(bf16[32,3584]{1,0:T(8,128)(2,1)S(1)} %pad_maximum_fusion.6), channel_id=1, source_target_pairs={{0,4},{4,8},{8,12},{12,14},{14,10},{10,6},{6,2},{2,0},{1,5},{5,9},... | collective-permute-start | bytes 688136 | tf_op jit(solution)/shard_map/ppermute | solution.py:71
  127.9 8.4 %collective-permute-start.22 = (bf16[32,3712]{1,0:T(8,128)(2,1)S(1)}, bf16[32,3712]{1,0:T(8,128)(2,1)S(1)}, u32[]{:S(2)}, u32[]{:S(2)}) collective-permute-start(bf16[32,3712]{1,0:T(8,128)(2,1)S(1)} %add_convert_fusion.2), channel_id=1, source_target_pairs={{0,4},{4,8},{8,12},{12,14},{14,10},{10,6},{6,2},{2,0},{1,5},{5,9},... | collective-permute-start | bytes 712712 | tf_op jit(solution)/shard_map/ppermute | solution.py:71
  129.8 8.1 %collective-permute-start.26 = (bf16[32,3712]{1,0:T(8,128)(2,1)S(1)}, bf16[32,3712]{1,0:T(8,128)(2,1)S(1)}, u32[]{:S(2)}, u32[]{:S(2)}) collective-permute-start(bf16[32,3712]{1,0:T(8,128)(2,1)S(1)} %add_convert_fusion), channel_id=1, source_target_pairs={{4,0},{8,4},{12,8},{14,12},{10,14},{6,10},{2,6},{0,2},{5,1},{9,5},... | collective-permute-start | bytes 712712 | tf_op jit(solution)/shard_map/ppermute | solution.py:72
  130.4 10.1 %collective-permute-start.33 = (bf16[32,3584]{1,0:T(8,128)(2,1)S(1)}, bf16[32,3584]{1,0:T(8,128)(2,1)S(1)}, u32[]{:S(2)}, u32[]{:S(2)}) collective-permute-start(bf16[32,3584]{1,0:T(8,128)(2,1)S(1)} %pad_maximum_fusion.7), channel_id=1, source_target_pairs={{4,0},{8,4},{12,8},{14,12},{10,14},{6,10},{2,6},{0,2},{5,1},{9,5},... | collective-permute-start | bytes 688136 | tf_op jit(solution)/shard_map/ppermute | solution.py:72
  130.7 12.9 %collective-permute-start.30 = (bf16[32,3584]{1,0:T(8,128)(2,1)S(1)}, bf16[32,3584]{1,0:T(8,128)(2,1)S(1)}, u32[]{:S(2)}, u32[]{:S(2)}) collective-permute-start(bf16[32,3584]{1,0:T(8,128)(2,1)S(1)} %add_convert_fusion.8), channel_id=1, source_target_pairs={{0,4},{4,8},{8,12},{12,14},{14,10},{10,6},{6,2},{2,0},{1,5},{5,9},... | collective-permute-start | bytes 688136 | tf_op jit(solution)/shard_map/ppermute | solution.py:71
  140.7 9.8 %collective-permute-start.34 = (bf16[32,3584]{1,0:T(8,128)(2,1)S(1)}, bf16[32,3584]{1,0:T(8,128)(2,1)S(1)}, u32[]{:S(2)}, u32[]{:S(2)}) collective-permute-start(bf16[32,3584]{1,0:T(8,128)(2,1)S(1)} %add_convert_fusion.6), channel_id=1, source_target_pairs={{4,0},{8,4},{12,8},{14,12},{10,14},{6,10},{2,6},{0,2},{5,1},{9,5},... | collective-permute-start | bytes 688136 | tf_op jit(solution)/shard_map/ppermute | solution.py:72
  143.9 11.3 %collective-permute-start.31 = (bf16[32,3584]{1,0:T(8,128)(2,1)S(1)}, bf16[32,3584]{1,0:T(8,128)(2,1)}, u32[]{:S(2)}, u32[]{:S(2)}) collective-permute-start(bf16[32,3584]{1,0:T(8,128)(2,1)S(1)} %add_convert_fusion.7), channel_id=1, source_target_pairs={{0,4},{4,8},{8,12},{12,14},{14,10},{10,6},{6,2},{2,0},{1,5},{5,9},... | collective-permute-start | bytes 688136 | tf_op jit(solution)/shard_map/ppermute | solution.py:71
  (58 other events, 392.1 us)

commit v2 on v1

v2 whole, which is shorter than its diff:
```python
import functools

import jax
import jax.numpy as jnp
import numpy as np
from jax import lax
from jax.experimental import pallas as pl
from jax.experimental.pallas import tpu as pltpu
from jax.sharding import PartitionSpec as P

MOST = 16
LANES = 128
VMEM_LIMIT = 56 * 2**20

route_scale = 2.5
adapter_scale = 2.0

bf16, f32 = jnp.bfloat16, jnp.float32
in_vmem = pl.BlockSpec(memory_space=pltpu.VMEM)
in_smem = pl.BlockSpec(memory_space=pltpu.SMEM)


def mm(left, right, axes=((1,), (0,))):
    return lax.dot_general(
        left, right, ((axes[0], axes[1]), ((), ())), preferred_element_type=jnp.float32
    )


def mm_nt(left, right):
    return mm(left, right, ((1,), (1,)))


def mm_tn(left, right):
    return mm(left, right, ((0,), (0,)))


def call(body, outs, specs, operands, cost, out_specs=None, grid=(), scratch=()):
    flops, moved = cost
    return pl.pallas_call(
        body,
        out_shape=outs,
        grid=grid,
        in_specs=specs,
        out_specs=out_specs if out_specs is not None else [in_vmem] * len(outs),
        scratch_shapes=list(scratch),
        compiler_params=pltpu.CompilerParams(vmem_limit_bytes=VMEM_LIMIT),
        cost_estimate=pl.CostEstimate(flops=flops, bytes_accessed=moved, transcendentals=0),
    )(*operands)


def struct(shape, dtype=bf16):
    return jax.ShapeDtypeStruct(shape, dtype)


def nbytes(arrays):
    return sum(a.size * a.dtype.itemsize for a in arrays)


def token_load_kernel(choice_ref, tokens_ref, load_ref):
    width = tokens_ref.shape[1]
    rows = tokens_ref.shape[0]
    load_ref[:, :width] = tokens_ref[...]
    names = lax.broadcasted_iota(jnp.int32, (rows, LANES), 1)
    hits = jnp.zeros((rows, LANES), f32)
    for k in range(choice_ref.shape[1]):
        hits += jnp.where(choice_ref[:, k : k + 1] == names, 1.0, 0.0)
    load_ref[:, width:] = hits.astype(bf16)


def cot_load_kernel(choice_ref, tokens_ref, router_ref, cot_ref, load_ref, hits_ref, affinity_ref):
    rows, width = tokens_ref.shape
    experts = router_ref.shape[1]
    load_ref[:, :width] = cot_ref[...]
    affinity = jax.nn.sigmoid(mm(tokens_ref[...], router_ref[...]))
    names = lax.broadcasted_iota(jnp.int32, (rows, experts), 1)
    hits = jnp.zeros((rows, experts), f32)
    for k in range(choice_ref.shape[1]):
        hits += jnp.where(choice_ref[:, k : k + 1] == names, 1.0, 0.0)
    chosen = hits * affinity
    gates = route_scale * chosen / jnp.sum(chosen, axis=1, keepdims=True)
    high = gates.astype(bf16)
    low = (gates - high.astype(f32)).astype(bf16)
    load_ref[:, width:] = jnp.zeros((rows, LANES), bf16)
    load_ref[:, width : width + experts] = high
    load_ref[:, width + experts : width + 2 * experts] = low
    hits_ref[...] = hits
    affinity_ref[...] = affinity


def block_values(refs):
    values = [ref[...] for ref in refs[:-2]]
    return values + [jnp.concatenate([refs[-2][...], refs[-1][...]], axis=0)]


def token_slots_kernel(count, info_ref, *refs):
    blocks, (kept_ref, sent_ref, select_ref) = refs[: count + 1], refs[count + 1 :]
    rows, load = blocks[0].shape
    width = load - LANES
    mine = 2 * info_ref[0] + info_ref[1]
    other = 2 * info_ref[0] + 1 - info_ref[1]
    spot = lax.broadcasted_iota(jnp.int32, (2 * MOST, LANES), 0)
    lane = lax.broadcasted_iota(jnp.int32, (2 * MOST, LANES), 1)
    names = jnp.where(lane == jnp.where(spot < MOST, mine, other), 1.0, 0.0).astype(bf16)
    early = lax.broadcasted_iota(jnp.int32, (rows, rows), 0)
    late = lax.broadcasted_iota(jnp.int32, (rows, rows), 1)
    earlier = jnp.where(early < late, 1.0, 0.0).astype(bf16)
    wanted = lax.broadcasted_iota(jnp.int32, (2 * MOST, rows), 0)
    wanted = jnp.where(wanted < MOST, wanted, wanted - MOST).astype(f32)
    for i, value in enumerate(block_values(blocks)):
        member = mm_nt(names, value[:, width:])
        before = mm(member.astype(bf16), earlier)
        select = jnp.where(before == wanted, member, 0.0).astype(bf16)
        select_ref[i] = select
        out = mm(select, value).astype(bf16)
        kept_ref[pl.ds(i * MOST, MOST)] = out[:MOST]
        sent_ref[pl.ds(i * MOST, MOST)] = out[MOST:]


def cot_slots_kernel(count, select_ref, *refs):
    blocks, (kept_ref, sent_ref) = refs[: count + 1], refs[count + 1 :]
    for i, value in enumerate(block_values(blocks)):
        out = mm(select_ref[i], value).astype(bf16)
        kept_ref[pl.ds(i * MOST, MOST)] = out[:MOST]
        sent_ref[pl.ds(i * MOST, MOST)] = out[MOST:]


def forward_kernel(
    count, first, info_ref, table_ref, kept_ref, came_ref, gate_ref, up_ref, down_ref,
    up_a_ref, up_b_ref, down_a_ref, down_b_ref,
    routed_ref, keep_ref, slope_ref, active_ref, low_up_ref, inner_ref, low_down_ref,
    rows_ref,
):
    step = pl.program_id(0)
    half, width = kept_ref.shape[0], rows_ref.shape[1]
    slots = 2 * half
    tile = gate_ref.shape[1]

    @pl.when(step == 0)
    def _():
        rows_ref[:half] = kept_ref[:, :width]
        rows_ref[half:] = came_ref[:, :width]
        low_up_ref[...] = mm(rows_ref[...], up_a_ref[...]).astype(bf16)
        chip, core = info_ref[0], info_ref[1]
        lane = lax.broadcasted_iota(jnp.int32, (slots, LANES), 1)
        tails = jnp.concatenate([kept_ref[:, width:], came_ref[:, width:]], axis=0).astype(f32)
        valid = jnp.sum(jnp.where(lane == 2 * chip + core, tails, 0.0), axis=1, keepdims=True)
        here = lax.broadcasted_iota(jnp.int32, (slots, 1), 0)
        there = lax.broadcasted_iota(jnp.int32, (1, slots), 1)
        source_here = jnp.zeros((slots, 1), jnp.int32)
        source_there = jnp.zeros((1, slots), jnp.int32)
        for i in range(2 * count):
            parity = core if i < count else 1 - core
            source = 2 * table_ref[chip, i % count] + parity
            source_here = jnp.where(here // MOST == i, source, source_here)
            source_there = jnp.where(there // MOST == i, source, source_there)
        ahead = jnp.where(source_there < source_here, 1.0, 0.0).astype(bf16)
        spread = jnp.broadcast_to(valid, (slots, LANES)).astype(bf16)
        rank = mm(ahead, spread) + (here % MOST).astype(f32)
        keep_ref[...] = jnp.where(rank < info_ref[2].astype(f32), valid, 0.0)

    @pl.when(step < first)
    def _():
        rows = rows_ref[...]
        pre_gate = mm(rows, gate_ref[...])
        pre_up = mm(rows, up_ref[...]) + adapter_scale * mm(low_up_ref[...], up_b_ref[...])
        logistic = jax.nn.sigmoid(pre_gate)
        active = pre_gate * logistic
        active_ref[...] = active
        slope_ref[...] = pre_up * (logistic * (1.0 + pre_gate * (1.0 - logistic)))
        inner_ref[:, pl.ds(pl.multiple_of(step * tile, tile), tile)] = (active * pre_up).astype(bf16)

    @pl.when(step == first)
    def _():
        low_down_ref[...] = mm(inner_ref[...], down_a_ref[...]).astype(bf16)

    @pl.when(step >= first)
    def _():
        value = mm(inner_ref[...], down_ref[...]) + adapter_scale * mm(
            low_down_ref[...], down_b_ref[...]
        )
        routed_ref[...] = (keep_ref[:, :1] * value).astype(bf16)


def weigh_kernel(
    info_ref, routed_ref, keep_ref, kept_ref, came_ref, grad_ref, out_kept_ref, out_sent_ref
):
    half, width = kept_ref.shape[0], routed_ref.shape[1]
    experts = info_ref[3]
    mine = 2 * info_ref[0] + info_ref[1]
    lane = lax.broadcasted_iota(jnp.int32, (half, LANES), 1)
    high_lane, low_lane = lane == mine, lane == mine + experts
    chunk = 4 * LANES
    for cot_ref, out_ref, base in ((kept_ref, out_kept_ref, 0), (came_ref, out_sent_ref, half)):
        tail = cot_ref[:, width:].astype(f32)
        gate = jnp.sum(jnp.where(high_lane | low_lane, tail, 0.0), axis=1, keepdims=True)
        grad_gate = keep_ref[pl.ds(base, half), :1] * gate
        total = jnp.zeros((half, LANES), f32)
        for at in range(0, width, chunk):
            cot = cot_ref[:, at : at + chunk].astype(f32)
            routed = routed_ref[pl.ds(base, half), at : at + chunk].astype(f32)
            grad_ref[pl.ds(base, half), at : at + chunk] = (grad_gate * cot).astype(bf16)
            out_ref[:, at : at + chunk] = (gate * routed).astype(bf16)
            product = cot * routed
            for part in range(0, chunk, LANES):
                total += product[:, part : part + LANES]
        dots = jnp.sum(total, axis=1, keepdims=True)
        high = dots.astype(bf16).astype(f32)
        out_ref[:, width:] = jnp.where(
            high_lane, high, jnp.where(low_lane, dots - high, 0.0)
        ).astype(bf16)


def parts_kernel(count, select_ref, kept_ref, came_ref, *outs):
    for i in range(count):
        at = pl.ds(i * MOST, MOST)
        both = jnp.concatenate([kept_ref[at], came_ref[at]], axis=0)
        part = mm_tn(select_ref[i], both).astype(bf16)
        if i < count - 1:
            outs[i][...] = part
        else:
            rows = part.shape[0] // 2
            outs[i][...] = part[:rows]
            outs[i + 1][...] = part[rows:]


def inner_grad_kernel(
    grad_ref, down_ref, down_b_ref, down_a_ref, slope_ref, active_ref, up_b_ref,
    gate_out_ref, up_out_ref, back_low_ref, back_up_ref, total_ref,
):
    step = pl.program_id(0)

    @pl.when(step == 0)
    def _():
        back_low_ref[...] = mm_nt(grad_ref[...], down_b_ref[...]).astype(bf16)
        total_ref[...] = jnp.zeros_like(total_ref)

    inner = mm_nt(grad_ref[...], down_ref[...]) + adapter_scale * mm_nt(
        back_low_ref[...], down_a_ref[...]
    )
    gate_out_ref[...] = (inner * slope_ref[...]).astype(bf16)
    grad_up = (inner * active_ref[...]).astype(bf16)
    up_out_ref[...] = grad_up
    total_ref[...] += mm_nt(grad_up, up_b_ref[...])

    @pl.when(step == pl.num_programs(0) - 1)
    def _():
        back_up_ref[...] = total_ref[...].astype(bf16)


def row_grad_kernel(
    grad_gate_ref, grad_up_ref, back_up_ref, gate_ref, up_ref, up_a_ref, kept_ref, sent_ref
):
    half = kept_ref.shape[0]
    value = (
        mm_nt(grad_gate_ref[...], gate_ref[...])
        + mm_nt(grad_up_ref[...], up_ref[...])
        + adapter_scale * mm_nt(back_up_ref[...], up_a_ref[...])
    ).astype(bf16)
    kept_ref[...] = value[:half]
    sent_ref[...] = value[half:]


def ring_of(count):
    if count == 8:
        order = [0, 2, 4, 6, 7, 5, 3, 1]
    else:
        order = list(range(count))
    ahead = [(order[i], order[(i + 1) % count]) for i in range(count)]
    back = [(b, a) for a, b in ahead]
    return order, ahead, back


def offsets_of(count):
    half = count // 2
    return [0] + [-k for k in range(1, half)] + list(range(1, half)) + [half]


def ring_gather(block, count):
    _, ahead, back = ring_of(count)
    half, rows = count // 2, block.shape[0] // 2
    from_behind, from_front = [block], [block]
    for _ in range(1, half):
        from_behind.append(lax.ppermute(from_behind[-1], "expert", ahead))
        from_front.append(lax.ppermute(from_front[-1], "expert", back))
    top = lax.ppermute(from_behind[-1][:rows], "expert", ahead)
    low = lax.ppermute(from_front[-1][rows:], "expert", back)
    return from_behind + from_front[1:] + [top, low]


def ring_scatter(parts, count):
    _, ahead, back = ring_of(count)
    half = count // 2
    narrow = lambda v: v.astype(bf16)
    wide = lambda v: v.astype(f32)
    rows = parts[-1].shape[0]
    forth = lax.ppermute(parts[-2], "expert", ahead)
    hither = lax.ppermute(parts[-1], "expert", back)
    for k in range(half - 1, 0, -1):
        front, rear = parts[half - 1 + k], parts[k]
        if k == half - 1:
            front = jnp.concatenate([narrow(wide(front[:rows]) + wide(forth)), front[rows:]], axis=0)
            rear = jnp.concatenate([rear[:rows], narrow(wide(rear[rows:]) + wide(hither))], axis=0)
        else:
            front, rear = narrow(wide(front) + wide(forth)), narrow(wide(rear) + wide(hither))
        forth = lax.ppermute(front, "expert", ahead)
        hither = lax.ppermute(rear, "expert", back)
    return wide(parts[0]) + wide(forth) + wide(hither)


def swap_cores(value):
    return lax.ppermute(value, "dp", [(0, 1), (1, 0)])


def make_per_device(count):
    order, _, _ = ring_of(count)
    offsets = offsets_of(count)
    place = [order.index(chip) for chip in range(count)]
    table = np.array(
        [[order[(place[c] + off) % count] for off in offsets] for c in range(count)], np.int32
    )

    def per_device(
        tokens,
        cotangent,
        expert_choice_index,
        capacity,
        router_matrix,
        gate_matrix,
        up_matrix,
        down_matrix,
        up_adapter_first,
        up_adapter_second,
        down_adapter_first,
        down_adapter_second,
    ):
        tok_count, width = tokens.shape
        experts = router_matrix.shape[1]
        load = width + LANES
        half = count * MOST
        slots = 2 * half
        chip, core = lax.axis_index("expert"), lax.axis_index("dp")
        info = jnp.stack([chip, core, capacity[0], jnp.int32(experts)]).astype(jnp.int32)
        gate_w, up_w, down_w = gate_matrix[0], up_matrix[0], down_matrix[0]
        up_a, up_b = up_adapter_first[0], up_adapter_second[0]
        down_a, down_b = down_adapter_first[0], down_adapter_second[0]
        hidden, rank = gate_w.shape[1], up_a.shape[1]

        (token_load,) = call(
            token_load_kernel, [struct((tok_count, load))], [in_vmem] * 2,
            (expert_choice_index, tokens), (0, 2 * nbytes([tokens])),
        )
        cot_load, hits, affinity = call(
            cot_load_kernel,
            [struct((tok_count, load))] + [struct((tok_count, experts), f32)] * 2,
            [in_vmem] * 4,
            (expert_choice_index, tokens, router_matrix, cotangent),
            (0, 8 * nbytes([tokens])),
        )

        token_blocks = ring_gather(token_load, count)
        cot_blocks = ring_gather(cot_load, count)

        kept, sent, select = call(
            functools.partial(token_slots_kernel, count),
            [struct((half, load))] * 2 + [struct((count, 2 * MOST, tok_count))],
            [in_smem] + [in_vmem] * (count + 1),
            (info, *token_blocks),
            (0, 2 * count * nbytes([token_load])),
        )
        came = swap_cores(sent)
        first, tile, wide_tile = 4, hidden // 4, 4 * LANES
        column = lambda j: jnp.minimum(j, first - 1)
        late = lambda j: jnp.maximum(j - first, 0)
        full = lambda shape: pl.BlockSpec(shape, lambda j: (0,) * len(shape))
        routed, keep, slope, active, low_up, inner, low_down = call(
            functools.partial(forward_kernel, count, first),
            [
                struct((slots, width)), struct((slots, LANES), f32),
                struct((slots, hidden), f32), struct((slots, hidden), f32),
                struct((slots, rank)), struct((slots, hidden)), struct((slots, rank)),
            ],
            [
                in_smem, in_smem, full((half, load)), full((half, load)),
                pl.BlockSpec((width, tile), lambda j: (0, column(j))),
                pl.BlockSpec((width, tile), lambda j: (0, column(j))),
                pl.BlockSpec((hidden, wide_tile), lambda j: (0, late(j))),
                full((width, rank)),
                pl.BlockSpec((rank, tile), lambda j: (0, column(j))),
                full((hidden, rank)),
                pl.BlockSpec((rank, wide_tile), lambda j: (0, late(j))),
            ],
            (info, jnp.asarray(table), kept, came, gate_w, up_w, down_w, up_a, up_b, down_a, down_b),
            (6 * slots * width * hidden, 3 * nbytes([gate_w])),
            out_specs=[
                pl.BlockSpec((slots, wide_tile), lambda j: (0, late(j))),
                full((slots, LANES)),
                pl.BlockSpec((slots, tile), lambda j: (0, column(j))),
                pl.BlockSpec((slots, tile), lambda j: (0, column(j))),
                full((slots, rank)), full((slots, hidden)), full((slots, rank)),
            ],
            grid=(first + width // wide_tile,),
            scratch=[pltpu.VMEM((slots, width), bf16)],
        )

        cot_kept, cot_sent = call(
            functools.partial(cot_slots_kernel, count),
            [struct((half, load))] * 2,
            [in_vmem] * (count + 2),
            (select, *cot_blocks),
            (0, 2 * count * nbytes([token_load])),
        )
        cot_came = swap_cores(cot_sent)
        grad_routed, mix_kept, mix_sent = call(
            weigh_kernel,
            [struct((slots, width))] + [struct((half, load))] * 2,
            [in_smem] + [in_vmem] * 4,
            (info, routed, keep, cot_kept, cot_came),
            (0, 4 * nbytes([routed])),
        )

        def to_tokens(kept, sent):
            came, columns = swap_cores(sent), kept.shape[1]
            parts = call(
                functools.partial(parts_kernel, count),
                [struct((tok_count, columns))] * (count - 1)
                + [struct((tok_count // 2, columns))] * 2,
                [in_vmem] * 3,
                (select, kept, came),
                (0, 3 * nbytes([kept, came])),
            )
            return ring_scatter(parts, count)

        mixed_all = to_tokens(mix_kept, mix_sent)
        mixed = mixed_all[:, :width].astype(bf16)

        grad_gate, grad_up, back_low, back_up = call(
            inner_grad_kernel,
            [struct((slots, hidden))] * 2 + [struct((slots, rank))] * 2,
            [
                full((slots, width)),
                pl.BlockSpec((tile, width), lambda j: (j, 0)),
                full((rank, width)),
                pl.BlockSpec((tile, rank), lambda j: (j, 0)),
                pl.BlockSpec((slots, tile), lambda j: (0, j)),
                pl.BlockSpec((slots, tile), lambda j: (0, j)),
                pl.BlockSpec((rank, tile), lambda j: (0, j)),
            ],
            (grad_routed, down_w, down_b, down_a, slope, active, up_b),
            (2 * slots * width * hidden, nbytes([gate_w])),
            out_specs=[pl.BlockSpec((slots, tile), lambda j: (0, j))] * 2
            + [full((slots, rank))] * 2,
            grid=(4,),
            scratch=[pltpu.VMEM((slots, rank), f32)],
        )
        back_kept, back_sent = call(
            row_grad_kernel,
            [struct((half, width))] * 2,
            [
                full((slots, hidden)), full((slots, hidden)), full((slots, rank)),
                pl.BlockSpec((wide_tile, hidden), lambda j: (j, 0)),
                pl.BlockSpec((wide_tile, hidden), lambda j: (j, 0)),
                pl.BlockSpec((wide_tile, rank), lambda j: (j, 0)),
            ],
            (grad_gate, grad_up, back_up, gate_w, up_w, up_a),
            (4 * slots * width * hidden, 2 * nbytes([gate_w])),
            out_specs=[pl.BlockSpec((half, wide_tile), lambda j: (0, j))] * 2,
            grid=(width // wide_tile,),
        )
        back_all = to_tokens(back_kept, back_sent)
        block = jnp.concatenate([kept[:, :width], came[:, :width]], axis=0)
        grad_up_a = adapter_scale * mm_tn(block, back_up)
        grad_up_b = adapter_scale * mm_tn(low_up, grad_up)
        grad_down_a = adapter_scale * mm_tn(inner, back_low)
        grad_down_b = adapter_scale * mm_tn(low_down, grad_routed)

        chosen = hits * affinity
        chosen_sum = jnp.sum(chosen, axis=1, keepdims=True)
        grad_gates = (
            mixed_all[:, width : width + experts]
            + mixed_all[:, width + experts : width + 2 * experts]
        )
        grad_chosen = route_scale * (
            grad_gates / chosen_sum
            - jnp.sum(grad_gates * chosen, axis=1, keepdims=True) / (chosen_sum * chosen_sum)
        )
        grad_logits = (hits * grad_chosen * affinity * (1.0 - affinity)).astype(bf16)
        input_grad = (back_all + mm_nt(grad_logits, router_matrix)).astype(bf16)
        gathered, step = grad_logits[None], 1
        while step < count:
            arrived = lax.ppermute(gathered, "expert", [(i, i ^ step) for i in range(count)])
            gathered = jnp.concatenate([gathered, arrived], axis=0)
            step *= 2
        chips = jnp.sum(
            jnp.where(jnp.arange(count)[:, None] == chip, jnp.asarray(table), 0), axis=0
        )
        pick = ((chips ^ chip)[:, None] == jnp.arange(count, dtype=jnp.int32)[None, :]).astype(bf16)
        ordered = mm(pick, gathered.reshape(count, -1)).astype(bf16)
        router_half = mm_tn(
            ordered.reshape(count * tok_count, experts),
            jnp.concatenate(token_blocks, axis=0)[:, :width],
        )
        router_grad = (router_half + swap_cores(router_half)).T
        return (
            mixed,
            input_grad,
            router_grad,
            grad_up_a.astype(bf16)[None],
            grad_up_b.astype(bf16)[None],
            grad_down_a.astype(bf16)[None],
            grad_down_b.astype(bf16)[None],
        )

    return per_device


def solution(mesh):
    rows = P(("groups", "expert", "dp"), None)
    whole = P(("groups", "expert", "dp"), None, None)
    weight = P(("expert", "dp"), None, None)
    return jax.shard_map(
        make_per_device(mesh.shape["expert"]),
        mesh=mesh,
        in_specs=(rows, rows, rows, P(("groups", "expert", "dp")), P()) + (weight,) * 7,
        out_specs=(rows, rows, P("groups", None), whole, whole, whole, whole),
        check_vma=False,
    )
```

time: 161 us -> 175 us (1.087)
  Pallas kernels: 0 us -> 62.6 us
  matrix products: 46.2 us -> 5.73 us
  other arithmetic: 12.5 us -> 2.47 us
  starting transfers between devices: 39.1 us -> 45.6 us
  waiting for transfers between devices: 39.5 us -> 35.2 us
    pallas_call x0 -> x10, Pallas kernels: none -> 62.6 us  [call(): pl.pallas_call(body, out_shape=outs, grid=grid, in_specs=specs, out_specs...]
    dot_general x37 -> x7, matrix products: 42.9 us -> 5.73 us  [mm(): lax.dot_general(left, right, ((axes[0], axes[1]), ((), ())), preferred_el...]
    ppermute x6, waiting for transfers between devices: 0.17 us -> 13.1 us  [ring_gather(): from_front.append(lax.ppermute(from_front[-1], 'expert', back))]
    ppermute x6, starting transfers between devices: 0.18 us -> 12.8 us  [ring_gather(): from_front.append(lax.ppermute(from_front[-1], 'expert', back))]
    ppermute x6, starting transfers between devices: 13.1 us -> 0.68 us  [ring_gather(): from_behind.append(lax.ppermute(from_behind[-1], 'expert', ahead))]
    ppermute x6, waiting for transfers between devices: 11.7 us -> 0.02 us  [ring_gather(): from_behind.append(lax.ppermute(from_behind[-1], 'expert', ahead))]
    unnamed x98 -> x112, local copies, waits for them, and re-layouts: 3.18 us -> 14.6 us
    concatenate x6 -> x5, local copies, waits for them, and re-layouts: 5.22 us -> 0.39 us  [the longest x4 0.37 us: per_device(): gathered = jnp.concatenate([gathered, arrived], axis=0)]
  transfers between devices with their start and end apart: 40 -> 40, of which waited for: 18 -> 12; matrix products, arithmetic and copies ran while one was open for 35% -> 12% of each run, Pallas kernels for 0% -> 21%
where the time goes in v2:
time: 175 us; the launch traced here: 174 us
  Pallas kernels  62.6 us (36%)
  starting transfers between devices  45.6 us (26%)
  waiting for transfers between devices  35.2 us (20%)
  local copies, waits for them, and re-layouts  20.9 us (12%)
  matrix products  5.73 us (3%)
  other arithmetic  2.47 us (1%)
  between operations  1.88 us (1%)
    pallas_call x10, Pallas kernels, call(): pl.pallas_call(body, out_shape=outs, grid=grid, in_specs=specs, out_specs...  62.6 us
    unnamed x112, local copies, waits for them, and re-layouts  14.6 us
    ppermute x6, waiting for transfers between devices, ring_scatter(): hither = lax.ppermute(rear, 'expert', back)  14.3 us
    ppermute x6, waiting for transfers between devices, ring_gather(): from_front.append(lax.ppermute(from_front[-1], 'expert', back))  13.1 us
    ppermute x6, starting transfers between devices, ring_gather(): from_front.append(lax.ppermute(from_front[-1], 'expert', back))  12.8 us
    ppermute x6, starting transfers between devices, ring_scatter(): forth = lax.ppermute(front, 'expert', ahead)  8.89 us
    ppermute x3, starting transfers between devices, per_device(): lax.ppermute(gathered, 'expert', [(i, i ^ step) for i in range(count)])  7.64 us
    ppermute x6, starting transfers between devices, ring_scatter(): hither = lax.ppermute(rear, 'expert', back)  6.07 us
  transfers between devices with their start and end apart: 40, of which 12 were waited for; matrix products, arithmetic and copies ran while one was open for 12% of the time, Pallas kernels for 21%

profile of v2, /device:TPU:0, one launch (start us, length us, event | category | flops | bytes accessed | tf_op | source)
XLA Modules:
  0.0 174.4 jit_solution(327153939524178927)
XLA Ops:
  3.8 3.0 %collective-permute-start.3 = (bf16[32,3712]{1,0:T(8,128)(2,1)}, bf16[32,3712]{1,0:T(8,128)(2,1)S(1)}, u32[]{:S(2)}, u32[]{:S(2)}) collective-permute-start(bf16[32,3712]{1,0:T(8,128)(2,1)} %shard_map.180.refs_0_), channel_id=1, source_target_pairs={{4,0},{8,4},{12,8},{14,12},{10,14},{6,10},{2,6},{0,2},{5,1},{9,5},... | collective-permute-start | bytes 712712 | tf_op jit(solution)/shard_map/ppermute | solution.py:284
  6.9 2.1 %copy.29.router_ref = bf16[3584,16]{1,0:T(8,128)(2,1)} copy(bf16[3584,16]{0,1:T(8,128)(2,1)} %param.17) | data formatting | bytes 229376 | tf_op args[4]
  9.0 2.5 %shard_map.183 = (bf16[32,3712]{1,0:T(8,128)(2,1)}, f32[32,16]{1,0:T(8,128)}, f32[32,16]{1,0:T(8,128)}) custom-call(s32[32,8]{1,0:T(8,128)} %copy.25.choice_ref, bf16[32,3584]{1,0:T(8,128)(2,1)} %tokens_ref.3, bf16[3584,16]{1,0:T(8,128)(2,1)} %copy.29.router_ref, bf16[32,3584]{1,0:T(8,128)(2,1)} %cot_ref.1), custom_call_target="tpu_custom_call" | custom-call | bytes 1835008 | tf_op jit(solution)/shard_map/pallas_call | solution.py:39
  17.9 2.0 %collective-permute-start.4 = (bf16[32,3712]{1,0:T(8,128)(2,1)S(1)}, bf16[32,3712]{1,0:T(8,128)(2,1)S(1)}, u32[]{:S(2)}, u32[]{:S(2)}) collective-permute-start(bf16[32,3712]{1,0:T(8,128)(2,1)S(1)} %collective-permute-done.3.refs_4_), channel_id=1, source_target_pairs={{4,0},{8,4},{12,8},{14,12},{10,14},{6,10},{2,6},{0,2},{5,1},{9,5},... | collective-permute-start | bytes 712712 | tf_op jit(solution)/shard_map/ppermute | solution.py:284
  22.1 4.5 %collective-permute-done.4.refs_5_ = bf16[32,3712]{1,0:T(8,128)(2,1)S(1)} collective-permute-done((bf16[32,3712]{1,0:T(8,128)(2,1)S(1)}, bf16[32,3712]{1,0:T(8,128)(2,1)S(1)}, u32[]{:S(2)}, u32[]{:S(2)}) %collective-permute-start.4) | collective-permute-done | bytes 237600 | tf_op jit(solution)/shard_map/ppermute | solution.py:284
  28.8 3.0 %collective-permute-done.13.refs_5_ = bf16[32,3712]{1,0:T(8,128)(2,1)S(1)} collective-permute-done((bf16[32,3712]{1,0:T(8,128)(2,1)S(1)}, bf16[32,3712]{1,0:T(8,128)(2,1)S(1)}, u32[]{:S(2)}, u32[]{:S(2)}) %collective-permute-start.13) | collective-permute-done | bytes 237600 | tf_op jit(solution)/shard_map/ppermute | solution.py:284
  33.9 3.0 %collective-permute-done.5.refs_6_ = bf16[32,3712]{1,0:T(8,128)(2,1)S(1)} collective-permute-done((bf16[32,3712]{1,0:T(8,128)(2,1)S(1)}, bf16[32,3712]{1,0:T(8,128)(2,1)S(1)}, u32[]{:S(2)}, u32[]{:S(2)}) %collective-permute-start.5) | collective-permute-done | bytes 237600 | tf_op jit(solution)/shard_map/ppermute | solution.py:284
  36.8 2.0 %collective-permute-start.7 = (bf16[16,3712]{1,0:T(8,128)(2,1)S(1)}, bf16[16,3712]{1,0:T(8,128)(2,1)S(1)}, u32[]{:S(2)}, u32[]{:S(2)}) collective-permute-start(bf16[16,3712]{1,0:T(8,128)(2,1)S(1)} %slice.74), channel_id=1, source_target_pairs={{4,0},{8,4},{12,8},{14,12},{10,14},{6,10},{2,6},{0,2},{5,1},{9,5},... | collective-permute-start | bytes 356360 | tf_op jit(solution)/shard_map/ppermute | solution.py:286
  39.0 2.6 %collective-permute-done.14.refs_6_ = bf16[32,3712]{1,0:T(8,128)(2,1)S(1)} collective-permute-done((bf16[32,3712]{1,0:T(8,128)(2,1)S(1)}, bf16[32,3712]{1,0:T(8,128)(2,1)S(1)}, u32[]{:S(2)}, u32[]{:S(2)}) %collective-permute-start.14) | collective-permute-done | bytes 237600 | tf_op jit(solution)/shard_map/ppermute | solution.py:284
  41.6 2.0 %collective-permute-start.16 = (bf16[16,3712]{1,0:T(8,128)(2,1)S(1)}, bf16[16,3712]{1,0:T(8,128)(2,1)S(1)}, u32[]{:S(2)}, u32[]{:S(2)}) collective-permute-start(bf16[16,3712]{1,0:T(8,128)(2,1)S(1)} %slice.76), channel_id=1, source_target_pairs={{4,0},{8,4},{12,8},{14,12},{10,14},{6,10},{2,6},{0,2},{5,1},{9,5},... | collective-permute-start | bytes 356360 | tf_op jit(solution)/shard_map/ppermute | solution.py:286
  45.8 5.6 %shard_map.181 = (bf16[128,3712]{1,0:T(8,128)(2,1)}, bf16[128,3712]{1,0:T(8,128)(2,1)}, bf16[8,32,32]{2,1,0:T(8,128)(2,1)}) custom-call(s32[4]{0:T(128)} %pad_add_fusion.info_ref, bf16[32,3712]{1,0:T(8,128)(2,1)} %shard_map.180.refs_0_, bf16[32,3712]{1,0:T(8,128)(2,1)} %copy-done.8, bf16[32,3712]{1,0:T(8,128)(2,1)} %copy-done.10, ...), custom_call_target="tpu_custom_call" | custom-call | bytes 3801088 | tf_op jit(solution)/shard_map/pallas_call | solution.py:39
  55.4 3.5 %shard_map.184 = (bf16[128,3712]{1,0:T(8,128)(2,1)}, bf16[128,3712]{1,0:T(8,128)(2,1)}) custom-call(bf16[8,32,32]{2,1,0:T(8,128)(2,1)} %get-tuple-element.49.select_ref, bf16[32,3712]{1,0:T(8,128)(2,1)} %get-tuple-element.54.refs_0_, bf16[32,3712]{1,0:T(8,128)(2,1)} %copy-done.30, bf16[32,3712]{1,0:T(8,128)(2,1)} %copy-done.32, bf16[32,3712]{1,0:T(8,128)(2,1)} %copy-done.14, ...), custom_call_target="tpu_custom_call" | custom-call | bytes 3801088 | tf_op jit(solution)/shard_map/pallas_call | solution.py:39
  60.4 18.6 %shard_map.182 = (bf16[256,3584]{1,0:T(8,128)(2,1)}, f32[256,128]{1,0:T(8,128)}, f32[256,1024]{1,0:T(8,128)}, f32[256,1024]{1,0:T(8,128)}, bf16[256,64]{1,0:T(8,...) custom-call(s32[4]{0:T(128)} %pad_add_fusion.info_ref, s32[8,8]{1,0:T(8,128)} %constant.8.clone.table_ref, ...), custom_call_target="tpu_custom_call" | custom-call | flops 5637144576 | bytes 22020096 | tf_op jit(solution)/shard_map/pallas_call | solution.py:39
  79.9 4.6 %shard_map.185 = (bf16[256,3584]{1,0:T(8,128)(2,1)}, bf16[128,3712]{1,0:T(8,128)(2,1)}, bf16[128,3712]{1,0:T(8,128)(2,1)}) custom-call(s32[4]{0:T(128)} %pad_add_fusion.info_ref, bf16[256,3584]{1,0:T(8,128)(2,1)} %get-tuple-element.52.routed_ref, f32[256,128]{1,0:T(8,128)} %get-tuple-element.53.keep_ref, bf16[128,3712]{1,0:T(8,128)(2,1)} %get-tuple-element.55.kept_ref, ...), custom_call_target="tpu_custom_call" | custom-call | bytes 7340032 | tf_op jit(solution)/shard_map/pallas_call | solution.py:39
  84.5 8.8 %shard_map.187 = (bf16[256,1024]{1,0:T(8,128)(2,1)}, bf16[256,1024]{1,0:T(8,128)(2,1)}, bf16[256,64]{1,0:T(8,128)(2,1)}, bf16[256,64]{1,0:T(8,128)(2,1)}) custom-call(bf16[256,3584]{1,0:T(8,128)(2,1)} %get-tuple-element.68.grad_ref, bf16[1024,3584]{1,0:T(8,128)(2,1)} %bitcast.31, bf16[64,3584]{1,0:T(8,128)(2,1)} %bitcast.41, bf16[1024,64]{1,0:T(8,128)(2,1)} %bitcast.39, ...), custom_call_target="tpu_custom_call" | custom-call | flops 1879048192 | bytes 7340032 | tf_op jit(solution)/shard_map/pallas_call | solution.py:39
  93.4 11.3 %shard_map.188 = (bf16[128,3584]{1,0:T(8,128)(2,1)}, bf16[128,3584]{1,0:T(8,128)(2,1)}) custom-call(bf16[256,1024]{1,0:T(8,128)(2,1)} %get-tuple-element.71.grad_gate_ref, bf16[256,1024]{1,0:T(8,128)(2,1)} %get-tuple-element.72.grad_up_ref, bf16[256,64]{1,0:T(8,128)(2,1)} %get-tuple-element.73.back_up_ref, bf16[3584,1024]{1,0:T(8,128)(2,1)} %bitcast.33, ...), custom_call_target="tpu_custom_call" | custom-call | flops 3758096384 | bytes 14680064 | tf_op jit(solution)/shard_map/pallas_call | solution.py:39
  110.4 3.0 %shard_map.189 = (bf16[32,3584]{1,0:T(8,128)(2,1)}, bf16[32,3584]{1,0:T(8,128)(2,1)}, bf16[32,3584]{1,0:T(8,128)(2,1)}, bf16[32,3584]{1,0:T(8,128)(2,1)}, bf16[3...) custom-call(bf16[8,32,32]{2,1,0:T(8,128)(2,1)} %get-tuple-element.49, ...), custom_call_target="tpu_custom_call" | custom-call | bytes 5505024 | tf_op jit(solution)/shard_map/pallas_call | solution.py:39
  119.2 3.0 %shard_map.186 = (bf16[32,3712]{1,0:T(8,128)(2,1)}, bf16[32,3712]{1,0:T(8,128)(2,1)}, bf16[32,3712]{1,0:T(8,128)(2,1)}, bf16[32,3712]{1,0:T(8,128)(2,1)}, bf16[3...) custom-call(bf16[8,32,32]{2,1,0:T(8,128)(2,1)} %get-tuple-element.49, ...), custom_call_target="tpu_custom_call" | custom-call | bytes 5701632 | tf_op jit(solution)/shard_map/pallas_call | solution.py:39
  128.5 3.4 %collective-permute-done.23 = bf16[16,3712]{1,0:T(8,128)(2,1)S(1)} collective-permute-done((bf16[16,3712]{1,0:T(8,128)(2,1)}, bf16[16,3712]{1,0:T(8,128)(2,1)S(1)}, u32[]{:S(2)}, u32[]{:S(2)}) %collective-permute-start.23) | collective-permute-done | bytes 118816 | tf_op jit(solution)/shard_map/ppermute | solution.py:297
  134.2 5.9 %collective-permute-done.24 = bf16[32,3712]{1,0:T(8,128)(2,1)S(1)} collective-permute-done((bf16[32,3712]{1,0:T(8,128)(2,1)S(1)}, bf16[32,3712]{1,0:T(8,128)(2,1)S(1)}, u32[]{:S(2)}, u32[]{:S(2)}) %collective-permute-start.24) | collective-permute-done | bytes 237600 | tf_op jit(solution)/shard_map/ppermute | solution.py:306
  142.3 4.0 %collective-permute-done.25 = bf16[32,3712]{1,0:T(8,128)(2,1)S(1)} collective-permute-done((bf16[32,3712]{1,0:T(8,128)(2,1)S(1)}, bf16[32,3712]{1,0:T(8,128)(2,1)S(1)}, u32[]{:S(2)}, u32[]{:S(2)}) %collective-permute-start.25) | collective-permute-done | bytes 237600 | tf_op jit(solution)/shard_map/ppermute | solution.py:306
  149.4 4.4 %collective-permute-done.26 = bf16[32,3712]{1,0:T(8,128)(2,1)S(1)} collective-permute-done((bf16[32,3712]{1,0:T(8,128)(2,1)S(1)}, bf16[32,3712]{1,0:T(8,128)(2,1)S(1)}, u32[]{:S(2)}, u32[]{:S(2)}) %collective-permute-start.26) | collective-permute-done | bytes 237600 | tf_op jit(solution)/shard_map/ppermute | solution.py:306
  162.2 4.4 %collective-permute-start.38 = (bf16[4,32,16]{2,1,0:T(8,128)(2,1)S(1)}, bf16[4,32,16]{2,1,0:T(8,128)(2,1)S(1)}, u32[]{:S(2)}, u32[]{:S(2)}) collective-permute-start(bf16[4,32,16]{2,1,0:T(8,128)(2,1)S(1)} %pad_maximum_fusion.4), channel_id=1, source_target_pairs={{0,8},{2,10},{4,12},{6,14},{8,0},{10,2},{12,4},{14,6},{1,9},{3,11}... | collective-permute-start | bytes 12296 | tf_op jit(solution)/shard_map/ppermute | solution.py:490
  166.7 2.5 %collective-permute-start.31 = (bf16[32,3584]{1,0:T(8,128)(2,1)S(1)}, bf16[32,3584]{1,0:T(8,128)(2,1)S(1)}, u32[]{:S(2)}, u32[]{:S(2)}) collective-permute-start(bf16[32,3584]{1,0:T(8,128)(2,1)S(1)} %add_convert_fusion.7), channel_id=1, source_target_pairs={{0,4},{4,8},{8,12},{12,14},{14,10},{10,6},{6,2},{2,0},{1,5},{5,9},... | collective-permute-start | bytes 688136 | tf_op jit(solution)/shard_map/ppermute | solution.py:305
  (230 shorter events, 62.9 us)
Async XLA Ops:
  3.8 14.0 %collective-permute-start.3 = (bf16[32,3712]{1,0:T(8,128)(2,1)}, bf16[32,3712]{1,0:T(8,128)(2,1)S(1)}, u32[]{:S(2)}, u32[]{:S(2)}) collective-permute-start(bf16[32,3712]{1,0:T(8,128)(2,1)} %shard_map.180.refs_0_), channel_id=1, source_target_pairs={{4,0},{8,4},{12,8},{14,12},{10,14},{6,10},{2,6},{0,2},{5,1},{9,5},... | collective-permute-start | bytes 712712 | tf_op jit(solution)/shard_map/ppermute | solution.py:284
  6.8 13.1 %collective-permute-start = (bf16[32,3712]{1,0:T(8,128)(2,1)}, bf16[32,3712]{1,0:T(8,128)(2,1)S(1)}, u32[]{:S(2)}, u32[]{:S(2)}) collective-permute-start(bf16[32,3712]{1,0:T(8,128)(2,1)} %shard_map.180.refs_0_), channel_id=1, source_target_pairs={{0,4},{4,8},{8,12},{12,14},{14,10},{10,6},{6,2},{2,0},{1,5},{5,9},... | collective-permute-start | bytes 712712 | tf_op jit(solution)/shard_map/ppermute | solution.py:283
  11.5 8.6 %collective-permute-start.12 = (bf16[32,3712]{1,0:T(8,128)(2,1)}, bf16[32,3712]{1,0:T(8,128)(2,1)S(1)}, u32[]{:S(2)}, u32[]{:S(2)}) collective-permute-start(bf16[32,3712]{1,0:T(8,128)(2,1)} %get-tuple-element.54.refs_0_), channel_id=1, source_target_pairs={{4,0},{8,4},{12,8},{14,12},{10,14},{6,10},{2,6},{0,2},{5,1},{9,5},... | collective-permute-start | bytes 712712 | tf_op jit(solution)/shard_map/ppermute | solution.py:284
  13.4 8.5 %collective-permute-start.9 = (bf16[32,3712]{1,0:T(8,128)(2,1)}, bf16[32,3712]{1,0:T(8,128)(2,1)S(1)}, u32[]{:S(2)}, u32[]{:S(2)}) collective-permute-start(bf16[32,3712]{1,0:T(8,128)(2,1)} %get-tuple-element.54.refs_0_), channel_id=1, source_target_pairs={{0,4},{4,8},{8,12},{12,14},{14,10},{10,6},{6,2},{2,0},{1,5},{5,9},... | collective-permute-start | bytes 712712 | tf_op jit(solution)/shard_map/ppermute | solution.py:283
  17.9 8.8 %collective-permute-start.4 = (bf16[32,3712]{1,0:T(8,128)(2,1)S(1)}, bf16[32,3712]{1,0:T(8,128)(2,1)S(1)}, u32[]{:S(2)}, u32[]{:S(2)}) collective-permute-start(bf16[32,3712]{1,0:T(8,128)(2,1)S(1)} %collective-permute-done.3.refs_4_), channel_id=1, source_target_pairs={{4,0},{8,4},{12,8},{14,12},{10,14},{6,10},{2,6},{0,2},{5,1},{9,5},... | collective-permute-start | bytes 712712 | tf_op jit(solution)/shard_map/ppermute | solution.py:284
  19.9 8.7 %collective-permute-start.1 = (bf16[32,3712]{1,0:T(8,128)(2,1)S(1)}, bf16[32,3712]{1,0:T(8,128)(2,1)S(1)}, u32[]{:S(2)}, u32[]{:S(2)}) collective-permute-start(bf16[32,3712]{1,0:T(8,128)(2,1)S(1)} %collective-permute-done.refs_1_), channel_id=1, source_target_pairs={{0,4},{4,8},{8,12},{12,14},{14,10},{10,6},{6,2},{2,0},{1,5},{5,9},... | collective-permute-start | bytes 712712 | tf_op jit(solution)/shard_map/ppermute | solution.py:283
  20.0 11.7 %collective-permute-start.13 = (bf16[32,3712]{1,0:T(8,128)(2,1)S(1)}, bf16[32,3712]{1,0:T(8,128)(2,1)S(1)}, u32[]{:S(2)}, u32[]{:S(2)}) collective-permute-start(bf16[32,3712]{1,0:T(8,128)(2,1)S(1)} %collective-permute-done.12.refs_4_), channel_id=1, source_target_pairs={{4,0},{8,4},{12,8},{14,12},{10,14},{6,10},{2,6},{0,2},{5,1},{9,5},... | collective-permute-start | bytes 712712 | tf_op jit(solution)/shard_map/ppermute | solution.py:284
  21.9 11.8 %collective-permute-start.10 = (bf16[32,3712]{1,0:T(8,128)(2,1)S(1)}, bf16[32,3712]{1,0:T(8,128)(2,1)S(1)}, u32[]{:S(2)}, u32[]{:S(2)}) collective-permute-start(bf16[32,3712]{1,0:T(8,128)(2,1)S(1)} %collective-permute-done.9.refs_1_), channel_id=1, source_target_pairs={{0,4},{4,8},{8,12},{12,14},{14,10},{10,6},{6,2},{2,0},{1,5},{5,9},... | collective-permute-start | bytes 712712 | tf_op jit(solution)/shard_map/ppermute | solution.py:283
  26.7 10.2 %collective-permute-start.5 = (bf16[32,3712]{1,0:T(8,128)(2,1)S(1)}, bf16[32,3712]{1,0:T(8,128)(2,1)S(1)}, u32[]{:S(2)}, u32[]{:S(2)}) collective-permute-start(bf16[32,3712]{1,0:T(8,128)(2,1)S(1)} %collective-permute-done.4.refs_5_), channel_id=1, source_target_pairs={{4,0},{8,4},{12,8},{14,12},{10,14},{6,10},{2,6},{0,2},{5,1},{9,5},... | collective-permute-start | bytes 712712 | tf_op jit(solution)/shard_map/ppermute | solution.py:284
  28.6 10.2 %collective-permute-start.2 = (bf16[32,3712]{1,0:T(8,128)(2,1)S(1)}, bf16[32,3712]{1,0:T(8,128)(2,1)S(1)}, u32[]{:S(2)}, u32[]{:S(2)}) collective-permute-start(bf16[32,3712]{1,0:T(8,128)(2,1)S(1)} %collective-permute-done.1.refs_2_), channel_id=1, source_target_pairs={{0,4},{4,8},{8,12},{12,14},{14,10},{10,6},{6,2},{2,0},{1,5},{5,9},... | collective-permute-start | bytes 712712 | tf_op jit(solution)/shard_map/ppermute | solution.py:283
  31.7 9.9 %collective-permute-start.14 = (bf16[32,3712]{1,0:T(8,128)(2,1)S(1)}, bf16[32,3712]{1,0:T(8,128)(2,1)S(1)}, u32[]{:S(2)}, u32[]{:S(2)}) collective-permute-start(bf16[32,3712]{1,0:T(8,128)(2,1)S(1)} %collective-permute-done.13.refs_5_), channel_id=1, source_target_pairs={{4,0},{8,4},{12,8},{14,12},{10,14},{6,10},{2,6},{0,2},{5,1},{9,5},... | collective-permute-start | bytes 712712 | tf_op jit(solution)/shard_map/ppermute | solution.py:284
  33.7 10.0 %collective-permute-start.11 = (bf16[32,3712]{1,0:T(8,128)(2,1)S(1)}, bf16[32,3712]{1,0:T(8,128)(2,1)S(1)}, u32[]{:S(2)}, u32[]{:S(2)}) collective-permute-start(bf16[32,3712]{1,0:T(8,128)(2,1)S(1)} %collective-permute-done.10.refs_2_), channel_id=1, source_target_pairs={{0,4},{4,8},{8,12},{12,14},{14,10},{10,6},{6,2},{2,0},{1,5},{5,9},... | collective-permute-start | bytes 712712 | tf_op jit(solution)/shard_map/ppermute | solution.py:283
  41.6 13.1 %collective-permute-start.16 = (bf16[16,3712]{1,0:T(8,128)(2,1)S(1)}, bf16[16,3712]{1,0:T(8,128)(2,1)S(1)}, u32[]{:S(2)}, u32[]{:S(2)}) collective-permute-start(bf16[16,3712]{1,0:T(8,128)(2,1)S(1)} %slice.76), channel_id=1, source_target_pairs={{4,0},{8,4},{12,8},{14,12},{10,14},{6,10},{2,6},{0,2},{5,1},{9,5},... | collective-permute-start | bytes 356360 | tf_op jit(solution)/shard_map/ppermute | solution.py:286
  43.7 11.1 %collective-permute-start.15 = (bf16[16,3712]{1,0:T(8,128)(2,1)S(1)}, bf16[16,3712]{1,0:T(8,128)(2,1)S(1)}, u32[]{:S(2)}, u32[]{:S(2)}) collective-permute-start(bf16[16,3712]{1,0:T(8,128)(2,1)S(1)} %slice.75), channel_id=1, source_target_pairs={{0,4},{4,8},{8,12},{12,14},{14,10},{10,6},{6,2},{2,0},{1,5},{5,9},... | collective-permute-start | bytes 356360 | tf_op jit(solution)/shard_map/ppermute | solution.py:285
  58.9 20.1 %collective-permute-start.17 = (bf16[128,3712]{1,0:T(8,128)(2,1)}, bf16[128,3712]{1,0:T(8,128)(2,1)S(1)}, u32[]{:S(2)}, u32[]{:S(2)}) collective-permute-start(bf16[128,3712]{1,0:T(8,128)(2,1)} %get-tuple-element.56), channel_id=1, source_target_pairs={{0,1},{1,0},{2,3},{3,2},{4,5},{5,4},{6,7},{7,6},{8,9},{9,8},{10,11... | collective-permute-start | bytes 2850824 | tf_op jit(solution)/shard_map/ppermute | solution.py:311
  104.8 13.5 %collective-permute-start.18 = (bf16[128,3712]{1,0:T(8,128)(2,1)S(1)}, bf16[128,3712]{1,0:T(8,128)(2,1)S(1)}, u32[]{:S(2)}, u32[]{:S(2)}) collective-permute-start(bf16[128,3712]{1,0:T(8,128)(2,1)S(1)} %copy-done.49), channel_id=1, source_target_pairs={{0,1},{1,0},{2,3},{3,2},{4,5},{5,4},{6,7},{7,6},{8,9},{9,8},{10,11... | collective-permute-start | bytes 2850824 | tf_op jit(solution)/shard_map/ppermute | solution.py:311
  113.4 12.8 %collective-permute-start.32 = (bf16[16,3584]{1,0:T(8,128)(2,1)}, bf16[16,3584]{1,0:T(8,128)(2,1)S(1)}, u32[]{:S(2)}, u32[]{:S(2)}) collective-permute-start(bf16[16,3584]{1,0:T(8,128)(2,1)} %get-tuple-element.84), channel_id=1, source_target_pairs={{4,0},{8,4},{12,8},{14,12},{10,14},{6,10},{2,6},{0,2},{5,1},{9,5},... | collective-permute-start | bytes 344072 | tf_op jit(solution)/shard_map/ppermute | solution.py:297
  117.8 10.1 %collective-permute-start.28 = (bf16[16,3584]{1,0:T(8,128)(2,1)}, bf16[16,3584]{1,0:T(8,128)(2,1)S(1)}, u32[]{:S(2)}, u32[]{:S(2)}) collective-permute-start(bf16[16,3584]{1,0:T(8,128)(2,1)} %get-tuple-element.80), channel_id=1, source_target_pairs={{0,4},{4,8},{8,12},{12,14},{14,10},{10,6},{6,2},{2,0},{1,5},{5,9},... | collective-permute-start | bytes 344072 | tf_op jit(solution)/shard_map/ppermute | solution.py:296
  124.1 8.6 %collective-permute-start.19 = (bf16[16,3712]{1,0:T(8,128)(2,1)}, bf16[16,3712]{1,0:T(8,128)(2,1)S(1)}, u32[]{:S(2)}, u32[]{:S(2)}) collective-permute-start(bf16[16,3712]{1,0:T(8,128)(2,1)} %get-tuple-element.63), channel_id=1, source_target_pairs={{0,4},{4,8},{8,12},{12,14},{14,10},{10,6},{6,2},{2,0},{1,5},{5,9},... | collective-permute-start | bytes 356360 | tf_op jit(solution)/shard_map/ppermute | solution.py:296
  126.2 22.4 %collective-permute-start.33 = (bf16[32,3584]{1,0:T(8,128)(2,1)S(1)}, bf16[32,3584]{1,0:T(8,128)(2,1)S(1)}, u32[]{:S(2)}, u32[]{:S(2)}) collective-permute-start(bf16[32,3584]{1,0:T(8,128)(2,1)S(1)} %pad_maximum_fusion.3), channel_id=1, source_target_pairs={{4,0},{8,4},{12,8},{14,12},{10,14},{6,10},{2,6},{0,2},{5,1},{9,5},... | collective-permute-start | bytes 688136 | tf_op jit(solution)/shard_map/ppermute | solution.py:306
  127.9 27.9 %collective-permute-start.29 = (bf16[32,3584]{1,0:T(8,128)(2,1)S(1)}, bf16[32,3584]{1,0:T(8,128)(2,1)S(1)}, u32[]{:S(2)}, u32[]{:S(2)}) collective-permute-start(bf16[32,3584]{1,0:T(8,128)(2,1)S(1)} %pad_maximum_fusion.2), channel_id=1, source_target_pairs={{0,4},{4,8},{8,12},{12,14},{14,10},{10,6},{6,2},{2,0},{1,5},{5,9},... | collective-permute-start | bytes 688136 | tf_op jit(solution)/shard_map/ppermute | solution.py:305
  148.7 10.9 %collective-permute-start.34 = (bf16[32,3584]{1,0:T(8,128)(2,1)S(1)}, bf16[32,3584]{1,0:T(8,128)(2,1)S(1)}, u32[]{:S(2)}, u32[]{:S(2)}) collective-permute-start(bf16[32,3584]{1,0:T(8,128)(2,1)S(1)} %add_convert_fusion.6), channel_id=1, source_target_pairs={{4,0},{8,4},{12,8},{14,12},{10,14},{6,10},{2,6},{0,2},{5,1},{9,5},... | collective-permute-start | bytes 688136 | tf_op jit(solution)/shard_map/ppermute | solution.py:306
  155.9 10.7 %collective-permute-start.30 = (bf16[32,3584]{1,0:T(8,128)(2,1)S(1)}, bf16[32,3584]{1,0:T(8,128)(2,1)S(1)}, u32[]{:S(2)}, u32[]{:S(2)}) collective-permute-start(bf16[32,3584]{1,0:T(8,128)(2,1)S(1)} %add_convert_fusion.8), channel_id=1, source_target_pairs={{0,4},{4,8},{8,12},{12,14},{14,10},{10,6},{6,2},{2,0},{1,5},{5,9},... | collective-permute-start | bytes 688136 | tf_op jit(solution)/shard_map/ppermute | solution.py:305
  159.7 11.3 %collective-permute-start.35 = (bf16[32,3584]{1,0:T(8,128)(2,1)S(1)}, bf16[32,3584]{1,0:T(8,128)(2,1)S(1)}, u32[]{:S(2)}, u32[]{:S(2)}) collective-permute-start(bf16[32,3584]{1,0:T(8,128)(2,1)S(1)} %add_convert_fusion.5), channel_id=1, source_target_pairs={{4,0},{8,4},{12,8},{14,12},{10,14},{6,10},{2,6},{0,2},{5,1},{9,5},... | collective-permute-start | bytes 688136 | tf_op jit(solution)/shard_map/ppermute | solution.py:306
  (67 other events, 671.7 us)

commit v3 on v1

v3 whole, which is shorter than its diff:
```python
import functools

import jax
import jax.numpy as jnp
import numpy as np
from jax import lax
from jax.experimental import pallas as pl
from jax.experimental.pallas import tpu as pltpu
from jax.sharding import PartitionSpec as P

MOST = 16
LANES = 128

route_scale = 2.5
adapter_scale = 2.0

bf16, f32 = jnp.bfloat16, jnp.float32
in_vmem = pl.BlockSpec(memory_space=pltpu.VMEM)
in_hbm = pl.BlockSpec(memory_space=pl.ANY)
plain = pl.BlockSpec()
in_smem = pl.BlockSpec(memory_space=pltpu.SMEM)


def mm(left, right, axes=((1,), (0,))):
    return lax.dot_general(
        left, right, ((axes[0], axes[1]), ((), ())), preferred_element_type=jnp.float32
    )


def mm_nt(left, right):
    return mm(left, right, ((1,), (1,)))


def mm_tn(left, right):
    return mm(left, right, ((0,), (0,)))


def call(body, outs, specs, operands, cost, scratch=(), mib=16, out_specs=None):
    flops, moved = cost
    return pl.pallas_call(
        body,
        out_shape=outs,
        in_specs=specs,
        out_specs=out_specs if out_specs is not None else [in_vmem] * len(outs),
        scratch_shapes=list(scratch),
        compiler_params=pltpu.CompilerParams(vmem_limit_bytes=mib * 2**20),
        cost_estimate=pl.CostEstimate(flops=flops, bytes_accessed=moved, transcendentals=0),
    )(*operands)


def struct(shape, dtype=bf16):
    return jax.ShapeDtypeStruct(shape, dtype)


def nbytes(arrays):
    return sum(a.size * a.dtype.itemsize for a in arrays)


def pieces(total, size):
    return [(at, min(size, total - at)) for at in range(0, total, size)]


def start_all(copies):
    for copy in copies:
        copy.start()


def hits_of(choice_ref, columns):
    rows = choice_ref.shape[0]
    names = lax.broadcasted_iota(jnp.int32, (rows, columns), 1)
    hits = jnp.zeros((rows, columns), f32)
    for k in range(choice_ref.shape[1]):
        hits += jnp.where(choice_ref[:, k : k + 1] == names, 1.0, 0.0)
    return hits


def token_load_kernel(choice_ref, tokens_ref, load_ref):
    width = tokens_ref.shape[1]
    load_ref[:, :width] = tokens_ref[...]
    load_ref[:, width:] = hits_of(choice_ref, LANES).astype(bf16)


def cot_load_kernel(choice_ref, tokens_ref, router_ref, cot_ref, load_ref, hits_ref, affinity_ref):
    rows, width = tokens_ref.shape
    experts = router_ref.shape[1]
    load_ref[:, :width] = cot_ref[...]
    affinity = jax.nn.sigmoid(mm(tokens_ref[...], router_ref[...]))
    hits = hits_of(choice_ref, experts)
    chosen = hits * affinity
    gates = route_scale * chosen / jnp.sum(chosen, axis=1, keepdims=True)
    high = gates.astype(bf16)
    low = (gates - high.astype(f32)).astype(bf16)
    load_ref[:, width:] = jnp.zeros((rows, LANES), bf16)
    load_ref[:, width : width + experts] = high
    load_ref[:, width + experts : width + 2 * experts] = low
    hits_ref[...] = hits
    affinity_ref[...] = affinity


def assemble(refs, all_ref):
    at = 0
    for ref in refs:
        all_ref[pl.ds(at, ref.shape[0])] = ref[...]
        at += ref.shape[0]


def expert_names(info_ref, slots, shift):
    mine = 2 * info_ref[0] + info_ref[1]
    other = 2 * info_ref[0] + 1 - info_ref[1]
    slot = lax.broadcasted_iota(jnp.int32, (slots, LANES), 0)
    lane = lax.broadcasted_iota(jnp.int32, (slots, LANES), 1)
    return jnp.where(lane == jnp.where(slot < slots // 2, mine, other) + shift, 1.0, 0.0).astype(bf16)


def token_slots_kernel(info_ref, *refs):
    blocks, (kept_ref, sent_ref, select_ref, all_ref) = refs[:-4], refs[-4:]
    rows, load = blocks[0].shape
    toks, slots = all_ref.shape[0], select_ref.shape[0]
    half = slots // 2
    assemble(blocks, all_ref)
    names = expert_names(info_ref, slots, 0)
    slot = lax.broadcasted_iota(jnp.int32, (slots, toks), 0)
    tok = lax.broadcasted_iota(jnp.int32, (slots, toks), 1)
    slot = jnp.where(slot < half, slot, slot - half)
    member = mm_nt(names, all_ref[:, load - LANES :])
    member = jnp.where(slot // MOST == tok // rows, member, 0.0)
    early = lax.broadcasted_iota(jnp.int32, (toks, toks), 0)
    late = lax.broadcasted_iota(jnp.int32, (toks, toks), 1)
    before = mm(member.astype(bf16), jnp.where(early < late, 1.0, 0.0).astype(bf16))
    select = jnp.where(before == (slot % MOST).astype(f32), member, 0.0).astype(bf16)
    select_ref[...] = select
    for at, size in pieces(load, 4 * LANES):
        out = mm(select, all_ref[:, at : at + size]).astype(bf16)
        kept_ref[:, at : at + size] = out[:half]
        sent_ref[:, at : at + size] = out[half:]


def cot_slots_kernel(info_ref, select_ref, *refs):
    blocks, (kept_ref, sent_ref, high_ref, low_ref, all_ref) = refs[:-5], refs[-5:]
    load = blocks[0].shape[1]
    slots, half, width = select_ref.shape[0], kept_ref.shape[0], kept_ref.shape[1]
    assemble(blocks, all_ref)
    gates = all_ref[:, width:]
    select = select_ref[...].astype(f32)
    high = (select * mm_nt(expert_names(info_ref, slots, 0), gates)).astype(bf16)
    low = (select * mm_nt(expert_names(info_ref, slots, info_ref[3]), gates)).astype(bf16)
    high_ref[...] = high
    low_ref[...] = low
    for at, size in pieces(width, 4 * LANES):
        cot = all_ref[:, at : at + size]
        out = (mm(high, cot) + mm(low, cot)).astype(bf16)
        kept_ref[:, at : at + size] = out[:half]
        sent_ref[:, at : at + size] = out[half:]


def inner_kernel(
    count, tiles, info_ref, table_ref, kept_ref, came_ref, gate_hbm, up_hbm, up_a_ref, up_b_ref,
    inner_ref, slope_ref, active_ref, low_up_ref, keep_ref,
    rows_ref, gate_ref, up_ref, sems,
):
    half, width = kept_ref.shape[0], rows_ref.shape[1]
    slots, tile = 2 * half, gate_ref.shape[1] // tiles
    copies = []
    for j in range(tiles):
        cols = pl.ds(j * tile, tile)
        copies.append(
            [
                pltpu.make_async_copy(gate_hbm.at[:, cols], gate_ref.at[:, cols], sems.at[2 * j]),
                pltpu.make_async_copy(up_hbm.at[:, cols], up_ref.at[:, cols], sems.at[2 * j + 1]),
            ]
        )
        start_all(copies[-1])
    rows_ref[:half] = kept_ref[:, :width]
    rows_ref[half:] = came_ref[:, :width]
    low_up_ref[...] = mm(rows_ref[...], up_a_ref[...]).astype(bf16)
    chip, core = info_ref[0], info_ref[1]
    lane = lax.broadcasted_iota(jnp.int32, (slots, LANES), 1)
    tails = jnp.concatenate([kept_ref[:, width:], came_ref[:, width:]], axis=0).astype(f32)
    valid = jnp.sum(jnp.where(lane == 2 * chip + core, tails, 0.0), axis=1, keepdims=True)
    here = lax.broadcasted_iota(jnp.int32, (slots, 1), 0)
    there = lax.broadcasted_iota(jnp.int32, (1, slots), 1)
    source_here = jnp.zeros((slots, 1), jnp.int32)
    source_there = jnp.zeros((1, slots), jnp.int32)
    for i in range(2 * count):
        source = 2 * table_ref[chip, i % count] + (core if i < count else 1 - core)
        source_here = jnp.where(here // MOST == i, source, source_here)
        source_there = jnp.where(there // MOST == i, source, source_there)
    ahead = jnp.where(source_there < source_here, 1.0, 0.0).astype(bf16)
    spread = jnp.broadcast_to(valid, (slots, LANES)).astype(bf16)
    rank = mm(ahead, spread) + (here % MOST).astype(f32)
    keep_ref[...] = jnp.where(rank < info_ref[2].astype(f32), valid, 0.0)
    for j in range(tiles):
        cols = slice(j * tile, (j + 1) * tile)
        copies[j][0].wait()
        pre_gate = mm(rows_ref[...], gate_ref[:, cols])
        copies[j][1].wait()
        pre_up = mm(rows_ref[...], up_ref[:, cols]) + adapter_scale * mm(
            low_up_ref[...], up_b_ref[:, cols]
        )
        logistic = jax.nn.sigmoid(pre_gate)
        active = pre_gate * logistic
        active_ref[:, cols] = active
        slope_ref[:, cols] = pre_up * (logistic * (1.0 + pre_gate * (1.0 - logistic)))
        inner_ref[:, cols] = (active * pre_up).astype(bf16)


def routed_kernel(
    tiles, inner_ref, keep_ref, down_hbm, down_a_ref, down_b_ref,
    kept_ref, sent_ref, low_down_ref, down_ref, sems,
):
    half, tile = kept_ref.shape[0], down_ref.shape[1] // tiles
    copies = []
    for j in range(tiles):
        cols = pl.ds(j * tile, tile)
        copies.append(pltpu.make_async_copy(down_hbm.at[:, cols], down_ref.at[:, cols], sems.at[j]))
    start_all(copies)
    low_down_ref[...] = mm(inner_ref[...], down_a_ref[...]).astype(bf16)
    keep = keep_ref[:, :1]
    for j in range(tiles):
        cols = slice(j * tile, (j + 1) * tile)
        copies[j].wait()
        value = mm(inner_ref[...], down_ref[:, cols]) + adapter_scale * mm(
            low_down_ref[...], down_b_ref[:, cols]
        )
        value = (keep * value).astype(bf16)
        kept_ref[:, cols] = value[:half]
        sent_ref[:, cols] = value[half:]


def write_parts(outs, at, size, part):
    row = 0
    for ref in outs:
        ref[:, at : at + size] = part[row : row + ref.shape[0]]
        row += ref.shape[0]


def mix_parts_kernel(
    blocks, info_ref, select_ref, high_ref, low_ref, kept_ref, came_ref, *refs
):
    cots, outs, (all_ref, routed_ref) = refs[:blocks], refs[blocks : 2 * blocks], refs[2 * blocks :]
    width, half, slots = kept_ref.shape[1], kept_ref.shape[0], select_ref.shape[0]
    assemble([ref.at[:, :width] for ref in cots], all_ref)
    routed_ref[:half] = kept_ref[...]
    routed_ref[half:] = came_ref[...]
    high = high_ref[...].astype(f32).T.astype(bf16)
    low = low_ref[...].astype(f32).T.astype(bf16)
    select = select_ref[...].astype(f32).T
    for at, size in pieces(width, 4 * LANES):
        rows = routed_ref[:, at : at + size]
        write_parts(outs, at, size, (mm(high, rows) + mm(low, rows)).astype(bf16))
    dots = select * mm_nt(all_ref[...], routed_ref[...])
    first = dots.astype(bf16)
    second = (dots - first.astype(f32)).astype(bf16)
    tail = mm(first, expert_names(info_ref, slots, 0)) + mm(
        second, expert_names(info_ref, slots, info_ref[3])
    )
    write_parts(outs, width, LANES, tail.astype(bf16))


def back_parts_kernel(select_ref, kept_ref, came_ref, *refs):
    outs, (rows_ref,) = refs[:-1], refs[-1:]
    width, half = kept_ref.shape[1], kept_ref.shape[0]
    rows_ref[:half] = kept_ref[...]
    rows_ref[half:] = came_ref[...]
    select = select_ref[...].astype(f32).T.astype(bf16)
    for at, size in pieces(width, 4 * LANES):
        write_parts(outs, at, size, mm(select, rows_ref[:, at : at + size]).astype(bf16))


def inner_grad_kernel(
    tiles, kept_ref, came_ref, keep_ref, down_hbm, down_b_ref, down_a_ref, slope_ref, active_ref,
    up_b_ref,
    grad_ref, gate_out_ref, up_out_ref, back_low_ref, back_up_ref, down_ref, sems,
):
    half, tile = kept_ref.shape[0], down_ref.shape[0] // tiles
    copies = []
    for j in range(tiles):
        rows = pl.ds(j * tile, tile)
        copies.append(pltpu.make_async_copy(down_hbm.at[rows], down_ref.at[rows], sems.at[j]))
    start_all(copies)
    keep = keep_ref[:, :1].astype(bf16)
    grad_ref[:half] = kept_ref[...] * keep[:half]
    grad_ref[half:] = came_ref[...] * keep[half:]
    back_low_ref[...] = mm_nt(grad_ref[...], down_b_ref[...]).astype(bf16)
    for j in range(tiles):
        cols = slice(j * tile, (j + 1) * tile)
        copies[j].wait()
        inner = mm_nt(grad_ref[...], down_ref[cols]) + adapter_scale * mm_nt(
            back_low_ref[...], down_a_ref[cols]
        )
        gate_out_ref[:, cols] = (inner * slope_ref[:, cols]).astype(bf16)
        up_out_ref[:, cols] = (inner * active_ref[:, cols]).astype(bf16)
    back_up_ref[...] = mm_nt(up_out_ref[...], up_b_ref[...]).astype(bf16)


def row_grad_kernel(
    tiles, grad_gate_ref, grad_up_ref, back_up_ref, gate_hbm, up_hbm, up_a_ref,
    kept_ref, sent_ref, gate_ref, up_ref, sems,
):
    half, tile = kept_ref.shape[0], gate_ref.shape[0] // tiles
    copies = []
    for j in range(tiles):
        rows = pl.ds(j * tile, tile)
        copies.append(
            [
                pltpu.make_async_copy(gate_hbm.at[rows], gate_ref.at[rows], sems.at[2 * j]),
                pltpu.make_async_copy(up_hbm.at[rows], up_ref.at[rows], sems.at[2 * j + 1]),
            ]
        )
        start_all(copies[-1])
    for j in range(tiles):
        cols = slice(j * tile, (j + 1) * tile)
        for copy in copies[j]:
            copy.wait()
        value = (
            mm_nt(grad_gate_ref[...], gate_ref[cols])
            + mm_nt(grad_up_ref[...], up_ref[cols])
            + adapter_scale * mm_nt(back_up_ref[...], up_a_ref[cols])
        ).astype(bf16)
        kept_ref[:, cols] = value[:half]
        sent_ref[:, cols] = value[half:]


def adapter_kernel(
    kept_ref, came_ref, back_up_ref, low_up_ref, grad_up_ref, inner_ref, back_low_ref,
    low_down_ref, grad_ref, up_a_ref, up_b_ref, down_a_ref, down_b_ref,
):
    width, half = grad_ref.shape[1], kept_ref.shape[0]
    scaled = lambda value: (adapter_scale * value).astype(bf16)
    back_up = back_up_ref[...]
    for at, size in pieces(width, 4 * LANES):
        cols = slice(at, at + size)
        up_a_ref[cols] = scaled(
            mm_tn(kept_ref[:, cols], back_up[:half]) + mm_tn(came_ref[:, cols], back_up[half:])
        )
        down_b_ref[:, cols] = scaled(mm_tn(low_down_ref[...], grad_ref[:, cols]))
    up_b_ref[...] = scaled(mm_tn(low_up_ref[...], grad_up_ref[...]))
    down_a_ref[...] = scaled(mm_tn(inner_ref[...], back_low_ref[...]))


def hop_kernel(front_ref, forth_ref, rear_ref, hither_ref, front_out_ref, rear_out_ref):
    rows, came = front_ref.shape[0], forth_ref.shape[0]
    plus = lambda a, b: (a[...].astype(f32) + b[...].astype(f32)).astype(bf16)
    if came < rows:
        front_out_ref[came:] = front_ref[came:]
        rear_out_ref[: rows - came] = rear_ref[: rows - came]
    front_out_ref[:came] = plus(front_ref.at[:came], forth_ref)
    rear_out_ref[rows - came :] = plus(rear_ref.at[rows - came :], hither_ref)


def mixed_kernel(
    own_ref, forth_ref, hither_ref, hits_ref, affinity_ref, router_ref,
    mixed_ref, logits_ref, term_ref,
):
    width, experts = mixed_ref.shape[1], hits_ref.shape[1]
    total = lambda cols: (
        own_ref[:, cols].astype(f32) + forth_ref[:, cols].astype(f32) + hither_ref[:, cols].astype(f32)
    )
    mixed_ref[...] = total(slice(0, width)).astype(bf16)
    tail = total(slice(width, width + LANES))
    grad_gates = tail[:, :experts] + tail[:, experts : 2 * experts]
    hits, affinity = hits_ref[...], affinity_ref[...]
    chosen = hits * affinity
    chosen_sum = jnp.sum(chosen, axis=1, keepdims=True)
    grad_chosen = route_scale * (
        grad_gates / chosen_sum
        - jnp.sum(grad_gates * chosen, axis=1, keepdims=True) / (chosen_sum * chosen_sum)
    )
    logits = (hits * grad_chosen * affinity * (1.0 - affinity)).astype(bf16)
    logits_ref[...] = logits
    term_ref[...] = mm_nt(logits, router_ref[...])


def input_grad_kernel(own_ref, forth_ref, hither_ref, term_ref, out_ref):
    out_ref[...] = (
        own_ref[...].astype(f32)
        + forth_ref[...].astype(f32)
        + hither_ref[...].astype(f32)
        + term_ref[...]
    ).astype(bf16)


def router_grad_kernel(count, info_ref, table_ref, logits_ref, *refs):
    blocks, (out_ref, all_ref) = refs[:-2], refs[-2:]
    width = out_ref.shape[1]
    assemble([ref.at[:, :width] for ref in blocks], all_ref)
    chip = info_ref[0]
    logits = jnp.concatenate(
        [logits_ref[table_ref[chip, i] ^ chip] for i in range(count)], axis=0
    )
    out_ref[...] = mm_tn(logits, all_ref[...])


def ring_of(count):
    if count == 8:
        order = [0, 2, 4, 6, 7, 5, 3, 1]
    else:
        order = list(range(count))
    ahead = [(order[i], order[(i + 1) % count]) for i in range(count)]
    back = [(b, a) for a, b in ahead]
    return order, ahead, back


def offsets_of(count):
    half = count // 2
    return [0] + [-k for k in range(1, half)] + list(range(1, half)) + [half]


def ring_gather(block, count):
    _, ahead, back = ring_of(count)
    half, rows = count // 2, block.shape[0] // 2
    from_behind, from_front = [block], [block]
    for _ in range(1, half):
        from_behind.append(lax.ppermute(from_behind[-1], "expert", ahead))
        from_front.append(lax.ppermute(from_front[-1], "expert", back))
    top = lax.ppermute(from_behind[-1][:rows], "expert", ahead)
    low = lax.ppermute(from_front[-1][rows:], "expert", back)
    return from_behind + from_front[1:] + [top, low]


def ring_scatter(parts, count):
    _, ahead, back = ring_of(count)
    half = count // 2
    forth = lax.ppermute(parts[-2], "expert", ahead)
    hither = lax.ppermute(parts[-1], "expert", back)
    for k in range(half - 1, 0, -1):
        front, rear = parts[half - 1 + k], parts[k]
        front, rear = call(
            hop_kernel, [struct(front.shape)] * 2, [in_vmem] * 4,
            (front, forth, rear, hither), (0, 3 * nbytes([front, rear])),
        )
        forth = lax.ppermute(front, "expert", ahead)
        hither = lax.ppermute(rear, "expert", back)
    return forth, hither


def swap_cores(value):
    return lax.ppermute(value, "dp", [(0, 1), (1, 0)])


def make_per_device(count):
    order, _, _ = ring_of(count)
    offsets = offsets_of(count)
    place = [order.index(chip) for chip in range(count)]
    table = np.array(
        [[order[(place[c] + off) % count] for off in offsets] for c in range(count)], np.int32
    )

    def per_device(
        tokens,
        cotangent,
        expert_choice_index,
        capacity,
        router_matrix,
        gate_matrix,
        up_matrix,
        down_matrix,
        up_adapter_first,
        up_adapter_second,
        down_adapter_first,
        down_adapter_second,
    ):
        tok_count, width = tokens.shape
        experts = router_matrix.shape[1]
        load = width + LANES
        half = count * MOST
        slots = 2 * half
        chip, core = lax.axis_index("expert"), lax.axis_index("dp")
        info = jnp.stack([chip, core, capacity[0], jnp.int32(experts)]).astype(jnp.int32)
        gate_w, up_w, down_w = gate_matrix[0], up_matrix[0], down_matrix[0]
        up_a, up_b = up_adapter_first[0], up_adapter_second[0]
        down_a, down_b = down_adapter_first[0], down_adapter_second[0]
        hidden, rank = gate_w.shape[1], up_a.shape[1]

        toks = count * tok_count
        tiles = 4
        rows_of = [tok_count] * (count - 1) + [tok_count // 2] * 2
        table_arr = jnp.asarray(table)

        (token_load,) = call(
            token_load_kernel, [struct((tok_count, load))], [plain] * 2,
            (expert_choice_index, tokens), (0, 2 * nbytes([tokens])),
        )
        cot_load, hits, affinity = call(
            cot_load_kernel,
            [struct((tok_count, load))] + [struct((tok_count, experts), f32)] * 2,
            [plain] * 4,
            (expert_choice_index, tokens, router_matrix, cotangent),
            (0, 8 * nbytes([tokens])),
        )

        token_blocks = ring_gather(token_load, count)
        cot_blocks = ring_gather(cot_load, count)

        kept, sent, select = call(
            token_slots_kernel,
            [struct((half, load))] * 2 + [struct((slots, toks))],
            [in_smem] + [in_vmem] * (count + 1),
            (info, *token_blocks),
            (2 * slots * toks * load, 2 * count * nbytes([token_load])),
            scratch=[pltpu.VMEM((toks, load), bf16)],
        )
        came = swap_cores(sent)
        inner, slope, active, low_up, keep = call(
            functools.partial(inner_kernel, count, tiles),
            [
                struct((slots, hidden)), struct((slots, hidden), f32), struct((slots, hidden), f32),
                struct((slots, rank)), struct((slots, LANES), f32),
            ],
            [in_smem, in_smem, in_vmem, in_vmem, in_hbm, in_hbm, plain, plain],
            (info, table_arr, kept, came, gate_w, up_w, up_a, up_b),
            (4 * slots * width * hidden, 2 * nbytes([gate_w])),
            scratch=[
                pltpu.VMEM((slots, width), bf16), pltpu.VMEM((width, hidden), bf16),
                pltpu.VMEM((width, hidden), bf16), pltpu.SemaphoreType.DMA((2 * tiles,)),
            ],
            mib=32,
        )
        routed_kept, routed_sent, low_down = call(
            functools.partial(routed_kernel, tiles),
            [struct((half, width))] * 2 + [struct((slots, rank))],
            [in_vmem, in_vmem, in_hbm, plain, plain],
            (inner, keep, down_w, down_a, down_b),
            (2 * slots * width * hidden, nbytes([gate_w])),
            scratch=[pltpu.VMEM((hidden, width), bf16), pltpu.SemaphoreType.DMA((tiles,))],
            mib=24,
        )
        routed_came = swap_cores(routed_sent)

        cot_kept, cot_sent, high, low = call(
            cot_slots_kernel,
            [struct((half, width))] * 2 + [struct((slots, toks))] * 2,
            [in_smem] + [in_vmem] * (count + 2),
            (info, select, *cot_blocks),
            (4 * slots * toks * load, 2 * count * nbytes([token_load])),
            scratch=[pltpu.VMEM((toks, load), bf16)],
        )
        cot_came = swap_cores(cot_sent)
        mix_parts = call(
            functools.partial(mix_parts_kernel, count + 1),
            [struct((rows, load)) for rows in rows_of],
            [in_smem] + [in_vmem] * (count + 6),
            (info, select, high, low, routed_kept, routed_came, *cot_blocks),
            (6 * slots * toks * load, 3 * count * nbytes([token_load])),
            scratch=[pltpu.VMEM((toks, width), bf16), pltpu.VMEM((slots, width), bf16)],
        )
        mix_forth, mix_hither = ring_scatter(mix_parts, count)

        grad_routed, grad_gate, grad_up, back_low, back_up = call(
            functools.partial(inner_grad_kernel, tiles),
            [struct((slots, width))] + [struct((slots, hidden))] * 2 + [struct((slots, rank))] * 2,
            [in_vmem] * 3 + [in_hbm, plain, plain, in_vmem, in_vmem, plain],
            (cot_kept, cot_came, keep, down_w, down_b, down_a, slope, active, up_b),
            (2 * slots * width * hidden, nbytes([gate_w])),
            scratch=[pltpu.VMEM((hidden, width), bf16), pltpu.SemaphoreType.DMA((tiles,))],
            mib=24,
        )
        back_kept, back_sent = call(
            functools.partial(row_grad_kernel, tiles),
            [struct((half, width))] * 2,
            [in_vmem] * 3 + [in_hbm, in_hbm, plain],
            (grad_gate, grad_up, back_up, gate_w, up_w, up_a),
            (4 * slots * width * hidden, 2 * nbytes([gate_w])),
            scratch=[
                pltpu.VMEM((width, hidden), bf16), pltpu.VMEM((width, hidden), bf16),
                pltpu.SemaphoreType.DMA((2 * tiles,)),
            ],
            mib=32,
        )
        back_came = swap_cores(back_sent)
        back_parts = call(
            back_parts_kernel,
            [struct((rows, width)) for rows in rows_of],
            [in_vmem] * 3,
            (select, back_kept, back_came),
            (2 * slots * toks * load, 2 * count * nbytes([token_load])),
            scratch=[pltpu.VMEM((slots, width), bf16)],
        )
        back_forth, back_hither = ring_scatter(back_parts, count)
        adapters = call(
            adapter_kernel,
            [
                struct((width, rank)), struct((rank, hidden)),
                struct((hidden, rank)), struct((rank, width)),
            ],
            [in_vmem] * 9,
            (kept, came, back_up, low_up, grad_up, inner, back_low, low_down, grad_routed),
            (8 * slots * width * rank, 4 * nbytes([grad_routed])),
            out_specs=[plain] * 4,
        )

        mixed, grad_logits, router_term = call(
            mixed_kernel,
            [
                struct((tok_count, width)), struct((tok_count, experts)),
                struct((tok_count, width), f32),
            ],
            [in_vmem] * 5 + [plain],
            (mix_parts[0], mix_forth, mix_hither, hits, affinity, router_matrix),
            (0, 4 * nbytes([mix_forth])),
            out_specs=[plain, in_vmem, in_vmem],
        )
        gathered, step = grad_logits[None], 1
        while step < count:
            arrived = lax.ppermute(gathered, "expert", [(i, i ^ step) for i in range(count)])
            gathered = jnp.concatenate([gathered, arrived], axis=0)
            step *= 2
        (router_half,) = call(
            functools.partial(router_grad_kernel, count),
            [struct((experts, width), f32)],
            [in_smem, in_smem] + [in_vmem] * (count + 2),
            (info, table_arr, gathered, *token_blocks),
            (0, count * nbytes([token_load])),
            scratch=[pltpu.VMEM((toks, width), bf16)],
        )
        router_grad = (router_half + swap_cores(router_half)).T
        (input_grad,) = call(
            input_grad_kernel,
            [struct((tok_count, width))],
            [in_vmem] * 4,
            (back_parts[0], back_forth, back_hither, router_term),
            (0, 4 * nbytes([back_forth])),
            out_specs=[plain],
        )
        return (mixed, input_grad, router_grad) + tuple(value[None] for value in adapters)

    return per_device


def solution(mesh):
    rows = P(("groups", "expert", "dp"), None)
    whole = P(("groups", "expert", "dp"), None, None)
    weight = P(("expert", "dp"), None, None)
    return jax.shard_map(
        make_per_device(mesh.shape["expert"]),
        mesh=mesh,
        in_specs=(rows, rows, rows, P(("groups", "expert", "dp")), P()) + (weight,) * 7,
        out_specs=(rows, rows, P("groups", None), whole, whole, whole, whole),
        check_vma=False,
    )
```

time: 161 us -> 171 us (1.062)
  Pallas kernels: 0 us -> 49.6 us
  matrix products: 46.2 us -> 0 us
  other arithmetic: 12.5 us -> 0.83 us
  local copies, waits for them, and re-layouts: 20.6 us -> 29 us
  waiting for transfers between devices: 39.5 us -> 45.6 us
  starting transfers between devices: 39.1 us -> 43.2 us
    pallas_call x0 -> x20, Pallas kernels: none -> 49.6 us  [call(): pl.pallas_call(body, out_shape=outs, in_specs=specs, out_specs=out_specs...]
    dot_general x41 -> x0, matrix products: 46.2 us -> none  [the longest x37 42.9 us: mm(): lax.dot_general(left, right, ((axes[0], axes[1]), ((), ())), preferred_el...]
    unnamed x98 -> x144, local copies, waits for them, and re-layouts: 3.18 us -> 27.6 us
    ppermute x6, waiting for transfers between devices: 0.17 us -> 18.7 us  [ring_gather(): from_front.append(lax.ppermute(from_front[-1], 'expert', back))]
    ppermute x6, waiting for transfers between devices: 11.7 us -> 0.02 us  [ring_gather(): from_behind.append(lax.ppermute(from_behind[-1], 'expert', ahead))]
    ppermute x6, starting transfers between devices: 0.18 us -> 10.5 us  [ring_gather(): from_front.append(lax.ppermute(from_front[-1], 'expert', back))]
    ppermute x6, starting transfers between devices: 13.1 us -> 3.18 us  [ring_gather(): from_behind.append(lax.ppermute(from_behind[-1], 'expert', ahead))]
    slice x13 -> x0, local copies, waits for them, and re-layouts: 6.86 us -> none  [the longest x2 2.8 us: to_tokens(): kept = rows[:count * MOST].reshape(count, MOST, -1)]
  transfers between devices with their start and end apart: 40 -> 40, of which waited for: 18 -> 17; matrix products, arithmetic and copies ran while one was open for 35% -> 5% of each run, Pallas kernels for 0% -> 29%
where the time goes in v3:
time: 171 us; the launch traced here: 170 us
  Pallas kernels  49.6 us (29%)
  waiting for transfers between devices  45.6 us (27%)
  starting transfers between devices  43.2 us (25%)
  local copies, waits for them, and re-layouts  29 us (17%)
  between operations  2.08 us (1%)
    pallas_call x20, Pallas kernels, call(): pl.pallas_call(body, out_shape=outs, in_specs=specs, out_specs=out_specs...  49.6 us
    unnamed x144, local copies, waits for them, and re-layouts  27.6 us
    ppermute x6, waiting for transfers between devices, ring_gather(): from_front.append(lax.ppermute(from_front[-1], 'expert', back))  18.7 us
    ppermute x6, waiting for transfers between devices, ring_scatter(): forth = lax.ppermute(front, 'expert', ahead)  11 us
    ppermute x6, starting transfers between devices, ring_gather(): from_front.append(lax.ppermute(from_front[-1], 'expert', back))  10.5 us
    ppermute x6, starting transfers between devices, ring_scatter(): forth = lax.ppermute(front, 'expert', ahead)  7.78 us
    ppermute x3, starting transfers between devices, per_device(): lax.ppermute(gathered, 'expert', [(i, i ^ step) for i in range(count)])  7.64 us
    ppermute x6, starting transfers between devices, ring_scatter(): hither = lax.ppermute(rear, 'expert', back)  4.95 us
  transfers between devices with their start and end apart: 40, of which 17 were waited for; matrix products, arithmetic and copies ran while one was open for 5% of the time, Pallas kernels for 29%

profile of v3, /device:TPU:0, one launch (start us, length us, event | category | flops | bytes accessed | tf_op | source)
XLA Modules:
  0.0 170.2 jit_solution(1483502526175473936)
XLA Ops:
  2.5 3.0 %collective-permute-start.3 = (bf16[32,3712]{1,0:T(8,128)(2,1)S(1)}, bf16[32,3712]{1,0:T(8,128)(2,1)S(1)}, u32[]{:S(2)}, u32[]{:S(2)}) collective-permute-start(bf16[32,3712]{1,0:T(8,128)(2,1)S(1)} %shard_map.180.refs_0_), channel_id=1, source_target_pairs={{4,0},{8,4},{12,8},{14,12},{10,14},{6,10},{2,6},{0,2},{5,1},{9,5},... | collective-permute-start | bytes 712712 | tf_op jit(solution)/shard_map/ppermute | solution.py:415
  5.6 5.7 %collective-permute-done.3.refs_4_ = bf16[32,3712]{1,0:T(8,128)(2,1)S(1)} collective-permute-done((bf16[32,3712]{1,0:T(8,128)(2,1)S(1)}, bf16[32,3712]{1,0:T(8,128)(2,1)S(1)}, u32[]{:S(2)}, u32[]{:S(2)}) %collective-permute-start.3) | collective-permute-done | bytes 237600 | tf_op jit(solution)/shard_map/ppermute | solution.py:415
  13.4 4.9 %collective-permute-done.4.refs_5_ = bf16[32,3712]{1,0:T(8,128)(2,1)S(1)} collective-permute-done((bf16[32,3712]{1,0:T(8,128)(2,1)S(1)}, bf16[32,3712]{1,0:T(8,128)(2,1)S(1)}, u32[]{:S(2)}, u32[]{:S(2)}) %collective-permute-start.4) | collective-permute-done | bytes 237600 | tf_op jit(solution)/shard_map/ppermute | solution.py:415
  30.1 1.9 %collective-permute-done.11.refs_4_ = bf16[32,3712]{1,0:T(8,128)(2,1)S(1)} collective-permute-done((bf16[32,3712]{1,0:T(8,128)(2,1)S(1)}, bf16[32,3712]{1,0:T(8,128)(2,1)S(1)}, u32[]{:S(2)}, u32[]{:S(2)}) %collective-permute-start.11) | collective-permute-done | bytes 237600 | tf_op jit(solution)/shard_map/ppermute | solution.py:415
  35.5 2.5 %shard_map.181 = (bf16[128,3712]{1,0:T(8,128)(2,1)S(1)}, bf16[128,3712]{1,0:T(8,128)(2,1)}, bf16[256,256]{1,0:T(8,128)(2,1)S(1)}) custom-call(s32[4]{0:T(128)S(1)} %pad_add_fusion.info_ref, bf16[32,3712]{1,0:T(8,128)(2,1)S(1)} %shard_map.180.refs_0_, bf16[32,3712]{1,0:T(8,128)(2,1)S(1)} %collective-permute-done.refs_1_, ...), custom_call_target="tpu_custom_call" | custom-call | flops 486539264 | bytes 3801088 | tf_op jit(solution)/shard_map/pallas_call | solution.py:40
  41.0 6.1 %collective-permute-done.13.refs_6_ = bf16[32,3712]{1,0:T(8,128)(2,1)S(1)} collective-permute-done((bf16[32,3712]{1,0:T(8,128)(2,1)S(1)}, bf16[32,3712]{1,0:T(8,128)(2,1)S(1)}, u32[]{:S(2)}, u32[]{:S(2)}) %collective-permute-start.13) | collective-permute-done | bytes 237600 | tf_op jit(solution)/shard_map/ppermute | solution.py:415
  49.3 2.8 %collective-permute-done.15.refs_8_ = bf16[16,3712]{1,0:T(8,128)(2,1)S(1)} collective-permute-done((bf16[16,3712]{1,0:T(8,128)(2,1)S(1)}, bf16[16,3712]{1,0:T(8,128)(2,1)S(1)}, u32[]{:S(2)}, u32[]{:S(2)}) %collective-permute-start.15) | collective-permute-done | bytes 118816 | tf_op jit(solution)/shard_map/ppermute | solution.py:417
  54.7 3.2 %shard_map.183 = (bf16[128,3584]{1,0:T(8,128)(2,1)S(1)}, bf16[128,3584]{1,0:T(8,128)(2,1)}, bf16[256,256]{1,0:T(8,128)(2,1)S(1)}, bf16[256,256]{1,0:T(8,128)(2,1)S(1)}) custom-call(s32[4]{0:T(128)S(1)} %pad_add_fusion.info_ref, bf16[256,256]{1,0:T(8,128)(2,1)S(1)} %get-tuple-element.69.select_ref, bf16[32,3712]{1,0:T(8,128)(2,1)S(1)} %get-tuple-element.70.refs_0_, ...), custom_call_target="tpu_custom_call" | custom-call | flops 973078528 | bytes 3801088 | tf_op jit(solution)/shard_map/pallas_call | solution.py:40
  61.5 2.4 %copy.23 = bf16[1,3584,64]{2,1,0:T(8,128)(2,1)} copy(bf16[1,3584,64]{1,2,0:T(8,128)(2,1)} %param.21) | data formatting | bytes 917504 | tf_op args[8]
  63.9 3.1 %copy-done = bf16[1,3584,1024]{2,1,0:T(8,128)(2,1)S(1)} copy-done((bf16[1,3584,1024]{2,1,0:T(8,128)(2,1)S(1)}, bf16[1,3584,1024]{2,1,0:T(8,128)(2,1)}, u32[]{:S(2)}) %copy-start) | copy-done | bytes 7340056
  67.0 3.1 %copy-done.2 = bf16[1,3584,1024]{2,1,0:T(8,128)(2,1)S(1)} copy-done((bf16[1,3584,1024]{2,1,0:T(8,128)(2,1)S(1)}, bf16[1,3584,1024]{2,1,0:T(8,128)(2,1)}, u32[]{:S(2)}) %copy-start.2) | copy-done | bytes 7340056
  73.8 13.4 %shard_map.184 = (bf16[256,1024]{1,0:T(8,128)(2,1)S(1)}, f32[256,1024]{1,0:T(8,128)S(1)}, f32[256,1024]{1,0:T(8,128)S(1)}, bf16[256,64]{1,0:T(8,128)(2,1)S(1)}, f32[256,128]{1,0:T(8,128)S(1)}) custom-call(s32[4]{0:T(128)S(1)} %copy-done.46, s32[8,8]{1,0:T(8,128)S(1)} %copy-done.43, bf16[128,3712]{1,0:T(8,128)(2,1)S(1)} %copy-done.8, ...), custom_call_target="tpu_custom_call" | custom-call | flops 3758096384 | bytes 14680064 | tf_op jit(solution)/shard_map/pallas_call | solution.py:40
  87.3 5.1 %shard_map.185 = (bf16[128,3584]{1,0:T(8,128)(2,1)S(1)}, bf16[128,3584]{1,0:T(8,128)(2,1)}, bf16[256,64]{1,0:T(8,128)(2,1)S(1)}) custom-call(bf16[256,1024]{1,0:T(8,128)(2,1)S(1)} %get-tuple-element.75.inner_ref, f32[256,128]{1,0:T(8,128)S(1)} %get-tuple-element.76.keep_ref, bf16[1024,3584]{1,0:T(8,128)(2,1)S(1)} %bitcast.18, bf16[1024,64]{1,0:T(8,128)(2,1)S(1)} %bitcast.28, ...), custom_call_target="tpu_custom_call" | custom-call | flops 1879048192 | bytes 7340032 | tf_op jit(solution)/shard_map/pallas_call | solution.py:40
  93.0 7.8 %shard_map.191 = (bf16[256,3584]{1,0:T(8,128)(2,1)S(1)}, bf16[256,1024]{1,0:T(8,128)(2,1)S(1)}, bf16[256,1024]{1,0:T(8,128)(2,1)S(1)}, bf16[256,64]{1,0:T(8,128)(2,1)S(1)}, bf16[256,64]{1,0:T(8,128)(2,1)S(1)}) custom-call(bf16[128,3584]{1,0:T(8,128)(2,1)S(1)} %copy-done.26, bf16[128,3584]{1,0:T(8,128)(2,1)} %collective-permute-done.26.came_ref, ...), custom_call_target="tpu_custom_call" | custom-call | flops 1879048192 | bytes 7340032 | tf_op jit(solution)/shard_map/pallas_call | solution.py:40
  100.8 3.1 %copy-done.1 = bf16[1,3584,1024]{2,1,0:T(8,128)(2,1)S(1)} copy-done((bf16[1,3584,1024]{2,1,0:T(8,128)(2,1)S(1)}, bf16[1,3584,1024]{2,1,0:T(8,128)(2,1)}, u32[]{:S(2)}) %copy-start.1) | copy-done | bytes 7340056
  103.9 6.8 %shard_map.192 = (bf16[128,3584]{1,0:T(8,128)(2,1)S(1)}, bf16[128,3584]{1,0:T(8,128)(2,1)S(1)}) custom-call(bf16[256,1024]{1,0:T(8,128)(2,1)S(1)} %get-tuple-element.101.grad_gate_ref, bf16[256,1024]{1,0:T(8,128)(2,1)S(1)} %get-tuple-element.102.grad_up_ref, bf16[256,64]{1,0:T(8,128)(2,1)S(1)} %get-tuple-element.103.back_up_ref, ...), custom_call_target="tpu_custom_call" | custom-call | flops 3758096384 | bytes 14680064 | tf_op jit(solution)/shard_map/pallas_call | solution.py:40
  111.1 3.1 %shard_map.186 = (bf16[32,3712]{1,0:T(8,128)(2,1)S(1)}, bf16[32,3712]{1,0:T(8,128)(2,1)S(1)}, bf16[32,3712]{1,0:T(8,128)(2,1)S(1)}, bf16[32,3712]{1,0:T(8,128)(2...) custom-call(s32[4]{0:T(128)S(1)} %copy-done.47, ...), custom_call_target="tpu_custom_call" | custom-call | flops 1459617792 | bytes 5701632 | tf_op jit(solution)/shard_map/pallas_call | solution.py:40
  116.3 3.5 %collective-permute-done.18.forth_ref = bf16[16,3712]{1,0:T(8,128)(2,1)S(1)} collective-permute-done((bf16[16,3712]{1,0:T(8,128)(2,1)S(1)}, bf16[16,3712]{1,0:T(8,128)(2,1)S(1)}, u32[]{:S(2)}, u32[]{:S(2)}) %collective-permute-start.18) | collective-permute-done | bytes 118816 | tf_op jit(solution)/shard_map/ppermute | solution.py:424
  122.1 5.1 %collective-permute-done.20.forth_ref = bf16[32,3712]{1,0:T(8,128)(2,1)S(1)} collective-permute-done((bf16[32,3712]{1,0:T(8,128)(2,1)S(1)}, bf16[32,3712]{1,0:T(8,128)(2,1)S(1)}, u32[]{:S(2)}, u32[]{:S(2)}) %collective-permute-start.20) | collective-permute-done | bytes 237600 | tf_op jit(solution)/shard_map/ppermute | solution.py:432
  133.0 2.3 %collective-permute-done.22.forth_ref = bf16[32,3712]{1,0:T(8,128)(2,1)S(1)} collective-permute-done((bf16[32,3712]{1,0:T(8,128)(2,1)S(1)}, bf16[32,3712]{1,0:T(8,128)(2,1)S(1)}, u32[]{:S(2)}, u32[]{:S(2)}) %collective-permute-start.22) | collective-permute-done | bytes 237600 | tf_op jit(solution)/shard_map/ppermute | solution.py:432
  140.5 3.6 %collective-permute-done.24.forth_ref = bf16[32,3712]{1,0:T(8,128)(2,1)S(1)} collective-permute-done((bf16[32,3712]{1,0:T(8,128)(2,1)S(1)}, bf16[32,3712]{1,0:T(8,128)(2,1)S(1)}, u32[]{:S(2)}, u32[]{:S(2)}) %collective-permute-start.24) | collective-permute-done | bytes 237600 | tf_op jit(solution)/shard_map/ppermute | solution.py:432
  151.2 4.6 %collective-permute-done.37 = bf16[2,32,16]{2,1,0:T(8,128)(2,1)S(1)} collective-permute-done((bf16[2,32,16]{2,1,0:T(8,128)(2,1)S(1)}, bf16[2,32,16]{2,1,0:T(8,128)(2,1)S(1)}, u32[]{:S(2)}, u32[]{:S(2)}) %collective-permute-start.37) | collective-permute-done | bytes 2080 | tf_op jit(solution)/shard_map/ppermute | solution.py:605
  155.8 4.8 %collective-permute-start.38 = (bf16[4,32,16]{2,1,0:T(8,128)(2,1)S(1)}, bf16[4,32,16]{2,1,0:T(8,128)(2,1)S(1)}, u32[]{:S(2)}, u32[]{:S(2)}) collective-permute-start(bf16[4,32,16]{2,1,0:T(8,128)(2,1)S(1)} %pad_maximum_fusion.1), channel_id=1, source_target_pairs={{0,8},{2,10},{4,12},{6,14},{8,0},{10,2},{12,4},{14,6},{1,9},{3,11}... | collective-permute-start | bytes 12296 | tf_op jit(solution)/shard_map/ppermute | solution.py:605
  164.0 2.9 %shard_map.199 = (bf16[3584,64]{1,0:T(8,128)(2,1)S(1)}, bf16[64,1024]{1,0:T(8,128)(2,1)}, bf16[1024,64]{1,0:T(8,128)(2,1)S(1)}, bf16[64,3584]{1,0:T(8,128)(2,1)}) custom-call(bf16[128,3712]{1,0:T(8,128)(2,1)S(1)} %copy-done.9, bf16[128,3712]{1,0:T(8,128)(2,1)} %collective-permute-done.16.came_ref, bf16[256,64]{1,0:T(8,128)(2,1)S(1)} %get-tuple-element.103.back_up_ref, ...), custom_call_target="tpu_custom_call" | custom-call | flops 469762048 | bytes 7340032 | tf_op jit(solution)/shard_map/pallas_call | solution.py:40
  (231 shorter events, 63.5 us)
Async XLA Ops:
  2.5 8.9 %collective-permute-start.3 = (bf16[32,3712]{1,0:T(8,128)(2,1)S(1)}, bf16[32,3712]{1,0:T(8,128)(2,1)S(1)}, u32[]{:S(2)}, u32[]{:S(2)}) collective-permute-start(bf16[32,3712]{1,0:T(8,128)(2,1)S(1)} %shard_map.180.refs_0_), channel_id=1, source_target_pairs={{4,0},{8,4},{12,8},{14,12},{10,14},{6,10},{2,6},{0,2},{5,1},{9,5},... | collective-permute-start | bytes 712712 | tf_op jit(solution)/shard_map/ppermute | solution.py:415
  5.5 7.5 %collective-permute-start = (bf16[32,3712]{1,0:T(8,128)(2,1)S(1)}, bf16[32,3712]{1,0:T(8,128)(2,1)S(1)}, u32[]{:S(2)}, u32[]{:S(2)}) collective-permute-start(bf16[32,3712]{1,0:T(8,128)(2,1)S(1)} %shard_map.180.refs_0_), channel_id=1, source_target_pairs={{0,4},{4,8},{8,12},{12,14},{14,10},{10,6},{6,2},{2,0},{1,5},{5,9},... | collective-permute-start | bytes 712712 | tf_op jit(solution)/shard_map/ppermute | solution.py:414
  18.3 7.7 %collective-permute-start.5 = (bf16[32,3712]{1,0:T(8,128)(2,1)S(1)}, bf16[32,3712]{1,0:T(8,128)(2,1)S(1)}, u32[]{:S(2)}, u32[]{:S(2)}) collective-permute-start(bf16[32,3712]{1,0:T(8,128)(2,1)S(1)} %collective-permute-done.4.refs_5_), channel_id=1, source_target_pairs={{4,0},{8,4},{12,8},{14,12},{10,14},{6,10},{2,6},{0,2},{5,1},{9,5},... | collective-permute-start | bytes 712712 | tf_op jit(solution)/shard_map/ppermute | solution.py:415
  19.7 8.4 %collective-permute-start.2 = (bf16[32,3712]{1,0:T(8,128)(2,1)S(1)}, bf16[32,3712]{1,0:T(8,128)(2,1)S(1)}, u32[]{:S(2)}, u32[]{:S(2)}) collective-permute-start(bf16[32,3712]{1,0:T(8,128)(2,1)S(1)} %collective-permute-done.1.refs_2_), channel_id=1, source_target_pairs={{0,4},{4,8},{8,12},{12,14},{14,10},{10,6},{6,2},{2,0},{1,5},{5,9},... | collective-permute-start | bytes 712712 | tf_op jit(solution)/shard_map/ppermute | solution.py:414
  24.0 8.0 %collective-permute-start.11 = (bf16[32,3712]{1,0:T(8,128)(2,1)S(1)}, bf16[32,3712]{1,0:T(8,128)(2,1)S(1)}, u32[]{:S(2)}, u32[]{:S(2)}) collective-permute-start(bf16[32,3712]{1,0:T(8,128)(2,1)S(1)} %get-tuple-element.70.refs_0_), channel_id=1, source_target_pairs={{4,0},{8,4},{12,8},{14,12},{10,14},{6,10},{2,6},{0,2},{5,1},{9,5},... | collective-permute-start | bytes 712712 | tf_op jit(solution)/shard_map/ppermute | solution.py:415
  25.3 8.1 %collective-permute-start.8 = (bf16[32,3712]{1,0:T(8,128)(2,1)S(1)}, bf16[32,3712]{1,0:T(8,128)(2,1)}, u32[]{:S(2)}, u32[]{:S(2)}) collective-permute-start(bf16[32,3712]{1,0:T(8,128)(2,1)S(1)} %get-tuple-element.70.refs_0_), channel_id=1, source_target_pairs={{0,4},{4,8},{8,12},{12,14},{14,10},{10,6},{6,2},{2,0},{1,5},{5,9},... | collective-permute-start | bytes 712712 | tf_op jit(solution)/shard_map/ppermute | solution.py:414
  26.7 7.8 %collective-permute-start.7 = (bf16[16,3712]{1,0:T(8,128)(2,1)}, bf16[16,3712]{1,0:T(8,128)(2,1)S(1)}, u32[]{:S(2)}, u32[]{:S(2)}) collective-permute-start(bf16[16,3712]{1,0:T(8,128)(2,1)} %slice.17), channel_id=1, source_target_pairs={{4,0},{8,4},{12,8},{14,12},{10,14},{6,10},{2,6},{0,2},{5,1},{9,5},... | collective-permute-start | bytes 356360 | tf_op jit(solution)/shard_map/ppermute | solution.py:417
  33.5 7.1 %collective-permute-start.9 = (bf16[32,3712]{1,0:T(8,128)(2,1)}, bf16[32,3712]{1,0:T(8,128)(2,1)S(1)}, u32[]{:S(2)}, u32[]{:S(2)}) collective-permute-start(bf16[32,3712]{1,0:T(8,128)(2,1)} %collective-permute-done.8.refs_1_), channel_id=1, source_target_pairs={{0,4},{4,8},{8,12},{12,14},{14,10},{10,6},{6,2},{2,0},{1,5},{5,9},... | collective-permute-start | bytes 712712 | tf_op jit(solution)/shard_map/ppermute | solution.py:414
  38.9 25.0 %collective-permute-start.16 = (bf16[128,3712]{1,0:T(8,128)(2,1)}, bf16[128,3712]{1,0:T(8,128)(2,1)}, u32[]{:S(2)}, u32[]{:S(2)}) collective-permute-start(bf16[128,3712]{1,0:T(8,128)(2,1)} %get-tuple-element.74), channel_id=1, source_target_pairs={{0,1},{1,0},{2,3},{3,2},{4,5},{5,4},{6,7},{7,6},{8,9},{9,8},{10,11... | collective-permute-start | bytes 2850824 | tf_op jit(solution)/shard_map/ppermute | solution.py:438
  39.0 8.2 %collective-permute-start.13 = (bf16[32,3712]{1,0:T(8,128)(2,1)S(1)}, bf16[32,3712]{1,0:T(8,128)(2,1)S(1)}, u32[]{:S(2)}, u32[]{:S(2)}) collective-permute-start(bf16[32,3712]{1,0:T(8,128)(2,1)S(1)} %collective-permute-done.12.refs_5_), channel_id=1, source_target_pairs={{4,0},{8,4},{12,8},{14,12},{10,14},{6,10},{2,6},{0,2},{5,1},{9,5},... | collective-permute-start | bytes 712712 | tf_op jit(solution)/shard_map/ppermute | solution.py:415
  40.6 8.2 %collective-permute-start.10 = (bf16[32,3712]{1,0:T(8,128)(2,1)S(1)}, bf16[32,3712]{1,0:T(8,128)(2,1)S(1)}, u32[]{:S(2)}, u32[]{:S(2)}) collective-permute-start(bf16[32,3712]{1,0:T(8,128)(2,1)S(1)} %collective-permute-done.9.refs_2_), channel_id=1, source_target_pairs={{0,4},{4,8},{8,12},{12,14},{14,10},{10,6},{6,2},{2,0},{1,5},{5,9},... | collective-permute-start | bytes 712712 | tf_op jit(solution)/shard_map/ppermute | solution.py:414
  60.2 32.7 %collective-permute-start.26 = (bf16[128,3584]{1,0:T(8,128)(2,1)}, bf16[128,3584]{1,0:T(8,128)(2,1)}, u32[]{:S(2)}, u32[]{:S(2)}) collective-permute-start(bf16[128,3584]{1,0:T(8,128)(2,1)} %get-tuple-element.98), channel_id=1, source_target_pairs={{0,1},{1,0},{2,3},{3,2},{4,5},{5,4},{6,7},{7,6},{8,9},{9,8},{10,11... | collective-permute-start | bytes 2752520 | tf_op jit(solution)/shard_map/ppermute | solution.py:438
  92.4 18.6 %collective-permute-start.17 = (bf16[128,3584]{1,0:T(8,128)(2,1)}, bf16[128,3584]{1,0:T(8,128)(2,1)S(1)}, u32[]{:S(2)}, u32[]{:S(2)}) collective-permute-start(bf16[128,3584]{1,0:T(8,128)(2,1)} %get-tuple-element.78), channel_id=1, source_target_pairs={{0,1},{1,0},{2,3},{3,2},{4,5},{5,4},{6,7},{7,6},{8,9},{9,8},{10,11... | collective-permute-start | bytes 2752520 | tf_op jit(solution)/shard_map/ppermute | solution.py:438
  110.8 19.4 %collective-permute-start.27 = (bf16[128,3584]{1,0:T(8,128)(2,1)S(1)}, bf16[128,3584]{1,0:T(8,128)(2,1)S(1)}, u32[]{:S(2)}, u32[]{:S(2)}) collective-permute-start(bf16[128,3584]{1,0:T(8,128)(2,1)S(1)} %get-tuple-element.105), channel_id=1, source_target_pairs={{0,1},{1,0},{2,3},{3,2},{4,5},{5,4},{6,7},{7,6},{8,9},{9,8},{10,11... | collective-permute-start | bytes 2752520 | tf_op jit(solution)/shard_map/ppermute | solution.py:438
  120.0 7.1 %collective-permute-start.20 = (bf16[32,3712]{1,0:T(8,128)(2,1)S(1)}, bf16[32,3712]{1,0:T(8,128)(2,1)S(1)}, u32[]{:S(2)}, u32[]{:S(2)}) collective-permute-start(bf16[32,3712]{1,0:T(8,128)(2,1)S(1)} %get-tuple-element.86), channel_id=1, source_target_pairs={{0,4},{4,8},{8,12},{12,14},{14,10},{10,6},{6,2},{2,0},{1,5},{5,9},... | collective-permute-start | bytes 712712 | tf_op jit(solution)/shard_map/ppermute | solution.py:432
  128.2 7.2 %collective-permute-start.22 = (bf16[32,3712]{1,0:T(8,128)(2,1)S(1)}, bf16[32,3712]{1,0:T(8,128)(2,1)S(1)}, u32[]{:S(2)}, u32[]{:S(2)}) collective-permute-start(bf16[32,3712]{1,0:T(8,128)(2,1)S(1)} %get-tuple-element.89), channel_id=1, source_target_pairs={{0,4},{4,8},{8,12},{12,14},{14,10},{10,6},{6,2},{2,0},{1,5},{5,9},... | collective-permute-start | bytes 712712 | tf_op jit(solution)/shard_map/ppermute | solution.py:432
  131.0 7.1 %collective-permute-start.28 = (bf16[16,3584]{1,0:T(8,128)(2,1)S(1)}, bf16[16,3584]{1,0:T(8,128)(2,1)S(1)}, u32[]{:S(2)}, u32[]{:S(2)}) collective-permute-start(bf16[16,3584]{1,0:T(8,128)(2,1)S(1)} %get-tuple-element.110), channel_id=1, source_target_pairs={{0,4},{4,8},{8,12},{12,14},{14,10},{10,6},{6,2},{2,0},{1,5},{5,9},... | collective-permute-start | bytes 344072 | tf_op jit(solution)/shard_map/ppermute | solution.py:424
  136.0 8.1 %collective-permute-start.24 = (bf16[32,3712]{1,0:T(8,128)(2,1)S(1)}, bf16[32,3712]{1,0:T(8,128)(2,1)S(1)}, u32[]{:S(2)}, u32[]{:S(2)}) collective-permute-start(bf16[32,3712]{1,0:T(8,128)(2,1)S(1)} %get-tuple-element.92), channel_id=1, source_target_pairs={{0,4},{4,8},{8,12},{12,14},{14,10},{10,6},{6,2},{2,0},{1,5},{5,9},... | collective-permute-start | bytes 712712 | tf_op jit(solution)/shard_map/ppermute | solution.py:432
  138.1 9.0 %collective-permute-start.30 = (bf16[32,3584]{1,0:T(8,128)(2,1)S(1)}, bf16[32,3584]{1,0:T(8,128)(2,1)S(1)}, u32[]{:S(2)}, u32[]{:S(2)}) collective-permute-start(bf16[32,3584]{1,0:T(8,128)(2,1)S(1)} %get-tuple-element.113), channel_id=1, source_target_pairs={{0,4},{4,8},{8,12},{12,14},{14,10},{10,6},{6,2},{2,0},{1,5},{5,9},... | collective-permute-start | bytes 688136 | tf_op jit(solution)/shard_map/ppermute | solution.py:432
  140.0 7.1 %collective-permute-start.31 = (bf16[32,3584]{1,0:T(8,128)(2,1)S(1)}, bf16[32,3584]{1,0:T(8,128)(2,1)S(1)}, u32[]{:S(2)}, u32[]{:S(2)}) collective-permute-start(bf16[32,3584]{1,0:T(8,128)(2,1)S(1)} %get-tuple-element.115), channel_id=1, source_target_pairs={{4,0},{8,4},{12,8},{14,12},{10,14},{6,10},{2,6},{0,2},{5,1},{9,5},... | collective-permute-start | bytes 688136 | tf_op jit(solution)/shard_map/ppermute | solution.py:433
  147.2 13.4 %collective-permute-start.32 = (bf16[32,3584]{1,0:T(8,128)(2,1)S(1)}, bf16[32,3584]{1,0:T(8,128)(2,1)S(1)}, u32[]{:S(2)}, u32[]{:S(2)}) collective-permute-start(bf16[32,3584]{1,0:T(8,128)(2,1)S(1)} %get-tuple-element.116), channel_id=1, source_target_pairs={{0,4},{4,8},{8,12},{12,14},{14,10},{10,6},{6,2},{2,0},{1,5},{5,9},... | collective-permute-start | bytes 688136 | tf_op jit(solution)/shard_map/ppermute | solution.py:432
  148.8 11.8 %collective-permute-start.33 = (bf16[32,3584]{1,0:T(8,128)(2,1)S(1)}, bf16[32,3584]{1,0:T(8,128)(2,1)S(1)}, u32[]{:S(2)}, u32[]{:S(2)}) collective-permute-start(bf16[32,3584]{1,0:T(8,128)(2,1)S(1)} %get-tuple-element.118), channel_id=1, source_target_pairs={{4,0},{8,4},{12,8},{14,12},{10,14},{6,10},{2,6},{0,2},{5,1},{9,5},... | collective-permute-start | bytes 688136 | tf_op jit(solution)/shard_map/ppermute | solution.py:433
  160.8 8.0 %collective-permute-start.34 = (bf16[32,3584]{1,0:T(8,128)(2,1)S(1)}, bf16[32,3584]{1,0:T(8,128)(2,1)S(1)}, u32[]{:S(2)}, u32[]{:S(2)}) collective-permute-start(bf16[32,3584]{1,0:T(8,128)(2,1)S(1)} %get-tuple-element.119), channel_id=1, source_target_pairs={{0,4},{4,8},{8,12},{12,14},{14,10},{10,6},{6,2},{2,0},{1,5},{5,9},... | collective-permute-start | bytes 688136 | tf_op jit(solution)/shard_map/ppermute | solution.py:432
  161.0 7.7 %collective-permute-start.35 = (bf16[32,3584]{1,0:T(8,128)(2,1)S(1)}, bf16[32,3584]{1,0:T(8,128)(2,1)S(1)}, u32[]{:S(2)}, u32[]{:S(2)}) collective-permute-start(bf16[32,3584]{1,0:T(8,128)(2,1)S(1)} %get-tuple-element.120), channel_id=1, source_target_pairs={{4,0},{8,4},{12,8},{14,12},{10,14},{6,10},{2,6},{0,2},{5,1},{9,5},... | collective-permute-start | bytes 688136 | tf_op jit(solution)/shard_map/ppermute | solution.py:433
  (85 other events, 1559.6 us)

commit v4 on v3

v4 whole, which is shorter than its diff:
```python
import functools

import jax
import jax.numpy as jnp
import numpy as np
from jax import lax
from jax.experimental import pallas as pl
from jax.experimental.pallas import tpu as pltpu
from jax.sharding import PartitionSpec as P

MOST = 16
LANES = 128
COST_SHARE = 10**6

route_scale = 2.5
adapter_scale = 2.0

bf16, f32 = jnp.bfloat16, jnp.float32
in_vmem = pl.BlockSpec(memory_space=pltpu.VMEM)
in_hbm = pl.BlockSpec(memory_space=pltpu.HBM)
in_smem = pl.BlockSpec(memory_space=pltpu.SMEM)


def mm(left, right, axes=((1,), (0,))):
    return lax.dot_general(
        left, right, ((axes[0], axes[1]), ((), ())), preferred_element_type=jnp.float32
    )


def mm_nt(left, right):
    return mm(left, right, ((1,), (1,)))


def mm_tn(left, right):
    return mm(left, right, ((0,), (0,)))


def call(body, outs, specs, operands, cost, scratch=(), mib=8, out_specs=None):
    flops, moved = cost
    return pl.pallas_call(
        body,
        out_shape=outs,
        in_specs=specs,
        out_specs=out_specs if out_specs is not None else [in_vmem] * len(outs),
        scratch_shapes=list(scratch),
        compiler_params=pltpu.CompilerParams(vmem_limit_bytes=mib * 2**20),
        cost_estimate=pl.CostEstimate(
            flops=flops // COST_SHARE, bytes_accessed=moved // COST_SHARE, transcendentals=0
        ),
    )(*operands)


def struct(shape, dtype=bf16):
    return jax.ShapeDtypeStruct(shape, dtype)


def nbytes(arrays):
    return sum(a.size * a.dtype.itemsize for a in arrays)


def pieces(total, size):
    return [(at, min(size, total - at)) for at in range(0, total, size)]


def start_all(copies):
    for copy in copies:
        copy.start()


def token_load_kernel(
    choice_hbm, tokens_hbm, router_hbm, load_ref, choice_ref, router_ref, sems
):
    width, experts = tokens_hbm.shape[1], router_ref.shape[0]
    copies = [
        pltpu.make_async_copy(choice_hbm, choice_ref, sems.at[0]),
        pltpu.make_async_copy(tokens_hbm, load_ref.at[:, pl.ds(0, width)], sems.at[1]),
        pltpu.make_async_copy(router_hbm, router_ref, sems.at[2]),
    ]
    start_all(copies)
    copies[0].wait()
    expert = lax.broadcasted_iota(jnp.int32, (LANES, choice_ref.shape[1]), 0)
    hits = jnp.zeros(expert.shape, f32)
    for k in range(choice_ref.shape[0]):
        hits += jnp.where(choice_ref[k : k + 1] == expert, 1.0, 0.0)
    load_ref[:, width:] = hits.T.astype(bf16)
    copies[1].wait()
    copies[2].wait()
    affinity = jax.nn.sigmoid(mm_nt(load_ref[:, :width], router_ref[...]))
    high = affinity.astype(bf16)
    load_ref[:, width + experts : width + 2 * experts] = high
    load_ref[:, width + 2 * experts : width + 3 * experts] = (affinity - high.astype(f32)).astype(bf16)


def fetch_kernel(count, *refs):
    sources, outs, sems = refs[:count], refs[count : 2 * count], refs[-1]
    copies = [
        pltpu.make_async_copy(source, out, sems.at[i])
        for i, (source, out) in enumerate(zip(sources, outs))
    ]
    start_all(copies)
    for copy in copies:
        copy.wait()


def assemble(refs, all_ref):
    at = 0
    for ref in refs:
        all_ref[pl.ds(at, ref.shape[0])] = ref[...]
        at += ref.shape[0]


def expert_names(info_ref, slots):
    mine = 2 * info_ref[0] + info_ref[1]
    other = 2 * info_ref[0] + 1 - info_ref[1]
    slot = lax.broadcasted_iota(jnp.int32, (slots, LANES), 0)
    lane = lax.broadcasted_iota(jnp.int32, (slots, LANES), 1)
    return jnp.where(lane == jnp.where(slot < slots // 2, mine, other), 1.0, 0.0).astype(bf16)


def token_slots_kernel(experts, info_ref, *refs):
    blocks, (kept_ref, sent_ref, select_ref, high_ref, low_ref, all_ref) = refs[:-6], refs[-6:]
    rows, load = blocks[0].shape
    toks, slots = all_ref.shape[0], select_ref.shape[0]
    half, width = slots // 2, load - LANES
    assemble(blocks, all_ref)
    tails = all_ref[:, width:]
    names = expert_names(info_ref, slots)
    slot = lax.broadcasted_iota(jnp.int32, (slots, toks), 0)
    tok = lax.broadcasted_iota(jnp.int32, (slots, toks), 1)
    slot = jnp.where(slot < half, slot, slot - half)
    member = jnp.where(slot // MOST == tok // rows, mm_nt(names, tails), 0.0)
    early = lax.broadcasted_iota(jnp.int32, (toks, toks), 0)
    late = lax.broadcasted_iota(jnp.int32, (toks, toks), 1)
    before = mm(member.astype(bf16), jnp.where(early < late, 1.0, 0.0).astype(bf16))
    select = jnp.where(before == (slot % MOST).astype(f32), member, 0.0)
    select_ref[...] = select.astype(bf16)
    for at, size in pieces(load, 4 * LANES):
        out = mm(select_ref[...], all_ref[:, at : at + size]).astype(bf16)
        kept_ref[:, at : at + size] = out[:half]
        sent_ref[:, at : at + size] = out[half:]
    lane = lax.broadcasted_iota(jnp.int32, (LANES, LANES), 0)
    expert = lax.broadcasted_iota(jnp.int32, (LANES, LANES), 1)
    parts = (lane == expert + experts) | (lane == expert + 2 * experts)
    affinity = mm(tails, jnp.where(parts & (expert < experts), 1.0, 0.0).astype(bf16))
    mine = lax.broadcasted_iota(jnp.int32, (toks, LANES), 1) < experts
    chosen = jnp.where(mine, tails.astype(f32) * affinity, 0.0)
    gates = route_scale * chosen / jnp.sum(chosen, axis=1, keepdims=True)
    high = gates.astype(bf16)
    low = (gates - high.astype(f32)).astype(bf16)
    high_ref[...] = (select * mm_nt(names, high)).astype(bf16)
    low_ref[...] = (select * mm_nt(names, low)).astype(bf16)


def cot_slots_kernel(high_ref, low_ref, *refs):
    blocks, (kept_ref, sent_ref, all_ref) = refs[:-3], refs[-3:]
    half, width = kept_ref.shape
    assemble(blocks, all_ref)
    for at, size in pieces(width, 4 * LANES):
        cot = all_ref[:, at : at + size]
        out = (mm(high_ref[...], cot) + mm(low_ref[...], cot)).astype(bf16)
        kept_ref[:, at : at + size] = out[:half]
        sent_ref[:, at : at + size] = out[half:]


def inner_kernel(
    count, tiles, info_ref, kept_ref, came_ref, gate_ref, up_a_ref, up_b_ref, up_hbm,
    inner_ref, slope_ref, active_ref, low_up_ref, keep_ref, rows_ref, up_ref, sems,
):
    half, width = kept_ref.shape[0], rows_ref.shape[1]
    slots, tile = 2 * half, gate_ref.shape[1] // tiles
    copy = pltpu.make_async_copy(up_hbm, up_ref, sems.at[0])
    copy.start()
    rows_ref[:half] = kept_ref[:, :width]
    rows_ref[half:] = came_ref[:, :width]
    low_up_ref[...] = mm_nt(rows_ref[...], up_a_ref[...]).astype(bf16)
    chip, core = info_ref[0], info_ref[1]
    lane = lax.broadcasted_iota(jnp.int32, (slots, LANES), 1)
    tails = jnp.concatenate([kept_ref[:, width:], came_ref[:, width:]], axis=0).astype(f32)
    valid = jnp.sum(jnp.where(lane == 2 * chip + core, tails, 0.0), axis=1, keepdims=True)
    here = lax.broadcasted_iota(jnp.int32, (slots, 1), 0)
    there = lax.broadcasted_iota(jnp.int32, (1, slots), 1)
    source_here = jnp.zeros((slots, 1), jnp.int32)
    source_there = jnp.zeros((1, slots), jnp.int32)
    for i in range(2 * count):
        source = 2 * info_ref[4 + i % count] + (core if i < count else 1 - core)
        source_here = jnp.where(here // MOST == i, source, source_here)
        source_there = jnp.where(there // MOST == i, source, source_there)
    ahead = jnp.where(source_there < source_here, 1.0, 0.0).astype(bf16)
    spread = jnp.broadcast_to(valid, (slots, LANES)).astype(bf16)
    rank = mm(ahead, spread) + (here % MOST).astype(f32)
    keep_ref[...] = jnp.where(rank < info_ref[2].astype(f32), valid, 0.0)
    for j in range(tiles):
        cols = slice(j * tile, (j + 1) * tile)
        pre_gate = mm(rows_ref[...], gate_ref[:, cols])
        logistic = jax.nn.sigmoid(pre_gate)
        active_ref[:, cols] = pre_gate * logistic
        slope_ref[:, cols] = logistic * (1.0 + pre_gate * (1.0 - logistic))
    copy.wait()
    for j in range(tiles):
        cols = slice(j * tile, (j + 1) * tile)
        pre_up = mm(rows_ref[...], up_ref[:, cols]) + adapter_scale * mm(
            low_up_ref[...], up_b_ref[:, cols]
        )
        slope_ref[:, cols] = slope_ref[:, cols] * pre_up
        inner_ref[:, cols] = (active_ref[:, cols] * pre_up).astype(bf16)


def routed_kernel(
    tiles, inner_ref, keep_ref, down_ref, down_a_ref, down_b_ref, kept_ref, sent_ref, low_down_ref
):
    half, tile = kept_ref.shape[0], down_ref.shape[1] // tiles
    low_down_ref[...] = mm_nt(inner_ref[...], down_a_ref[...]).astype(bf16)
    keep = keep_ref[:, :1]
    for j in range(tiles):
        cols = slice(j * tile, (j + 1) * tile)
        value = mm(inner_ref[...], down_ref[:, cols]) + adapter_scale * mm(
            low_down_ref[...], down_b_ref[:, cols]
        )
        value = (keep * value).astype(bf16)
        kept_ref[:, cols] = value[:half]
        sent_ref[:, cols] = value[half:]


def write_parts(outs, at, size, part):
    row = 0
    for ref in outs:
        ref[:, at : at + size] = part[row : row + ref.shape[0]]
        row += ref.shape[0]


def mix_parts_kernel(high_ref, low_ref, kept_ref, came_ref, *refs):
    outs, (rows_ref,) = refs[:-1], refs[-1:]
    half, width = kept_ref.shape
    rows_ref[:half] = kept_ref[...]
    rows_ref[half:] = came_ref[...]
    high = high_ref[...].astype(f32).T.astype(bf16)
    low = low_ref[...].astype(f32).T.astype(bf16)
    for at, size in pieces(width, 4 * LANES):
        rows = rows_ref[:, at : at + size]
        write_parts(outs, at, size, (mm(high, rows) + mm(low, rows)).astype(bf16))


def token_places(count, info_ref, toks):
    rows = toks // count
    here = lax.broadcasted_iota(jnp.int32, (toks, toks), 0)
    place = jnp.zeros((toks, toks), jnp.int32)
    for i in range(count):
        place = jnp.where(here // rows == i, rows * (info_ref[4 + i] - i) + here, place)
    return jnp.where(place == lax.broadcasted_iota(jnp.int32, (toks, toks), 1), 1.0, 0.0).astype(bf16)


def gate_grad_kernel(count, info_ref, select_ref, kept_ref, came_ref, all_ref, out_ref, rows_ref):
    half = kept_ref.shape[0]
    rows_ref[:half] = kept_ref[...]
    rows_ref[half:] = came_ref[...]
    dots = select_ref[...].astype(f32) * mm_nt(rows_ref[...], all_ref[...])
    own = jnp.sum(dots[:half], axis=0, keepdims=True)
    other = jnp.sum(dots[half:], axis=0, keepdims=True)
    first = info_ref[1] == 0
    row = lax.broadcasted_iota(jnp.int32, out_ref.shape[1:], 0)
    out = jnp.zeros(out_ref.shape[1:], f32)
    for i, value in enumerate((jnp.where(first, own, other), jnp.where(first, other, own))):
        high = value.astype(bf16).astype(f32)
        out = jnp.where(row == 2 * i, high, jnp.where(row == 2 * i + 1, value - high, out))
    out_ref[0] = mm(out.astype(bf16), token_places(count, info_ref, out.shape[1])).astype(bf16)


def back_parts_kernel(select_ref, kept_ref, came_ref, *refs):
    outs, (rows_ref,) = refs[:-1], refs[-1:]
    width, half = kept_ref.shape[1], kept_ref.shape[0]
    rows_ref[:half] = kept_ref[...]
    rows_ref[half:] = came_ref[...]
    select = select_ref[...].astype(f32).T.astype(bf16)
    for at, size in pieces(width, 4 * LANES):
        write_parts(outs, at, size, mm(select, rows_ref[:, at : at + size]).astype(bf16))


def inner_grad_kernel(
    tiles, kept_ref, came_ref, keep_ref, down_ref, down_b_ref, down_a_ref, slope_ref, active_ref,
    up_b_ref, grad_ref, gate_out_ref, up_out_ref, back_low_ref, back_up_ref,
):
    half, tile = kept_ref.shape[0], down_ref.shape[0] // tiles
    keep = keep_ref[:, :1].astype(bf16)
    grad_ref[:half] = kept_ref[...] * keep[:half]
    grad_ref[half:] = came_ref[...] * keep[half:]
    back_low_ref[...] = mm_nt(grad_ref[...], down_b_ref[...]).astype(bf16)
    for j in range(tiles):
        cols = slice(j * tile, (j + 1) * tile)
        inner = mm_nt(grad_ref[...], down_ref[cols]) + adapter_scale * mm(
            back_low_ref[...], down_a_ref[:, cols]
        )
        gate_out_ref[:, cols] = (inner * slope_ref[:, cols]).astype(bf16)
        up_out_ref[:, cols] = (inner * active_ref[:, cols]).astype(bf16)
    back_up_ref[...] = mm_nt(up_out_ref[...], up_b_ref[...]).astype(bf16)


def row_grad_kernel(
    tiles, grad_gate_ref, grad_up_ref, back_up_ref, gate_ref, up_ref, up_a_ref, kept_ref, sent_ref
):
    half, tile = kept_ref.shape[0], gate_ref.shape[0] // tiles
    for j in range(tiles):
        cols = slice(j * tile, (j + 1) * tile)
        value = (
            mm_nt(grad_gate_ref[...], gate_ref[cols])
            + mm_nt(grad_up_ref[...], up_ref[cols])
            + adapter_scale * mm(back_up_ref[...], up_a_ref[:, cols])
        ).astype(bf16)
        kept_ref[:, cols] = value[:half]
        sent_ref[:, cols] = value[half:]


def adapter_kernel(
    kept_ref, came_ref, back_up_ref, low_up_ref, grad_up_ref, inner_ref, back_low_ref,
    low_down_ref, grad_ref, up_a_ref, up_b_ref, down_a_ref, down_b_ref,
):
    width, half = grad_ref.shape[1], kept_ref.shape[0]
    scaled = lambda value: (adapter_scale * value).astype(bf16)
    back_up = back_up_ref[...]
    for at, size in pieces(width, 4 * LANES):
        cols = slice(at, at + size)
        up_a_ref[:, cols] = scaled(
            mm_tn(back_up[:half], kept_ref[:, cols]) + mm_tn(back_up[half:], came_ref[:, cols])
        )
        down_b_ref[:, cols] = scaled(mm_tn(low_down_ref[...], grad_ref[:, cols]))
    up_b_ref[...] = scaled(mm_tn(low_up_ref[...], grad_up_ref[...]))
    down_a_ref[...] = scaled(mm_tn(back_low_ref[...], inner_ref[...]))


def hop_kernel(*refs):
    for i in range(len(refs) // 3):
        own, came, out = refs[2 * i], refs[2 * i + 1], refs[2 * len(refs) // 3 + i]
        out[...] = (own[...].astype(f32) + came[...].astype(f32)).astype(bf16)


def mixed_kernel(own_ref, forth_ref, hither_ref, out_ref):
    out_ref[...] = (
        own_ref[...].astype(f32) + forth_ref[...].astype(f32) + hither_ref[...].astype(f32)
    ).astype(bf16)


def input_grad_kernel(own_ref, forth_ref, hither_ref, term_ref, out_ref):
    out_ref[...] = (
        own_ref[...].astype(f32)
        + forth_ref[...].astype(f32)
        + hither_ref[...].astype(f32)
        + term_ref[...]
    ).astype(bf16)


def router_grad_kernel(count, info_ref, dots_ref, router_ref, all_ref, out_ref, term_ref):
    experts, width = out_ref.shape
    rows, toks = term_ref.shape[0], all_ref.shape[0]
    tails = all_ref[:, width:].astype(f32).T
    hits = tails[:experts]
    affinity = tails[experts : 2 * experts] + tails[2 * experts : 3 * experts]
    expert = lax.broadcasted_iota(jnp.int32, (experts, toks), 0)
    grad_gates = jnp.zeros((experts, toks), f32)
    gathered = jnp.concatenate([dots_ref[i] for i in range(count)], axis=0)
    gathered = mm_nt(gathered, token_places(count, info_ref, toks))
    for i in range(count):
        name = 2 * (info_ref[0] ^ i)
        dots = gathered[i * dots_ref.shape[1] : (i + 1) * dots_ref.shape[1]]
        grad_gates = jnp.where(expert == name, dots[0:1] + dots[1:2], grad_gates)
        grad_gates = jnp.where(expert == name + 1, dots[2:3] + dots[3:4], grad_gates)
    chosen = hits * affinity
    chosen_sum = jnp.sum(chosen, axis=0, keepdims=True)
    grad_chosen = route_scale * (
        grad_gates / chosen_sum
        - jnp.sum(grad_gates * chosen, axis=0, keepdims=True) / (chosen_sum * chosen_sum)
    )
    logits = (hits * grad_chosen * affinity * (1.0 - affinity)).astype(bf16)
    out_ref[...] = mm(logits, all_ref[:, :width])
    term_ref[...] = mm_tn(logits[:, :rows], router_ref[...])


def ring_of(count):
    if count == 8:
        order = [0, 2, 4, 6, 7, 5, 3, 1]
    else:
        order = list(range(count))
    ahead = [(order[i], order[(i + 1) % count]) for i in range(count)]
    back = [(b, a) for a, b in ahead]
    return order, ahead, back


def offsets_of(count):
    half = count // 2
    return [0] + [-k for k in range(1, half)] + list(range(1, half)) + [half]


def tie(*values):
    return lax.optimization_barrier(values)


class Ring:
    def __init__(self, count, far_ahead):
        _, ahead, back = ring_of(count)
        self.half = count // 2
        self.far, self.near = (ahead, back) if far_ahead else (back, ahead)
        self.far_ahead = far_ahead

    def gather_hop(self, far, near):
        far.append(lax.ppermute(far[-1], "expert", self.far))
        if len(near) < self.half:
            near.append(lax.ppermute(near[-1], "expert", self.near))

    def gathered(self, far, near):
        behind, front = (far, near) if self.far_ahead else (near, far)
        return behind[: self.half] + front[1 : self.half] + [far[self.half]]

    def scatter_starts(self, parts):
        half = self.half
        to_front = [parts[half - 1 + k] for k in range(half - 1, 0, -1)]
        to_rear = [parts[k] for k in range(half - 1, 0, -1)]
        far, near = (to_front, to_rear) if self.far_ahead else (to_rear, to_front)
        return [parts[-1]] + far, near

    def scatter_hop(self, outs, came, step):
        (far_out, near_out), (far, near) = outs, came
        if step == 0:
            far_part, near_part = far_out[0], near_out[0]
        else:
            operands = [far_out[step], far]
            if step < self.half - 1:
                operands += [near_out[step], near]
            added = call(
                hop_kernel,
                [struct(far.shape)] * (len(operands) // 2),
                [in_vmem] * len(operands),
                operands,
                (0, 3 * nbytes(operands) // 2),
            )
            far_part, near_part = added[0], added[-1]
        far = lax.ppermute(far_part, "expert", self.far)
        if step < self.half - 1:
            near = lax.ppermute(near_part, "expert", self.near)
        return far, near


def double(gathered, step):
    size = lax.axis_size("expert")
    came = lax.ppermute(gathered, "expert", [(i, i ^ step) for i in range(size)])
    return jnp.concatenate([gathered, came], axis=0)


def swap_cores(value):
    return lax.ppermute(value, "dp", [(0, 1), (1, 0)])


def make_per_device(count):
    order, _, _ = ring_of(count)
    offsets = offsets_of(count)
    place = [order.index(chip) for chip in range(count)]
    table = np.array(
        [[order[(place[c] + off) % count] for off in offsets] for c in range(count)], np.int32
    )

    def per_device(
        tokens,
        cotangent,
        expert_choice_index,
        capacity,
        router_matrix,
        gate_matrix,
        up_matrix,
        down_matrix,
        up_adapter_first,
        up_adapter_second,
        down_adapter_first,
        down_adapter_second,
    ):
        tok_count, width = tokens.shape
        experts = router_matrix.shape[1]
        load = width + LANES
        half = count * MOST
        slots = 2 * half
        chip, core = lax.axis_index("expert"), lax.axis_index("dp")
        chips = jnp.sum(
            jnp.where(jnp.arange(count)[:, None] == chip, jnp.asarray(table), 0), axis=0
        )
        info = jnp.concatenate([jnp.stack([chip, core, capacity[0]]), chips[:1], chips])
        info = info.astype(jnp.int32)
        gate_w, up_w, down_w = gate_matrix[0], up_matrix[0], down_matrix[0]
        up_a, up_b = up_adapter_first[0], up_adapter_second[0]
        down_a, down_b = down_adapter_first[0], down_adapter_second[0]
        hidden, rank = gate_w.shape[1], up_a.shape[1]

        toks = count * tok_count
        tiles = 4
        up_a, down_a, router = up_a.T, down_a.T, router_matrix.T
        choice = expert_choice_index.T
        ring_token, ring_cot = Ring(count, True), Ring(count, False)
        hops = count // 2

        stay = lambda *arrays: [pltpu.with_memory_space_constraint(a, pltpu.HBM) for a in arrays]

        (token_load,) = call(
            token_load_kernel, [struct((tok_count, load))], [in_hbm] * 3,
            stay(choice, tokens, router), (0, 2 * nbytes([tokens])),
            scratch=[
                pltpu.VMEM(choice.shape, jnp.int32), pltpu.VMEM(router.shape, bf16),
                pltpu.SemaphoreType.DMA((3,)),
            ],
        )

        tok_far, tok_near = [token_load], [token_load]
        ring_token.gather_hop(tok_far, tok_near)
        cot_load, tok_far[1] = tie(cotangent, tok_far[1])
        cot_far, cot_near = [cot_load], [cot_load]
        ring_token.gather_hop(tok_far, tok_near)
        ring_cot.gather_hop(cot_far, cot_near)
        for hop in range(2, hops):
            ring_token.gather_hop(tok_far, tok_near)
            if hop == hops - 2:
                tok_far[-1], cot_far[1], cot_near[1] = tie(tok_far[-1], cot_far[1], cot_near[1])
            if hop < hops - 1:
                ring_cot.gather_hop(cot_far, cot_near)
        token_blocks = ring_token.gathered(tok_far, tok_near)

        kept, sent, select, high, low, token_all = call(
            functools.partial(token_slots_kernel, experts),
            [struct((half, load))] * 2 + [struct((slots, toks))] * 3 + [struct((toks, load))],
            [in_smem] + [in_vmem] * count,
            (info, *token_blocks),
            (2 * slots * toks * load, 2 * count * nbytes([token_load])),
        )
        sent, cot_far[-1], cot_near[-1] = tie(sent, cot_far[-1], cot_near[-1])
        came = swap_cores(sent)
        kept, gate_late = tie(kept, gate_w)
        gate_v, up_a_v, up_b_v = call(
            functools.partial(fetch_kernel, 3),
            [pltpu.VMEM(a.shape, bf16) for a in (gate_w, up_a, up_b)],
            [in_hbm] * 3,
            stay(gate_late, up_a, up_b),
            (0, nbytes([gate_w])),
            scratch=[pltpu.SemaphoreType.DMA((3,))],
            mib=1,
        )
        ring_cot.gather_hop(cot_far, cot_near)
        inner, slope, active, low_up, keep = call(
            functools.partial(inner_kernel, count, tiles),
            [
                struct((slots, hidden)), struct((slots, hidden), f32), struct((slots, hidden), f32),
                struct((slots, rank)), struct((slots, LANES), f32),
            ],
            [in_smem] + [in_vmem] * 5 + [in_hbm],
            (info, kept, came, gate_v, up_a_v, up_b_v, *stay(up_w)),
            (4 * slots * width * hidden, 2 * nbytes([gate_w])),
            scratch=[
                pltpu.VMEM((slots, width), bf16), pltpu.VMEM(up_w.shape, bf16),
                pltpu.SemaphoreType.DMA((1,)),
            ],
            mib=16,
        )
        inner, cot_far[-1], cot_near[-1] = tie(inner, cot_far[-1], cot_near[-1])
        while len(cot_far) <= hops:
            ring_cot.gather_hop(cot_far, cot_near)
        routed_kept, routed_sent, low_down = call(
            functools.partial(routed_kernel, tiles),
            [struct((half, width))] * 2 + [struct((slots, rank))],
            [in_vmem] * 5,
            (inner, keep, down_w, down_a, down_b),
            (2 * slots * width * hidden, nbytes([gate_w])),
        )
        routed_sent, cot_far[-1] = tie(routed_sent, cot_far[-1])
        routed_came = swap_cores(routed_sent)

        mix_parts = call(
            mix_parts_kernel,
            [struct((tok_count, width))] * count,
            [in_vmem] * 4,
            (high, low, routed_kept, routed_came),
            (4 * slots * toks * load, 3 * count * nbytes([token_load])),
            scratch=[pltpu.VMEM((slots, width), bf16)],
        )
        cot_blocks = ring_cot.gathered(cot_far, cot_near)
        mix_parts = list(mix_parts)
        mix_outs = ring_token.scatter_starts(mix_parts)
        mix_came = [ring_token.scatter_hop(mix_outs, (None, None), 0)]

        cot_kept, cot_sent, cot_all = call(
            cot_slots_kernel,
            [struct((half, width))] * 2 + [struct((toks, width))],
            [in_vmem] * (count + 2),
            (high, low, *cot_blocks),
            (4 * slots * toks * load, 2 * count * nbytes([token_load])),
        )
        cot_came = swap_cores(cot_sent)
        (dots,) = call(
            functools.partial(gate_grad_kernel, count),
            [struct((1, 2 * 8, toks))],
            [in_smem] + [in_vmem] * 4,
            (info, select, routed_kept, routed_came, cot_all),
            (2 * slots * toks * load, 2 * count * nbytes([token_load])),
            scratch=[pltpu.VMEM((slots, width), bf16)],
        )
        cot_came, dots = tie(cot_came, dots)
        grad_routed, grad_gate, grad_up, back_low, back_up = call(
            functools.partial(inner_grad_kernel, tiles),
            [struct((slots, width))] + [struct((slots, hidden))] * 2 + [struct((slots, rank))] * 2,
            [in_vmem] * 9,
            (cot_kept, cot_came, keep, down_w, down_b, down_a, slope, active, up_b_v),
            (2 * slots * width * hidden, nbytes([gate_w])),
        )
        dots = double(dots, 1)
        grad_up, dots, *mix_came[0] = tie(grad_up, dots, *mix_came[0])
        mix_came.append(ring_token.scatter_hop(mix_outs, mix_came[-1], 1))
        back_kept, back_sent = call(
            functools.partial(row_grad_kernel, tiles),
            [struct((half, width))] * 2,
            [in_vmem] * 6,
            (grad_gate, grad_up, back_up, gate_v, up_w, up_a_v),
            (4 * slots * width * hidden, 2 * nbytes([gate_w])),
        )
        dots = double(dots, 2)
        back_sent, dots, *mix_came[1] = tie(back_sent, dots, *mix_came[1])
        back_came = swap_cores(back_sent)
        back_parts = call(
            back_parts_kernel,
            [struct((tok_count, width))] * count,
            [in_vmem] * 3,
            (select, back_kept, back_came),
            (2 * slots * toks * load, 2 * count * nbytes([token_load])),
            scratch=[pltpu.VMEM((slots, width), bf16)],
        )
        back_parts = list(back_parts)
        back_outs = ring_cot.scatter_starts(back_parts)
        back_came = [ring_cot.scatter_hop(back_outs, (None, None), 0)]
        step = 4
        while step < count:
            dots = double(dots, step)
            step *= 2
        back_up_late = back_up
        for hop in range(1, hops):
            if hop + 1 < hops:
                mix_came.append(ring_token.scatter_hop(mix_outs, mix_came[-1], hop + 1))
            tied = tie(*back_came[-1], *mix_came[-1], back_up_late)
            back_came[-1], mix_came[-1], back_up_late = tied[:2], tied[2:4], tied[4]
            if hop > 1:
                back_came[-1], dots = tie(back_came[-1], dots)
            back_came.append(ring_cot.scatter_hop(back_outs, back_came[-1], hop))
        adapters = call(
            adapter_kernel,
            [
                struct((rank, width)), struct((rank, hidden)),
                struct((rank, hidden)), struct((rank, width)),
            ],
            [in_vmem] * 9,
            (kept, came, back_up_late, low_up, grad_up, inner, back_low, low_down,
             grad_routed),
            (8 * slots * width * rank, 4 * nbytes([grad_routed])),
            out_specs=[pl.BlockSpec()] * 4,
        )
        adapters = (adapters[0].T, adapters[1], adapters[2].T, adapters[3])

        (mixed,) = call(
            mixed_kernel,
            [struct((tok_count, width))],
            [in_vmem] * 3,
            (mix_parts[0], *mix_came[-1]),
            (0, 4 * nbytes([token_load])),
            out_specs=[pl.BlockSpec()],
        )
        router_half, router_term = call(
            functools.partial(router_grad_kernel, count),
            [struct((experts, width), f32), struct((tok_count, width), f32)],
            [in_smem] + [in_vmem] * 3,
            (info, dots, router, token_all),
            (0, count * nbytes([token_load])),
        )
        router_grad = (router_half + swap_cores(router_half)).T
        (input_grad,) = call(
            input_grad_kernel,
            [struct((tok_count, width))],
            [in_vmem] * 4,
            (back_parts[0], *back_came[-1], router_term),
            (0, 4 * nbytes([token_load])),
            out_specs=[pl.BlockSpec()],
        )
        return (mixed, input_grad, router_grad) + tuple(value[None] for value in adapters)

    return per_device


def solution(mesh):
    rows = P(("groups", "expert", "dp"), None)
    whole = P(("groups", "expert", "dp"), None, None)
    weight = P(("expert", "dp"), None, None)
    return jax.shard_map(
        make_per_device(mesh.shape["expert"]),
        mesh=mesh,
        in_specs=(rows, rows, rows, P(("groups", "expert", "dp")), P()) + (weight,) * 7,
        out_specs=(rows, rows, P("groups", None), whole, whole, whole, whole),
        check_vma=False,
    )
```

time: 171 us -> 124 us (0.73)
  local copies, waits for them, and re-layouts: 29 us -> 0.16 us
  Pallas kernels: 49.6 us -> 34.9 us
  starting transfers between devices: 43.2 us -> 35.1 us
  waiting for transfers between devices: 45.6 us -> 50.5 us
    unnamed x144 -> x16, local copies, waits for them, and re-layouts: 27.6 us -> 0.04 us
    pallas_call x20 -> x21, Pallas kernels: 49.6 us -> 34.9 us  [call(): pl.pallas_call(body, out_shape=outs, in_specs=specs, out_specs=out_specs...]
    ppermute x35 -> x31, starting transfers between devices: 42.4 us -> 34.4 us  [the longest x8 10.9 us: gather_hop(): far.append(lax.ppermute(far[-1], 'expert', self.far))]
    ppermute x35 -> x31, waiting for transfers between devices: 45.6 us -> 49.5 us  [the longest x8 21.8 us: gather_hop(): far.append(lax.ppermute(far[-1], 'expert', self.far))]
  transfers between devices with their start and end apart: 40 -> 36, of which waited for: 17 -> 17; matrix products, arithmetic and copies ran while one was open for 5% -> 1% of each run, Pallas kernels for 29% -> 25%
where the time goes in v4:
time: 124 us
  waiting for transfers between devices  50.5 us (41%)
  starting transfers between devices  35.1 us (28%)
  Pallas kernels  34.9 us (28%)
  between operations  1.58 us (1%)
  other arithmetic  1.51 us (1%)
    pallas_call x21, Pallas kernels, call(): pl.pallas_call(body, out_shape=outs, in_specs=specs, out_specs=out_specs...  34.9 us
    ppermute x8, waiting for transfers between devices, gather_hop(): far.append(lax.ppermute(far[-1], 'expert', self.far))  21.8 us
    ppermute x8, waiting for transfers between devices, scatter_hop(): far = lax.ppermute(far_part, 'expert', self.far)  15.5 us
    ppermute x8, starting transfers between devices, gather_hop(): far.append(lax.ppermute(far[-1], 'expert', self.far))  10.9 us
    ppermute x8, starting transfers between devices, scatter_hop(): far = lax.ppermute(far_part, 'expert', self.far)  9.31 us
    ppermute x3, waiting for transfers between devices, double(): lax.ppermute(gathered, 'expert', [(i, i ^ step) for i in range(size)])  7.51 us
    ppermute x6, starting transfers between devices, scatter_hop(): near = lax.ppermute(near_part, 'expert', self.near)  6.39 us
    ppermute x6, starting transfers between devices, gather_hop(): near.append(lax.ppermute(near[-1], 'expert', self.near))  4.8 us
  transfers between devices with their start and end apart: 36, of which 17 were waited for; matrix products, arithmetic and copies ran while one was open for 1% of the time, Pallas kernels for 25%

profile of v4, /device:TPU:0, one launch (start us, length us, event | category | flops | bytes accessed | tf_op | source)
XLA Modules:
  0.0 123.8 jit_solution(14228760285289981724)
XLA Ops:
  2.0 3.1 %collective-permute-start = (bf16[32,3712]{1,0:T(8,128)(2,1)S(1)}, bf16[32,3712]{1,0:T(8,128)(2,1)S(1)}, u32[]{:S(2)}, u32[]{:S(2)}) collective-permute-start(bf16[32,3712]{1,0:T(8,128)(2,1)S(1)} %shard_map.180.refs_0_), channel_id=1, source_target_pairs={{0,4},{4,8},{8,12},{12,14},{14,10},{10,6},{6,2},{2,0},{1,5},{5,9},... | collective-permute-start | bytes 712712 | tf_op jit(solution)/shard_map/ppermute | solution.py:403
  5.1 5.7 %collective-permute-done.refs_1_ = bf16[32,3712]{1,0:T(8,128)(2,1)S(1)} collective-permute-done((bf16[32,3712]{1,0:T(8,128)(2,1)S(1)}, bf16[32,3712]{1,0:T(8,128)(2,1)S(1)}, u32[]{:S(2)}, u32[]{:S(2)}) %collective-permute-start) | collective-permute-done | bytes 237600 | tf_op jit(solution)/shard_map/ppermute | solution.py:403
  10.8 1.8 %collective-permute-start.1 = (bf16[32,3712]{1,0:T(8,128)(2,1)S(1)}, bf16[32,3712]{1,0:T(8,128)(2,1)S(1)}, u32[]{:S(2)}, u32[]{:S(2)}) collective-permute-start(bf16[32,3712]{1,0:T(8,128)(2,1)S(1)} %collective-permute-done.refs_1_), channel_id=1, source_target_pairs={{0,4},{4,8},{8,12},{12,14},{14,10},{10,6},{6,2},{2,0},{1,5},{5,9},... | collective-permute-start | bytes 712712 | tf_op jit(solution)/shard_map/ppermute | solution.py:403
  12.8 4.9 %collective-permute-done.1.refs_2_ = bf16[32,3712]{1,0:T(8,128)(2,1)S(1)} collective-permute-done((bf16[32,3712]{1,0:T(8,128)(2,1)S(1)}, bf16[32,3712]{1,0:T(8,128)(2,1)S(1)}, u32[]{:S(2)}, u32[]{:S(2)}) %collective-permute-start.1) | collective-permute-done | bytes 237600 | tf_op jit(solution)/shard_map/ppermute | solution.py:403
  21.8 5.4 %collective-permute-done.3.refs_4_ = bf16[32,3584]{1,0:T(8,128)(2,1)S(1)} collective-permute-done((bf16[32,3584]{1,0:T(8,128)(2,1)}, bf16[32,3584]{1,0:T(8,128)(2,1)S(1)}, u32[]{:S(2)}, u32[]{:S(2)}) %collective-permute-start.3) | collective-permute-done | bytes 229408 | tf_op jit(solution)/shard_map/ppermute | solution.py:403
  30.1 1.6 %collective-permute-start.10 = (bf16[32,3584]{1,0:T(8,128)(2,1)S(1)}, bf16[32,3584]{1,0:T(8,128)(2,1)S(1)}, u32[]{:S(2)}, u32[]{:S(2)}) collective-permute-start(bf16[32,3584]{1,0:T(8,128)(2,1)S(1)} %collective-permute-done.4.refs_1_), channel_id=1, source_target_pairs={{0,4},{4,8},{8,12},{12,14},{14,10},{10,6},{6,2},{2,0},{1,5},{5,9},... | collective-permute-start | bytes 688136 | tf_op jit(solution)/shard_map/ppermute | solution.py:405
  33.7 2.6 %collective-permute-done.8.refs_7_ = bf16[32,3712]{1,0:T(8,128)(2,1)S(1)} collective-permute-done((bf16[32,3712]{1,0:T(8,128)(2,1)S(1)}, bf16[32,3712]{1,0:T(8,128)(2,1)S(1)}, u32[]{:S(2)}, u32[]{:S(2)}) %collective-permute-start.8) | collective-permute-done | bytes 237600 | tf_op jit(solution)/shard_map/ppermute | solution.py:403
  36.3 1.8 %shard_map.181 = (bf16[128,3712]{1,0:T(8,128)(2,1)S(1)}, bf16[128,3712]{1,0:T(8,128)(2,1)S(1)}, bf16[256,256]{1,0:T(8,128)(2,1)S(1)}, bf16[256,256]{1,0:T(8,128)...) custom-call(s32[12]{0:T(128)S(1)} %concatenate.12.info_ref, ...), custom_call_target="tpu_custom_call" | custom-call | flops 486 | bytes 3 | tf_op jit(solution)/shard_map/pallas_call | solution.py:40
  40.8 3.3 %shard_map.182 = (bf16[3584,1024]{1,0:T(8,128)(2,1)S(1)}, bf16[64,3584]{1,0:T(8,128)(2,1)S(1)}, bf16[64,1024]{1,0:T(8,128)(2,1)S(1)}) custom-call(bf16[3584,1024]{1,0:T(8,128)(2,1)} %bitcast.40, bf16[64,3584]{1,0:T(8,128)(2,1)} %bitcast.41, bf16[64,1024]{1,0:T(8,128)(2,1)} %bitcast.42), custom_call_target="tpu_custom_call" | custom-call | bytes 7 | tf_op jit(solution)/shard_map/pallas_call | solution.py:40
  44.1 6.5 %shard_map.183 = (bf16[256,1024]{1,0:T(8,128)(2,1)S(1)}, f32[256,1024]{1,0:T(8,128)S(1)}, f32[256,1024]{1,0:T(8,128)S(1)}, bf16[256,64]{1,0:T(8,128)(2,1)S(1)}, f32[256,128]{1,0:T(8,128)S(1)}) custom-call(s32[12]{0:T(128)S(1)} %concatenate.12.info_ref, bf16[128,3712]{1,0:T(8,128)(2,1)S(1)} %get-tuple-element.116.kept_ref, ...), custom_call_target="tpu_custom_call" | custom-call | flops 3758 | bytes 14 | tf_op jit(solution)/shard_map/pallas_call | solution.py:40
  51.8 3.3 %shard_map.184 = (bf16[128,3584]{1,0:T(8,128)(2,1)S(1)}, bf16[128,3584]{1,0:T(8,128)(2,1)S(1)}, bf16[256,64]{1,0:T(8,128)(2,1)S(1)}) custom-call(bf16[256,1024]{1,0:T(8,128)(2,1)S(1)} %get-tuple-element.128.inner_ref, f32[256,128]{1,0:T(8,128)S(1)} %get-tuple-element.129.keep_ref, bf16[1024,3584]{1,0:T(8,128)(2,1)S(1)} %bitcast.32, ...), custom_call_target="tpu_custom_call" | custom-call | flops 1879 | bytes 7 | tf_op jit(solution)/shard_map/pallas_call | solution.py:40
  55.1 3.1 %collective-permute-done.14.refs_7_ = bf16[32,3584]{1,0:T(8,128)(2,1)S(1)} collective-permute-done((bf16[32,3584]{1,0:T(8,128)(2,1)S(1)}, bf16[32,3584]{1,0:T(8,128)(2,1)S(1)}, u32[]{:S(2)}, u32[]{:S(2)}) %collective-permute-start.14) | collective-permute-done | bytes 229408 | tf_op jit(solution)/shard_map/ppermute | solution.py:403
  66.4 4.1 %shard_map.188 = (bf16[256,3584]{1,0:T(8,128)(2,1)S(1)}, bf16[256,1024]{1,0:T(8,128)(2,1)S(1)}, bf16[256,1024]{1,0:T(8,128)(2,1)S(1)}, bf16[256,64]{1,0:T(8,128)(2,1)S(1)}, bf16[256,64]{1,0:T(8,128)(2,1)S(1)}) custom-call(bf16[128,3584]{1,0:T(8,128)(2,1)S(1)} %get-tuple-element.138.kept_ref, bf16[128,3584]{1,0:T(8,128)(2,1)S(1)} %collective-permute-done.16.came_ref, ...), custom_call_target="tpu_custom_call" | custom-call | flops 1879 | bytes 7 | tf_op jit(solution)/shard_map/pallas_call | solution.py:40
  70.6 1.6 %collective-permute-start.21 = (bf16[32,3584]{1,0:T(8,128)(2,1)S(1)}, bf16[32,3584]{1,0:T(8,128)(2,1)S(1)}, u32[]{:S(2)}, u32[]{:S(2)}) collective-permute-start(bf16[32,3584]{1,0:T(8,128)(2,1)S(1)} %get-tuple-element.158), channel_id=1, source_target_pairs={{0,4},{4,8},{8,12},{12,14},{14,10},{10,6},{6,2},{2,0},{1,5},{5,9},... | collective-permute-start | bytes 688136 | tf_op jit(solution)/shard_map/ppermute | solution.py:434
  72.7 1.6 %collective-permute-start.20 = (bf16[2,16,256]{2,1,0:T(8,128)(2,1)S(1)}, bf16[2,16,256]{2,1,0:T(8,128)(2,1)S(1)}, u32[]{:S(2)}, u32[]{:S(2)}) collective-permute-start(bf16[2,16,256]{2,1,0:T(8,128)(2,1)S(1)} %pad_maximum_fusion.2), channel_id=1, source_target_pairs={{0,4},{2,6},{4,0},{6,2},{8,12},{10,14},{12,8},{14,10},{1,5},{3,7},... | collective-permute-start | bytes 49160 | tf_op jit(solution)/shard_map/ppermute | solution.py:442
  74.3 5.1 %shard_map.189 = (bf16[128,3584]{1,0:T(8,128)(2,1)S(1)}, bf16[128,3584]{1,0:T(8,128)(2,1)S(1)}) custom-call(bf16[256,1024]{1,0:T(8,128)(2,1)S(1)} %get-tuple-element.144.grad_gate_ref, bf16[256,1024]{1,0:T(8,128)(2,1)S(1)} %get-tuple-element.149.grad_up_ref, bf16[256,64]{1,0:T(8,128)(2,1)S(1)} %get-tuple-element.204.back_up_ref, ...), custom_call_target="tpu_custom_call" | custom-call | flops 3758 | bytes 14 | tf_op jit(solution)/shard_map/pallas_call | solution.py:40
  84.7 3.3 %collective-permute-done.26.refs_1_ = bf16[32,3584]{1,0:T(8,128)(2,1)S(1)} collective-permute-done((bf16[32,3584]{1,0:T(8,128)(2,1)S(1)}, bf16[32,3584]{1,0:T(8,128)(2,1)S(1)}, u32[]{:S(2)}, u32[]{:S(2)}) %collective-permute-start.26) | collective-permute-done | bytes 229408 | tf_op jit(solution)/shard_map/ppermute | solution.py:434
  89.2 4.5 %collective-permute-done.24.refs_1_ = bf16[32,3584]{1,0:T(8,128)(2,1)S(1)} collective-permute-done((bf16[32,3584]{1,0:T(8,128)(2,1)S(1)}, bf16[32,3584]{1,0:T(8,128)(2,1)S(1)}, u32[]{:S(2)}, u32[]{:S(2)}) %collective-permute-start.24) | collective-permute-done | bytes 229408 | tf_op jit(solution)/shard_map/ppermute | solution.py:434
  93.8 1.8 %collective-permute-start.30 = (bf16[32,3584]{1,0:T(8,128)(2,1)S(1)}, bf16[32,3584]{1,0:T(8,128)(2,1)S(1)}, u32[]{:S(2)}, u32[]{:S(2)}) collective-permute-start(bf16[32,3584]{1,0:T(8,128)(2,1)S(1)} %shard_map.194), channel_id=1, source_target_pairs={{0,4},{4,8},{8,12},{12,14},{14,10},{10,6},{6,2},{2,0},{1,5},{5,9},... | collective-permute-start | bytes 688136 | tf_op jit(solution)/shard_map/ppermute | solution.py:434
  96.1 1.7 %collective-permute-start.29 = (bf16[32,3584]{1,0:T(8,128)(2,1)S(1)}, bf16[32,3584]{1,0:T(8,128)(2,1)S(1)}, u32[]{:S(2)}, u32[]{:S(2)}) collective-permute-start(bf16[32,3584]{1,0:T(8,128)(2,1)S(1)} %get-tuple-element.175), channel_id=1, source_target_pairs={{0,4},{4,8},{8,12},{12,14},{14,10},{10,6},{6,2},{2,0},{1,5},{5,9},... | collective-permute-start | bytes 688136 | tf_op jit(solution)/shard_map/ppermute | solution.py:436
  98.2 7.5 %collective-permute-done.31 = bf16[4,16,256]{2,1,0:T(8,128)(2,1)S(1)} collective-permute-done((bf16[4,16,256]{2,1,0:T(8,128)(2,1)S(1)}, bf16[4,16,256]{2,1,0:T(8,128)(2,1)S(1)}, u32[]{:S(2)}, u32[]{:S(2)}) %collective-permute-start.31) | collective-permute-done | bytes 32800 | tf_op jit(solution)/shard_map/ppermute | solution.py:442
  108.2 4.3 %collective-permute-done.32.refs_1_ = bf16[32,3584]{1,0:T(8,128)(2,1)S(1)} collective-permute-done((bf16[32,3584]{1,0:T(8,128)(2,1)S(1)}, bf16[32,3584]{1,0:T(8,128)(2,1)S(1)}, u32[]{:S(2)}, u32[]{:S(2)}) %collective-permute-start.32) | collective-permute-done | bytes 229408 | tf_op jit(solution)/shard_map/ppermute | solution.py:434
  116.4 1.8 %shard_map.200 = (bf16[64,3584]{1,0:T(8,128)(2,1)}, bf16[64,1024]{1,0:T(8,128)(2,1)}, bf16[64,1024]{1,0:T(8,128)(2,1)}, bf16[64,3584]{1,0:T(8,128)(2,1)}) custom-call(bf16[128,3712]{1,0:T(8,128)(2,1)S(1)} %get-tuple-element.116.kept_ref, bf16[128,3712]{1,0:T(8,128)(2,1)S(1)} %collective-permute-done.11.came_ref, ...), custom_call_target="tpu_custom_call" | custom-call | flops 469 | bytes 7 | tf_op jit(solution)/shard_map/pallas_call | solution.py:40
  119.6 3.3 %collective-permute-done.34.forth_ref = bf16[32,3584]{1,0:T(8,128)(2,1)S(1)} collective-permute-done((bf16[32,3584]{1,0:T(8,128)(2,1)S(1)}, bf16[32,3584]{1,0:T(8,128)(2,1)S(1)}, u32[]{:S(2)}, u32[]{:S(2)}) %collective-permute-start.34) | collective-permute-done | bytes 229408 | tf_op jit(solution)/shard_map/ppermute | solution.py:434
  (94 shorter events, 38.3 us)
Async XLA Ops:
  2.0 8.8 %collective-permute-start = (bf16[32,3712]{1,0:T(8,128)(2,1)S(1)}, bf16[32,3712]{1,0:T(8,128)(2,1)S(1)}, u32[]{:S(2)}, u32[]{:S(2)}) collective-permute-start(bf16[32,3712]{1,0:T(8,128)(2,1)S(1)} %shard_map.180.refs_0_), channel_id=1, source_target_pairs={{0,4},{4,8},{8,12},{12,14},{14,10},{10,6},{6,2},{2,0},{1,5},{5,9},... | collective-permute-start | bytes 712712 | tf_op jit(solution)/shard_map/ppermute | solution.py:403
  5.0 7.5 %collective-permute-start.5 = (bf16[32,3712]{1,0:T(8,128)(2,1)S(1)}, bf16[32,3712]{1,0:T(8,128)(2,1)S(1)}, u32[]{:S(2)}, u32[]{:S(2)}) collective-permute-start(bf16[32,3712]{1,0:T(8,128)(2,1)S(1)} %shard_map.180.refs_0_), channel_id=1, source_target_pairs={{4,0},{8,4},{12,8},{14,12},{10,14},{6,10},{2,6},{0,2},{5,1},{9,5},... | collective-permute-start | bytes 712712 | tf_op jit(solution)/shard_map/ppermute | solution.py:405
  12.6 8.7 %collective-permute-start.6 = (bf16[32,3712]{1,0:T(8,128)(2,1)S(1)}, bf16[32,3712]{1,0:T(8,128)(2,1)S(1)}, u32[]{:S(2)}, u32[]{:S(2)}) collective-permute-start(bf16[32,3712]{1,0:T(8,128)(2,1)S(1)} %collective-permute-done.5.refs_4_), channel_id=1, source_target_pairs={{4,0},{8,4},{12,8},{14,12},{10,14},{6,10},{2,6},{0,2},{5,1},{9,5},... | collective-permute-start | bytes 712712 | tf_op jit(solution)/shard_map/ppermute | solution.py:405
  17.7 11.0 %collective-permute-start.2 = (bf16[32,3712]{1,0:T(8,128)(2,1)S(1)}, bf16[32,3712]{1,0:T(8,128)(2,1)S(1)}, u32[]{:S(2)}, u32[]{:S(2)}) collective-permute-start(bf16[32,3712]{1,0:T(8,128)(2,1)S(1)} %collective-permute-done.1.refs_2_), channel_id=1, source_target_pairs={{0,4},{4,8},{8,12},{12,14},{14,10},{10,6},{6,2},{2,0},{1,5},{5,9},... | collective-permute-start | bytes 712712 | tf_op jit(solution)/shard_map/ppermute | solution.py:403
  19.2 8.0 %collective-permute-start.3 = (bf16[32,3584]{1,0:T(8,128)(2,1)}, bf16[32,3584]{1,0:T(8,128)(2,1)S(1)}, u32[]{:S(2)}, u32[]{:S(2)}) collective-permute-start(bf16[32,3584]{1,0:T(8,128)(2,1)} %refs_0_), channel_id=1, source_target_pairs={{4,0},{8,4},{12,8},{14,12},{10,14},{6,10},{2,6},{0,2},{5,1},{9,5},... | collective-permute-start | bytes 688136 | tf_op jit(solution)/shard_map/ppermute | solution.py:403
  19.8 8.9 %collective-permute-start.4 = (bf16[32,3584]{1,0:T(8,128)(2,1)}, bf16[32,3584]{1,0:T(8,128)(2,1)S(1)}, u32[]{:S(2)}, u32[]{:S(2)}) collective-permute-start(bf16[32,3584]{1,0:T(8,128)(2,1)} %refs_0_), channel_id=1, source_target_pairs={{0,4},{4,8},{8,12},{12,14},{14,10},{10,6},{6,2},{2,0},{1,5},{5,9},... | collective-permute-start | bytes 688136 | tf_op jit(solution)/shard_map/ppermute | solution.py:405
  21.2 12.4 %collective-permute-start.7 = (bf16[32,3712]{1,0:T(8,128)(2,1)S(1)}, bf16[32,3712]{1,0:T(8,128)(2,1)S(1)}, u32[]{:S(2)}, u32[]{:S(2)}) collective-permute-start(bf16[32,3712]{1,0:T(8,128)(2,1)S(1)} %collective-permute-done.6.refs_5_), channel_id=1, source_target_pairs={{4,0},{8,4},{12,8},{14,12},{10,14},{6,10},{2,6},{0,2},{5,1},{9,5},... | collective-permute-start | bytes 712712 | tf_op jit(solution)/shard_map/ppermute | solution.py:405
  28.7 7.6 %collective-permute-start.8 = (bf16[32,3712]{1,0:T(8,128)(2,1)S(1)}, bf16[32,3712]{1,0:T(8,128)(2,1)S(1)}, u32[]{:S(2)}, u32[]{:S(2)}) collective-permute-start(bf16[32,3712]{1,0:T(8,128)(2,1)S(1)} %collective-permute-done.2.refs_3_), channel_id=1, source_target_pairs={{0,4},{4,8},{8,12},{12,14},{14,10},{10,6},{6,2},{2,0},{1,5},{5,9},... | collective-permute-start | bytes 712712 | tf_op jit(solution)/shard_map/ppermute | solution.py:403
  30.1 8.7 %collective-permute-start.10 = (bf16[32,3584]{1,0:T(8,128)(2,1)S(1)}, bf16[32,3584]{1,0:T(8,128)(2,1)S(1)}, u32[]{:S(2)}, u32[]{:S(2)}) collective-permute-start(bf16[32,3584]{1,0:T(8,128)(2,1)S(1)} %collective-permute-done.4.refs_1_), channel_id=1, source_target_pairs={{0,4},{4,8},{8,12},{12,14},{14,10},{10,6},{6,2},{2,0},{1,5},{5,9},... | collective-permute-start | bytes 688136 | tf_op jit(solution)/shard_map/ppermute | solution.py:405
  38.7 12.0 %collective-permute-start.12 = (bf16[32,3584]{1,0:T(8,128)(2,1)S(1)}, bf16[32,3584]{1,0:T(8,128)(2,1)S(1)}, u32[]{:S(2)}, u32[]{:S(2)}) collective-permute-start(bf16[32,3584]{1,0:T(8,128)(2,1)S(1)} %collective-permute-done.9.refs_5_), channel_id=1, source_target_pairs={{4,0},{8,4},{12,8},{14,12},{10,14},{6,10},{2,6},{0,2},{5,1},{9,5},... | collective-permute-start | bytes 688136 | tf_op jit(solution)/shard_map/ppermute | solution.py:403
  39.8 10.9 %collective-permute-start.13 = (bf16[32,3584]{1,0:T(8,128)(2,1)S(1)}, bf16[32,3584]{1,0:T(8,128)(2,1)S(1)}, u32[]{:S(2)}, u32[]{:S(2)}) collective-permute-start(bf16[32,3584]{1,0:T(8,128)(2,1)S(1)} %collective-permute-done.10.refs_2_), channel_id=1, source_target_pairs={{0,4},{4,8},{8,12},{12,14},{14,10},{10,6},{6,2},{2,0},{1,5},{5,9},... | collective-permute-start | bytes 688136 | tf_op jit(solution)/shard_map/ppermute | solution.py:405
  50.7 7.5 %collective-permute-start.14 = (bf16[32,3584]{1,0:T(8,128)(2,1)S(1)}, bf16[32,3584]{1,0:T(8,128)(2,1)S(1)}, u32[]{:S(2)}, u32[]{:S(2)}) collective-permute-start(bf16[32,3584]{1,0:T(8,128)(2,1)S(1)} %collective-permute-done.12.refs_6_), channel_id=1, source_target_pairs={{4,0},{8,4},{12,8},{14,12},{10,14},{6,10},{2,6},{0,2},{5,1},{9,5},... | collective-permute-start | bytes 688136 | tf_op jit(solution)/shard_map/ppermute | solution.py:403
  61.9 8.6 %collective-permute-start.18 = (bf16[32,3584]{1,0:T(8,128)(2,1)S(1)}, bf16[32,3584]{1,0:T(8,128)(2,1)S(1)}, u32[]{:S(2)}, u32[]{:S(2)}) collective-permute-start(bf16[32,3584]{1,0:T(8,128)(2,1)S(1)} %get-tuple-element.147), channel_id=1, source_target_pairs={{0,4},{4,8},{8,12},{12,14},{14,10},{10,6},{6,2},{2,0},{1,5},{5,9},... | collective-permute-start | bytes 688136 | tf_op jit(solution)/shard_map/ppermute | solution.py:434
  63.0 7.5 %collective-permute-start.19 = (bf16[32,3584]{1,0:T(8,128)(2,1)S(1)}, bf16[32,3584]{1,0:T(8,128)(2,1)S(1)}, u32[]{:S(2)}, u32[]{:S(2)}) collective-permute-start(bf16[32,3584]{1,0:T(8,128)(2,1)S(1)} %get-tuple-element.148), channel_id=1, source_target_pairs={{4,0},{8,4},{12,8},{14,12},{10,14},{6,10},{2,6},{0,2},{5,1},{9,5},... | collective-permute-start | bytes 688136 | tf_op jit(solution)/shard_map/ppermute | solution.py:436
  70.6 8.8 %collective-permute-start.21 = (bf16[32,3584]{1,0:T(8,128)(2,1)S(1)}, bf16[32,3584]{1,0:T(8,128)(2,1)S(1)}, u32[]{:S(2)}, u32[]{:S(2)}) collective-permute-start(bf16[32,3584]{1,0:T(8,128)(2,1)S(1)} %get-tuple-element.158), channel_id=1, source_target_pairs={{0,4},{4,8},{8,12},{12,14},{14,10},{10,6},{6,2},{2,0},{1,5},{5,9},... | collective-permute-start | bytes 688136 | tf_op jit(solution)/shard_map/ppermute | solution.py:434
  79.6 8.4 %collective-permute-start.26 = (bf16[32,3584]{1,0:T(8,128)(2,1)S(1)}, bf16[32,3584]{1,0:T(8,128)(2,1)S(1)}, u32[]{:S(2)}, u32[]{:S(2)}) collective-permute-start(bf16[32,3584]{1,0:T(8,128)(2,1)S(1)} %get-tuple-element.169), channel_id=1, source_target_pairs={{0,4},{4,8},{8,12},{12,14},{14,10},{10,6},{6,2},{2,0},{1,5},{5,9},... | collective-permute-start | bytes 688136 | tf_op jit(solution)/shard_map/ppermute | solution.py:434
  80.6 8.7 %collective-permute-start.27 = (bf16[32,3584]{1,0:T(8,128)(2,1)S(1)}, bf16[32,3584]{1,0:T(8,128)(2,1)S(1)}, u32[]{:S(2)}, u32[]{:S(2)}) collective-permute-start(bf16[32,3584]{1,0:T(8,128)(2,1)S(1)} %get-tuple-element.170), channel_id=1, source_target_pairs={{4,0},{8,4},{12,8},{14,12},{10,14},{6,10},{2,6},{0,2},{5,1},{9,5},... | collective-permute-start | bytes 688136 | tf_op jit(solution)/shard_map/ppermute | solution.py:436
  82.6 11.1 %collective-permute-start.24 = (bf16[32,3584]{1,0:T(8,128)(2,1)S(1)}, bf16[32,3584]{1,0:T(8,128)(2,1)S(1)}, u32[]{:S(2)}, u32[]{:S(2)}) collective-permute-start(bf16[32,3584]{1,0:T(8,128)(2,1)S(1)} %get-tuple-element.163), channel_id=1, source_target_pairs={{4,0},{8,4},{12,8},{14,12},{10,14},{6,10},{2,6},{0,2},{5,1},{9,5},... | collective-permute-start | bytes 688136 | tf_op jit(solution)/shard_map/ppermute | solution.py:434
  83.2 10.6 %collective-permute-start.25 = (bf16[32,3584]{1,0:T(8,128)(2,1)S(1)}, bf16[32,3584]{1,0:T(8,128)(2,1)S(1)}, u32[]{:S(2)}, u32[]{:S(2)}) collective-permute-start(bf16[32,3584]{1,0:T(8,128)(2,1)S(1)} %get-tuple-element.164), channel_id=1, source_target_pairs={{0,4},{4,8},{8,12},{12,14},{14,10},{10,6},{6,2},{2,0},{1,5},{5,9},... | collective-permute-start | bytes 688136 | tf_op jit(solution)/shard_map/ppermute | solution.py:436
  93.8 11.8 %collective-permute-start.30 = (bf16[32,3584]{1,0:T(8,128)(2,1)S(1)}, bf16[32,3584]{1,0:T(8,128)(2,1)S(1)}, u32[]{:S(2)}, u32[]{:S(2)}) collective-permute-start(bf16[32,3584]{1,0:T(8,128)(2,1)S(1)} %shard_map.194), channel_id=1, source_target_pairs={{0,4},{4,8},{8,12},{12,14},{14,10},{10,6},{6,2},{2,0},{1,5},{5,9},... | collective-permute-start | bytes 688136 | tf_op jit(solution)/shard_map/ppermute | solution.py:434
  95.7 10.0 %collective-permute-start.28 = (bf16[32,3584]{1,0:T(8,128)(2,1)S(1)}, bf16[32,3584]{1,0:T(8,128)(2,1)S(1)}, u32[]{:S(2)}, u32[]{:S(2)}) collective-permute-start(bf16[32,3584]{1,0:T(8,128)(2,1)S(1)} %get-tuple-element.174), channel_id=1, source_target_pairs={{4,0},{8,4},{12,8},{14,12},{10,14},{6,10},{2,6},{0,2},{5,1},{9,5},... | collective-permute-start | bytes 688136 | tf_op jit(solution)/shard_map/ppermute | solution.py:434
  96.1 10.0 %collective-permute-start.29 = (bf16[32,3584]{1,0:T(8,128)(2,1)S(1)}, bf16[32,3584]{1,0:T(8,128)(2,1)S(1)}, u32[]{:S(2)}, u32[]{:S(2)}) collective-permute-start(bf16[32,3584]{1,0:T(8,128)(2,1)S(1)} %get-tuple-element.175), channel_id=1, source_target_pairs={{0,4},{4,8},{8,12},{12,14},{14,10},{10,6},{6,2},{2,0},{1,5},{5,9},... | collective-permute-start | bytes 688136 | tf_op jit(solution)/shard_map/ppermute | solution.py:436
  97.8 7.9 %collective-permute-start.31 = (bf16[4,16,256]{2,1,0:T(8,128)(2,1)S(1)}, bf16[4,16,256]{2,1,0:T(8,128)(2,1)S(1)}, u32[]{:S(2)}, u32[]{:S(2)}) collective-permute-start(bf16[4,16,256]{2,1,0:T(8,128)(2,1)S(1)} %pad_maximum_fusion.1), channel_id=1, source_target_pairs={{0,8},{2,10},{4,12},{6,14},{8,0},{10,2},{12,4},{14,6},{1,9},{3,11}... | collective-permute-start | bytes 98312 | tf_op jit(solution)/shard_map/ppermute | solution.py:442
  114.9 8.1 %collective-permute-start.34 = (bf16[32,3584]{1,0:T(8,128)(2,1)S(1)}, bf16[32,3584]{1,0:T(8,128)(2,1)S(1)}, u32[]{:S(2)}, u32[]{:S(2)}) collective-permute-start(bf16[32,3584]{1,0:T(8,128)(2,1)S(1)} %shard_map.197), channel_id=1, source_target_pairs={{4,0},{8,4},{12,8},{14,12},{10,14},{6,10},{2,6},{0,2},{5,1},{9,5},... | collective-permute-start | bytes 688136 | tf_op jit(solution)/shard_map/ppermute | solution.py:434
  (20 other events, 165.3 us)

commit v5 on v4

--- a/solution.py
+++ b/solution.py
@@ -118,7 +118,7 @@
 
 
 def token_slots_kernel(experts, info_ref, *refs):
-    blocks, (kept_ref, sent_ref, select_ref, high_ref, low_ref, all_ref) = refs[:-6], refs[-6:]
+    blocks, (kept_ref, sent_ref, select_ref, high_ref, low_ref, all_ref) = refs[2:-6], refs[-6:]
     rows, load = blocks[0].shape
     toks, slots = all_ref.shape[0], select_ref.shape[0]
     half, width = slots // 2, load - LANES
@@ -163,13 +163,11 @@
 
 
 def inner_kernel(
-    count, tiles, info_ref, kept_ref, came_ref, gate_ref, up_a_ref, up_b_ref, up_hbm,
-    inner_ref, slope_ref, active_ref, low_up_ref, keep_ref, rows_ref, up_ref, sems,
+    count, tiles, info_ref, kept_ref, came_ref, gate_ref, up_a_ref, up_b_ref, up_ref,
+    inner_ref, slope_ref, active_ref, low_up_ref, keep_ref, rows_ref,
 ):
     half, width = kept_ref.shape[0], rows_ref.shape[1]
     slots, tile = 2 * half, gate_ref.shape[1] // tiles
-    copy = pltpu.make_async_copy(up_hbm, up_ref, sems.at[0])
-    copy.start()
     rows_ref[:half] = kept_ref[:, :width]
     rows_ref[half:] = came_ref[:, :width]
     low_up_ref[...] = mm_nt(rows_ref[...], up_a_ref[...]).astype(bf16)
@@ -192,17 +190,14 @@
     for j in range(tiles):
         cols = slice(j * tile, (j + 1) * tile)
         pre_gate = mm(rows_ref[...], gate_ref[:, cols])
-        logistic = jax.nn.sigmoid(pre_gate)
-        active_ref[:, cols] = pre_gate * logistic
-        slope_ref[:, cols] = logistic * (1.0 + pre_gate * (1.0 - logistic))
-    copy.wait()
-    for j in range(tiles):
-        cols = slice(j * tile, (j + 1) * tile)
         pre_up = mm(rows_ref[...], up_ref[:, cols]) + adapter_scale * mm(
             low_up_ref[...], up_b_ref[:, cols]
         )
-        slope_ref[:, cols] = slope_ref[:, cols] * pre_up
-        inner_ref[:, cols] = (active_ref[:, cols] * pre_up).astype(bf16)
+        logistic = jax.nn.sigmoid(pre_gate)
+        active = pre_gate * logistic
+        active_ref[:, cols] = active
+        slope_ref[:, cols] = pre_up * (logistic * (1.0 + pre_gate * (1.0 - logistic)))
+        inner_ref[:, cols] = (active * pre_up).astype(bf16)
 
 
 def routed_kernel(
@@ -326,10 +321,14 @@
     down_a_ref[...] = scaled(mm_tn(back_low_ref[...], inner_ref[...]))
 
 
-def hop_kernel(*refs):
-    for i in range(len(refs) // 3):
-        own, came, out = refs[2 * i], refs[2 * i + 1], refs[2 * len(refs) // 3 + i]
-        out[...] = (own[...].astype(f32) + came[...].astype(f32)).astype(bf16)
+def hop_kernel(front_ref, forth_ref, rear_ref, hither_ref, front_out_ref, rear_out_ref):
+    rows, came = front_ref.shape[0], forth_ref.shape[0]
+    plus = lambda a, b: (a[...].astype(f32) + b[...].astype(f32)).astype(bf16)
+    if came < rows:
+        front_out_ref[came:] = front_ref[came:]
+        rear_out_ref[: rows - came] = rear_ref[: rows - came]
+    front_out_ref[:came] = plus(front_ref.at[:came], forth_ref)
+    rear_out_ref[rows - came :] = plus(rear_ref.at[rows - came :], hither_ref)
 
 
 def mixed_kernel(own_ref, forth_ref, hither_ref, out_ref):
@@ -408,33 +407,19 @@
         behind, front = (far, near) if self.far_ahead else (near, far)
         return behind[: self.half] + front[1 : self.half] + [far[self.half]]
 
-    def scatter_starts(self, parts):
-        half = self.half
-        to_front = [parts[half - 1 + k] for k in range(half - 1, 0, -1)]
-        to_rear = [parts[k] for k in range(half - 1, 0, -1)]
-        far, near = (to_front, to_rear) if self.far_ahead else (to_rear, to_front)
-        return [parts[-1]] + far, near
-
-    def scatter_hop(self, outs, came, step):
-        (far_out, near_out), (far, near) = outs, came
-        if step == 0:
-            far_part, near_part = far_out[0], near_out[0]
-        else:
-            operands = [far_out[step], far]
-            if step < self.half - 1:
-                operands += [near_out[step], near]
-            added = call(
-                hop_kernel,
-                [struct(far.shape)] * (len(operands) // 2),
-                [in_vmem] * len(operands),
-                operands,
-                (0, 3 * nbytes(operands) // 2),
-            )
-            far_part, near_part = added[0], added[-1]
-        far = lax.ppermute(far_part, "expert", self.far)
-        if step < self.half - 1:
-            near = lax.ppermute(near_part, "expert", self.near)
-        return far, near
+
+def scatter_hop(parts, count, came, step):
+    _, ahead, back = ring_of(count)
+    half = count // 2
+    if step == 0:
+        front, rear = parts[-2], parts[-1]
+    else:
+        front, rear = parts[count - 1 - step], parts[half - step]
+        front, rear = call(
+            hop_kernel, [struct(front.shape)] * 2, [in_vmem] * 4,
+            (front, came[0], rear, came[1]), (0, 3 * nbytes([front, rear])),
+        )
+    return lax.ppermute(front, "expert", ahead), lax.ppermute(rear, "expert", back)
 
 
 def double(gathered, step):
@@ -491,8 +476,20 @@
         choice = expert_choice_index.T
         ring_token, ring_cot = Ring(count, True), Ring(count, False)
         hops = count // 2
+        rows_of = [tok_count] * (count - 1) + [tok_count // 2] * 2
 
         stay = lambda *arrays: [pltpu.with_memory_space_constraint(a, pltpu.HBM) for a in arrays]
+
+        def fetch(*arrays):
+            return call(
+                functools.partial(fetch_kernel, len(arrays)),
+                [pltpu.VMEM(a.shape, bf16) for a in arrays],
+                [in_hbm] * len(arrays),
+                stay(*arrays),
+                (0, nbytes(arrays)),
+                scratch=[pltpu.SemaphoreType.DMA((len(arrays),))],
+                mib=1,
+            )
 
         (token_load,) = call(
             token_load_kernel, [struct((tok_count, load))], [in_hbm] * 3,
@@ -505,37 +502,31 @@
 
         tok_far, tok_near = [token_load], [token_load]
         ring_token.gather_hop(tok_far, tok_near)
-        cot_load, tok_far[1] = tie(cotangent, tok_far[1])
-        cot_far, cot_near = [cot_load], [cot_load]
+        cot_far, cot_near = [cotangent], [cotangent]
         ring_token.gather_hop(tok_far, tok_near)
+        tok_near[-1], gate_late = tie(tok_near[-1], gate_w)
         ring_cot.gather_hop(cot_far, cot_near)
+        gate_v, up_a_v, up_b_v = fetch(gate_late, up_a, up_b)
         for hop in range(2, hops):
+            if hop == hops - 1:
+                tok_far[-1], up_b_v = tie(tok_far[-1], up_b_v)
+            tok_far[-1], cot_far[-1], cot_near[-1] = tie(tok_far[-1], cot_far[-1], cot_near[-1])
             ring_token.gather_hop(tok_far, tok_near)
+            ring_cot.gather_hop(cot_far, cot_near)
             if hop == hops - 2:
-                tok_far[-1], cot_far[1], cot_near[1] = tie(tok_far[-1], cot_far[1], cot_near[1])
-            if hop < hops - 1:
-                ring_cot.gather_hop(cot_far, cot_near)
+                tok_near[-1], up_late = tie(tok_near[-1], up_w)
+        (up_v,) = fetch(up_late)
         token_blocks = ring_token.gathered(tok_far, tok_near)
 
         kept, sent, select, high, low, token_all = call(
             functools.partial(token_slots_kernel, experts),
             [struct((half, load))] * 2 + [struct((slots, toks))] * 3 + [struct((toks, load))],
-            [in_smem] + [in_vmem] * count,
-            (info, *token_blocks),
+            [in_smem] + [in_vmem] * (count + 2),
+            (info, gate_v, up_v, *token_blocks),
             (2 * slots * toks * load, 2 * count * nbytes([token_load])),
         )
         sent, cot_far[-1], cot_near[-1] = tie(sent, cot_far[-1], cot_near[-1])
         came = swap_cores(sent)
-        kept, gate_late = tie(kept, gate_w)
-        gate_v, up_a_v, up_b_v = call(
-            functools.partial(fetch_kernel, 3),
-            [pltpu.VMEM(a.shape, bf16) for a in (gate_w, up_a, up_b)],
-            [in_hbm] * 3,
-            stay(gate_late, up_a, up_b),
-            (0, nbytes([gate_w])),
-            scratch=[pltpu.SemaphoreType.DMA((3,))],
-            mib=1,
-        )
         ring_cot.gather_hop(cot_far, cot_near)
         inner, slope, active, low_up, keep = call(
             functools.partial(inner_kernel, count, tiles),
@@ -543,18 +534,11 @@
                 struct((slots, hidden)), struct((slots, hidden), f32), struct((slots, hidden), f32),
                 struct((slots, rank)), struct((slots, LANES), f32),
             ],
-            [in_smem] + [in_vmem] * 5 + [in_hbm],
-            (info, kept, came, gate_v, up_a_v, up_b_v, *stay(up_w)),
+            [in_smem] + [in_vmem] * 6,
+            (info, kept, came, gate_v, up_a_v, up_b_v, up_v),
             (4 * slots * width * hidden, 2 * nbytes([gate_w])),
-            scratch=[
-                pltpu.VMEM((slots, width), bf16), pltpu.VMEM(up_w.shape, bf16),
-                pltpu.SemaphoreType.DMA((1,)),
-            ],
-            mib=16,
-        )
-        inner, cot_far[-1], cot_near[-1] = tie(inner, cot_far[-1], cot_near[-1])
-        while len(cot_far) <= hops:
-            ring_cot.gather_hop(cot_far, cot_near)
+            scratch=[pltpu.VMEM((slots, width), bf16)],
+        )
         routed_kept, routed_sent, low_down = call(
             functools.partial(routed_kernel, tiles),
             [struct((half, width))] * 2 + [struct((slots, rank))],
@@ -562,22 +546,9 @@
             (inner, keep, down_w, down_a, down_b),
             (2 * slots * width * hidden, nbytes([gate_w])),
         )
-        routed_sent, cot_far[-1] = tie(routed_sent, cot_far[-1])
+        routed_sent, high = tie(routed_sent, high)
         routed_came = swap_cores(routed_sent)
-
-        mix_parts = call(
-            mix_parts_kernel,
-            [struct((tok_count, width))] * count,
-            [in_vmem] * 4,
-            (high, low, routed_kept, routed_came),
-            (4 * slots * toks * load, 3 * count * nbytes([token_load])),
-            scratch=[pltpu.VMEM((slots, width), bf16)],
-        )
         cot_blocks = ring_cot.gathered(cot_far, cot_near)
-        mix_parts = list(mix_parts)
-        mix_outs = ring_token.scatter_starts(mix_parts)
-        mix_came = [ring_token.scatter_hop(mix_outs, (None, None), 0)]
-
         cot_kept, cot_sent, cot_all = call(
             cot_slots_kernel,
             [struct((half, width))] * 2 + [struct((toks, width))],
@@ -586,6 +557,50 @@
             (4 * slots * toks * load, 2 * count * nbytes([token_load])),
         )
         cot_came = swap_cores(cot_sent)
+        routed_came, cot_kept = tie(routed_came, cot_kept)
+
+        mix_parts = call(
+            mix_parts_kernel,
+            [struct((rows, width)) for rows in rows_of],
+            [in_vmem] * 4,
+            (high, low, routed_kept, routed_came),
+            (4 * slots * toks * load, 3 * count * nbytes([token_load])),
+            scratch=[pltpu.VMEM((slots, width), bf16)],
+        )
+        mix_parts = list(mix_parts)
+        cot_came, mix_parts[-1] = tie(cot_came, mix_parts[-1])
+        mix_came = [scatter_hop(mix_parts, count, None, 0)]
+
+        grad_routed, grad_gate, grad_up, back_low, back_up = call(
+            functools.partial(inner_grad_kernel, tiles),
+            [struct((slots, width))] + [struct((slots, hidden))] * 2 + [struct((slots, rank))] * 2,
+            [in_vmem] * 9,
+            (cot_kept, cot_came, keep, down_w, down_b, down_a, slope, active, up_b_v),
+            (2 * slots * width * hidden, nbytes([gate_w])),
+        )
+        grad_up, *mix_came[0] = tie(grad_up, *mix_came[0])
+        mix_came.append(scatter_hop(mix_parts, count, mix_came[0], 1))
+        back_kept, back_sent = call(
+            functools.partial(row_grad_kernel, tiles),
+            [struct((half, width))] * 2,
+            [in_vmem] * 6,
+            (grad_gate, grad_up, back_up, gate_v, up_v, up_a_v),
+            (4 * slots * width * hidden, 2 * nbytes([gate_w])),
+        )
+        back_sent, *mix_came[1] = tie(back_sent, *mix_came[1])
+        back_came = swap_cores(back_sent)
+        mix_came.append(scatter_hop(mix_parts, count, mix_came[1], 2))
+        back_parts = call(
+            back_parts_kernel,
+            [struct((rows, width)) for rows in rows_of],
+            [in_vmem] * 3,
+            (select, back_kept, back_came),
+            (2 * slots * toks * load, 2 * count * nbytes([token_load])),
+            scratch=[pltpu.VMEM((slots, width), bf16)],
+        )
+        back_parts = list(back_parts)
+        routed_came, *mix_came[2] = tie(routed_came, *mix_came[2])
+        back_came = [scatter_hop(back_parts, count, None, 0)]
         (dots,) = call(
             functools.partial(gate_grad_kernel, count),
             [struct((1, 2 * 8, toks))],
@@ -594,51 +609,24 @@
             (2 * slots * toks * load, 2 * count * nbytes([token_load])),
             scratch=[pltpu.VMEM((slots, width), bf16)],
         )
-        cot_came, dots = tie(cot_came, dots)
-        grad_routed, grad_gate, grad_up, back_low, back_up = call(
-            functools.partial(inner_grad_kernel, tiles),
-            [struct((slots, width))] + [struct((slots, hidden))] * 2 + [struct((slots, rank))] * 2,
-            [in_vmem] * 9,
-            (cot_kept, cot_came, keep, down_w, down_b, down_a, slope, active, up_b_v),
-            (2 * slots * width * hidden, nbytes([gate_w])),
-        )
-        dots = double(dots, 1)
-        grad_up, dots, *mix_came[0] = tie(grad_up, dots, *mix_came[0])
-        mix_came.append(ring_token.scatter_hop(mix_outs, mix_came[-1], 1))
-        back_kept, back_sent = call(
-            functools.partial(row_grad_kernel, tiles),
-            [struct((half, width))] * 2,
-            [in_vmem] * 6,
-            (grad_gate, grad_up, back_up, gate_v, up_w, up_a_v),
-            (4 * slots * width * hidden, 2 * nbytes([gate_w])),
-        )
-        dots = double(dots, 2)
-        back_sent, dots, *mix_came[1] = tie(back_sent, dots, *mix_came[1])
-        back_came = swap_cores(back_sent)
-        back_parts = call(
-            back_parts_kernel,
-            [struct((tok_count, width))] * count,
-            [in_vmem] * 3,
-            (select, back_kept, back_came),
-            (2 * slots * toks * load, 2 * count * nbytes([token_load])),
-            scratch=[pltpu.VMEM((slots, width), bf16)],
-        )
-        back_parts = list(back_parts)
-        back_outs = ring_cot.scatter_starts(back_parts)
-        back_came = [ring_cot.scatter_hop(back_outs, (None, None), 0)]
-        step = 4
+        step = 1
+        back_up_late = back_up
+        for hop in range(1, hops):
+            if hop + 2 < hops:
+                mix_came.append(scatter_hop(mix_parts, count, mix_came[-1], hop + 2))
+            if hop == hops - 1:
+                tied = tie(*back_came[-1], back_up_late, dots, *mix_came[-1])
+                mix_came[-1] = tied[4:]
+            else:
+                tied = tie(*back_came[-1], back_up_late, dots)
+            back_came[-1], back_up_late, dots = tied[:2], tied[2], tied[3]
+            back_came.append(scatter_hop(back_parts, count, back_came[-1], hop))
+            if step < count:
+                dots = double(dots, step)
+                step *= 2
         while step < count:
             dots = double(dots, step)
             step *= 2
-        back_up_late = back_up
-        for hop in range(1, hops):
-            if hop + 1 < hops:
-                mix_came.append(ring_token.scatter_hop(mix_outs, mix_came[-1], hop + 1))
-            tied = tie(*back_came[-1], *mix_came[-1], back_up_late)
-            back_came[-1], mix_came[-1], back_up_late = tied[:2], tied[2:4], tied[4]
-            if hop > 1:
-                back_came[-1], dots = tie(back_came[-1], dots)
-            back_came.append(ring_cot.scatter_hop(back_outs, back_came[-1], hop))
         adapters = call(
             adapter_kernel,
             [

time: 124 us -> 118 us (0.952)
  waiting for transfers between devices: 50.5 us -> 37.9 us
  local copies, waits for them, and re-layouts: 0.16 us -> 4.95 us
  Pallas kernels: 34.9 us -> 38.3 us
    ppermute x14 -> x16, waiting for transfers between devices: 18.1 us -> 8.14 us  [the longest x8 4.66 us: scatter_hop(): lax.ppermute(rear, 'expert', back)]
    ppermute x8, waiting for transfers between devices: 21.8 us -> 12.2 us  [gather_hop(): far.append(lax.ppermute(far[-1], 'expert', self.far))]
    ppermute x3, waiting for transfers between devices: 7.51 us -> 12.3 us  [double(): lax.ppermute(gathered, 'expert', [(i, i ^ step) for i in range(size)])]
    unnamed x16 -> x18, local copies, waits for them, and re-layouts: 0.04 us -> 4.83 us
    pallas_call x21 -> x22, Pallas kernels: 34.9 us -> 38.3 us  [call(): pl.pallas_call(body, out_shape=outs, in_specs=specs, out_specs=out_specs...]
    ppermute x5, waiting for transfers between devices: 1.03 us -> 3.03 us  [swap_cores(): return lax.ppermute(value, 'dp', [(0, 1), (1, 0)])]
    ppermute x3, starting transfers between devices: 3 us -> 1.54 us  [double(): lax.ppermute(gathered, 'expert', [(i, i ^ step) for i in range(size)])]
    ppermute x14 -> x16, starting transfers between devices: 15.7 us -> 16.6 us  [the longest x8 9.86 us: scatter_hop(): lax.ppermute(front, 'expert', ahead)]
  transfers between devices with their start and end apart: 36 -> 38, of which waited for: 17 -> 16; matrix products, arithmetic and copies ran while one was open for 1% -> 0% of each run, Pallas kernels for 25% -> 31%
where the time goes in v5:
time: 118 us
  Pallas kernels  38.3 us (32%)
  waiting for transfers between devices  37.9 us (32%)
  starting transfers between devices  34.2 us (29%)
  local copies, waits for them, and re-layouts  4.95 us (4%)
  between operations  1.6 us (1%)
    pallas_call x22, Pallas kernels, call(): pl.pallas_call(body, out_shape=outs, in_specs=specs, out_specs=out_specs...  38.3 us
    ppermute x3, waiting for transfers between devices, double(): lax.ppermute(gathered, 'expert', [(i, i ^ step) for i in range(size)])  12.3 us
    ppermute x8, waiting for transfers between devices, gather_hop(): far.append(lax.ppermute(far[-1], 'expert', self.far))  12.2 us
    ppermute x8, starting transfers between devices, scatter_hop(): lax.ppermute(front, 'expert', ahead)  9.86 us
    ppermute x8, starting transfers between devices, gather_hop(): far.append(lax.ppermute(far[-1], 'expert', self.far))  9.83 us
    ppermute x8, starting transfers between devices, scatter_hop(): lax.ppermute(rear, 'expert', back)  6.73 us
    ppermute x6, starting transfers between devices, gather_hop(): near.append(lax.ppermute(near[-1], 'expert', self.near))  5.44 us
    unnamed x18, local copies, waits for them, and re-layouts  4.83 us
  transfers between devices with their start and end apart: 38, of which 16 were waited for; matrix products, arithmetic and copies ran while one was open for 0% of the time, Pallas kernels for 31%

profile of v5, /device:TPU:0, one launch (start us, length us, event | category | flops | bytes accessed | tf_op | source)
XLA Modules:
  0.0 117.8 jit_solution(2172406546058387131)
XLA Ops:
  2.0 3.1 %collective-permute-start.3 = (bf16[32,3712]{1,0:T(8,128)(2,1)S(1)}, bf16[32,3712]{1,0:T(8,128)(2,1)S(1)}, u32[]{:S(2)}, u32[]{:S(2)}) collective-permute-start(bf16[32,3712]{1,0:T(8,128)(2,1)S(1)} %shard_map.180.refs_2_), channel_id=1, source_target_pairs={{0,4},{4,8},{8,12},{12,14},{14,10},{10,6},{6,2},{2,0},{1,5},{5,9},... | collective-permute-start | bytes 712712 | tf_op jit(solution)/shard_map/ppermute | solution.py:402
  5.1 5.7 %collective-permute-done.3.refs_3_ = bf16[32,3712]{1,0:T(8,128)(2,1)S(1)} collective-permute-done((bf16[32,3712]{1,0:T(8,128)(2,1)S(1)}, bf16[32,3712]{1,0:T(8,128)(2,1)S(1)}, u32[]{:S(2)}, u32[]{:S(2)}) %collective-permute-start.3) | collective-permute-done | bytes 237600 | tf_op jit(solution)/shard_map/ppermute | solution.py:402
  10.8 1.8 %collective-permute-start.4 = (bf16[32,3712]{1,0:T(8,128)(2,1)S(1)}, bf16[32,3712]{1,0:T(8,128)(2,1)S(1)}, u32[]{:S(2)}, u32[]{:S(2)}) collective-permute-start(bf16[32,3712]{1,0:T(8,128)(2,1)S(1)} %collective-permute-done.3.refs_3_), channel_id=1, source_target_pairs={{0,4},{4,8},{8,12},{12,14},{14,10},{10,6},{6,2},{2,0},{1,5},{5,9},... | collective-permute-start | bytes 712712 | tf_op jit(solution)/shard_map/ppermute | solution.py:402
  12.8 1.8 %collective-permute-start.6 = (bf16[32,3584]{1,0:T(8,128)(2,1)}, bf16[32,3584]{1,0:T(8,128)(2,1)S(1)}, u32[]{:S(2)}, u32[]{:S(2)}) collective-permute-start(bf16[32,3584]{1,0:T(8,128)(2,1)} %refs_0_.1), channel_id=1, source_target_pairs={{0,4},{4,8},{8,12},{12,14},{14,10},{10,6},{6,2},{2,0},{1,5},{5,9},... | collective-permute-start | bytes 688136 | tf_op jit(solution)/shard_map/ppermute | solution.py:404
  14.8 6.5 %collective-permute-done.5.refs_4_ = bf16[32,3584]{1,0:T(8,128)(2,1)S(1)} collective-permute-done((bf16[32,3584]{1,0:T(8,128)(2,1)}, bf16[32,3584]{1,0:T(8,128)(2,1)S(1)}, u32[]{:S(2)}, u32[]{:S(2)}) %collective-permute-start.5) | collective-permute-done | bytes 229408 | tf_op jit(solution)/shard_map/ppermute | solution.py:402
  26.7 3.1 %shard_map.181 = (bf16[3584,1024]{1,0:T(8,128)(2,1)S(1)}, bf16[64,3584]{1,0:T(8,128)(2,1)S(1)}, bf16[64,1024]{1,0:T(8,128)(2,1)S(1)}) custom-call(bf16[3584,1024]{1,0:T(8,128)(2,1)} %bitcast.37, bf16[64,3584]{1,0:T(8,128)(2,1)} %bitcast.38, bf16[64,1024]{1,0:T(8,128)(2,1)} %bitcast.39), custom_call_target="tpu_custom_call" | custom-call | bytes 7 | tf_op jit(solution)/shard_map/pallas_call | solution.py:40
  29.9 2.9 %copy-done = bf16[3584,1024]{1,0:T(8,128)(2,1)} copy-done((bf16[3584,1024]{1,0:T(8,128)(2,1)}, bf16[3584,1024]{1,0:T(8,128)(2,1)S(1)}, u32[]{:S(2)}) %copy-start) | copy-done | bytes 7340056
  37.9 3.2 %shard_map.182.refs_1_.up_ref = bf16[3584,1024]{1,0:T(8,128)(2,1)S(1)} custom-call(bf16[3584,1024]{1,0:T(8,128)(2,1)} %bitcast.36), custom_call_target="tpu_custom_call" | custom-call | bytes 7 | tf_op jit(solution)/shard_map/pallas_call | solution.py:40
  41.2 1.9 %copy-done.1 = bf16[3584,1024]{1,0:T(8,128)(2,1)S(1)} copy-done((bf16[3584,1024]{1,0:T(8,128)(2,1)S(1)}, bf16[3584,1024]{1,0:T(8,128)(2,1)}, u32[]{:S(2)}) %copy-start.1) | copy-done | bytes 7340056
  43.1 1.8 %shard_map.183 = (bf16[128,3712]{1,0:T(8,128)(2,1)S(1)}, bf16[128,3712]{1,0:T(8,128)(2,1)S(1)}, bf16[256,256]{1,0:T(8,128)(2,1)S(1)}, bf16[256,256]{1,0:T(8,128)...) custom-call(s32[12]{0:T(128)S(1)} %concatenate.12.info_ref, bf16[3584,1024]{1,0:T(8,128)(2,1)S(1)} %copy-done.1, ...), custom_call_target="tpu_custom_call" | custom-call | flops 486 | bytes 3 | tf_op jit(solution)/shard_map/pallas_call | solution.py:40
  45.7 1.8 %collective-permute-done.13.came_ref = bf16[128,3712]{1,0:T(8,128)(2,1)S(1)} collective-permute-done((bf16[128,3712]{1,0:T(8,128)(2,1)S(1)}, bf16[128,3712]{1,0:T(8,128)(2,1)S(1)}, u32[]{:S(2)}, u32[]{:S(2)}) %collective-permute-start.13) | collective-permute-done | bytes 950304 | tf_op jit(solution)/shard_map/ppermute | solution.py:432
  47.5 5.5 %shard_map.184 = (bf16[256,1024]{1,0:T(8,128)(2,1)S(1)}, f32[256,1024]{1,0:T(8,128)S(1)}, f32[256,1024]{1,0:T(8,128)S(1)}, bf16[256,64]{1,0:T(8,128)(2,1)S(1)}, f32[256,128]{1,0:T(8,128)S(1)}) custom-call(s32[12]{0:T(128)S(1)} %concatenate.12.info_ref, bf16[128,3712]{1,0:T(8,128)(2,1)S(1)} %get-tuple-element.125.kept_ref, ...), custom_call_target="tpu_custom_call" | custom-call | flops 3758 | bytes 14 | tf_op jit(solution)/shard_map/pallas_call | solution.py:40
  53.1 3.4 %shard_map.185 = (bf16[128,3584]{1,0:T(8,128)(2,1)S(1)}, bf16[128,3584]{1,0:T(8,128)(2,1)S(1)}, bf16[256,64]{1,0:T(8,128)(2,1)S(1)}) custom-call(bf16[256,1024]{1,0:T(8,128)(2,1)S(1)} %get-tuple-element.132.inner_ref, f32[256,128]{1,0:T(8,128)S(1)} %get-tuple-element.133.keep_ref, bf16[1024,3584]{1,0:T(8,128)(2,1)S(1)} %bitcast.28, ...), custom_call_target="tpu_custom_call" | custom-call | flops 1879 | bytes 7 | tf_op jit(solution)/shard_map/pallas_call | solution.py:40
  56.7 2.2 %shard_map.186 = (bf16[128,3584]{1,0:T(8,128)(2,1)S(1)}, bf16[128,3584]{1,0:T(8,128)(2,1)S(1)}, bf16[256,3584]{1,0:T(8,128)(2,1)S(1)}) custom-call(bf16[256,256]{1,0:T(8,128)(2,1)S(1)} %get-tuple-element.136.high_ref, bf16[256,256]{1,0:T(8,128)(2,1)S(1)} %get-tuple-element.137.low_ref, bf16[32,3584]{1,0:T(8,128)(2,1)S(1)} %copy-done.5, ...), custom_call_target="tpu_custom_call" | custom-call | flops 973 | bytes 3 | tf_op jit(solution)/shard_map/pallas_call | solution.py:40
  63.5 4.2 %shard_map.188 = (bf16[256,3584]{1,0:T(8,128)(2,1)S(1)}, bf16[256,1024]{1,0:T(8,128)(2,1)S(1)}, bf16[256,1024]{1,0:T(8,128)(2,1)S(1)}, bf16[256,64]{1,0:T(8,128)(2,1)S(1)}, bf16[256,64]{1,0:T(8,128)(2,1)S(1)}) custom-call(bf16[128,3584]{1,0:T(8,128)(2,1)S(1)} %get-tuple-element.146.kept_ref, bf16[128,3584]{1,0:T(8,128)(2,1)S(1)} %collective-permute-done.16.came_ref, ...), custom_call_target="tpu_custom_call" | custom-call | flops 1879 | bytes 7 | tf_op jit(solution)/shard_map/pallas_call | solution.py:40
  69.9 5.1 %shard_map.189 = (bf16[128,3584]{1,0:T(8,128)(2,1)S(1)}, bf16[128,3584]{1,0:T(8,128)(2,1)S(1)}) custom-call(bf16[256,1024]{1,0:T(8,128)(2,1)S(1)} %get-tuple-element.152.grad_gate_ref, bf16[256,1024]{1,0:T(8,128)(2,1)S(1)} %get-tuple-element.156.grad_up_ref, bf16[256,64]{1,0:T(8,128)(2,1)S(1)} %get-tuple-element.212.back_up_ref, ...), custom_call_target="tpu_custom_call" | custom-call | flops 3758 | bytes 14 | tf_op jit(solution)/shard_map/pallas_call | solution.py:40
  76.6 1.6 %collective-permute-start.24 = (bf16[32,3584]{1,0:T(8,128)(2,1)S(1)}, bf16[32,3584]{1,0:T(8,128)(2,1)S(1)}, u32[]{:S(2)}, u32[]{:S(2)}) collective-permute-start(bf16[32,3584]{1,0:T(8,128)(2,1)S(1)} %get-tuple-element.175), channel_id=1, source_target_pairs={{0,4},{4,8},{8,12},{12,14},{14,10},{10,6},{6,2},{2,0},{1,5},{5,9},... | collective-permute-start | bytes 688136 | tf_op jit(solution)/shard_map/ppermute | solution.py:422
  79.6 1.6 %collective-permute-start.22 = (bf16[16,3584]{1,0:T(8,128)(2,1)S(1)}, bf16[16,3584]{1,0:T(8,128)(2,1)S(1)}, u32[]{:S(2)}, u32[]{:S(2)}) collective-permute-start(bf16[16,3584]{1,0:T(8,128)(2,1)S(1)} %get-tuple-element.169), channel_id=1, source_target_pairs={{0,4},{4,8},{8,12},{12,14},{14,10},{10,6},{6,2},{2,0},{1,5},{5,9},... | collective-permute-start | bytes 344072 | tf_op jit(solution)/shard_map/ppermute | solution.py:422
  81.7 3.3 %collective-permute-done.24.forth_ref = bf16[32,3584]{1,0:T(8,128)(2,1)S(1)} collective-permute-done((bf16[32,3584]{1,0:T(8,128)(2,1)S(1)}, bf16[32,3584]{1,0:T(8,128)(2,1)S(1)}, u32[]{:S(2)}, u32[]{:S(2)}) %collective-permute-start.24) | collective-permute-done | bytes 229408 | tf_op jit(solution)/shard_map/ppermute | solution.py:422
  93.2 4.0 %collective-permute-done.28 = bf16[1,16,256]{2,1,0:T(8,128)(2,1)S(1)} collective-permute-done((bf16[1,16,256]{2,1,0:T(8,128)(2,1)S(1)}, bf16[1,16,256]{2,1,0:T(8,128)(2,1)S(1)}, u32[]{:S(2)}, u32[]{:S(2)}) %collective-permute-start.28) | collective-permute-done | bytes 8224 | tf_op jit(solution)/shard_map/ppermute | solution.py:427
  101.2 5.6 %collective-permute-done.31 = bf16[2,16,256]{2,1,0:T(8,128)(2,1)S(1)} collective-permute-done((bf16[2,16,256]{2,1,0:T(8,128)(2,1)S(1)}, bf16[2,16,256]{2,1,0:T(8,128)(2,1)S(1)}, u32[]{:S(2)}, u32[]{:S(2)}) %collective-permute-start.31) | collective-permute-done | bytes 16416 | tf_op jit(solution)/shard_map/ppermute | solution.py:427
  108.0 1.7 %collective-permute-start.35 = (bf16[32,3584]{1,0:T(8,128)(2,1)S(1)}, bf16[32,3584]{1,0:T(8,128)(2,1)S(1)}, u32[]{:S(2)}, u32[]{:S(2)}) collective-permute-start(bf16[32,3584]{1,0:T(8,128)(2,1)S(1)} %get-tuple-element.207), channel_id=1, source_target_pairs={{4,0},{8,4},{12,8},{14,12},{10,14},{6,10},{2,6},{0,2},{5,1},{9,5},... | collective-permute-start | bytes 688136 | tf_op jit(solution)/shard_map/ppermute | solution.py:422
  109.7 2.6 %collective-permute-done.36 = bf16[4,16,256]{2,1,0:T(8,128)(2,1)S(1)} collective-permute-done((bf16[4,16,256]{2,1,0:T(8,128)(2,1)S(1)}, bf16[4,16,256]{2,1,0:T(8,128)(2,1)S(1)}, u32[]{:S(2)}, u32[]{:S(2)}) %collective-permute-start.36) | collective-permute-done | bytes 32800 | tf_op jit(solution)/shard_map/ppermute | solution.py:427
  113.6 1.8 %shard_map.201 = (bf16[64,3584]{1,0:T(8,128)(2,1)}, bf16[64,1024]{1,0:T(8,128)(2,1)}, bf16[64,1024]{1,0:T(8,128)(2,1)}, bf16[64,3584]{1,0:T(8,128)(2,1)}) custom-call(bf16[128,3712]{1,0:T(8,128)(2,1)S(1)} %get-tuple-element.125.kept_ref, bf16[128,3712]{1,0:T(8,128)(2,1)S(1)} %collective-permute-done.13.came_ref, ...), custom_call_target="tpu_custom_call" | custom-call | flops 469 | bytes 7 | tf_op jit(solution)/shard_map/pallas_call | solution.py:40
  (100 shorter events, 39.7 us)
Async XLA Ops:
  2.0 8.8 %collective-permute-start.3 = (bf16[32,3712]{1,0:T(8,128)(2,1)S(1)}, bf16[32,3712]{1,0:T(8,128)(2,1)S(1)}, u32[]{:S(2)}, u32[]{:S(2)}) collective-permute-start(bf16[32,3712]{1,0:T(8,128)(2,1)S(1)} %shard_map.180.refs_2_), channel_id=1, source_target_pairs={{0,4},{4,8},{8,12},{12,14},{14,10},{10,6},{6,2},{2,0},{1,5},{5,9},... | collective-permute-start | bytes 712712 | tf_op jit(solution)/shard_map/ppermute | solution.py:402
  5.1 9.5 %collective-permute-start = (bf16[32,3712]{1,0:T(8,128)(2,1)S(1)}, bf16[32,3712]{1,0:T(8,128)(2,1)S(1)}, u32[]{:S(2)}, u32[]{:S(2)}) collective-permute-start(bf16[32,3712]{1,0:T(8,128)(2,1)S(1)} %shard_map.180.refs_2_), channel_id=1, source_target_pairs={{4,0},{8,4},{12,8},{14,12},{10,14},{6,10},{2,6},{0,2},{5,1},{9,5},... | collective-permute-start | bytes 712712 | tf_op jit(solution)/shard_map/ppermute | solution.py:404
  10.8 11.9 %collective-permute-start.4 = (bf16[32,3712]{1,0:T(8,128)(2,1)S(1)}, bf16[32,3712]{1,0:T(8,128)(2,1)S(1)}, u32[]{:S(2)}, u32[]{:S(2)}) collective-permute-start(bf16[32,3712]{1,0:T(8,128)(2,1)S(1)} %collective-permute-done.3.refs_3_), channel_id=1, source_target_pairs={{0,4},{4,8},{8,12},{12,14},{14,10},{10,6},{6,2},{2,0},{1,5},{5,9},... | collective-permute-start | bytes 712712 | tf_op jit(solution)/shard_map/ppermute | solution.py:402
  12.6 8.8 %collective-permute-start.5 = (bf16[32,3584]{1,0:T(8,128)(2,1)}, bf16[32,3584]{1,0:T(8,128)(2,1)S(1)}, u32[]{:S(2)}, u32[]{:S(2)}) collective-permute-start(bf16[32,3584]{1,0:T(8,128)(2,1)} %refs_0_.1), channel_id=1, source_target_pairs={{4,0},{8,4},{12,8},{14,12},{10,14},{6,10},{2,6},{0,2},{5,1},{9,5},... | collective-permute-start | bytes 688136 | tf_op jit(solution)/shard_map/ppermute | solution.py:402
  12.8 9.8 %collective-permute-start.6 = (bf16[32,3584]{1,0:T(8,128)(2,1)}, bf16[32,3584]{1,0:T(8,128)(2,1)S(1)}, u32[]{:S(2)}, u32[]{:S(2)}) collective-permute-start(bf16[32,3584]{1,0:T(8,128)(2,1)} %refs_0_.1), channel_id=1, source_target_pairs={{0,4},{4,8},{8,12},{12,14},{14,10},{10,6},{6,2},{2,0},{1,5},{5,9},... | collective-permute-start | bytes 688136 | tf_op jit(solution)/shard_map/ppermute | solution.py:404
  14.6 11.6 %collective-permute-start.1 = (bf16[32,3712]{1,0:T(8,128)(2,1)S(1)}, bf16[32,3712]{1,0:T(8,128)(2,1)S(1)}, u32[]{:S(2)}, u32[]{:S(2)}) collective-permute-start(bf16[32,3712]{1,0:T(8,128)(2,1)S(1)} %collective-permute-done.refs_6_), channel_id=1, source_target_pairs={{4,0},{8,4},{12,8},{14,12},{10,14},{6,10},{2,6},{0,2},{5,1},{9,5},... | collective-permute-start | bytes 712712 | tf_op jit(solution)/shard_map/ppermute | solution.py:404
  22.7 10.1 %collective-permute-start.7 = (bf16[32,3712]{1,0:T(8,128)(2,1)S(1)}, bf16[32,3712]{1,0:T(8,128)(2,1)S(1)}, u32[]{:S(2)}, u32[]{:S(2)}) collective-permute-start(bf16[32,3712]{1,0:T(8,128)(2,1)S(1)} %collective-permute-done.4.refs_4_), channel_id=1, source_target_pairs={{0,4},{4,8},{8,12},{12,14},{14,10},{10,6},{6,2},{2,0},{1,5},{5,9},... | collective-permute-start | bytes 712712 | tf_op jit(solution)/shard_map/ppermute | solution.py:402
  24.1 8.7 %collective-permute-start.8 = (bf16[32,3584]{1,0:T(8,128)(2,1)S(1)}, bf16[32,3584]{1,0:T(8,128)(2,1)S(1)}, u32[]{:S(2)}, u32[]{:S(2)}) collective-permute-start(bf16[32,3584]{1,0:T(8,128)(2,1)S(1)} %collective-permute-done.5.refs_4_), channel_id=1, source_target_pairs={{4,0},{8,4},{12,8},{14,12},{10,14},{6,10},{2,6},{0,2},{5,1},{9,5},... | collective-permute-start | bytes 688136 | tf_op jit(solution)/shard_map/ppermute | solution.py:402
  24.7 8.9 %collective-permute-start.9 = (bf16[32,3584]{1,0:T(8,128)(2,1)S(1)}, bf16[32,3584]{1,0:T(8,128)(2,1)S(1)}, u32[]{:S(2)}, u32[]{:S(2)}) collective-permute-start(bf16[32,3584]{1,0:T(8,128)(2,1)S(1)} %collective-permute-done.6.refs_1_), channel_id=1, source_target_pairs={{0,4},{4,8},{8,12},{12,14},{14,10},{10,6},{6,2},{2,0},{1,5},{5,9},... | collective-permute-start | bytes 688136 | tf_op jit(solution)/shard_map/ppermute | solution.py:404
  26.2 11.7 %collective-permute-start.2 = (bf16[32,3712]{1,0:T(8,128)(2,1)S(1)}, bf16[32,3712]{1,0:T(8,128)(2,1)S(1)}, u32[]{:S(2)}, u32[]{:S(2)}) collective-permute-start(bf16[32,3712]{1,0:T(8,128)(2,1)S(1)} %collective-permute-done.1.refs_7_), channel_id=1, source_target_pairs={{4,0},{8,4},{12,8},{14,12},{10,14},{6,10},{2,6},{0,2},{5,1},{9,5},... | collective-permute-start | bytes 712712 | tf_op jit(solution)/shard_map/ppermute | solution.py:404
  35.0 9.9 %collective-permute-start.11 = (bf16[32,3584]{1,0:T(8,128)(2,1)S(1)}, bf16[32,3584]{1,0:T(8,128)(2,1)}, u32[]{:S(2)}, u32[]{:S(2)}) collective-permute-start(bf16[32,3584]{1,0:T(8,128)(2,1)S(1)} %collective-permute-done.8.refs_5_), channel_id=1, source_target_pairs={{4,0},{8,4},{12,8},{14,12},{10,14},{6,10},{2,6},{0,2},{5,1},{9,5},... | collective-permute-start | bytes 688136 | tf_op jit(solution)/shard_map/ppermute | solution.py:402
  35.6 9.3 %collective-permute-start.12 = (bf16[32,3584]{1,0:T(8,128)(2,1)S(1)}, bf16[32,3584]{1,0:T(8,128)(2,1)}, u32[]{:S(2)}, u32[]{:S(2)}) collective-permute-start(bf16[32,3584]{1,0:T(8,128)(2,1)S(1)} %collective-permute-done.9.refs_2_), channel_id=1, source_target_pairs={{0,4},{4,8},{8,12},{12,14},{14,10},{10,6},{6,2},{2,0},{1,5},{5,9},... | collective-permute-start | bytes 688136 | tf_op jit(solution)/shard_map/ppermute | solution.py:404
  45.0 11.7 %collective-permute-start.15 = (bf16[32,3584]{1,0:T(8,128)(2,1)}, bf16[32,3584]{1,0:T(8,128)(2,1)S(1)}, u32[]{:S(2)}, u32[]{:S(2)}) collective-permute-start(bf16[32,3584]{1,0:T(8,128)(2,1)} %collective-permute-done.11.refs_6_), channel_id=1, source_target_pairs={{4,0},{8,4},{12,8},{14,12},{10,14},{6,10},{2,6},{0,2},{5,1},{9,5},... | collective-permute-start | bytes 688136 | tf_op jit(solution)/shard_map/ppermute | solution.py:402
  76.6 8.5 %collective-permute-start.24 = (bf16[32,3584]{1,0:T(8,128)(2,1)S(1)}, bf16[32,3584]{1,0:T(8,128)(2,1)S(1)}, u32[]{:S(2)}, u32[]{:S(2)}) collective-permute-start(bf16[32,3584]{1,0:T(8,128)(2,1)S(1)} %get-tuple-element.175), channel_id=1, source_target_pairs={{0,4},{4,8},{8,12},{12,14},{14,10},{10,6},{6,2},{2,0},{1,5},{5,9},... | collective-permute-start | bytes 688136 | tf_op jit(solution)/shard_map/ppermute | solution.py:422
  78.2 8.4 %collective-permute-start.25 = (bf16[32,3584]{1,0:T(8,128)(2,1)S(1)}, bf16[32,3584]{1,0:T(8,128)(2,1)S(1)}, u32[]{:S(2)}, u32[]{:S(2)}) collective-permute-start(bf16[32,3584]{1,0:T(8,128)(2,1)S(1)} %get-tuple-element.176), channel_id=1, source_target_pairs={{4,0},{8,4},{12,8},{14,12},{10,14},{6,10},{2,6},{0,2},{5,1},{9,5},... | collective-permute-start | bytes 688136 | tf_op jit(solution)/shard_map/ppermute | solution.py:422
  79.6 8.4 %collective-permute-start.22 = (bf16[16,3584]{1,0:T(8,128)(2,1)S(1)}, bf16[16,3584]{1,0:T(8,128)(2,1)S(1)}, u32[]{:S(2)}, u32[]{:S(2)}) collective-permute-start(bf16[16,3584]{1,0:T(8,128)(2,1)S(1)} %get-tuple-element.169), channel_id=1, source_target_pairs={{0,4},{4,8},{8,12},{12,14},{14,10},{10,6},{6,2},{2,0},{1,5},{5,9},... | collective-permute-start | bytes 344072 | tf_op jit(solution)/shard_map/ppermute | solution.py:422
  88.5 8.8 %collective-permute-start.26 = (bf16[32,3584]{1,0:T(8,128)(2,1)S(1)}, bf16[32,3584]{1,0:T(8,128)(2,1)S(1)}, u32[]{:S(2)}, u32[]{:S(2)}) collective-permute-start(bf16[32,3584]{1,0:T(8,128)(2,1)S(1)} %get-tuple-element.182), channel_id=1, source_target_pairs={{0,4},{4,8},{8,12},{12,14},{14,10},{10,6},{6,2},{2,0},{1,5},{5,9},... | collective-permute-start | bytes 688136 | tf_op jit(solution)/shard_map/ppermute | solution.py:422
  90.0 8.5 %collective-permute-start.27 = (bf16[32,3584]{1,0:T(8,128)(2,1)S(1)}, bf16[32,3584]{1,0:T(8,128)(2,1)S(1)}, u32[]{:S(2)}, u32[]{:S(2)}) collective-permute-start(bf16[32,3584]{1,0:T(8,128)(2,1)S(1)} %get-tuple-element.183), channel_id=1, source_target_pairs={{4,0},{8,4},{12,8},{14,12},{10,14},{6,10},{2,6},{0,2},{5,1},{9,5},... | collective-permute-start | bytes 688136 | tf_op jit(solution)/shard_map/ppermute | solution.py:422
  91.1 15.8 %collective-permute-start.32 = (bf16[32,3584]{1,0:T(8,128)(2,1)S(1)}, bf16[32,3584]{1,0:T(8,128)(2,1)S(1)}, u32[]{:S(2)}, u32[]{:S(2)}) collective-permute-start(bf16[32,3584]{1,0:T(8,128)(2,1)S(1)} %get-tuple-element.197), channel_id=1, source_target_pairs={{0,4},{4,8},{8,12},{12,14},{14,10},{10,6},{6,2},{2,0},{1,5},{5,9},... | collective-permute-start | bytes 688136 | tf_op jit(solution)/shard_map/ppermute | solution.py:422
  92.2 14.6 %collective-permute-start.33 = (bf16[32,3584]{1,0:T(8,128)(2,1)S(1)}, bf16[32,3584]{1,0:T(8,128)(2,1)S(1)}, u32[]{:S(2)}, u32[]{:S(2)}) collective-permute-start(bf16[32,3584]{1,0:T(8,128)(2,1)S(1)} %get-tuple-element.198), channel_id=1, source_target_pairs={{4,0},{8,4},{12,8},{14,12},{10,14},{6,10},{2,6},{0,2},{5,1},{9,5},... | collective-permute-start | bytes 688136 | tf_op jit(solution)/shard_map/ppermute | solution.py:422
  98.7 8.2 %collective-permute-start.29 = (bf16[32,3584]{1,0:T(8,128)(2,1)S(1)}, bf16[32,3584]{1,0:T(8,128)(2,1)S(1)}, u32[]{:S(2)}, u32[]{:S(2)}) collective-permute-start(bf16[32,3584]{1,0:T(8,128)(2,1)S(1)} %get-tuple-element.189), channel_id=1, source_target_pairs={{0,4},{4,8},{8,12},{12,14},{14,10},{10,6},{6,2},{2,0},{1,5},{5,9},... | collective-permute-start | bytes 688136 | tf_op jit(solution)/shard_map/ppermute | solution.py:422
  99.2 7.7 %collective-permute-start.30 = (bf16[32,3584]{1,0:T(8,128)(2,1)S(1)}, bf16[32,3584]{1,0:T(8,128)(2,1)S(1)}, u32[]{:S(2)}, u32[]{:S(2)}) collective-permute-start(bf16[32,3584]{1,0:T(8,128)(2,1)S(1)} %get-tuple-element.190), channel_id=1, source_target_pairs={{4,0},{8,4},{12,8},{14,12},{10,14},{6,10},{2,6},{0,2},{5,1},{9,5},... | collective-permute-start | bytes 688136 | tf_op jit(solution)/shard_map/ppermute | solution.py:422
  107.6 8.6 %collective-permute-start.34 = (bf16[32,3584]{1,0:T(8,128)(2,1)S(1)}, bf16[32,3584]{1,0:T(8,128)(2,1)S(1)}, u32[]{:S(2)}, u32[]{:S(2)}) collective-permute-start(bf16[32,3584]{1,0:T(8,128)(2,1)S(1)} %get-tuple-element.206), channel_id=1, source_target_pairs={{0,4},{4,8},{8,12},{12,14},{14,10},{10,6},{6,2},{2,0},{1,5},{5,9},... | collective-permute-start | bytes 688136 | tf_op jit(solution)/shard_map/ppermute | solution.py:422
  108.0 8.2 %collective-permute-start.35 = (bf16[32,3584]{1,0:T(8,128)(2,1)S(1)}, bf16[32,3584]{1,0:T(8,128)(2,1)S(1)}, u32[]{:S(2)}, u32[]{:S(2)}) collective-permute-start(bf16[32,3584]{1,0:T(8,128)(2,1)S(1)} %get-tuple-element.207), channel_id=1, source_target_pairs={{4,0},{8,4},{12,8},{14,12},{10,14},{6,10},{2,6},{0,2},{5,1},{9,5},... | collective-permute-start | bytes 688136 | tf_op jit(solution)/shard_map/ppermute | solution.py:422
  (23 other events, 185.8 us)

commit v6 on v5

--- a/solution.py
+++ b/solution.py
@@ -118,7 +118,7 @@
 
 
 def token_slots_kernel(experts, info_ref, *refs):
-    blocks, (kept_ref, sent_ref, select_ref, high_ref, low_ref, all_ref) = refs[2:-6], refs[-6:]
+    blocks, (kept_ref, sent_ref, select_ref, high_ref, low_ref, all_ref) = refs[1:-6], refs[-6:]
     rows, load = blocks[0].shape
     toks, slots = all_ref.shape[0], select_ref.shape[0]
     half, width = slots // 2, load - LANES
@@ -163,11 +163,13 @@
 
 
 def inner_kernel(
-    count, tiles, info_ref, kept_ref, came_ref, gate_ref, up_a_ref, up_b_ref, up_ref,
-    inner_ref, slope_ref, active_ref, low_up_ref, keep_ref, rows_ref,
+    count, tiles, info_ref, kept_ref, came_ref, gate_ref, up_a_ref, up_b_ref, up_hbm,
+    inner_ref, slope_ref, active_ref, low_up_ref, keep_ref, rows_ref, up_ref, sems,
 ):
     half, width = kept_ref.shape[0], rows_ref.shape[1]
     slots, tile = 2 * half, gate_ref.shape[1] // tiles
+    copy = pltpu.make_async_copy(up_hbm, up_ref, sems.at[0])
+    copy.start()
     rows_ref[:half] = kept_ref[:, :width]
     rows_ref[half:] = came_ref[:, :width]
     low_up_ref[...] = mm_nt(rows_ref[...], up_a_ref[...]).astype(bf16)
@@ -190,14 +192,17 @@
     for j in range(tiles):
         cols = slice(j * tile, (j + 1) * tile)
         pre_gate = mm(rows_ref[...], gate_ref[:, cols])
+        logistic = jax.nn.sigmoid(pre_gate)
+        active_ref[:, cols] = pre_gate * logistic
+        slope_ref[:, cols] = logistic * (1.0 + pre_gate * (1.0 - logistic))
+    copy.wait()
+    for j in range(tiles):
+        cols = slice(j * tile, (j + 1) * tile)
         pre_up = mm(rows_ref[...], up_ref[:, cols]) + adapter_scale * mm(
             low_up_ref[...], up_b_ref[:, cols]
         )
-        logistic = jax.nn.sigmoid(pre_gate)
-        active = pre_gate * logistic
-        active_ref[:, cols] = active
-        slope_ref[:, cols] = pre_up * (logistic * (1.0 + pre_gate * (1.0 - logistic)))
-        inner_ref[:, cols] = (active * pre_up).astype(bf16)
+        slope_ref[:, cols] = slope_ref[:, cols] * pre_up
+        inner_ref[:, cols] = (active_ref[:, cols] * pre_up).astype(bf16)
 
 
 def routed_kernel(
@@ -504,25 +509,22 @@
         ring_token.gather_hop(tok_far, tok_near)
         cot_far, cot_near = [cotangent], [cotangent]
         ring_token.gather_hop(tok_far, tok_near)
-        tok_near[-1], gate_late = tie(tok_near[-1], gate_w)
         ring_cot.gather_hop(cot_far, cot_near)
+        for hop in range(2, hops):
+            ring_token.gather_hop(tok_far, tok_near)
+            if hop == hops - 2:
+                tok_far[-1], cot_far[1], cot_near[1] = tie(tok_far[-1], cot_far[1], cot_near[1])
+                tok_near[-1], gate_late = tie(tok_near[-1], gate_w)
+            if hop < hops - 1:
+                ring_cot.gather_hop(cot_far, cot_near)
         gate_v, up_a_v, up_b_v = fetch(gate_late, up_a, up_b)
-        for hop in range(2, hops):
-            if hop == hops - 1:
-                tok_far[-1], up_b_v = tie(tok_far[-1], up_b_v)
-            tok_far[-1], cot_far[-1], cot_near[-1] = tie(tok_far[-1], cot_far[-1], cot_near[-1])
-            ring_token.gather_hop(tok_far, tok_near)
-            ring_cot.gather_hop(cot_far, cot_near)
-            if hop == hops - 2:
-                tok_near[-1], up_late = tie(tok_near[-1], up_w)
-        (up_v,) = fetch(up_late)
         token_blocks = ring_token.gathered(tok_far, tok_near)
 
         kept, sent, select, high, low, token_all = call(
             functools.partial(token_slots_kernel, experts),
             [struct((half, load))] * 2 + [struct((slots, toks))] * 3 + [struct((toks, load))],
-            [in_smem] + [in_vmem] * (count + 2),
-            (info, gate_v, up_v, *token_blocks),
+            [in_smem] + [in_vmem] * (count + 1),
+            (info, gate_v, *token_blocks),
             (2 * slots * toks * load, 2 * count * nbytes([token_load])),
         )
         sent, cot_far[-1], cot_near[-1] = tie(sent, cot_far[-1], cot_near[-1])
@@ -534,11 +536,18 @@
                 struct((slots, hidden)), struct((slots, hidden), f32), struct((slots, hidden), f32),
                 struct((slots, rank)), struct((slots, LANES), f32),
             ],
-            [in_smem] + [in_vmem] * 6,
-            (info, kept, came, gate_v, up_a_v, up_b_v, up_v),
+            [in_smem] + [in_vmem] * 5 + [in_hbm],
+            (info, kept, came, gate_v, up_a_v, up_b_v, *stay(up_w)),
             (4 * slots * width * hidden, 2 * nbytes([gate_w])),
-            scratch=[pltpu.VMEM((slots, width), bf16)],
-        )
+            scratch=[
+                pltpu.VMEM((slots, width), bf16), pltpu.VMEM(up_w.shape, bf16),
+                pltpu.SemaphoreType.DMA((1,)),
+            ],
+            mib=16,
+        )
+        inner, cot_far[-1], cot_near[-1] = tie(inner, cot_far[-1], cot_near[-1])
+        while len(cot_far) <= hops:
+            ring_cot.gather_hop(cot_far, cot_near)
         routed_kept, routed_sent, low_down = call(
             functools.partial(routed_kernel, tiles),
             [struct((half, width))] * 2 + [struct((slots, rank))],
@@ -546,7 +555,7 @@
             (inner, keep, down_w, down_a, down_b),
             (2 * slots * width * hidden, nbytes([gate_w])),
         )
-        routed_sent, high = tie(routed_sent, high)
+        routed_sent, high, cot_far[-1] = tie(routed_sent, high, cot_far[-1])
         routed_came = swap_cores(routed_sent)
         cot_blocks = ring_cot.gathered(cot_far, cot_near)
         cot_kept, cot_sent, cot_all = call(
@@ -584,7 +593,7 @@
             functools.partial(row_grad_kernel, tiles),
             [struct((half, width))] * 2,
             [in_vmem] * 6,
-            (grad_gate, grad_up, back_up, gate_v, up_v, up_a_v),
+            (grad_gate, grad_up, back_up, gate_v, up_w, up_a_v),
             (4 * slots * width * hidden, 2 * nbytes([gate_w])),
         )
         back_sent, *mix_came[1] = tie(back_sent, *mix_came[1])
@@ -620,6 +629,22 @@
             else:
                 tied = tie(*back_came[-1], back_up_late, dots)
             back_came[-1], back_up_late, dots = tied[:2], tied[2], tied[3]
+            if hop == 1:
+                adapters = call(
+                    adapter_kernel,
+                    [
+                        struct((rank, width)), struct((rank, hidden)),
+                        struct((rank, hidden)), struct((rank, width)),
+                    ],
+                    [in_vmem] * 9,
+                    (kept, came, back_up_late, low_up, grad_up, inner, back_low, low_down,
+                     grad_routed),
+                    (8 * slots * width * rank, 4 * nbytes([grad_routed])),
+                    out_specs=[pl.BlockSpec()] * 4,
+                )
+                adapters = list(adapters)
+            if hop == 2:
+                *back_came[-1], adapters[1] = tie(*back_came[-1], adapters[1])
             back_came.append(scatter_hop(back_parts, count, back_came[-1], hop))
             if step < count:
                 dots = double(dots, step)
@@ -627,18 +652,6 @@
         while step < count:
             dots = double(dots, step)
             step *= 2
-        adapters = call(
-            adapter_kernel,
-            [
-                struct((rank, width)), struct((rank, hidden)),
-                struct((rank, hidden)), struct((rank, width)),
-            ],
-            [in_vmem] * 9,
-            (kept, came, back_up_late, low_up, grad_up, inner, back_low, low_down,
-             grad_routed),
-            (8 * slots * width * rank, 4 * nbytes([grad_routed])),
-            out_specs=[pl.BlockSpec()] * 4,
-        )
         adapters = (adapters[0].T, adapters[1], adapters[2].T, adapters[3])
 
         (mixed,) = call(

time: 118 us -> 114 us (0.966)
  local copies, waits for them, and re-layouts: 4.95 us -> 0.16 us
  Pallas kernels: 38.3 us -> 34.9 us
  waiting for transfers between devices: 37.9 us -> 39.9 us
  starting transfers between devices: 34.2 us -> 36 us
    ppermute x8, waiting for transfers between devices: 12.2 us -> 19 us  [gather_hop(): far.append(lax.ppermute(far[-1], 'expert', self.far))]
    unnamed x18 -> x16, local copies, waits for them, and re-layouts: 4.83 us -> 0.04 us
    pallas_call x22 -> x21, Pallas kernels: 38.3 us -> 34.9 us  [call(): pl.pallas_call(body, out_shape=outs, in_specs=specs, out_specs=out_specs...]
    ppermute x3, waiting for transfers between devices: 12.3 us -> 9.44 us  [double(): lax.ppermute(gathered, 'expert', [(i, i ^ step) for i in range(size)])]
    ppermute x8, starting transfers between devices: 9.83 us -> 11.3 us  [gather_hop(): far.append(lax.ppermute(far[-1], 'expert', self.far))]
    ppermute x5, waiting for transfers between devices: 3.03 us -> 1.61 us  [swap_cores(): return lax.ppermute(value, 'dp', [(0, 1), (1, 0)])]
    ppermute x3, starting transfers between devices: 1.54 us -> 2.76 us  [double(): lax.ppermute(gathered, 'expert', [(i, i ^ step) for i in range(size)])]
  transfers between devices with their start and end apart: 38 -> 38, of which waited for: 16 -> 20; matrix products, arithmetic and copies ran while one was open for 0% -> 1% of each run, Pallas kernels for 31% -> 29%
where the time goes in v6:
time: 114 us
  waiting for transfers between devices  39.9 us (35%)
  starting transfers between devices  36 us (32%)
  Pallas kernels  34.9 us (31%)
  between operations  1.56 us (1%)
  other arithmetic  1.51 us (1%)
    pallas_call x21, Pallas kernels, call(): pl.pallas_call(body, out_shape=outs, in_specs=specs, out_specs=out_specs...  34.9 us
    ppermute x8, waiting for transfers between devices, gather_hop(): far.append(lax.ppermute(far[-1], 'expert', self.far))  19 us
    ppermute x8, starting transfers between devices, gather_hop(): far.append(lax.ppermute(far[-1], 'expert', self.far))  11.3 us
    ppermute x8, starting transfers between devices, scatter_hop(): lax.ppermute(front, 'expert', ahead)  10 us
    ppermute x3, waiting for transfers between devices, double(): lax.ppermute(gathered, 'expert', [(i, i ^ step) for i in range(size)])  9.44 us
    ppermute x8, starting transfers between devices, scatter_hop(): lax.ppermute(rear, 'expert', back)  6.55 us
    ppermute x8, waiting for transfers between devices, scatter_hop(): lax.ppermute(rear, 'expert', back)  4.85 us
    ppermute x6, starting transfers between devices, gather_hop(): near.append(lax.ppermute(near[-1], 'expert', self.near))  4.68 us
  transfers between devices with their start and end apart: 38, of which 20 were waited for; matrix products, arithmetic and copies ran while one was open for 1% of the time, Pallas kernels for 29%

profile of v6, /device:TPU:0, one launch (start us, length us, event | category | flops | bytes accessed | tf_op | source)
XLA Modules:
  0.0 114.1 jit_solution(81742665282592880)
XLA Ops:
  2.0 3.1 %collective-permute-start.3 = (bf16[32,3712]{1,0:T(8,128)(2,1)S(1)}, bf16[32,3712]{1,0:T(8,128)(2,1)S(1)}, u32[]{:S(2)}, u32[]{:S(2)}) collective-permute-start(bf16[32,3712]{1,0:T(8,128)(2,1)S(1)} %shard_map.180.refs_1_), channel_id=1, source_target_pairs={{0,4},{4,8},{8,12},{12,14},{14,10},{10,6},{6,2},{2,0},{1,5},{5,9},... | collective-permute-start | bytes 712712 | tf_op jit(solution)/shard_map/ppermute | solution.py:407
  5.1 5.7 %collective-permute-done.3.refs_2_ = bf16[32,3712]{1,0:T(8,128)(2,1)S(1)} collective-permute-done((bf16[32,3712]{1,0:T(8,128)(2,1)S(1)}, bf16[32,3712]{1,0:T(8,128)(2,1)S(1)}, u32[]{:S(2)}, u32[]{:S(2)}) %collective-permute-start.3) | collective-permute-done | bytes 237600 | tf_op jit(solution)/shard_map/ppermute | solution.py:407
  10.8 1.8 %collective-permute-start.4 = (bf16[32,3712]{1,0:T(8,128)(2,1)S(1)}, bf16[32,3712]{1,0:T(8,128)(2,1)S(1)}, u32[]{:S(2)}, u32[]{:S(2)}) collective-permute-start(bf16[32,3712]{1,0:T(8,128)(2,1)S(1)} %collective-permute-done.3.refs_2_), channel_id=1, source_target_pairs={{0,4},{4,8},{8,12},{12,14},{14,10},{10,6},{6,2},{2,0},{1,5},{5,9},... | collective-permute-start | bytes 712712 | tf_op jit(solution)/shard_map/ppermute | solution.py:407
  12.8 4.9 %collective-permute-done.4.refs_3_ = bf16[32,3712]{1,0:T(8,128)(2,1)S(1)} collective-permute-done((bf16[32,3712]{1,0:T(8,128)(2,1)S(1)}, bf16[32,3712]{1,0:T(8,128)(2,1)S(1)}, u32[]{:S(2)}, u32[]{:S(2)}) %collective-permute-start.4) | collective-permute-done | bytes 237600 | tf_op jit(solution)/shard_map/ppermute | solution.py:407
  17.7 1.5 %collective-permute-start.5 = (bf16[32,3712]{1,0:T(8,128)(2,1)S(1)}, bf16[32,3712]{1,0:T(8,128)(2,1)S(1)}, u32[]{:S(2)}, u32[]{:S(2)}) collective-permute-start(bf16[32,3712]{1,0:T(8,128)(2,1)S(1)} %collective-permute-done.4.refs_3_), channel_id=1, source_target_pairs={{0,4},{4,8},{8,12},{12,14},{14,10},{10,6},{6,2},{2,0},{1,5},{5,9},... | collective-permute-start | bytes 712712 | tf_op jit(solution)/shard_map/ppermute | solution.py:407
  21.8 5.4 %collective-permute-done.6.refs_4_ = bf16[32,3584]{1,0:T(8,128)(2,1)S(1)} collective-permute-done((bf16[32,3584]{1,0:T(8,128)(2,1)}, bf16[32,3584]{1,0:T(8,128)(2,1)S(1)}, u32[]{:S(2)}, u32[]{:S(2)}) %collective-permute-start.6) | collective-permute-done | bytes 229408 | tf_op jit(solution)/shard_map/ppermute | solution.py:407
  33.7 3.1 %shard_map.181 = (bf16[3584,1024]{1,0:T(8,128)(2,1)S(1)}, bf16[64,3584]{1,0:T(8,128)(2,1)S(1)}, bf16[64,1024]{1,0:T(8,128)(2,1)S(1)}) custom-call(bf16[3584,1024]{1,0:T(8,128)(2,1)} %bitcast.40, bf16[64,3584]{1,0:T(8,128)(2,1)} %bitcast.41, bf16[64,1024]{1,0:T(8,128)(2,1)} %bitcast.42), custom_call_target="tpu_custom_call" | custom-call | bytes 7 | tf_op jit(solution)/shard_map/pallas_call | solution.py:40
  36.8 1.8 %shard_map.182 = (bf16[128,3712]{1,0:T(8,128)(2,1)S(1)}, bf16[128,3712]{1,0:T(8,128)(2,1)S(1)}, bf16[256,256]{1,0:T(8,128)(2,1)S(1)}, bf16[256,256]{1,0:T(8,128)...) custom-call(s32[12]{0:T(128)S(1)} %concatenate.12.info_ref, ...), custom_call_target="tpu_custom_call" | custom-call | flops 486 | bytes 3 | tf_op jit(solution)/shard_map/pallas_call | solution.py:40
  41.3 6.4 %shard_map.183 = (bf16[256,1024]{1,0:T(8,128)(2,1)S(1)}, f32[256,1024]{1,0:T(8,128)S(1)}, f32[256,1024]{1,0:T(8,128)S(1)}, bf16[256,64]{1,0:T(8,128)(2,1)S(1)}, f32[256,128]{1,0:T(8,128)S(1)}) custom-call(s32[12]{0:T(128)S(1)} %concatenate.12.info_ref, bf16[128,3712]{1,0:T(8,128)(2,1)S(1)} %get-tuple-element.116.kept_ref, ...), custom_call_target="tpu_custom_call" | custom-call | flops 3758 | bytes 14 | tf_op jit(solution)/shard_map/pallas_call | solution.py:40
  49.1 3.4 %shard_map.184 = (bf16[128,3584]{1,0:T(8,128)(2,1)S(1)}, bf16[128,3584]{1,0:T(8,128)(2,1)S(1)}, bf16[256,64]{1,0:T(8,128)(2,1)S(1)}) custom-call(bf16[256,1024]{1,0:T(8,128)(2,1)S(1)} %get-tuple-element.126.inner_ref, f32[256,128]{1,0:T(8,128)S(1)} %get-tuple-element.127.keep_ref, bf16[1024,3584]{1,0:T(8,128)(2,1)S(1)} %bitcast.32, ...), custom_call_target="tpu_custom_call" | custom-call | flops 1879 | bytes 7 | tf_op jit(solution)/shard_map/pallas_call | solution.py:40
  52.6 2.9 %collective-permute-done.14.refs_7_ = bf16[32,3584]{1,0:T(8,128)(2,1)S(1)} collective-permute-done((bf16[32,3584]{1,0:T(8,128)(2,1)S(1)}, bf16[32,3584]{1,0:T(8,128)(2,1)S(1)}, u32[]{:S(2)}, u32[]{:S(2)}) %collective-permute-start.14) | collective-permute-done | bytes 229408 | tf_op jit(solution)/shard_map/ppermute | solution.py:407
  61.3 4.2 %shard_map.187 = (bf16[256,3584]{1,0:T(8,128)(2,1)S(1)}, bf16[256,1024]{1,0:T(8,128)(2,1)S(1)}, bf16[256,1024]{1,0:T(8,128)(2,1)S(1)}, bf16[256,64]{1,0:T(8,128)(2,1)S(1)}, bf16[256,64]{1,0:T(8,128)(2,1)S(1)}) custom-call(bf16[128,3584]{1,0:T(8,128)(2,1)S(1)} %get-tuple-element.141.kept_ref, bf16[128,3584]{1,0:T(8,128)(2,1)S(1)} %collective-permute-done.16.came_ref, ...), custom_call_target="tpu_custom_call" | custom-call | flops 1879 | bytes 7 | tf_op jit(solution)/shard_map/pallas_call | solution.py:40
  65.6 1.6 %collective-permute-start.19 = (bf16[32,3584]{1,0:T(8,128)(2,1)S(1)}, bf16[32,3584]{1,0:T(8,128)(2,1)S(1)}, u32[]{:S(2)}, u32[]{:S(2)}) collective-permute-start(bf16[32,3584]{1,0:T(8,128)(2,1)S(1)} %get-tuple-element.159), channel_id=1, source_target_pairs={{0,4},{4,8},{8,12},{12,14},{14,10},{10,6},{6,2},{2,0},{1,5},{5,9},... | collective-permute-start | bytes 688136 | tf_op jit(solution)/shard_map/ppermute | solution.py:427
  67.7 5.1 %shard_map.188 = (bf16[128,3584]{1,0:T(8,128)(2,1)S(1)}, bf16[128,3584]{1,0:T(8,128)(2,1)S(1)}) custom-call(bf16[256,1024]{1,0:T(8,128)(2,1)S(1)} %get-tuple-element.147.grad_gate_ref, bf16[256,1024]{1,0:T(8,128)(2,1)S(1)} %get-tuple-element.151.grad_up_ref, bf16[256,64]{1,0:T(8,128)(2,1)S(1)} %get-tuple-element.179.back_up_ref, ...), custom_call_target="tpu_custom_call" | custom-call | flops 3758 | bytes 14 | tf_op jit(solution)/shard_map/pallas_call | solution.py:40
  74.4 1.6 %collective-permute-start.24 = (bf16[32,3584]{1,0:T(8,128)(2,1)S(1)}, bf16[32,3584]{1,0:T(8,128)(2,1)S(1)}, u32[]{:S(2)}, u32[]{:S(2)}) collective-permute-start(bf16[32,3584]{1,0:T(8,128)(2,1)S(1)} %get-tuple-element.170), channel_id=1, source_target_pairs={{0,4},{4,8},{8,12},{12,14},{14,10},{10,6},{6,2},{2,0},{1,5},{5,9},... | collective-permute-start | bytes 688136 | tf_op jit(solution)/shard_map/ppermute | solution.py:427
  77.4 1.6 %collective-permute-start.22 = (bf16[16,3584]{1,0:T(8,128)(2,1)S(1)}, bf16[16,3584]{1,0:T(8,128)(2,1)S(1)}, u32[]{:S(2)}, u32[]{:S(2)}) collective-permute-start(bf16[16,3584]{1,0:T(8,128)(2,1)S(1)} %get-tuple-element.164), channel_id=1, source_target_pairs={{0,4},{4,8},{8,12},{12,14},{14,10},{10,6},{6,2},{2,0},{1,5},{5,9},... | collective-permute-start | bytes 344072 | tf_op jit(solution)/shard_map/ppermute | solution.py:427
  79.5 3.3 %collective-permute-done.24.forth_ref = bf16[32,3584]{1,0:T(8,128)(2,1)S(1)} collective-permute-done((bf16[32,3584]{1,0:T(8,128)(2,1)S(1)}, bf16[32,3584]{1,0:T(8,128)(2,1)S(1)}, u32[]{:S(2)}, u32[]{:S(2)}) %collective-permute-start.24) | collective-permute-done | bytes 229408 | tf_op jit(solution)/shard_map/ppermute | solution.py:427
  82.8 1.6 %collective-permute-done.25.hither_ref = bf16[32,3584]{1,0:T(8,128)(2,1)S(1)} collective-permute-done((bf16[32,3584]{1,0:T(8,128)(2,1)S(1)}, bf16[32,3584]{1,0:T(8,128)(2,1)S(1)}, u32[]{:S(2)}, u32[]{:S(2)}) %collective-permute-start.25) | collective-permute-done | bytes 229408 | tf_op jit(solution)/shard_map/ppermute | solution.py:427
  86.3 1.6 %collective-permute-start.26 = (bf16[32,3584]{1,0:T(8,128)(2,1)S(1)}, bf16[32,3584]{1,0:T(8,128)(2,1)S(1)}, u32[]{:S(2)}, u32[]{:S(2)}) collective-permute-start(bf16[32,3584]{1,0:T(8,128)(2,1)S(1)} %get-tuple-element.177), channel_id=1, source_target_pairs={{0,4},{4,8},{8,12},{12,14},{14,10},{10,6},{6,2},{2,0},{1,5},{5,9},... | collective-permute-start | bytes 688136 | tf_op jit(solution)/shard_map/ppermute | solution.py:427
  91.0 1.8 %shard_map.194 = (bf16[64,3584]{1,0:T(8,128)(2,1)}, bf16[64,1024]{1,0:T(8,128)(2,1)}, bf16[64,1024]{1,0:T(8,128)(2,1)}, bf16[64,3584]{1,0:T(8,128)(2,1)}) custom-call(bf16[128,3712]{1,0:T(8,128)(2,1)S(1)} %get-tuple-element.116.kept_ref, bf16[128,3712]{1,0:T(8,128)(2,1)S(1)} %collective-permute-done.11.came_ref, ...), custom_call_target="tpu_custom_call" | custom-call | flops 469 | bytes 7 | tf_op jit(solution)/shard_map/pallas_call | solution.py:40
  92.8 2.2 %collective-permute-done.28 = bf16[1,16,256]{2,1,0:T(8,128)(2,1)S(1)} collective-permute-done((bf16[1,16,256]{2,1,0:T(8,128)(2,1)S(1)}, bf16[1,16,256]{2,1,0:T(8,128)(2,1)S(1)}, u32[]{:S(2)}, u32[]{:S(2)}) %collective-permute-start.28) | collective-permute-done | bytes 8224 | tf_op jit(solution)/shard_map/ppermute | solution.py:432
  99.7 5.0 %collective-permute-done.31 = bf16[2,16,256]{2,1,0:T(8,128)(2,1)S(1)} collective-permute-done((bf16[2,16,256]{2,1,0:T(8,128)(2,1)S(1)}, bf16[2,16,256]{2,1,0:T(8,128)(2,1)S(1)}, u32[]{:S(2)}, u32[]{:S(2)}) %collective-permute-start.31) | collective-permute-done | bytes 16416 | tf_op jit(solution)/shard_map/ppermute | solution.py:432
  106.3 1.7 %collective-permute-start.35 = (bf16[32,3584]{1,0:T(8,128)(2,1)S(1)}, bf16[32,3584]{1,0:T(8,128)(2,1)S(1)}, u32[]{:S(2)}, u32[]{:S(2)}) collective-permute-start(bf16[32,3584]{1,0:T(8,128)(2,1)S(1)} %get-tuple-element.208), channel_id=1, source_target_pairs={{4,0},{8,4},{12,8},{14,12},{10,14},{6,10},{2,6},{0,2},{5,1},{9,5},... | collective-permute-start | bytes 688136 | tf_op jit(solution)/shard_map/ppermute | solution.py:427
  108.1 2.2 %collective-permute-done.36 = bf16[4,16,256]{2,1,0:T(8,128)(2,1)S(1)} collective-permute-done((bf16[4,16,256]{2,1,0:T(8,128)(2,1)S(1)}, bf16[4,16,256]{2,1,0:T(8,128)(2,1)S(1)}, u32[]{:S(2)}, u32[]{:S(2)}) %collective-permute-start.36) | collective-permute-done | bytes 32800 | tf_op jit(solution)/shard_map/ppermute | solution.py:432
  (98 shorter events, 38.7 us)
Async XLA Ops:
  2.0 8.8 %collective-permute-start.3 = (bf16[32,3712]{1,0:T(8,128)(2,1)S(1)}, bf16[32,3712]{1,0:T(8,128)(2,1)S(1)}, u32[]{:S(2)}, u32[]{:S(2)}) collective-permute-start(bf16[32,3712]{1,0:T(8,128)(2,1)S(1)} %shard_map.180.refs_1_), channel_id=1, source_target_pairs={{0,4},{4,8},{8,12},{12,14},{14,10},{10,6},{6,2},{2,0},{1,5},{5,9},... | collective-permute-start | bytes 712712 | tf_op jit(solution)/shard_map/ppermute | solution.py:407
  5.0 7.5 %collective-permute-start = (bf16[32,3712]{1,0:T(8,128)(2,1)S(1)}, bf16[32,3712]{1,0:T(8,128)(2,1)S(1)}, u32[]{:S(2)}, u32[]{:S(2)}) collective-permute-start(bf16[32,3712]{1,0:T(8,128)(2,1)S(1)} %shard_map.180.refs_1_), channel_id=1, source_target_pairs={{4,0},{8,4},{12,8},{14,12},{10,14},{6,10},{2,6},{0,2},{5,1},{9,5},... | collective-permute-start | bytes 712712 | tf_op jit(solution)/shard_map/ppermute | solution.py:409
  12.6 8.7 %collective-permute-start.1 = (bf16[32,3712]{1,0:T(8,128)(2,1)S(1)}, bf16[32,3712]{1,0:T(8,128)(2,1)S(1)}, u32[]{:S(2)}, u32[]{:S(2)}) collective-permute-start(bf16[32,3712]{1,0:T(8,128)(2,1)S(1)} %collective-permute-done.refs_5_), channel_id=1, source_target_pairs={{4,0},{8,4},{12,8},{14,12},{10,14},{6,10},{2,6},{0,2},{5,1},{9,5},... | collective-permute-start | bytes 712712 | tf_op jit(solution)/shard_map/ppermute | solution.py:409
  17.7 11.0 %collective-permute-start.5 = (bf16[32,3712]{1,0:T(8,128)(2,1)S(1)}, bf16[32,3712]{1,0:T(8,128)(2,1)S(1)}, u32[]{:S(2)}, u32[]{:S(2)}) collective-permute-start(bf16[32,3712]{1,0:T(8,128)(2,1)S(1)} %collective-permute-done.4.refs_3_), channel_id=1, source_target_pairs={{0,4},{4,8},{8,12},{12,14},{14,10},{10,6},{6,2},{2,0},{1,5},{5,9},... | collective-permute-start | bytes 712712 | tf_op jit(solution)/shard_map/ppermute | solution.py:407
  19.2 8.0 %collective-permute-start.6 = (bf16[32,3584]{1,0:T(8,128)(2,1)}, bf16[32,3584]{1,0:T(8,128)(2,1)S(1)}, u32[]{:S(2)}, u32[]{:S(2)}) collective-permute-start(bf16[32,3584]{1,0:T(8,128)(2,1)} %refs_0_.1), channel_id=1, source_target_pairs={{4,0},{8,4},{12,8},{14,12},{10,14},{6,10},{2,6},{0,2},{5,1},{9,5},... | collective-permute-start | bytes 688136 | tf_op jit(solution)/shard_map/ppermute | solution.py:407
  19.8 8.9 %collective-permute-start.7 = (bf16[32,3584]{1,0:T(8,128)(2,1)}, bf16[32,3584]{1,0:T(8,128)(2,1)S(1)}, u32[]{:S(2)}, u32[]{:S(2)}) collective-permute-start(bf16[32,3584]{1,0:T(8,128)(2,1)} %refs_0_.1), channel_id=1, source_target_pairs={{0,4},{4,8},{8,12},{12,14},{14,10},{10,6},{6,2},{2,0},{1,5},{5,9},... | collective-permute-start | bytes 688136 | tf_op jit(solution)/shard_map/ppermute | solution.py:409
  21.2 12.4 %collective-permute-start.2 = (bf16[32,3712]{1,0:T(8,128)(2,1)S(1)}, bf16[32,3712]{1,0:T(8,128)(2,1)S(1)}, u32[]{:S(2)}, u32[]{:S(2)}) collective-permute-start(bf16[32,3712]{1,0:T(8,128)(2,1)S(1)} %collective-permute-done.1.refs_6_), channel_id=1, source_target_pairs={{4,0},{8,4},{12,8},{14,12},{10,14},{6,10},{2,6},{0,2},{5,1},{9,5},... | collective-permute-start | bytes 712712 | tf_op jit(solution)/shard_map/ppermute | solution.py:409
  28.7 8.1 %collective-permute-start.8 = (bf16[32,3712]{1,0:T(8,128)(2,1)S(1)}, bf16[32,3712]{1,0:T(8,128)(2,1)S(1)}, u32[]{:S(2)}, u32[]{:S(2)}) collective-permute-start(bf16[32,3712]{1,0:T(8,128)(2,1)S(1)} %collective-permute-done.5.refs_4_), channel_id=1, source_target_pairs={{0,4},{4,8},{8,12},{12,14},{14,10},{10,6},{6,2},{2,0},{1,5},{5,9},... | collective-permute-start | bytes 712712 | tf_op jit(solution)/shard_map/ppermute | solution.py:407
  30.1 8.6 %collective-permute-start.9 = (bf16[32,3584]{1,0:T(8,128)(2,1)S(1)}, bf16[32,3584]{1,0:T(8,128)(2,1)S(1)}, u32[]{:S(2)}, u32[]{:S(2)}) collective-permute-start(bf16[32,3584]{1,0:T(8,128)(2,1)S(1)} %collective-permute-done.6.refs_4_), channel_id=1, source_target_pairs={{4,0},{8,4},{12,8},{14,12},{10,14},{6,10},{2,6},{0,2},{5,1},{9,5},... | collective-permute-start | bytes 688136 | tf_op jit(solution)/shard_map/ppermute | solution.py:407
  30.7 8.0 %collective-permute-start.10 = (bf16[32,3584]{1,0:T(8,128)(2,1)S(1)}, bf16[32,3584]{1,0:T(8,128)(2,1)S(1)}, u32[]{:S(2)}, u32[]{:S(2)}) collective-permute-start(bf16[32,3584]{1,0:T(8,128)(2,1)S(1)} %collective-permute-done.7.refs_1_), channel_id=1, source_target_pairs={{0,4},{4,8},{8,12},{12,14},{14,10},{10,6},{6,2},{2,0},{1,5},{5,9},... | collective-permute-start | bytes 688136 | tf_op jit(solution)/shard_map/ppermute | solution.py:409
  38.8 9.0 %collective-permute-start.12 = (bf16[32,3584]{1,0:T(8,128)(2,1)S(1)}, bf16[32,3584]{1,0:T(8,128)(2,1)S(1)}, u32[]{:S(2)}, u32[]{:S(2)}) collective-permute-start(bf16[32,3584]{1,0:T(8,128)(2,1)S(1)} %collective-permute-done.9.refs_5_), channel_id=1, source_target_pairs={{4,0},{8,4},{12,8},{14,12},{10,14},{6,10},{2,6},{0,2},{5,1},{9,5},... | collective-permute-start | bytes 688136 | tf_op jit(solution)/shard_map/ppermute | solution.py:407
  39.8 7.9 %collective-permute-start.13 = (bf16[32,3584]{1,0:T(8,128)(2,1)S(1)}, bf16[32,3584]{1,0:T(8,128)(2,1)S(1)}, u32[]{:S(2)}, u32[]{:S(2)}) collective-permute-start(bf16[32,3584]{1,0:T(8,128)(2,1)S(1)} %collective-permute-done.10.refs_2_), channel_id=1, source_target_pairs={{0,4},{4,8},{8,12},{12,14},{14,10},{10,6},{6,2},{2,0},{1,5},{5,9},... | collective-permute-start | bytes 688136 | tf_op jit(solution)/shard_map/ppermute | solution.py:409
  47.7 7.7 %collective-permute-start.14 = (bf16[32,3584]{1,0:T(8,128)(2,1)S(1)}, bf16[32,3584]{1,0:T(8,128)(2,1)S(1)}, u32[]{:S(2)}, u32[]{:S(2)}) collective-permute-start(bf16[32,3584]{1,0:T(8,128)(2,1)S(1)} %collective-permute-done.12.refs_6_), channel_id=1, source_target_pairs={{4,0},{8,4},{12,8},{14,12},{10,14},{6,10},{2,6},{0,2},{5,1},{9,5},... | collective-permute-start | bytes 688136 | tf_op jit(solution)/shard_map/ppermute | solution.py:407
  65.6 7.4 %collective-permute-start.19 = (bf16[32,3584]{1,0:T(8,128)(2,1)S(1)}, bf16[32,3584]{1,0:T(8,128)(2,1)S(1)}, u32[]{:S(2)}, u32[]{:S(2)}) collective-permute-start(bf16[32,3584]{1,0:T(8,128)(2,1)S(1)} %get-tuple-element.159), channel_id=1, source_target_pairs={{0,4},{4,8},{8,12},{12,14},{14,10},{10,6},{6,2},{2,0},{1,5},{5,9},... | collective-permute-start | bytes 688136 | tf_op jit(solution)/shard_map/ppermute | solution.py:427
  74.4 8.5 %collective-permute-start.24 = (bf16[32,3584]{1,0:T(8,128)(2,1)S(1)}, bf16[32,3584]{1,0:T(8,128)(2,1)S(1)}, u32[]{:S(2)}, u32[]{:S(2)}) collective-permute-start(bf16[32,3584]{1,0:T(8,128)(2,1)S(1)} %get-tuple-element.170), channel_id=1, source_target_pairs={{0,4},{4,8},{8,12},{12,14},{14,10},{10,6},{6,2},{2,0},{1,5},{5,9},... | collective-permute-start | bytes 688136 | tf_op jit(solution)/shard_map/ppermute | solution.py:427
  76.0 8.4 %collective-permute-start.25 = (bf16[32,3584]{1,0:T(8,128)(2,1)S(1)}, bf16[32,3584]{1,0:T(8,128)(2,1)S(1)}, u32[]{:S(2)}, u32[]{:S(2)}) collective-permute-start(bf16[32,3584]{1,0:T(8,128)(2,1)S(1)} %get-tuple-element.171), channel_id=1, source_target_pairs={{4,0},{8,4},{12,8},{14,12},{10,14},{6,10},{2,6},{0,2},{5,1},{9,5},... | collective-permute-start | bytes 688136 | tf_op jit(solution)/shard_map/ppermute | solution.py:427
  77.4 8.4 %collective-permute-start.22 = (bf16[16,3584]{1,0:T(8,128)(2,1)S(1)}, bf16[16,3584]{1,0:T(8,128)(2,1)S(1)}, u32[]{:S(2)}, u32[]{:S(2)}) collective-permute-start(bf16[16,3584]{1,0:T(8,128)(2,1)S(1)} %get-tuple-element.164), channel_id=1, source_target_pairs={{0,4},{4,8},{8,12},{12,14},{14,10},{10,6},{6,2},{2,0},{1,5},{5,9},... | collective-permute-start | bytes 344072 | tf_op jit(solution)/shard_map/ppermute | solution.py:427
  79.0 7.2 %collective-permute-start.23 = (bf16[16,3584]{1,0:T(8,128)(2,1)S(1)}, bf16[16,3584]{1,0:T(8,128)(2,1)S(1)}, u32[]{:S(2)}, u32[]{:S(2)}) collective-permute-start(bf16[16,3584]{1,0:T(8,128)(2,1)S(1)} %get-tuple-element.165), channel_id=1, source_target_pairs={{4,0},{8,4},{12,8},{14,12},{10,14},{6,10},{2,6},{0,2},{5,1},{9,5},... | collective-permute-start | bytes 344072 | tf_op jit(solution)/shard_map/ppermute | solution.py:427
  86.3 8.8 %collective-permute-start.26 = (bf16[32,3584]{1,0:T(8,128)(2,1)S(1)}, bf16[32,3584]{1,0:T(8,128)(2,1)S(1)}, u32[]{:S(2)}, u32[]{:S(2)}) collective-permute-start(bf16[32,3584]{1,0:T(8,128)(2,1)S(1)} %get-tuple-element.177), channel_id=1, source_target_pairs={{0,4},{4,8},{8,12},{12,14},{14,10},{10,6},{6,2},{2,0},{1,5},{5,9},... | collective-permute-start | bytes 688136 | tf_op jit(solution)/shard_map/ppermute | solution.py:427
  87.8 8.5 %collective-permute-start.27 = (bf16[32,3584]{1,0:T(8,128)(2,1)S(1)}, bf16[32,3584]{1,0:T(8,128)(2,1)S(1)}, u32[]{:S(2)}, u32[]{:S(2)}) collective-permute-start(bf16[32,3584]{1,0:T(8,128)(2,1)S(1)} %get-tuple-element.178), channel_id=1, source_target_pairs={{4,0},{8,4},{12,8},{14,12},{10,14},{6,10},{2,6},{0,2},{5,1},{9,5},... | collective-permute-start | bytes 688136 | tf_op jit(solution)/shard_map/ppermute | solution.py:427
  88.9 15.8 %collective-permute-start.32 = (bf16[32,3584]{1,0:T(8,128)(2,1)S(1)}, bf16[32,3584]{1,0:T(8,128)(2,1)S(1)}, u32[]{:S(2)}, u32[]{:S(2)}) collective-permute-start(bf16[32,3584]{1,0:T(8,128)(2,1)S(1)} %get-tuple-element.198), channel_id=1, source_target_pairs={{0,4},{4,8},{8,12},{12,14},{14,10},{10,6},{6,2},{2,0},{1,5},{5,9},... | collective-permute-start | bytes 688136 | tf_op jit(solution)/shard_map/ppermute | solution.py:427
  90.0 14.6 %collective-permute-start.33 = (bf16[32,3584]{1,0:T(8,128)(2,1)S(1)}, bf16[32,3584]{1,0:T(8,128)(2,1)S(1)}, u32[]{:S(2)}, u32[]{:S(2)}) collective-permute-start(bf16[32,3584]{1,0:T(8,128)(2,1)S(1)} %get-tuple-element.199), channel_id=1, source_target_pairs={{4,0},{8,4},{12,8},{14,12},{10,14},{6,10},{2,6},{0,2},{5,1},{9,5},... | collective-permute-start | bytes 688136 | tf_op jit(solution)/shard_map/ppermute | solution.py:427
  96.5 8.2 %collective-permute-start.29 = (bf16[32,3584]{1,0:T(8,128)(2,1)S(1)}, bf16[32,3584]{1,0:T(8,128)(2,1)S(1)}, u32[]{:S(2)}, u32[]{:S(2)}) collective-permute-start(bf16[32,3584]{1,0:T(8,128)(2,1)S(1)} %get-tuple-element.191), channel_id=1, source_target_pairs={{0,4},{4,8},{8,12},{12,14},{14,10},{10,6},{6,2},{2,0},{1,5},{5,9},... | collective-permute-start | bytes 688136 | tf_op jit(solution)/shard_map/ppermute | solution.py:427
  97.6 7.0 %collective-permute-start.30 = (bf16[32,3584]{1,0:T(8,128)(2,1)S(1)}, bf16[32,3584]{1,0:T(8,128)(2,1)S(1)}, u32[]{:S(2)}, u32[]{:S(2)}) collective-permute-start(bf16[32,3584]{1,0:T(8,128)(2,1)S(1)} %get-tuple-element.192), channel_id=1, source_target_pairs={{4,0},{8,4},{12,8},{14,12},{10,14},{6,10},{2,6},{0,2},{5,1},{9,5},... | collective-permute-start | bytes 688136 | tf_op jit(solution)/shard_map/ppermute | solution.py:427
  (22 other events, 164.0 us)

commit v7 on v6

--- a/solution.py
+++ b/solution.py
@@ -201,22 +201,24 @@
         pre_up = mm(rows_ref[...], up_ref[:, cols]) + adapter_scale * mm(
             low_up_ref[...], up_b_ref[:, cols]
         )
-        slope_ref[:, cols] = slope_ref[:, cols] * pre_up
-        inner_ref[:, cols] = (active_ref[:, cols] * pre_up).astype(bf16)
+        keep = jnp.concatenate([keep_ref[...]] * (tile // LANES), axis=1)
+        active = keep * active_ref[:, cols]
+        active_ref[:, cols] = active
+        slope_ref[:, cols] = slope_ref[:, cols] * (keep * pre_up)
+        inner_ref[:, cols] = (active * pre_up).astype(bf16)
 
 
 def routed_kernel(
-    tiles, inner_ref, keep_ref, down_ref, down_a_ref, down_b_ref, kept_ref, sent_ref, low_down_ref
+    tiles, inner_ref, down_ref, down_a_ref, down_b_ref, kept_ref, sent_ref, low_down_ref
 ):
     half, tile = kept_ref.shape[0], down_ref.shape[1] // tiles
     low_down_ref[...] = mm_nt(inner_ref[...], down_a_ref[...]).astype(bf16)
-    keep = keep_ref[:, :1]
     for j in range(tiles):
         cols = slice(j * tile, (j + 1) * tile)
         value = mm(inner_ref[...], down_ref[:, cols]) + adapter_scale * mm(
             low_down_ref[...], down_b_ref[:, cols]
         )
-        value = (keep * value).astype(bf16)
+        value = value.astype(bf16)
         kept_ref[:, cols] = value[:half]
         sent_ref[:, cols] = value[half:]
 
@@ -276,13 +278,12 @@
 
 
 def inner_grad_kernel(
-    tiles, kept_ref, came_ref, keep_ref, down_ref, down_b_ref, down_a_ref, slope_ref, active_ref,
+    tiles, kept_ref, came_ref, down_ref, down_b_ref, down_a_ref, slope_ref, active_ref,
     up_b_ref, grad_ref, gate_out_ref, up_out_ref, back_low_ref, back_up_ref,
 ):
     half, tile = kept_ref.shape[0], down_ref.shape[0] // tiles
-    keep = keep_ref[:, :1].astype(bf16)
-    grad_ref[:half] = kept_ref[...] * keep[:half]
-    grad_ref[half:] = came_ref[...] * keep[half:]
+    grad_ref[:half] = kept_ref[...]
+    grad_ref[half:] = came_ref[...]
     back_low_ref[...] = mm_nt(grad_ref[...], down_b_ref[...]).astype(bf16)
     for j in range(tiles):
         cols = slice(j * tile, (j + 1) * tile)
@@ -324,6 +325,12 @@
         down_b_ref[:, cols] = scaled(mm_tn(low_down_ref[...], grad_ref[:, cols]))
     up_b_ref[...] = scaled(mm_tn(low_up_ref[...], grad_up_ref[...]))
     down_a_ref[...] = scaled(mm_tn(back_low_ref[...], inner_ref[...]))
+
+
+def halves_kernel(behind_ref, front_ref, top_ref, low_ref):
+    rows = top_ref.shape[0]
+    top_ref[...] = behind_ref[:rows]
+    low_ref[...] = front_ref[rows:]
 
 
 def hop_kernel(front_ref, forth_ref, rear_ref, hither_ref, front_out_ref, rear_out_ref):
@@ -408,9 +415,19 @@
         if len(near) < self.half:
             near.append(lax.ppermute(near[-1], "expert", self.near))
 
-    def gathered(self, far, near):
+    def last_hop(self, far, near):
+        ahead, back = (self.far, self.near) if self.far_ahead else (self.near, self.far)
         behind, front = (far, near) if self.far_ahead else (near, far)
-        return behind[: self.half] + front[1 : self.half] + [far[self.half]]
+        rows, columns = far[-1].shape
+        top, low = call(
+            halves_kernel, [struct((rows // 2, columns))] * 2, [in_vmem] * 2,
+            (behind[-1], front[-1]), (0, nbytes([far[-1]])),
+        )
+        return lax.ppermute(top, "expert", ahead), lax.ppermute(low, "expert", back)
+
+    def gathered(self, far, near, *opposite):
+        behind, front = (far, near) if self.far_ahead else (near, far)
+        return behind[: self.half] + front[1 : self.half] + list(opposite or [far[self.half]])
 
 
 def scatter_hop(parts, count, came, step):
@@ -508,6 +525,7 @@
         tok_far, tok_near = [token_load], [token_load]
         ring_token.gather_hop(tok_far, tok_near)
         cot_far, cot_near = [cotangent], [cotangent]
+        tok_near[-1], info = tie(tok_near[-1], info)
         ring_token.gather_hop(tok_far, tok_near)
         ring_cot.gather_hop(cot_far, cot_near)
         for hop in range(2, hops):
@@ -530,38 +548,38 @@
         sent, cot_far[-1], cot_near[-1] = tie(sent, cot_far[-1], cot_near[-1])
         came = swap_cores(sent)
         ring_cot.gather_hop(cot_far, cot_near)
-        inner, slope, active, low_up, keep = call(
+        inner, slope, active, low_up = call(
             functools.partial(inner_kernel, count, tiles),
             [
                 struct((slots, hidden)), struct((slots, hidden), f32), struct((slots, hidden), f32),
-                struct((slots, rank)), struct((slots, LANES), f32),
+                struct((slots, rank)),
             ],
             [in_smem] + [in_vmem] * 5 + [in_hbm],
             (info, kept, came, gate_v, up_a_v, up_b_v, *stay(up_w)),
             (4 * slots * width * hidden, 2 * nbytes([gate_w])),
             scratch=[
-                pltpu.VMEM((slots, width), bf16), pltpu.VMEM(up_w.shape, bf16),
+                pltpu.VMEM((slots, LANES), f32), pltpu.VMEM((slots, width), bf16),
+                pltpu.VMEM(up_w.shape, bf16),
                 pltpu.SemaphoreType.DMA((1,)),
             ],
             mib=16,
         )
         inner, cot_far[-1], cot_near[-1] = tie(inner, cot_far[-1], cot_near[-1])
-        while len(cot_far) <= hops:
-            ring_cot.gather_hop(cot_far, cot_near)
+        cot_top, cot_low = ring_cot.last_hop(cot_far, cot_near)
         routed_kept, routed_sent, low_down = call(
             functools.partial(routed_kernel, tiles),
             [struct((half, width))] * 2 + [struct((slots, rank))],
-            [in_vmem] * 5,
-            (inner, keep, down_w, down_a, down_b),
+            [in_vmem] * 4,
+            (inner, down_w, down_a, down_b),
             (2 * slots * width * hidden, nbytes([gate_w])),
         )
-        routed_sent, high, cot_far[-1] = tie(routed_sent, high, cot_far[-1])
+        routed_sent, high, cot_top, cot_low = tie(routed_sent, high, cot_top, cot_low)
         routed_came = swap_cores(routed_sent)
-        cot_blocks = ring_cot.gathered(cot_far, cot_near)
+        cot_blocks = ring_cot.gathered(cot_far, cot_near, cot_top, cot_low)
         cot_kept, cot_sent, cot_all = call(
             cot_slots_kernel,
             [struct((half, width))] * 2 + [struct((toks, width))],
-            [in_vmem] * (count + 2),
+            [in_vmem] * (count + 3),
             (high, low, *cot_blocks),
             (4 * slots * toks * load, 2 * count * nbytes([token_load])),
         )
@@ -583,8 +601,8 @@
         grad_routed, grad_gate, grad_up, back_low, back_up = call(
             functools.partial(inner_grad_kernel, tiles),
             [struct((slots, width))] + [struct((slots, hidden))] * 2 + [struct((slots, rank))] * 2,
-            [in_vmem] * 9,
-            (cot_kept, cot_came, keep, down_w, down_b, down_a, slope, active, up_b_v),
+            [in_vmem] * 8,
+            (cot_kept, cot_came, down_w, down_b, down_a, slope, active, up_b_v),
             (2 * slots * width * hidden, nbytes([gate_w])),
         )
         grad_up, *mix_came[0] = tie(grad_up, *mix_came[0])

time: 114 us -> 112 us (0.982)
  waiting for transfers between devices: 39.9 us -> 38.4 us
    ppermute x8 -> x7, waiting for transfers between devices: 19 us -> 16.3 us  [gather_hop(): far.append(lax.ppermute(far[-1], 'expert', self.far))]
    ppermute x0 -> x2, starting transfers between devices: none -> 2.08 us  [the longest x1 1.18 us: last_hop(): lax.ppermute(top, 'expert', ahead)]
    ppermute x8 -> x7, starting transfers between devices: 11.3 us -> 9.99 us  [gather_hop(): far.append(lax.ppermute(far[-1], 'expert', self.far))]
    pallas_call x21 -> x22, Pallas kernels: 34.9 us -> 34.8 us  [call(): pl.pallas_call(body, out_shape=outs, in_specs=specs, out_specs=out_specs...]
  transfers between devices with their start and end apart: 38 -> 39, of which waited for: 20 -> 21; matrix products, arithmetic and copies ran while one was open for 1% -> 1% of each run, Pallas kernels for 29% -> 30%
where the time goes in v7:
time: 112 us
  waiting for transfers between devices  38.4 us (34%)
  starting transfers between devices  35.9 us (32%)
  Pallas kernels  34.8 us (31%)
  between operations  1.56 us (1%)
  other arithmetic  1.51 us (1%)
    pallas_call x22, Pallas kernels, call(): pl.pallas_call(body, out_shape=outs, in_specs=specs, out_specs=out_specs...  34.8 us
    ppermute x7, waiting for transfers between devices, gather_hop(): far.append(lax.ppermute(far[-1], 'expert', self.far))  16.3 us
    ppermute x3, waiting for transfers between devices, double(): lax.ppermute(gathered, 'expert', [(i, i ^ step) for i in range(size)])  10.1 us
    ppermute x7, starting transfers between devices, gather_hop(): far.append(lax.ppermute(far[-1], 'expert', self.far))  9.99 us
    ppermute x8, starting transfers between devices, scatter_hop(): lax.ppermute(front, 'expert', ahead)  9.8 us
    ppermute x8, starting transfers between devices, scatter_hop(): lax.ppermute(rear, 'expert', back)  6.79 us
    ppermute x8, waiting for transfers between devices, scatter_hop(): lax.ppermute(rear, 'expert', back)  4.96 us
    ppermute x6, starting transfers between devices, gather_hop(): near.append(lax.ppermute(near[-1], 'expert', self.near))  4.6 us
  transfers between devices with their start and end apart: 39, of which 21 were waited for; matrix products, arithmetic and copies ran while one was open for 1% of the time, Pallas kernels for 30%

profile of v7, /device:TPU:0, one launch (start us, length us, event | category | flops | bytes accessed | tf_op | source)
XLA Modules:
  0.0 112.3 jit_solution(13586508015329367851)
XLA Ops:
  2.0 3.1 %collective-permute-start.3 = (bf16[32,3712]{1,0:T(8,128)(2,1)S(1)}, bf16[32,3712]{1,0:T(8,128)(2,1)S(1)}, u32[]{:S(2)}, u32[]{:S(2)}) collective-permute-start(bf16[32,3712]{1,0:T(8,128)(2,1)S(1)} %shard_map.180.refs_1_), channel_id=1, source_target_pairs={{0,4},{4,8},{8,12},{12,14},{14,10},{10,6},{6,2},{2,0},{1,5},{5,9},... | collective-permute-start | bytes 712712 | tf_op jit(solution)/shard_map/ppermute | solution.py:414
  5.1 5.7 %collective-permute-done.3.refs_2_ = bf16[32,3712]{1,0:T(8,128)(2,1)S(1)} collective-permute-done((bf16[32,3712]{1,0:T(8,128)(2,1)S(1)}, bf16[32,3712]{1,0:T(8,128)(2,1)S(1)}, u32[]{:S(2)}, u32[]{:S(2)}) %collective-permute-start.3) | collective-permute-done | bytes 237600 | tf_op jit(solution)/shard_map/ppermute | solution.py:414
  10.8 1.8 %collective-permute-start.4 = (bf16[32,3712]{1,0:T(8,128)(2,1)S(1)}, bf16[32,3712]{1,0:T(8,128)(2,1)S(1)}, u32[]{:S(2)}, u32[]{:S(2)}) collective-permute-start(bf16[32,3712]{1,0:T(8,128)(2,1)S(1)} %collective-permute-done.3.refs_2_), channel_id=1, source_target_pairs={{0,4},{4,8},{8,12},{12,14},{14,10},{10,6},{6,2},{2,0},{1,5},{5,9},... | collective-permute-start | bytes 712712 | tf_op jit(solution)/shard_map/ppermute | solution.py:414
  14.4 3.4 %collective-permute-done.4.refs_3_ = bf16[32,3712]{1,0:T(8,128)(2,1)S(1)} collective-permute-done((bf16[32,3712]{1,0:T(8,128)(2,1)S(1)}, bf16[32,3712]{1,0:T(8,128)(2,1)S(1)}, u32[]{:S(2)}, u32[]{:S(2)}) %collective-permute-start.4) | collective-permute-done | bytes 237600 | tf_op jit(solution)/shard_map/ppermute | solution.py:414
  17.7 1.5 %collective-permute-start.5 = (bf16[32,3712]{1,0:T(8,128)(2,1)S(1)}, bf16[32,3712]{1,0:T(8,128)(2,1)S(1)}, u32[]{:S(2)}, u32[]{:S(2)}) collective-permute-start(bf16[32,3712]{1,0:T(8,128)(2,1)S(1)} %collective-permute-done.4.refs_3_), channel_id=1, source_target_pairs={{0,4},{4,8},{8,12},{12,14},{14,10},{10,6},{6,2},{2,0},{1,5},{5,9},... | collective-permute-start | bytes 712712 | tf_op jit(solution)/shard_map/ppermute | solution.py:414
  19.8 1.5 %collective-permute-start.7 = (bf16[32,3584]{1,0:T(8,128)(2,1)}, bf16[32,3584]{1,0:T(8,128)(2,1)S(1)}, u32[]{:S(2)}, u32[]{:S(2)}) collective-permute-start(bf16[32,3584]{1,0:T(8,128)(2,1)} %refs_0_.1), channel_id=1, source_target_pairs={{0,4},{4,8},{8,12},{12,14},{14,10},{10,6},{6,2},{2,0},{1,5},{5,9},... | collective-permute-start | bytes 688136 | tf_op jit(solution)/shard_map/ppermute | solution.py:416
  21.8 6.2 %collective-permute-done.6.refs_4_ = bf16[32,3584]{1,0:T(8,128)(2,1)S(1)} collective-permute-done((bf16[32,3584]{1,0:T(8,128)(2,1)}, bf16[32,3584]{1,0:T(8,128)(2,1)S(1)}, u32[]{:S(2)}, u32[]{:S(2)}) %collective-permute-start.6) | collective-permute-done | bytes 229408 | tf_op jit(solution)/shard_map/ppermute | solution.py:414
  32.1 3.1 %shard_map.181 = (bf16[3584,1024]{1,0:T(8,128)(2,1)S(1)}, bf16[64,3584]{1,0:T(8,128)(2,1)S(1)}, bf16[64,1024]{1,0:T(8,128)(2,1)S(1)}) custom-call(bf16[3584,1024]{1,0:T(8,128)(2,1)} %bitcast.40, bf16[64,3584]{1,0:T(8,128)(2,1)} %bitcast.41, bf16[64,1024]{1,0:T(8,128)(2,1)} %bitcast.42), custom_call_target="tpu_custom_call" | custom-call | bytes 7 | tf_op jit(solution)/shard_map/pallas_call | solution.py:40
  36.3 1.8 %shard_map.182 = (bf16[128,3712]{1,0:T(8,128)(2,1)S(1)}, bf16[128,3712]{1,0:T(8,128)(2,1)S(1)}, bf16[256,256]{1,0:T(8,128)(2,1)S(1)}, bf16[256,256]{1,0:T(8,128)...) custom-call(s32[12]{0:T(128)S(1)} %concatenate.12.info_ref, ...), custom_call_target="tpu_custom_call" | custom-call | flops 486 | bytes 3 | tf_op jit(solution)/shard_map/pallas_call | solution.py:40
  41.2 6.5 %shard_map.183 = (bf16[256,1024]{1,0:T(8,128)(2,1)S(1)}, f32[256,1024]{1,0:T(8,128)S(1)}, f32[256,1024]{1,0:T(8,128)S(1)}, bf16[256,64]{1,0:T(8,128)(2,1)S(1)}) custom-call(s32[12]{0:T(128)S(1)} %concatenate.12.info_ref, bf16[128,3712]{1,0:T(8,128)(2,1)S(1)} %get-tuple-element.122.kept_ref, bf16[128,3712]{1,0:T(8,128)(2,1)S(1)} %collective-permute-done.11.came_ref, ...), custom_call_target="tpu_custom_call" | custom-call | flops 3758 | bytes 14 | tf_op jit(solution)/shard_map/pallas_call | solution.py:40
  49.9 3.4 %shard_map.184 = (bf16[128,3584]{1,0:T(8,128)(2,1)S(1)}, bf16[128,3584]{1,0:T(8,128)(2,1)S(1)}, bf16[256,64]{1,0:T(8,128)(2,1)S(1)}) custom-call(bf16[256,1024]{1,0:T(8,128)(2,1)S(1)} %get-tuple-element.132.inner_ref, bf16[1024,3584]{1,0:T(8,128)(2,1)S(1)} %bitcast.32, bf16[64,1024]{1,0:T(8,128)(2,1)S(1)} %bitcast.36, bf16[64,3584]{1,0:T(8,128)(2,1)S(1)} %bitcast.34), custom_call_target="tpu_custom_call" | custom-call | flops 1879 | bytes 7 | tf_op jit(solution)/shard_map/pallas_call | solution.py:40
  59.7 4.0 %shard_map.188 = (bf16[256,3584]{1,0:T(8,128)(2,1)S(1)}, bf16[256,1024]{1,0:T(8,128)(2,1)S(1)}, bf16[256,1024]{1,0:T(8,128)(2,1)S(1)}, bf16[256,64]{1,0:T(8,128)(2,1)S(1)}, bf16[256,64]{1,0:T(8,128)(2,1)S(1)}) custom-call(bf16[128,3584]{1,0:T(8,128)(2,1)S(1)} %get-tuple-element.149.kept_ref, bf16[128,3584]{1,0:T(8,128)(2,1)S(1)} %collective-permute-done.17.came_ref, ...), custom_call_target="tpu_custom_call" | custom-call | flops 1879 | bytes 7 | tf_op jit(solution)/shard_map/pallas_call | solution.py:40
  63.8 1.6 %collective-permute-start.20 = (bf16[32,3584]{1,0:T(8,128)(2,1)S(1)}, bf16[32,3584]{1,0:T(8,128)(2,1)S(1)}, u32[]{:S(2)}, u32[]{:S(2)}) collective-permute-start(bf16[32,3584]{1,0:T(8,128)(2,1)S(1)} %get-tuple-element.167), channel_id=1, source_target_pairs={{0,4},{4,8},{8,12},{12,14},{14,10},{10,6},{6,2},{2,0},{1,5},{5,9},... | collective-permute-start | bytes 688136 | tf_op jit(solution)/shard_map/ppermute | solution.py:444
  65.9 5.1 %shard_map.189 = (bf16[128,3584]{1,0:T(8,128)(2,1)S(1)}, bf16[128,3584]{1,0:T(8,128)(2,1)S(1)}) custom-call(bf16[256,1024]{1,0:T(8,128)(2,1)S(1)} %get-tuple-element.155.grad_gate_ref, bf16[256,1024]{1,0:T(8,128)(2,1)S(1)} %get-tuple-element.159.grad_up_ref, bf16[256,64]{1,0:T(8,128)(2,1)S(1)} %get-tuple-element.187.back_up_ref, ...), custom_call_target="tpu_custom_call" | custom-call | flops 3758 | bytes 14 | tf_op jit(solution)/shard_map/pallas_call | solution.py:40
  72.6 1.6 %collective-permute-start.25 = (bf16[32,3584]{1,0:T(8,128)(2,1)S(1)}, bf16[32,3584]{1,0:T(8,128)(2,1)S(1)}, u32[]{:S(2)}, u32[]{:S(2)}) collective-permute-start(bf16[32,3584]{1,0:T(8,128)(2,1)S(1)} %get-tuple-element.178), channel_id=1, source_target_pairs={{0,4},{4,8},{8,12},{12,14},{14,10},{10,6},{6,2},{2,0},{1,5},{5,9},... | collective-permute-start | bytes 688136 | tf_op jit(solution)/shard_map/ppermute | solution.py:444
  75.6 1.6 %collective-permute-start.23 = (bf16[16,3584]{1,0:T(8,128)(2,1)S(1)}, bf16[16,3584]{1,0:T(8,128)(2,1)S(1)}, u32[]{:S(2)}, u32[]{:S(2)}) collective-permute-start(bf16[16,3584]{1,0:T(8,128)(2,1)S(1)} %get-tuple-element.172), channel_id=1, source_target_pairs={{0,4},{4,8},{8,12},{12,14},{14,10},{10,6},{6,2},{2,0},{1,5},{5,9},... | collective-permute-start | bytes 344072 | tf_op jit(solution)/shard_map/ppermute | solution.py:444
  77.7 3.3 %collective-permute-done.25.forth_ref = bf16[32,3584]{1,0:T(8,128)(2,1)S(1)} collective-permute-done((bf16[32,3584]{1,0:T(8,128)(2,1)S(1)}, bf16[32,3584]{1,0:T(8,128)(2,1)S(1)}, u32[]{:S(2)}, u32[]{:S(2)}) %collective-permute-start.25) | collective-permute-done | bytes 229408 | tf_op jit(solution)/shard_map/ppermute | solution.py:444
  81.1 1.6 %collective-permute-done.26.hither_ref = bf16[32,3584]{1,0:T(8,128)(2,1)S(1)} collective-permute-done((bf16[32,3584]{1,0:T(8,128)(2,1)S(1)}, bf16[32,3584]{1,0:T(8,128)(2,1)S(1)}, u32[]{:S(2)}, u32[]{:S(2)}) %collective-permute-start.26) | collective-permute-done | bytes 229408 | tf_op jit(solution)/shard_map/ppermute | solution.py:444
  84.5 1.6 %collective-permute-start.27 = (bf16[32,3584]{1,0:T(8,128)(2,1)S(1)}, bf16[32,3584]{1,0:T(8,128)(2,1)S(1)}, u32[]{:S(2)}, u32[]{:S(2)}) collective-permute-start(bf16[32,3584]{1,0:T(8,128)(2,1)S(1)} %get-tuple-element.185), channel_id=1, source_target_pairs={{0,4},{4,8},{8,12},{12,14},{14,10},{10,6},{6,2},{2,0},{1,5},{5,9},... | collective-permute-start | bytes 688136 | tf_op jit(solution)/shard_map/ppermute | solution.py:444
  89.2 1.8 %shard_map.195 = (bf16[64,3584]{1,0:T(8,128)(2,1)}, bf16[64,1024]{1,0:T(8,128)(2,1)}, bf16[64,1024]{1,0:T(8,128)(2,1)}, bf16[64,3584]{1,0:T(8,128)(2,1)}) custom-call(bf16[128,3712]{1,0:T(8,128)(2,1)S(1)} %get-tuple-element.122.kept_ref, bf16[128,3712]{1,0:T(8,128)(2,1)S(1)} %collective-permute-done.11.came_ref, ...), custom_call_target="tpu_custom_call" | custom-call | flops 469 | bytes 7 | tf_op jit(solution)/shard_map/pallas_call | solution.py:40
  91.0 2.3 %collective-permute-done.29 = bf16[1,16,256]{2,1,0:T(8,128)(2,1)S(1)} collective-permute-done((bf16[1,16,256]{2,1,0:T(8,128)(2,1)S(1)}, bf16[1,16,256]{2,1,0:T(8,128)(2,1)S(1)}, u32[]{:S(2)}, u32[]{:S(2)}) %collective-permute-start.29) | collective-permute-done | bytes 8224 | tf_op jit(solution)/shard_map/ppermute | solution.py:449
  97.5 5.4 %collective-permute-done.32 = bf16[2,16,256]{2,1,0:T(8,128)(2,1)S(1)} collective-permute-done((bf16[2,16,256]{2,1,0:T(8,128)(2,1)S(1)}, bf16[2,16,256]{2,1,0:T(8,128)(2,1)S(1)}, u32[]{:S(2)}, u32[]{:S(2)}) %collective-permute-start.32) | collective-permute-done | bytes 16416 | tf_op jit(solution)/shard_map/ppermute | solution.py:449
  104.3 1.7 %collective-permute-start.36 = (bf16[32,3584]{1,0:T(8,128)(2,1)S(1)}, bf16[32,3584]{1,0:T(8,128)(2,1)S(1)}, u32[]{:S(2)}, u32[]{:S(2)}) collective-permute-start(bf16[32,3584]{1,0:T(8,128)(2,1)S(1)} %get-tuple-element.216), channel_id=1, source_target_pairs={{4,0},{8,4},{12,8},{14,12},{10,14},{6,10},{2,6},{0,2},{5,1},{9,5},... | collective-permute-start | bytes 688136 | tf_op jit(solution)/shard_map/ppermute | solution.py:444
  106.0 2.4 %collective-permute-done.37 = bf16[4,16,256]{2,1,0:T(8,128)(2,1)S(1)} collective-permute-done((bf16[4,16,256]{2,1,0:T(8,128)(2,1)S(1)}, bf16[4,16,256]{2,1,0:T(8,128)(2,1)S(1)}, u32[]{:S(2)}, u32[]{:S(2)}) %collective-permute-start.37) | collective-permute-done | bytes 32800 | tf_op jit(solution)/shard_map/ppermute | solution.py:449
  (101 shorter events, 38.7 us)
Async XLA Ops:
  2.0 8.8 %collective-permute-start.3 = (bf16[32,3712]{1,0:T(8,128)(2,1)S(1)}, bf16[32,3712]{1,0:T(8,128)(2,1)S(1)}, u32[]{:S(2)}, u32[]{:S(2)}) collective-permute-start(bf16[32,3712]{1,0:T(8,128)(2,1)S(1)} %shard_map.180.refs_1_), channel_id=1, source_target_pairs={{0,4},{4,8},{8,12},{12,14},{14,10},{10,6},{6,2},{2,0},{1,5},{5,9},... | collective-permute-start | bytes 712712 | tf_op jit(solution)/shard_map/ppermute | solution.py:414
  5.0 9.1 %collective-permute-start = (bf16[32,3712]{1,0:T(8,128)(2,1)S(1)}, bf16[32,3712]{1,0:T(8,128)(2,1)S(1)}, u32[]{:S(2)}, u32[]{:S(2)}) collective-permute-start(bf16[32,3712]{1,0:T(8,128)(2,1)S(1)} %shard_map.180.refs_1_), channel_id=1, source_target_pairs={{4,0},{8,4},{12,8},{14,12},{10,14},{6,10},{2,6},{0,2},{5,1},{9,5},... | collective-permute-start | bytes 712712 | tf_op jit(solution)/shard_map/ppermute | solution.py:416
  14.1 7.1 %collective-permute-start.1 = (bf16[32,3712]{1,0:T(8,128)(2,1)S(1)}, bf16[32,3712]{1,0:T(8,128)(2,1)S(1)}, u32[]{:S(2)}, u32[]{:S(2)}) collective-permute-start(bf16[32,3712]{1,0:T(8,128)(2,1)S(1)} %collective-permute-done.refs_5_), channel_id=1, source_target_pairs={{4,0},{8,4},{12,8},{14,12},{10,14},{6,10},{2,6},{0,2},{5,1},{9,5},... | collective-permute-start | bytes 712712 | tf_op jit(solution)/shard_map/ppermute | solution.py:416
  17.7 11.0 %collective-permute-start.5 = (bf16[32,3712]{1,0:T(8,128)(2,1)S(1)}, bf16[32,3712]{1,0:T(8,128)(2,1)S(1)}, u32[]{:S(2)}, u32[]{:S(2)}) collective-permute-start(bf16[32,3712]{1,0:T(8,128)(2,1)S(1)} %collective-permute-done.4.refs_3_), channel_id=1, source_target_pairs={{0,4},{4,8},{8,12},{12,14},{14,10},{10,6},{6,2},{2,0},{1,5},{5,9},... | collective-permute-start | bytes 712712 | tf_op jit(solution)/shard_map/ppermute | solution.py:414
  19.2 8.7 %collective-permute-start.6 = (bf16[32,3584]{1,0:T(8,128)(2,1)}, bf16[32,3584]{1,0:T(8,128)(2,1)S(1)}, u32[]{:S(2)}, u32[]{:S(2)}) collective-permute-start(bf16[32,3584]{1,0:T(8,128)(2,1)} %refs_0_.1), channel_id=1, source_target_pairs={{4,0},{8,4},{12,8},{14,12},{10,14},{6,10},{2,6},{0,2},{5,1},{9,5},... | collective-permute-start | bytes 688136 | tf_op jit(solution)/shard_map/ppermute | solution.py:414
  19.8 8.9 %collective-permute-start.7 = (bf16[32,3584]{1,0:T(8,128)(2,1)}, bf16[32,3584]{1,0:T(8,128)(2,1)S(1)}, u32[]{:S(2)}, u32[]{:S(2)}) collective-permute-start(bf16[32,3584]{1,0:T(8,128)(2,1)} %refs_0_.1), channel_id=1, source_target_pairs={{0,4},{4,8},{8,12},{12,14},{14,10},{10,6},{6,2},{2,0},{1,5},{5,9},... | collective-permute-start | bytes 688136 | tf_op jit(solution)/shard_map/ppermute | solution.py:416
  21.2 10.9 %collective-permute-start.2 = (bf16[32,3712]{1,0:T(8,128)(2,1)S(1)}, bf16[32,3712]{1,0:T(8,128)(2,1)S(1)}, u32[]{:S(2)}, u32[]{:S(2)}) collective-permute-start(bf16[32,3712]{1,0:T(8,128)(2,1)S(1)} %collective-permute-done.1.refs_6_), channel_id=1, source_target_pairs={{4,0},{8,4},{12,8},{14,12},{10,14},{6,10},{2,6},{0,2},{5,1},{9,5},... | collective-permute-start | bytes 712712 | tf_op jit(solution)/shard_map/ppermute | solution.py:416
  28.7 7.6 %collective-permute-start.8 = (bf16[32,3712]{1,0:T(8,128)(2,1)S(1)}, bf16[32,3712]{1,0:T(8,128)(2,1)S(1)}, u32[]{:S(2)}, u32[]{:S(2)}) collective-permute-start(bf16[32,3712]{1,0:T(8,128)(2,1)S(1)} %collective-permute-done.5.refs_4_), channel_id=1, source_target_pairs={{0,4},{4,8},{8,12},{12,14},{14,10},{10,6},{6,2},{2,0},{1,5},{5,9},... | collective-permute-start | bytes 712712 | tf_op jit(solution)/shard_map/ppermute | solution.py:414
  30.1 8.0 %collective-permute-start.9 = (bf16[32,3584]{1,0:T(8,128)(2,1)S(1)}, bf16[32,3584]{1,0:T(8,128)(2,1)S(1)}, u32[]{:S(2)}, u32[]{:S(2)}) collective-permute-start(bf16[32,3584]{1,0:T(8,128)(2,1)S(1)} %collective-permute-done.6.refs_4_), channel_id=1, source_target_pairs={{4,0},{8,4},{12,8},{14,12},{10,14},{6,10},{2,6},{0,2},{5,1},{9,5},... | collective-permute-start | bytes 688136 | tf_op jit(solution)/shard_map/ppermute | solution.py:414
  30.7 8.0 %collective-permute-start.10 = (bf16[32,3584]{1,0:T(8,128)(2,1)S(1)}, bf16[32,3584]{1,0:T(8,128)(2,1)S(1)}, u32[]{:S(2)}, u32[]{:S(2)}) collective-permute-start(bf16[32,3584]{1,0:T(8,128)(2,1)S(1)} %collective-permute-done.7.refs_1_), channel_id=1, source_target_pairs={{0,4},{4,8},{8,12},{12,14},{14,10},{10,6},{6,2},{2,0},{1,5},{5,9},... | collective-permute-start | bytes 688136 | tf_op jit(solution)/shard_map/ppermute | solution.py:416
  38.7 9.0 %collective-permute-start.12 = (bf16[32,3584]{1,0:T(8,128)(2,1)S(1)}, bf16[32,3584]{1,0:T(8,128)(2,1)S(1)}, u32[]{:S(2)}, u32[]{:S(2)}) collective-permute-start(bf16[32,3584]{1,0:T(8,128)(2,1)S(1)} %collective-permute-done.9.refs_5_), channel_id=1, source_target_pairs={{4,0},{8,4},{12,8},{14,12},{10,14},{6,10},{2,6},{0,2},{5,1},{9,5},... | collective-permute-start | bytes 688136 | tf_op jit(solution)/shard_map/ppermute | solution.py:414
  39.8 7.9 %collective-permute-start.13 = (bf16[32,3584]{1,0:T(8,128)(2,1)S(1)}, bf16[32,3584]{1,0:T(8,128)(2,1)S(1)}, u32[]{:S(2)}, u32[]{:S(2)}) collective-permute-start(bf16[32,3584]{1,0:T(8,128)(2,1)S(1)} %collective-permute-done.10.refs_2_), channel_id=1, source_target_pairs={{0,4},{4,8},{8,12},{12,14},{14,10},{10,6},{6,2},{2,0},{1,5},{5,9},... | collective-permute-start | bytes 688136 | tf_op jit(solution)/shard_map/ppermute | solution.py:416
  63.8 7.4 %collective-permute-start.20 = (bf16[32,3584]{1,0:T(8,128)(2,1)S(1)}, bf16[32,3584]{1,0:T(8,128)(2,1)S(1)}, u32[]{:S(2)}, u32[]{:S(2)}) collective-permute-start(bf16[32,3584]{1,0:T(8,128)(2,1)S(1)} %get-tuple-element.167), channel_id=1, source_target_pairs={{0,4},{4,8},{8,12},{12,14},{14,10},{10,6},{6,2},{2,0},{1,5},{5,9},... | collective-permute-start | bytes 688136 | tf_op jit(solution)/shard_map/ppermute | solution.py:444
  65.4 7.0 %collective-permute-start.21 = (bf16[32,3584]{1,0:T(8,128)(2,1)S(1)}, bf16[32,3584]{1,0:T(8,128)(2,1)S(1)}, u32[]{:S(2)}, u32[]{:S(2)}) collective-permute-start(bf16[32,3584]{1,0:T(8,128)(2,1)S(1)} %get-tuple-element.168), channel_id=1, source_target_pairs={{4,0},{8,4},{12,8},{14,12},{10,14},{6,10},{2,6},{0,2},{5,1},{9,5},... | collective-permute-start | bytes 688136 | tf_op jit(solution)/shard_map/ppermute | solution.py:444
  72.6 8.5 %collective-permute-start.25 = (bf16[32,3584]{1,0:T(8,128)(2,1)S(1)}, bf16[32,3584]{1,0:T(8,128)(2,1)S(1)}, u32[]{:S(2)}, u32[]{:S(2)}) collective-permute-start(bf16[32,3584]{1,0:T(8,128)(2,1)S(1)} %get-tuple-element.178), channel_id=1, source_target_pairs={{0,4},{4,8},{8,12},{12,14},{14,10},{10,6},{6,2},{2,0},{1,5},{5,9},... | collective-permute-start | bytes 688136 | tf_op jit(solution)/shard_map/ppermute | solution.py:444
  74.2 8.4 %collective-permute-start.26 = (bf16[32,3584]{1,0:T(8,128)(2,1)S(1)}, bf16[32,3584]{1,0:T(8,128)(2,1)S(1)}, u32[]{:S(2)}, u32[]{:S(2)}) collective-permute-start(bf16[32,3584]{1,0:T(8,128)(2,1)S(1)} %get-tuple-element.179), channel_id=1, source_target_pairs={{4,0},{8,4},{12,8},{14,12},{10,14},{6,10},{2,6},{0,2},{5,1},{9,5},... | collective-permute-start | bytes 688136 | tf_op jit(solution)/shard_map/ppermute | solution.py:444
  75.6 8.4 %collective-permute-start.23 = (bf16[16,3584]{1,0:T(8,128)(2,1)S(1)}, bf16[16,3584]{1,0:T(8,128)(2,1)S(1)}, u32[]{:S(2)}, u32[]{:S(2)}) collective-permute-start(bf16[16,3584]{1,0:T(8,128)(2,1)S(1)} %get-tuple-element.172), channel_id=1, source_target_pairs={{0,4},{4,8},{8,12},{12,14},{14,10},{10,6},{6,2},{2,0},{1,5},{5,9},... | collective-permute-start | bytes 344072 | tf_op jit(solution)/shard_map/ppermute | solution.py:444
  77.3 7.2 %collective-permute-start.24 = (bf16[16,3584]{1,0:T(8,128)(2,1)S(1)}, bf16[16,3584]{1,0:T(8,128)(2,1)S(1)}, u32[]{:S(2)}, u32[]{:S(2)}) collective-permute-start(bf16[16,3584]{1,0:T(8,128)(2,1)S(1)} %get-tuple-element.173), channel_id=1, source_target_pairs={{4,0},{8,4},{12,8},{14,12},{10,14},{6,10},{2,6},{0,2},{5,1},{9,5},... | collective-permute-start | bytes 344072 | tf_op jit(solution)/shard_map/ppermute | solution.py:444
  84.5 8.8 %collective-permute-start.27 = (bf16[32,3584]{1,0:T(8,128)(2,1)S(1)}, bf16[32,3584]{1,0:T(8,128)(2,1)S(1)}, u32[]{:S(2)}, u32[]{:S(2)}) collective-permute-start(bf16[32,3584]{1,0:T(8,128)(2,1)S(1)} %get-tuple-element.185), channel_id=1, source_target_pairs={{0,4},{4,8},{8,12},{12,14},{14,10},{10,6},{6,2},{2,0},{1,5},{5,9},... | collective-permute-start | bytes 688136 | tf_op jit(solution)/shard_map/ppermute | solution.py:444
  86.1 8.5 %collective-permute-start.28 = (bf16[32,3584]{1,0:T(8,128)(2,1)S(1)}, bf16[32,3584]{1,0:T(8,128)(2,1)S(1)}, u32[]{:S(2)}, u32[]{:S(2)}) collective-permute-start(bf16[32,3584]{1,0:T(8,128)(2,1)S(1)} %get-tuple-element.186), channel_id=1, source_target_pairs={{4,0},{8,4},{12,8},{14,12},{10,14},{6,10},{2,6},{0,2},{5,1},{9,5},... | collective-permute-start | bytes 688136 | tf_op jit(solution)/shard_map/ppermute | solution.py:444
  87.1 15.8 %collective-permute-start.33 = (bf16[32,3584]{1,0:T(8,128)(2,1)S(1)}, bf16[32,3584]{1,0:T(8,128)(2,1)S(1)}, u32[]{:S(2)}, u32[]{:S(2)}) collective-permute-start(bf16[32,3584]{1,0:T(8,128)(2,1)S(1)} %get-tuple-element.206), channel_id=1, source_target_pairs={{0,4},{4,8},{8,12},{12,14},{14,10},{10,6},{6,2},{2,0},{1,5},{5,9},... | collective-permute-start | bytes 688136 | tf_op jit(solution)/shard_map/ppermute | solution.py:444
  88.3 14.6 %collective-permute-start.34 = (bf16[32,3584]{1,0:T(8,128)(2,1)S(1)}, bf16[32,3584]{1,0:T(8,128)(2,1)S(1)}, u32[]{:S(2)}, u32[]{:S(2)}) collective-permute-start(bf16[32,3584]{1,0:T(8,128)(2,1)S(1)} %get-tuple-element.207), channel_id=1, source_target_pairs={{4,0},{8,4},{12,8},{14,12},{10,14},{6,10},{2,6},{0,2},{5,1},{9,5},... | collective-permute-start | bytes 688136 | tf_op jit(solution)/shard_map/ppermute | solution.py:444
  94.7 8.2 %collective-permute-start.30 = (bf16[32,3584]{1,0:T(8,128)(2,1)S(1)}, bf16[32,3584]{1,0:T(8,128)(2,1)S(1)}, u32[]{:S(2)}, u32[]{:S(2)}) collective-permute-start(bf16[32,3584]{1,0:T(8,128)(2,1)S(1)} %get-tuple-element.199), channel_id=1, source_target_pairs={{0,4},{4,8},{8,12},{12,14},{14,10},{10,6},{6,2},{2,0},{1,5},{5,9},... | collective-permute-start | bytes 688136 | tf_op jit(solution)/shard_map/ppermute | solution.py:444
  95.4 7.5 %collective-permute-start.31 = (bf16[32,3584]{1,0:T(8,128)(2,1)S(1)}, bf16[32,3584]{1,0:T(8,128)(2,1)S(1)}, u32[]{:S(2)}, u32[]{:S(2)}) collective-permute-start(bf16[32,3584]{1,0:T(8,128)(2,1)S(1)} %get-tuple-element.200), channel_id=1, source_target_pairs={{4,0},{8,4},{12,8},{14,12},{10,14},{6,10},{2,6},{0,2},{5,1},{9,5},... | collective-permute-start | bytes 688136 | tf_op jit(solution)/shard_map/ppermute | solution.py:444
  (23 other events, 169.0 us)

commit v8 on v7

--- a/solution.py
+++ b/solution.py
@@ -349,7 +349,10 @@
     ).astype(bf16)
 
 
-def input_grad_kernel(own_ref, forth_ref, hither_ref, term_ref, out_ref):
+def input_grad_kernel(
+    own_ref, forth_ref, hither_ref, term_ref, half_ref, came_ref, out_ref, router_ref
+):
+    router_ref[...] = half_ref[...] + came_ref[...]
     out_ref[...] = (
         own_ref[...].astype(f32)
         + forth_ref[...].astype(f32)
@@ -369,7 +372,8 @@
     gathered = jnp.concatenate([dots_ref[i] for i in range(count)], axis=0)
     gathered = mm_nt(gathered, token_places(count, info_ref, toks))
     for i in range(count):
-        name = 2 * (info_ref[0] ^ i)
+        far = sum(count >> (bit + 1) for bit in range(count.bit_length()) if i >> bit & 1)
+        name = 2 * (info_ref[0] ^ far)
         dots = gathered[i * dots_ref.shape[1] : (i + 1) * dots_ref.shape[1]]
         grad_gates = jnp.where(expert == name, dots[0:1] + dots[1:2], grad_gates)
         grad_gates = jnp.where(expert == name + 1, dots[2:3] + dots[3:4], grad_gates)
@@ -531,7 +535,7 @@
         for hop in range(2, hops):
             ring_token.gather_hop(tok_far, tok_near)
             if hop == hops - 2:
-                tok_far[-1], cot_far[1], cot_near[1] = tie(tok_far[-1], cot_far[1], cot_near[1])
+                tok_far[-1], cot_near[1] = tie(tok_far[-1], cot_near[1])
                 tok_near[-1], gate_late = tie(tok_near[-1], gate_w)
             if hop < hops - 1:
                 ring_cot.gather_hop(cot_far, cot_near)
@@ -567,7 +571,7 @@
         inner, cot_far[-1], cot_near[-1] = tie(inner, cot_far[-1], cot_near[-1])
         cot_top, cot_low = ring_cot.last_hop(cot_far, cot_near)
         routed_kept, routed_sent, low_down = call(
-            functools.partial(routed_kernel, tiles),
+            functools.partial(routed_kernel, width // (4 * LANES)),
             [struct((half, width))] * 2 + [struct((slots, rank))],
             [in_vmem] * 4,
             (inner, down_w, down_a, down_b),
@@ -608,13 +612,22 @@
         grad_up, *mix_came[0] = tie(grad_up, *mix_came[0])
         mix_came.append(scatter_hop(mix_parts, count, mix_came[0], 1))
         back_kept, back_sent = call(
-            functools.partial(row_grad_kernel, tiles),
+            functools.partial(row_grad_kernel, width // (4 * LANES)),
             [struct((half, width))] * 2,
             [in_vmem] * 6,
             (grad_gate, grad_up, back_up, gate_v, up_w, up_a_v),
             (4 * slots * width * hidden, 2 * nbytes([gate_w])),
         )
-        back_sent, *mix_came[1] = tie(back_sent, *mix_came[1])
+        routed_came, back_kept = tie(routed_came, back_kept)
+        (dots,) = call(
+            functools.partial(gate_grad_kernel, count),
+            [struct((1, 2 * 8, toks))],
+            [in_smem] + [in_vmem] * 4,
+            (info, select, routed_kept, routed_came, cot_all),
+            (2 * slots * toks * load, 2 * count * nbytes([token_load])),
+            scratch=[pltpu.VMEM((slots, width), bf16)],
+        )
+        back_sent, dots, *mix_came[1] = tie(back_sent, dots, *mix_came[1])
         back_came = swap_cores(back_sent)
         mix_came.append(scatter_hop(mix_parts, count, mix_came[1], 2))
         back_parts = call(
@@ -626,24 +639,16 @@
             scratch=[pltpu.VMEM((slots, width), bf16)],
         )
         back_parts = list(back_parts)
-        routed_came, *mix_came[2] = tie(routed_came, *mix_came[2])
         back_came = [scatter_hop(back_parts, count, None, 0)]
-        (dots,) = call(
-            functools.partial(gate_grad_kernel, count),
-            [struct((1, 2 * 8, toks))],
-            [in_smem] + [in_vmem] * 4,
-            (info, select, routed_kept, routed_came, cot_all),
-            (2 * slots * toks * load, 2 * count * nbytes([token_load])),
-            scratch=[pltpu.VMEM((slots, width), bf16)],
-        )
-        step = 1
+        dots, step = double(dots, count // 2), count // 4
         back_up_late = back_up
+        *back_came[0], mix2_far, mix2_near = tie(*back_came[0], *mix_came[2])
+        mix_came[2] = (mix2_far, mix2_near)
         for hop in range(1, hops):
             if hop + 2 < hops:
                 mix_came.append(scatter_hop(mix_parts, count, mix_came[-1], hop + 2))
             if hop == hops - 1:
-                tied = tie(*back_came[-1], back_up_late, dots, *mix_came[-1])
-                mix_came[-1] = tied[4:]
+                tied = tie(*back_came[-1], back_up_late, dots)
             else:
                 tied = tie(*back_came[-1], back_up_late, dots)
             back_came[-1], back_up_late, dots = tied[:2], tied[2], tied[3]
@@ -664,12 +669,12 @@
             if hop == 2:
                 *back_came[-1], adapters[1] = tie(*back_came[-1], adapters[1])
             back_came.append(scatter_hop(back_parts, count, back_came[-1], hop))
-            if step < count:
+            if step > 0:
                 dots = double(dots, step)
-                step *= 2
-        while step < count:
+                step //= 2
+        while step > 0:
             dots = double(dots, step)
-            step *= 2
+            step //= 2
         adapters = (adapters[0].T, adapters[1], adapters[2].T, adapters[3])
 
         (mixed,) = call(
@@ -687,15 +692,15 @@
             (info, dots, router, token_all),
             (0, count * nbytes([token_load])),
         )
-        router_grad = (router_half + swap_cores(router_half)).T
-        (input_grad,) = call(
+        input_grad, router_grad = call(
             input_grad_kernel,
-            [struct((tok_count, width))],
-            [in_vmem] * 4,
-            (back_parts[0], *back_came[-1], router_term),
+            [struct((tok_count, width)), struct((experts, width), f32)],
+            [in_vmem] * 6,
+            (back_parts[0], *back_came[-1], router_term, router_half, swap_cores(router_half)),
             (0, 4 * nbytes([token_load])),
-            out_specs=[pl.BlockSpec()],
-        )
+            out_specs=[pl.BlockSpec()] * 2,
+        )
+        router_grad = router_grad.T
         return (mixed, input_grad, router_grad) + tuple(value[None] for value in adapters)
 
     return per_device

time: 112 us -> 111 us (level)
  starting transfers between devices: 35.9 us -> 38.3 us
  waiting for transfers between devices: 38.4 us -> 36.1 us
    ppermute x7, waiting for transfers between devices: 16.3 us -> 9.41 us  [gather_hop(): far.append(lax.ppermute(far[-1], 'expert', self.far))]
    ppermute x6, waiting for transfers between devices: 1.38 us -> 8.23 us  [gather_hop(): near.append(lax.ppermute(near[-1], 'expert', self.near))]
    ppermute x8, waiting for transfers between devices: 4.96 us -> 1.56 us  [scatter_hop(): lax.ppermute(rear, 'expert', back)]
    ppermute x3, starting transfers between devices: 1.98 us -> 4.25 us  [double(): lax.ppermute(gathered, 'expert', [(i, i ^ step) for i in range(size)])]
    ppermute x3, waiting for transfers between devices: 10.1 us -> 12 us  [double(): lax.ppermute(gathered, 'expert', [(i, i ^ step) for i in range(size)])]
  transfers between devices with their start and end apart: 39 -> 39, of which waited for: 21 -> 18; matrix products, arithmetic and copies ran while one was open for 1% -> 1% of each run, Pallas kernels for 30% -> 28%
where the time goes in v8:
time: 111 us
  starting transfers between devices  38.3 us (35%)
  waiting for transfers between devices  36.1 us (33%)
  Pallas kernels  33.9 us (31%)
  between operations  1.57 us (1%)
    pallas_call x22, Pallas kernels, call(): pl.pallas_call(body, out_shape=outs, in_specs=specs, out_specs=out_specs...  33.9 us
    ppermute x3, waiting for transfers between devices, double(): lax.ppermute(gathered, 'expert', [(i, i ^ step) for i in range(size)])  12 us
    ppermute x7, starting transfers between devices, gather_hop(): far.append(lax.ppermute(far[-1], 'expert', self.far))  9.89 us
    ppermute x7, waiting for transfers between devices, gather_hop(): far.append(lax.ppermute(far[-1], 'expert', self.far))  9.41 us
    ppermute x8, starting transfers between devices, scatter_hop(): lax.ppermute(front, 'expert', ahead)  9.15 us
    ppermute x6, waiting for transfers between devices, gather_hop(): near.append(lax.ppermute(near[-1], 'expert', self.near))  8.23 us
    ppermute x8, starting transfers between devices, scatter_hop(): lax.ppermute(rear, 'expert', back)  7.54 us
    ppermute x6, starting transfers between devices, gather_hop(): near.append(lax.ppermute(near[-1], 'expert', self.near))  4.7 us
  transfers between devices with their start and end apart: 39, of which 18 were waited for; matrix products, arithmetic and copies ran while one was open for 1% of the time, Pallas kernels for 28%

profile of v8, /device:TPU:0, one launch (start us, length us, event | category | flops | bytes accessed | tf_op | source)
XLA Modules:
  0.0 110.8 jit_solution(12467535904247829937)
XLA Ops:
  2.0 3.1 %collective-permute-start.3 = (bf16[32,3712]{1,0:T(8,128)(2,1)S(1)}, bf16[32,3712]{1,0:T(8,128)(2,1)S(1)}, u32[]{:S(2)}, u32[]{:S(2)}) collective-permute-start(bf16[32,3712]{1,0:T(8,128)(2,1)S(1)} %shard_map.180.refs_1_), channel_id=1, source_target_pairs={{0,4},{4,8},{8,12},{12,14},{14,10},{10,6},{6,2},{2,0},{1,5},{5,9},... | collective-permute-start | bytes 712712 | tf_op jit(solution)/shard_map/ppermute | solution.py:418
  5.1 5.7 %collective-permute-done.3.refs_2_ = bf16[32,3712]{1,0:T(8,128)(2,1)S(1)} collective-permute-done((bf16[32,3712]{1,0:T(8,128)(2,1)S(1)}, bf16[32,3712]{1,0:T(8,128)(2,1)S(1)}, u32[]{:S(2)}, u32[]{:S(2)}) %collective-permute-start.3) | collective-permute-done | bytes 237600 | tf_op jit(solution)/shard_map/ppermute | solution.py:418
  10.8 1.8 %collective-permute-start.4 = (bf16[32,3712]{1,0:T(8,128)(2,1)S(1)}, bf16[32,3712]{1,0:T(8,128)(2,1)S(1)}, u32[]{:S(2)}, u32[]{:S(2)}) collective-permute-start(bf16[32,3712]{1,0:T(8,128)(2,1)S(1)} %collective-permute-done.3.refs_2_), channel_id=1, source_target_pairs={{0,4},{4,8},{8,12},{12,14},{14,10},{10,6},{6,2},{2,0},{1,5},{5,9},... | collective-permute-start | bytes 712712 | tf_op jit(solution)/shard_map/ppermute | solution.py:418
  14.4 3.4 %collective-permute-done.4.refs_3_ = bf16[32,3712]{1,0:T(8,128)(2,1)S(1)} collective-permute-done((bf16[32,3712]{1,0:T(8,128)(2,1)S(1)}, bf16[32,3712]{1,0:T(8,128)(2,1)S(1)}, u32[]{:S(2)}, u32[]{:S(2)}) %collective-permute-start.4) | collective-permute-done | bytes 237600 | tf_op jit(solution)/shard_map/ppermute | solution.py:418
  17.7 1.5 %collective-permute-start.5 = (bf16[32,3712]{1,0:T(8,128)(2,1)S(1)}, bf16[32,3712]{1,0:T(8,128)(2,1)S(1)}, u32[]{:S(2)}, u32[]{:S(2)}) collective-permute-start(bf16[32,3712]{1,0:T(8,128)(2,1)S(1)} %collective-permute-done.4.refs_3_), channel_id=1, source_target_pairs={{0,4},{4,8},{8,12},{12,14},{14,10},{10,6},{6,2},{2,0},{1,5},{5,9},... | collective-permute-start | bytes 712712 | tf_op jit(solution)/shard_map/ppermute | solution.py:418
  19.2 1.6 %collective-permute-start.6 = (bf16[32,3584]{1,0:T(8,128)(2,1)}, bf16[32,3584]{1,0:T(8,128)(2,1)S(1)}, u32[]{:S(2)}, u32[]{:S(2)}) collective-permute-start(bf16[32,3584]{1,0:T(8,128)(2,1)} %refs_0_.1), channel_id=1, source_target_pairs={{0,4},{4,8},{8,12},{12,14},{14,10},{10,6},{6,2},{2,0},{1,5},{5,9},... | collective-permute-start | bytes 688136 | tf_op jit(solution)/shard_map/ppermute | solution.py:420
  21.8 6.9 %collective-permute-done.6.refs_1_ = bf16[32,3584]{1,0:T(8,128)(2,1)S(1)} collective-permute-done((bf16[32,3584]{1,0:T(8,128)(2,1)}, bf16[32,3584]{1,0:T(8,128)(2,1)S(1)}, u32[]{:S(2)}, u32[]{:S(2)}) %collective-permute-start.6) | collective-permute-done | bytes 229408 | tf_op jit(solution)/shard_map/ppermute | solution.py:420
  32.8 3.1 %shard_map.181 = (bf16[3584,1024]{1,0:T(8,128)(2,1)S(1)}, bf16[64,3584]{1,0:T(8,128)(2,1)S(1)}, bf16[64,1024]{1,0:T(8,128)(2,1)S(1)}) custom-call(bf16[3584,1024]{1,0:T(8,128)(2,1)} %bitcast.39, bf16[64,3584]{1,0:T(8,128)(2,1)} %bitcast.40, bf16[64,1024]{1,0:T(8,128)(2,1)} %bitcast.41), custom_call_target="tpu_custom_call" | custom-call | bytes 7 | tf_op jit(solution)/shard_map/pallas_call | solution.py:40
  36.3 1.8 %shard_map.182 = (bf16[128,3712]{1,0:T(8,128)(2,1)S(1)}, bf16[128,3712]{1,0:T(8,128)(2,1)S(1)}, bf16[256,256]{1,0:T(8,128)(2,1)S(1)}, bf16[256,256]{1,0:T(8,128)...) custom-call(s32[12]{0:T(128)S(1)} %concatenate.12.info_ref, ...), custom_call_target="tpu_custom_call" | custom-call | flops 486 | bytes 3 | tf_op jit(solution)/shard_map/pallas_call | solution.py:40
  41.2 6.5 %shard_map.183 = (bf16[256,1024]{1,0:T(8,128)(2,1)S(1)}, f32[256,1024]{1,0:T(8,128)S(1)}, f32[256,1024]{1,0:T(8,128)S(1)}, bf16[256,64]{1,0:T(8,128)(2,1)S(1)}) custom-call(s32[12]{0:T(128)S(1)} %concatenate.12.info_ref, bf16[128,3712]{1,0:T(8,128)(2,1)S(1)} %get-tuple-element.125.kept_ref, bf16[128,3712]{1,0:T(8,128)(2,1)S(1)} %collective-permute-done.11.came_ref, ...), custom_call_target="tpu_custom_call" | custom-call | flops 3758 | bytes 14 | tf_op jit(solution)/shard_map/pallas_call | solution.py:40
  49.9 3.1 %shard_map.184 = (bf16[128,3584]{1,0:T(8,128)(2,1)S(1)}, bf16[128,3584]{1,0:T(8,128)(2,1)S(1)}, bf16[256,64]{1,0:T(8,128)(2,1)S(1)}) custom-call(bf16[256,1024]{1,0:T(8,128)(2,1)S(1)} %get-tuple-element.134.inner_ref, bf16[1024,3584]{1,0:T(8,128)(2,1)S(1)} %bitcast.31, bf16[64,1024]{1,0:T(8,128)(2,1)S(1)} %bitcast.35, bf16[64,3584]{1,0:T(8,128)(2,1)S(1)} %bitcast.33), custom_call_target="tpu_custom_call" | custom-call | flops 1879 | bytes 7 | tf_op jit(solution)/shard_map/pallas_call | solution.py:40
  59.7 4.0 %shard_map.188 = (bf16[256,3584]{1,0:T(8,128)(2,1)S(1)}, bf16[256,1024]{1,0:T(8,128)(2,1)S(1)}, bf16[256,1024]{1,0:T(8,128)(2,1)S(1)}, bf16[256,64]{1,0:T(8,128)(2,1)S(1)}, bf16[256,64]{1,0:T(8,128)(2,1)S(1)}) custom-call(bf16[128,3584]{1,0:T(8,128)(2,1)S(1)} %get-tuple-element.152.kept_ref, bf16[128,3584]{1,0:T(8,128)(2,1)S(1)} %collective-permute-done.17.came_ref, ...), custom_call_target="tpu_custom_call" | custom-call | flops 1879 | bytes 7 | tf_op jit(solution)/shard_map/pallas_call | solution.py:40
  63.8 1.6 %collective-permute-start.20 = (bf16[32,3584]{1,0:T(8,128)(2,1)S(1)}, bf16[32,3584]{1,0:T(8,128)(2,1)S(1)}, u32[]{:S(2)}, u32[]{:S(2)}) collective-permute-start(bf16[32,3584]{1,0:T(8,128)(2,1)S(1)} %get-tuple-element.173), channel_id=1, source_target_pairs={{0,4},{4,8},{8,12},{12,14},{14,10},{10,6},{6,2},{2,0},{1,5},{5,9},... | collective-permute-start | bytes 688136 | tf_op jit(solution)/shard_map/ppermute | solution.py:448
  65.9 4.5 %shard_map.189 = (bf16[128,3584]{1,0:T(8,128)(2,1)S(1)}, bf16[128,3584]{1,0:T(8,128)(2,1)S(1)}) custom-call(bf16[256,1024]{1,0:T(8,128)(2,1)S(1)} %get-tuple-element.158.grad_gate_ref, bf16[256,1024]{1,0:T(8,128)(2,1)S(1)} %get-tuple-element.162.grad_up_ref, bf16[256,64]{1,0:T(8,128)(2,1)S(1)} %get-tuple-element.201.back_up_ref, ...), custom_call_target="tpu_custom_call" | custom-call | flops 3758 | bytes 14 | tf_op jit(solution)/shard_map/pallas_call | solution.py:40
  72.6 1.6 %collective-permute-start.25 = (bf16[32,3584]{1,0:T(8,128)(2,1)S(1)}, bf16[32,3584]{1,0:T(8,128)(2,1)S(1)}, u32[]{:S(2)}, u32[]{:S(2)}) collective-permute-start(bf16[32,3584]{1,0:T(8,128)(2,1)S(1)} %get-tuple-element.182), channel_id=1, source_target_pairs={{0,4},{4,8},{8,12},{12,14},{14,10},{10,6},{6,2},{2,0},{1,5},{5,9},... | collective-permute-start | bytes 688136 | tf_op jit(solution)/shard_map/ppermute | solution.py:448
  74.7 2.5 %collective-permute-start.29 = (bf16[1,16,256]{2,1,0:T(8,128)(2,1)S(1)}, bf16[1,16,256]{2,1,0:T(8,128)(2,1)S(1)}, u32[]{:S(2)}, u32[]{:S(2)}) collective-permute-start(bf16[1,16,256]{2,1,0:T(8,128)(2,1)S(1)} %shard_map.190), channel_id=1, source_target_pairs={{0,8},{2,10},{4,12},{6,14},{8,0},{10,2},{12,4},{14,6},{1,9},{3,11}... | collective-permute-start | bytes 24584 | tf_op jit(solution)/shard_map/ppermute | solution.py:453
  80.0 3.9 %collective-permute-done.29 = bf16[1,16,256]{2,1,0:T(8,128)(2,1)S(1)} collective-permute-done((bf16[1,16,256]{2,1,0:T(8,128)(2,1)S(1)}, bf16[1,16,256]{2,1,0:T(8,128)(2,1)S(1)}, u32[]{:S(2)}, u32[]{:S(2)}) %collective-permute-start.29) | collective-permute-done | bytes 8224 | tf_op jit(solution)/shard_map/ppermute | solution.py:453
  84.7 1.7 %collective-permute-start.30 = (bf16[32,3584]{1,0:T(8,128)(2,1)S(1)}, bf16[32,3584]{1,0:T(8,128)(2,1)S(1)}, u32[]{:S(2)}, u32[]{:S(2)}) collective-permute-start(bf16[32,3584]{1,0:T(8,128)(2,1)S(1)} %get-tuple-element.199), channel_id=1, source_target_pairs={{0,4},{4,8},{8,12},{12,14},{14,10},{10,6},{6,2},{2,0},{1,5},{5,9},... | collective-permute-start | bytes 688136 | tf_op jit(solution)/shard_map/ppermute | solution.py:448
  86.8 1.7 %collective-permute-start.32 = (bf16[2,16,256]{2,1,0:T(8,128)(2,1)S(1)}, bf16[2,16,256]{2,1,0:T(8,128)(2,1)S(1)}, u32[]{:S(2)}, u32[]{:S(2)}) collective-permute-start(bf16[2,16,256]{2,1,0:T(8,128)(2,1)S(1)} %pad_maximum_fusion.2), channel_id=1, source_target_pairs={{0,4},{2,6},{4,0},{6,2},{8,12},{10,14},{12,8},{14,10},{1,5},{3,7},... | collective-permute-start | bytes 49160 | tf_op jit(solution)/shard_map/ppermute | solution.py:453
  88.4 1.8 %shard_map.197 = (bf16[64,3584]{1,0:T(8,128)(2,1)}, bf16[64,1024]{1,0:T(8,128)(2,1)}, bf16[64,1024]{1,0:T(8,128)(2,1)}, bf16[64,3584]{1,0:T(8,128)(2,1)}) custom-call(bf16[128,3712]{1,0:T(8,128)(2,1)S(1)} %get-tuple-element.125.kept_ref, bf16[128,3712]{1,0:T(8,128)(2,1)S(1)} %collective-permute-done.11.came_ref, ...), custom_call_target="tpu_custom_call" | custom-call | flops 469 | bytes 7 | tf_op jit(solution)/shard_map/pallas_call | solution.py:40
  90.2 3.2 %collective-permute-done.32 = bf16[2,16,256]{2,1,0:T(8,128)(2,1)S(1)} collective-permute-done((bf16[2,16,256]{2,1,0:T(8,128)(2,1)S(1)}, bf16[2,16,256]{2,1,0:T(8,128)(2,1)S(1)}, u32[]{:S(2)}, u32[]{:S(2)}) %collective-permute-start.32) | collective-permute-done | bytes 16416 | tf_op jit(solution)/shard_map/ppermute | solution.py:453
  94.0 1.7 %collective-permute-start.34 = (bf16[32,3584]{1,0:T(8,128)(2,1)S(1)}, bf16[32,3584]{1,0:T(8,128)(2,1)S(1)}, u32[]{:S(2)}, u32[]{:S(2)}) collective-permute-start(bf16[32,3584]{1,0:T(8,128)(2,1)S(1)} %get-tuple-element.214), channel_id=1, source_target_pairs={{4,0},{8,4},{12,8},{14,12},{10,14},{6,10},{2,6},{0,2},{5,1},{9,5},... | collective-permute-start | bytes 688136 | tf_op jit(solution)/shard_map/ppermute | solution.py:448
  97.9 4.9 %collective-permute-done.35 = bf16[4,16,256]{2,1,0:T(8,128)(2,1)S(1)} collective-permute-done((bf16[4,16,256]{2,1,0:T(8,128)(2,1)S(1)}, bf16[4,16,256]{2,1,0:T(8,128)(2,1)S(1)}, u32[]{:S(2)}, u32[]{:S(2)}) %collective-permute-start.35) | collective-permute-done | bytes 32800 | tf_op jit(solution)/shard_map/ppermute | solution.py:453
  108.2 1.7 %collective-permute-done.36.forth_ref = bf16[32,3584]{1,0:T(8,128)(2,1)S(1)} collective-permute-done((bf16[32,3584]{1,0:T(8,128)(2,1)S(1)}, bf16[32,3584]{1,0:T(8,128)(2,1)S(1)}, u32[]{:S(2)}, u32[]{:S(2)}) %collective-permute-start.36) | collective-permute-done | bytes 229408 | tf_op jit(solution)/shard_map/ppermute | solution.py:448
  (100 shorter events, 35.9 us)
Async XLA Ops:
  2.0 8.8 %collective-permute-start.3 = (bf16[32,3712]{1,0:T(8,128)(2,1)S(1)}, bf16[32,3712]{1,0:T(8,128)(2,1)S(1)}, u32[]{:S(2)}, u32[]{:S(2)}) collective-permute-start(bf16[32,3712]{1,0:T(8,128)(2,1)S(1)} %shard_map.180.refs_1_), channel_id=1, source_target_pairs={{0,4},{4,8},{8,12},{12,14},{14,10},{10,6},{6,2},{2,0},{1,5},{5,9},... | collective-permute-start | bytes 712712 | tf_op jit(solution)/shard_map/ppermute | solution.py:418
  5.0 9.1 %collective-permute-start = (bf16[32,3712]{1,0:T(8,128)(2,1)S(1)}, bf16[32,3712]{1,0:T(8,128)(2,1)S(1)}, u32[]{:S(2)}, u32[]{:S(2)}) collective-permute-start(bf16[32,3712]{1,0:T(8,128)(2,1)S(1)} %shard_map.180.refs_1_), channel_id=1, source_target_pairs={{4,0},{8,4},{12,8},{14,12},{10,14},{6,10},{2,6},{0,2},{5,1},{9,5},... | collective-permute-start | bytes 712712 | tf_op jit(solution)/shard_map/ppermute | solution.py:420
  14.1 7.1 %collective-permute-start.1 = (bf16[32,3712]{1,0:T(8,128)(2,1)S(1)}, bf16[32,3712]{1,0:T(8,128)(2,1)S(1)}, u32[]{:S(2)}, u32[]{:S(2)}) collective-permute-start(bf16[32,3712]{1,0:T(8,128)(2,1)S(1)} %collective-permute-done.refs_5_), channel_id=1, source_target_pairs={{4,0},{8,4},{12,8},{14,12},{10,14},{6,10},{2,6},{0,2},{5,1},{9,5},... | collective-permute-start | bytes 712712 | tf_op jit(solution)/shard_map/ppermute | solution.py:420
  17.7 11.0 %collective-permute-start.5 = (bf16[32,3712]{1,0:T(8,128)(2,1)S(1)}, bf16[32,3712]{1,0:T(8,128)(2,1)S(1)}, u32[]{:S(2)}, u32[]{:S(2)}) collective-permute-start(bf16[32,3712]{1,0:T(8,128)(2,1)S(1)} %collective-permute-done.4.refs_3_), channel_id=1, source_target_pairs={{0,4},{4,8},{8,12},{12,14},{14,10},{10,6},{6,2},{2,0},{1,5},{5,9},... | collective-permute-start | bytes 712712 | tf_op jit(solution)/shard_map/ppermute | solution.py:418
  19.2 9.5 %collective-permute-start.6 = (bf16[32,3584]{1,0:T(8,128)(2,1)}, bf16[32,3584]{1,0:T(8,128)(2,1)S(1)}, u32[]{:S(2)}, u32[]{:S(2)}) collective-permute-start(bf16[32,3584]{1,0:T(8,128)(2,1)} %refs_0_.1), channel_id=1, source_target_pairs={{0,4},{4,8},{8,12},{12,14},{14,10},{10,6},{6,2},{2,0},{1,5},{5,9},... | collective-permute-start | bytes 688136 | tf_op jit(solution)/shard_map/ppermute | solution.py:420
  20.8 9.3 %collective-permute-start.8 = (bf16[32,3584]{1,0:T(8,128)(2,1)}, bf16[32,3584]{1,0:T(8,128)(2,1)S(1)}, u32[]{:S(2)}, u32[]{:S(2)}) collective-permute-start(bf16[32,3584]{1,0:T(8,128)(2,1)} %refs_0_.1), channel_id=1, source_target_pairs={{4,0},{8,4},{12,8},{14,12},{10,14},{6,10},{2,6},{0,2},{5,1},{9,5},... | collective-permute-start | bytes 688136 | tf_op jit(solution)/shard_map/ppermute | solution.py:418
  21.2 11.6 %collective-permute-start.2 = (bf16[32,3712]{1,0:T(8,128)(2,1)S(1)}, bf16[32,3712]{1,0:T(8,128)(2,1)S(1)}, u32[]{:S(2)}, u32[]{:S(2)}) collective-permute-start(bf16[32,3712]{1,0:T(8,128)(2,1)S(1)} %collective-permute-done.1.refs_6_), channel_id=1, source_target_pairs={{4,0},{8,4},{12,8},{14,12},{10,14},{6,10},{2,6},{0,2},{5,1},{9,5},... | collective-permute-start | bytes 712712 | tf_op jit(solution)/shard_map/ppermute | solution.py:420
  28.7 7.6 %collective-permute-start.7 = (bf16[32,3712]{1,0:T(8,128)(2,1)S(1)}, bf16[32,3712]{1,0:T(8,128)(2,1)S(1)}, u32[]{:S(2)}, u32[]{:S(2)}) collective-permute-start(bf16[32,3712]{1,0:T(8,128)(2,1)S(1)} %collective-permute-done.5.refs_4_), channel_id=1, source_target_pairs={{0,4},{4,8},{8,12},{12,14},{14,10},{10,6},{6,2},{2,0},{1,5},{5,9},... | collective-permute-start | bytes 712712 | tf_op jit(solution)/shard_map/ppermute | solution.py:418
  30.1 8.0 %collective-permute-start.9 = (bf16[32,3584]{1,0:T(8,128)(2,1)S(1)}, bf16[32,3584]{1,0:T(8,128)(2,1)S(1)}, u32[]{:S(2)}, u32[]{:S(2)}) collective-permute-start(bf16[32,3584]{1,0:T(8,128)(2,1)S(1)} %collective-permute-done.8.refs_4_), channel_id=1, source_target_pairs={{4,0},{8,4},{12,8},{14,12},{10,14},{6,10},{2,6},{0,2},{5,1},{9,5},... | collective-permute-start | bytes 688136 | tf_op jit(solution)/shard_map/ppermute | solution.py:418
  30.7 8.0 %collective-permute-start.10 = (bf16[32,3584]{1,0:T(8,128)(2,1)S(1)}, bf16[32,3584]{1,0:T(8,128)(2,1)S(1)}, u32[]{:S(2)}, u32[]{:S(2)}) collective-permute-start(bf16[32,3584]{1,0:T(8,128)(2,1)S(1)} %collective-permute-done.6.refs_1_), channel_id=1, source_target_pairs={{0,4},{4,8},{8,12},{12,14},{14,10},{10,6},{6,2},{2,0},{1,5},{5,9},... | collective-permute-start | bytes 688136 | tf_op jit(solution)/shard_map/ppermute | solution.py:420
  38.7 9.0 %collective-permute-start.12 = (bf16[32,3584]{1,0:T(8,128)(2,1)S(1)}, bf16[32,3584]{1,0:T(8,128)(2,1)S(1)}, u32[]{:S(2)}, u32[]{:S(2)}) collective-permute-start(bf16[32,3584]{1,0:T(8,128)(2,1)S(1)} %collective-permute-done.9.refs_5_), channel_id=1, source_target_pairs={{4,0},{8,4},{12,8},{14,12},{10,14},{6,10},{2,6},{0,2},{5,1},{9,5},... | collective-permute-start | bytes 688136 | tf_op jit(solution)/shard_map/ppermute | solution.py:418
  39.8 7.9 %collective-permute-start.13 = (bf16[32,3584]{1,0:T(8,128)(2,1)S(1)}, bf16[32,3584]{1,0:T(8,128)(2,1)S(1)}, u32[]{:S(2)}, u32[]{:S(2)}) collective-permute-start(bf16[32,3584]{1,0:T(8,128)(2,1)S(1)} %collective-permute-done.10.refs_2_), channel_id=1, source_target_pairs={{0,4},{4,8},{8,12},{12,14},{14,10},{10,6},{6,2},{2,0},{1,5},{5,9},... | collective-permute-start | bytes 688136 | tf_op jit(solution)/shard_map/ppermute | solution.py:420
  63.8 7.9 %collective-permute-start.20 = (bf16[32,3584]{1,0:T(8,128)(2,1)S(1)}, bf16[32,3584]{1,0:T(8,128)(2,1)S(1)}, u32[]{:S(2)}, u32[]{:S(2)}) collective-permute-start(bf16[32,3584]{1,0:T(8,128)(2,1)S(1)} %get-tuple-element.173), channel_id=1, source_target_pairs={{0,4},{4,8},{8,12},{12,14},{14,10},{10,6},{6,2},{2,0},{1,5},{5,9},... | collective-permute-start | bytes 688136 | tf_op jit(solution)/shard_map/ppermute | solution.py:448
  65.4 7.0 %collective-permute-start.21 = (bf16[32,3584]{1,0:T(8,128)(2,1)S(1)}, bf16[32,3584]{1,0:T(8,128)(2,1)S(1)}, u32[]{:S(2)}, u32[]{:S(2)}) collective-permute-start(bf16[32,3584]{1,0:T(8,128)(2,1)S(1)} %get-tuple-element.174), channel_id=1, source_target_pairs={{4,0},{8,4},{12,8},{14,12},{10,14},{6,10},{2,6},{0,2},{5,1},{9,5},... | collective-permute-start | bytes 688136 | tf_op jit(solution)/shard_map/ppermute | solution.py:448
  72.6 11.3 %collective-permute-start.25 = (bf16[32,3584]{1,0:T(8,128)(2,1)S(1)}, bf16[32,3584]{1,0:T(8,128)(2,1)S(1)}, u32[]{:S(2)}, u32[]{:S(2)}) collective-permute-start(bf16[32,3584]{1,0:T(8,128)(2,1)S(1)} %get-tuple-element.182), channel_id=1, source_target_pairs={{0,4},{4,8},{8,12},{12,14},{14,10},{10,6},{6,2},{2,0},{1,5},{5,9},... | collective-permute-start | bytes 688136 | tf_op jit(solution)/shard_map/ppermute | solution.py:448
  74.2 9.7 %collective-permute-start.26 = (bf16[32,3584]{1,0:T(8,128)(2,1)S(1)}, bf16[32,3584]{1,0:T(8,128)(2,1)S(1)}, u32[]{:S(2)}, u32[]{:S(2)}) collective-permute-start(bf16[32,3584]{1,0:T(8,128)(2,1)S(1)} %get-tuple-element.183), channel_id=1, source_target_pairs={{4,0},{8,4},{12,8},{14,12},{10,14},{6,10},{2,6},{0,2},{5,1},{9,5},... | collective-permute-start | bytes 688136 | tf_op jit(solution)/shard_map/ppermute | solution.py:448
  74.7 9.2 %collective-permute-start.29 = (bf16[1,16,256]{2,1,0:T(8,128)(2,1)S(1)}, bf16[1,16,256]{2,1,0:T(8,128)(2,1)S(1)}, u32[]{:S(2)}, u32[]{:S(2)}) collective-permute-start(bf16[1,16,256]{2,1,0:T(8,128)(2,1)S(1)} %shard_map.190), channel_id=1, source_target_pairs={{0,8},{2,10},{4,12},{6,14},{8,0},{10,2},{12,4},{14,6},{1,9},{3,11}... | collective-permute-start | bytes 24584 | tf_op jit(solution)/shard_map/ppermute | solution.py:453
  84.7 8.7 %collective-permute-start.30 = (bf16[32,3584]{1,0:T(8,128)(2,1)S(1)}, bf16[32,3584]{1,0:T(8,128)(2,1)S(1)}, u32[]{:S(2)}, u32[]{:S(2)}) collective-permute-start(bf16[32,3584]{1,0:T(8,128)(2,1)S(1)} %get-tuple-element.199), channel_id=1, source_target_pairs={{0,4},{4,8},{8,12},{12,14},{14,10},{10,6},{6,2},{2,0},{1,5},{5,9},... | collective-permute-start | bytes 688136 | tf_op jit(solution)/shard_map/ppermute | solution.py:448
  86.4 7.0 %collective-permute-start.31 = (bf16[32,3584]{1,0:T(8,128)(2,1)S(1)}, bf16[32,3584]{1,0:T(8,128)(2,1)S(1)}, u32[]{:S(2)}, u32[]{:S(2)}) collective-permute-start(bf16[32,3584]{1,0:T(8,128)(2,1)S(1)} %get-tuple-element.200), channel_id=1, source_target_pairs={{4,0},{8,4},{12,8},{14,12},{10,14},{6,10},{2,6},{0,2},{5,1},{9,5},... | collective-permute-start | bytes 688136 | tf_op jit(solution)/shard_map/ppermute | solution.py:448
  93.5 9.3 %collective-permute-start.33 = (bf16[32,3584]{1,0:T(8,128)(2,1)S(1)}, bf16[32,3584]{1,0:T(8,128)(2,1)S(1)}, u32[]{:S(2)}, u32[]{:S(2)}) collective-permute-start(bf16[32,3584]{1,0:T(8,128)(2,1)S(1)} %get-tuple-element.213), channel_id=1, source_target_pairs={{0,4},{4,8},{8,12},{12,14},{14,10},{10,6},{6,2},{2,0},{1,5},{5,9},... | collective-permute-start | bytes 688136 | tf_op jit(solution)/shard_map/ppermute | solution.py:448
  94.0 8.9 %collective-permute-start.34 = (bf16[32,3584]{1,0:T(8,128)(2,1)S(1)}, bf16[32,3584]{1,0:T(8,128)(2,1)S(1)}, u32[]{:S(2)}, u32[]{:S(2)}) collective-permute-start(bf16[32,3584]{1,0:T(8,128)(2,1)S(1)} %get-tuple-element.214), channel_id=1, source_target_pairs={{4,0},{8,4},{12,8},{14,12},{10,14},{6,10},{2,6},{0,2},{5,1},{9,5},... | collective-permute-start | bytes 688136 | tf_op jit(solution)/shard_map/ppermute | solution.py:448
  95.6 7.2 %collective-permute-start.35 = (bf16[4,16,256]{2,1,0:T(8,128)(2,1)S(1)}, bf16[4,16,256]{2,1,0:T(8,128)(2,1)S(1)}, u32[]{:S(2)}, u32[]{:S(2)}) collective-permute-start(bf16[4,16,256]{2,1,0:T(8,128)(2,1)S(1)} %pad_maximum_fusion.1), channel_id=1, source_target_pairs={{0,2},{2,0},{4,6},{6,4},{8,10},{10,8},{12,14},{14,12},{1,3},{3,1},... | collective-permute-start | bytes 98312 | tf_op jit(solution)/shard_map/ppermute | solution.py:453
  95.8 11.6 %collective-permute-start.27 = (bf16[32,3584]{1,0:T(8,128)(2,1)S(1)}, bf16[32,3584]{1,0:T(8,128)(2,1)S(1)}, u32[]{:S(2)}, u32[]{:S(2)}) collective-permute-start(bf16[32,3584]{1,0:T(8,128)(2,1)S(1)} %get-tuple-element.187), channel_id=1, source_target_pairs={{0,4},{4,8},{8,12},{12,14},{14,10},{10,6},{6,2},{2,0},{1,5},{5,9},... | collective-permute-start | bytes 688136 | tf_op jit(solution)/shard_map/ppermute | solution.py:448
  96.4 11.0 %collective-permute-start.28 = (bf16[32,3584]{1,0:T(8,128)(2,1)S(1)}, bf16[32,3584]{1,0:T(8,128)(2,1)S(1)}, u32[]{:S(2)}, u32[]{:S(2)}) collective-permute-start(bf16[32,3584]{1,0:T(8,128)(2,1)S(1)} %get-tuple-element.188), channel_id=1, source_target_pairs={{4,0},{8,4},{12,8},{14,12},{10,14},{6,10},{2,6},{0,2},{5,1},{9,5},... | collective-permute-start | bytes 688136 | tf_op jit(solution)/shard_map/ppermute | solution.py:448
  (23 other events, 171.7 us)
